TPU v7x, 32 devices: a whole 2x2x4 slice. The times are simulated.
32 devices in a mesh: dp: 4 (over x, core), expert: 8 (over z, y).
Axes of the slice: x: 2, y: 2, z: 4, core: 2. Of those that a mesh axis runs over, the one named last changes fastest.
Arguments:
- tokens: bfloat16 [4096, 3072], P(('dp', 'expert')), may hold values from -6 to 6
- routes: int32 [4096, 2], P(('dp', 'expert')), may hold values from 0 to 7, as said below
- router_gates: int32 [4096, 2], P(('dp', 'expert')), may hold values from 1024 to 32767
- hidden_cotangent: bfloat16 [4096, 2, 768], P(('dp', 'expert')), may hold values from -6 to 6
- weights: bfloat16 [2, 8, 768, 3072], P(None, None, 'expert', 'dp'), may hold values from -0.109375 to 0.109375
- first_moment: bfloat16 [2, 8, 768, 3072], P(None, None, 'expert', 'dp'), may hold values from -6 to 6
- second_moment: bfloat16 [2, 8, 768, 3072], P(None, None, 'expert', 'dp'), may hold values from 0.5 to 4
Outputs:
- token_grads: bfloat16 [4096, 3072], P(('dp', 'expert'))
- new_weights: bfloat16 [2, 8, 768, 3072], P(None, 'expert', None, 'dp')
- new_first: bfloat16 [2, 8, 768, 3072], P(None, 'expert', None, 'dp')
- new_second: bfloat16 [2, 8, 768, 3072], P(None, 'expert', None, 'dp')
Inputs may be any that keep to these rules, and one draw needn't show every extreme that they name: `routes`: each row names 2 different experts; the rows of one device name any one expert at most 48 times.
All inputs are finite; a program needn't handle non-finite values.
Results may differ from a plain program's by a relative error of at most 0.0075.
Values may be sent and summed in bfloat16 or wider, within the bound.
No kernel may reach another device: no remote copies, remote signals or barrier semaphores. Data moves between devices by JAX's collectives and lax.ppermute only.
A program may use at most 128 MiB of HBM per device.

v0:
```python
import jax
import jax.numpy as jnp
from jax import lax
from jax.sharding import PartitionSpec as P

gate_unit = 32768.0
loss_scale = 16.0
beta_one = 0.9
beta_two = 0.95
step_size = 0.001
adam_eps = 1e-08


def per_device(
    tokens, routes, router_gates, hidden_cotangent, weights, first_moment, second_moment
):
    row_count = tokens.shape[0]
    model_width = tokens.shape[1]
    per_token = routes.shape[1]
    hidden_units = hidden_cotangent.shape[2]
    experts = weights.shape[1]
    capacity = 3 * row_count * per_token // (2 * experts)
    routings = row_count * per_token
    owned_weights, owned_first, owned_second = (
        lax.all_to_all(weights, "expert", split_axis=1, concat_axis=2, tiled=True),
        lax.all_to_all(first_moment, "expert", split_axis=1, concat_axis=2, tiled=True),
        lax.all_to_all(second_moment, "expert", split_axis=1, concat_axis=2, tiled=True),
    )
    full_weights = lax.all_gather(owned_weights, "dp", axis=3, tiled=True)[:, 0]
    flat_route = routes.reshape(-1)
    onehot = (flat_route[:, None] == jnp.arange(experts, dtype=jnp.int32)[None, :]).astype(
        jnp.int32
    )
    position = jnp.sum((jnp.cumsum(onehot, axis=0) - onehot) * onehot, axis=1)
    target = flat_route * capacity + position
    routing_ids = jnp.arange(routings, dtype=jnp.int32)
    slot_table = jnp.full((experts * capacity,), routings, jnp.int32).at[target].set(routing_ids)
    filled = slot_table < routings
    token_index = jnp.where(filled, slot_table // per_token, 0)
    gate_factor = router_gates.astype(jnp.float32) / gate_unit
    scaled = (gate_factor[:, :, None] * hidden_cotangent.astype(jnp.float32)).astype(jnp.bfloat16)
    scaled = scaled.reshape(routings, hidden_units)
    send_rows = jnp.where(
        filled[:, None], jnp.take(tokens, token_index, axis=0), jnp.zeros((), jnp.bfloat16)
    )
    send_rows = send_rows.reshape(experts, capacity, model_width)
    send_grads = jnp.where(
        filled[:, None],
        jnp.take(scaled, jnp.minimum(slot_table, routings - 1), axis=0),
        jnp.zeros((), jnp.bfloat16),
    )
    send_grads = send_grads.reshape(experts, capacity, hidden_units)
    rows_in = lax.all_to_all(send_rows, "expert", split_axis=0, concat_axis=0, tiled=True)
    grads_in = lax.all_to_all(send_grads, "expert", split_axis=0, concat_axis=0, tiled=True)
    sources = rows_in.shape[0]
    slots_in = rows_in.shape[1]
    flat_rows = rows_in.reshape(sources * slots_in, model_width)
    projected = jnp.einsum(
        "rd,ahd->rah", flat_rows, full_weights, preferred_element_type=jnp.float32
    )
    pre_gate = projected[:, 0]
    pre_up = projected[:, 1]
    sigmoid_gate = jax.nn.sigmoid(pre_gate)
    upstream = grads_in.reshape(sources * slots_in, hidden_units).astype(jnp.float32)
    grad_up = (upstream * pre_gate * sigmoid_gate).astype(jnp.bfloat16)
    grad_gate = (upstream * pre_up * sigmoid_gate * (1.0 + pre_gate * (1.0 - sigmoid_gate))).astype(
        jnp.bfloat16
    )
    paired = jnp.stack([grad_gate, grad_up], axis=1)
    backward = jnp.einsum(
        "rah,ahd->rd", paired, full_weights, preferred_element_type=jnp.float32
    ).astype(jnp.bfloat16)
    backward, paired, received = (
        backward.reshape(sources, slots_in, model_width),
        paired.reshape(sources, slots_in, 2, hidden_units),
        rows_in,
    )
    returned = lax.all_to_all(backward, "expert", split_axis=0, concat_axis=0, tiled=True)
    selector = (token_index[None, :] == jnp.arange(row_count, dtype=jnp.int32)[:, None]) & filled[
        None, :
    ]
    token_grads = jnp.dot(
        selector.astype(jnp.bfloat16),
        returned.reshape(experts * capacity, model_width),
        preferred_element_type=jnp.float32,
    ).astype(jnp.bfloat16)
    received_count = received.shape[0] * received.shape[1]
    rows_mat = received.reshape(received_count, model_width)
    paired_mat = paired.reshape(received_count, 2, hidden_units)
    partial_sum = jnp.einsum(
        "rah,rd->ahd", paired_mat, rows_mat, preferred_element_type=jnp.float32
    )
    summed = lax.psum_scatter(
        partial_sum.astype(jnp.bfloat16), "dp", scatter_dimension=2, tiled=True
    ).astype(jnp.float32)
    gradient = (summed / loss_scale)[:, None]
    moment_one = beta_one * owned_first.astype(jnp.float32) + (1.0 - beta_one) * gradient
    moment_two = (
        beta_two * owned_second.astype(jnp.float32) + (1.0 - beta_two) * gradient * gradient
    )
    updated = owned_weights.astype(jnp.float32) - step_size * moment_one / (
        jnp.sqrt(moment_two) + adam_eps
    )
    return (
        token_grads,
        updated.astype(jnp.bfloat16),
        moment_one.astype(jnp.bfloat16),
        moment_two.astype(jnp.bfloat16),
    )


def solution(mesh):
    placed = (
        P(("dp", "expert"), None),
        P(("dp", "expert"), None),
        P(("dp", "expert"), None),
        P(("dp", "expert"), None, None),
        P(None, None, "expert", "dp"),
        P(None, None, "expert", "dp"),
        P(None, None, "expert", "dp"),
    )
    return jax.shard_map(
        per_device,
        mesh=mesh,
        in_specs=placed,
        out_specs=(
            P(("dp", "expert"), None),
            P(None, "expert", None, "dp"),
            P(None, "expert", None, "dp"),
            P(None, "expert", None, "dp"),
        ),
        check_vma=False,
    )
```

profile of v0, /device:TPU:0, one launch (start us, length us, event | category | flops | bytes accessed | tf_op | source)
XLA Modules:
  0.0 368.5 jit_solution(11217551472732781222)
XLA Ops:
  7.2 1.9 copy.28
  9.1 60.9 %all_to_all.45 = bf16[2,8,96,768]{3,2,0,1:T(8,128)(2,1)S(1)} all-to-all(bf16[2,8,96,768]{3,2,0,1:T(8,128)(2,1)S(1)} %copy.28), channel_id=1, replica_groups=mesh['dp'=4,'expert'=8] {'expert'}, dimensions={1} | all-to-all | bytes 4718592 | tf_op jit(solution)/shard_map/all_to_all | solution.py:25
  70.1 1.6 copy.29
  71.6 0.7 copy-done.6
  72.3 0.1 copy.25
  72.4 0.1 eq.42
  72.6 0.1 eq.38
  72.7 0.1 copy.24
  72.8 0.1 mul.98
  73.0 0.6 reduce-window.6
  73.6 0.2 slice_reduce_fusion
  73.8 0.1 fusion.22
  73.9 1.4 scatter_custom_fusion
  75.4 0.1 broadcast_in_dim.73
  75.4 0.1 broadcast_in_dim.65
  75.6 3.6 gather_fusion.1
  79.1 4.0 %select_select_fusion = bf16[8,48,3072]{2,1,0:T(8,128)(2,1)} fusion(bf16[8,48,3072]{2,1,0:T(8,128)(2,1)} %bitcast.60, pred[8,48]{1,0:T(8,128)(4,1)S(1)} %broadcast_in_dim.73, pred[8,48]{1,0:T(8,128)(4,1)S(1)} %broadcast_in_dim.65), kind=kLoop, calls=%fused_computation.22 | loop fusion | flops 2359296 | bytes 4719360 | tf_op jit(solution)/shard_map/jit(_where)/select_n | solution.py:43
  83.1 4.5 %all-to-all-start.1 = ((bf16[8,48,3072]{2,1,0:T(8,128)(2,1)}), bf16[8,48,3072]{2,1,0:T(8,128)(2,1)}, u32[]{:S(2)}, u32[]{:S(2)}) async-start(bf16[8,48,3072]{2,1,0:T(8,128)(2,1)} %select_select_fusion), calls=%async_computation.1 | async-start | bytes 4718592 | tf_op jit(solution)/shard_map/all_to_all | solution.py:53
  87.6 0.1 copy.27
  87.8 0.4 multiply_convert_fusion
  88.2 0.1 reshape.157
  88.4 2.6 gather_fusion
  91.1 2.0 select_select_fusion.1
  93.1 47.3 %all-to-all-done.1 = bf16[8,48,3072]{2,1,0:T(8,128)(2,1)} async-done(((bf16[8,48,3072]{2,1,0:T(8,128)(2,1)}), bf16[8,48,3072]{2,1,0:T(8,128)(2,1)}, u32[]{:S(2)}, u32[]{:S(2)}) %all-to-all-start.1) | async-done | bytes 2359328 | tf_op jit(solution)/shard_map/all_to_all | solution.py:53
  140.4 3.6 all-to-all-start
  144.1 0.2 reduce-scatter.2.cloned.1.call-start
  144.3 9.7 %fusion.2 = f32[384,2,768]{2,0,1:T(8,128)} fusion(bf16[384,3072,1]{1,0,2:T(8,128)(2,1)} %bitcast.8, bf16[2,1,768,3072]{3,2,0,1:T(8,128)(2,1)} %all-gather.2.cloned.1.call-done), kind=kOutput, calls=%fused_computation.5 | convolution fusion | flops 3623878656 | bytes 14155776 | tf_op jit(solution)/shard_map/rd,ahd->rah/dot_general | solution.py:58
  154.0 6.2 %all-to-all-done = bf16[8,48,768]{2,1,0:T(8,128)(2,1)S(1)} async-done(((bf16[8,48,768]{2,1,0:T(8,128)(2,1)}), bf16[8,48,768]{2,1,0:T(8,128)(2,1)S(1)}, u32[]{:S(2)}, u32[]{:S(2)}) %all-to-all-start) | async-done | bytes 589856 | tf_op jit(solution)/shard_map/all_to_all | solution.py:54
  160.1 2.2 fusion.14
  162.3 0.8 copy-done.2
  163.1 0.2 copy-done.4
  163.3 9.2 %convolution_convert_fusion = bf16[2,768,3072]{2,1,0:T(8,128)(2,1)} fusion(bf16[384,3072,1]{1,0,2:T(8,128)(2,1)} %bitcast.8, bf16[384,1,768]{2,0,1:T(8,128)(2,1)S(1)} %get-tuple-element.22, bf16[384,1,768]{2,0,1:T(8,128)(2,1)S(1)} %get-tuple-element.21), kind=kOutput, calls=%fused_computation.10 | convolution fusion | flops 3629187072 | bytes 12976128 | tf_op jit(solution)/shard_map/rah,rd->ahd/dot_general | solution.py:90
  172.6 3.2 copy.34
  175.8 4.4 %all-to-all-start.5 = ((bf16[2,8,96,768]{3,2,0,1:T(8,128)(2,1)}), bf16[2,8,96,768]{3,2,0,1:T(8,128)(2,1)}, u32[]{:S(2)}, u32[]{:S(2)}) async-start(bf16[2,8,96,768]{3,2,0,1:T(8,128)(2,1)} %copy.34), calls=%async_computation.6 | async-start | bytes 4718592 | tf_op jit(solution)/shard_map/all_to_all | solution.py:27
  180.2 3.9 %copy.31 = bf16[2,8,96,768]{3,2,0,1:T(8,128)(2,1)} copy(bf16[2,8,96,768]{3,2,1,0:T(8,128)(2,1)} %param.12) | data formatting | bytes 4718592 | tf_op args[5]
  184.0 49.5 %all-to-all-done.5 = bf16[2,8,96,768]{3,2,0,1:T(8,128)(2,1)} async-done(((bf16[2,8,96,768]{3,2,0,1:T(8,128)(2,1)}), bf16[2,8,96,768]{3,2,0,1:T(8,128)(2,1)}, u32[]{:S(2)}, u32[]{:S(2)}) %all-to-all-start.5) | async-done | bytes 2359328 | tf_op jit(solution)/shard_map/all_to_all | solution.py:27
  233.6 4.4 %all-to-all-start.4 = ((bf16[2,8,96,768]{3,2,0,1:T(8,128)(2,1)}), bf16[2,8,96,768]{3,2,0,1:T(8,128)(2,1)}, u32[]{:S(2)}, u32[]{:S(2)}) async-start(bf16[2,8,96,768]{3,2,0,1:T(8,128)(2,1)} %copy.31), calls=%async_computation.4 | async-start | bytes 4718592 | tf_op jit(solution)/shard_map/all_to_all | solution.py:26
  238.0 9.1 %bitcast_convert_fusion = bf16[384,3072]{1,0:T(8,128)(2,1)} fusion(bf16[2,1,768,3072]{3,2,0,1:T(8,128)(2,1)} %all-gather.2.cloned.1.call-done, bf16[384,1,768]{2,0,1:T(8,128)(2,1)} %copy-done.4, bf16[384,1,768]{2,0,1:T(8,128)(2,1)S(1)} %copy-done.3), kind=kOutput, calls=%fused_computation.16 | convolution fusion | flops 3625648128 | bytes 12976128 | tf_op jit(solution)/shard_map/rah,ahd->rd/dot_general | solution.py:70
  247.1 44.3 %all-to-all-done.4 = bf16[2,8,96,768]{3,2,0,1:T(8,128)(2,1)} async-done(((bf16[2,8,96,768]{3,2,0,1:T(8,128)(2,1)}), bf16[2,8,96,768]{3,2,0,1:T(8,128)(2,1)}, u32[]{:S(2)}, u32[]{:S(2)}) %all-to-all-start.4) | async-done | bytes 2359328 | tf_op jit(solution)/shard_map/all_to_all | solution.py:26
  291.4 4.6 %all-to-all-start.3 = ((bf16[8,48,3072]{2,1,0:T(8,128)(2,1)}), bf16[8,48,3072]{2,1,0:T(8,128)(2,1)}, u32[]{:S(2)}, u32[]{:S(2)}) async-start(bf16[8,48,3072]{2,1,0:T(8,128)(2,1)} %bitcast.65), calls=%async_computation.3 | async-start | bytes 4718592 | tf_op jit(solution)/shard_map/all_to_all | solution.py:78
  296.0 2.2 convert_multiply_fusion.3
  298.2 2.6 copy.35
  300.8 2.2 convert_multiply_fusion.4
  303.0 2.5 copy.32
  305.5 2.7 copy.30
  308.2 41.1 %all-to-all-done.3 = bf16[8,48,3072]{2,1,0:T(8,128)(2,1)} async-done(((bf16[8,48,3072]{2,1,0:T(8,128)(2,1)}), bf16[8,48,3072]{2,1,0:T(8,128)(2,1)}, u32[]{:S(2)}, u32[]{:S(2)}) %all-to-all-start.3) | async-done | bytes 2359328 | tf_op jit(solution)/shard_map/all_to_all | solution.py:78
  349.2 3.1 convolution_convert_fusion.1
  352.4 9.3 %fusion.11 = (bf16[2,768,768]{2,1,0:T(8,128)(2,1)}, bf16[2,768,768]{2,1,0:T(8,128)(2,1)}, bf16[2,768,768]{2,1,0:T(8,128)(2,1)}) fusion(bf16[2,768,768]{2,1,0:T(8,128)(2,1)} %reduce-scatter.2.cloned.1.call-done, f32[2,8,96,768]{3,2,1,0:T(8,128)} %copy.35, f32[2,8,96,768]{3,2,1,0:T(8,128)} %copy.32, f32[2,8,96,768]{3,2,1,0:T(8,128)} %copy.30), kind=kLoop, calls=%fused_computation.21 | loop fusion | flops 16515072 | bytes 23592960 | tf_op jit(solution)/shard_map/convert_element_type | solution.py:108
  (31 shorter events, 0.3 us)
Async XLA Ops:
  7.2 68.4 %copy-start = (bf16[128,3072]{1,0:T(8,128)(2,1)S(1)}, bf16[128,3072]{1,0:T(8,128)(2,1)}, u32[]{:S(2)}) copy-start(bf16[128,3072]{1,0:T(8,128)(2,1)} %param.7) | copy-start | bytes 2359300
  7.2 137.1 %all-gather.2.cloned.1.call-start = ((), (), s32[]{:S(2)}) async-start(), calls=%async_computation.7 | async-start | bytes 11796480 | tf_op jit(solution)/shard_map/all_gather | solution.py:29
  71.6 0.7 copy-start.6
  83.1 4.5 %copy-start.7 = (s32[128,2]{0,1:T(2,128)S(1)}, s32[128,2]{0,1:T(2,128)}, u32[]{:S(2)}) copy-start(s32[128,2]{0,1:T(2,128)} %param.9) | copy-start | bytes 3076
  83.1 4.6 %copy-start.5 = (bf16[128,2,768]{2,1,0:T(2,128)(2,1)S(1)}, bf16[128,2,768]{2,1,0:T(2,128)(2,1)}, u32[]{:S(2)}) copy-start(bf16[128,2,768]{2,1,0:T(2,128)(2,1)} %param.10) | copy-start | bytes 1179652
  83.1 57.3 %all-to-all-start.1 = ((bf16[8,48,3072]{2,1,0:T(8,128)(2,1)}), bf16[8,48,3072]{2,1,0:T(8,128)(2,1)}, u32[]{:S(2)}, u32[]{:S(2)}) async-start(bf16[8,48,3072]{2,1,0:T(8,128)(2,1)} %select_select_fusion), calls=%async_computation.1 | async-start | bytes 4718592 | tf_op jit(solution)/shard_map/all_to_all | solution.py:53
  140.4 19.7 %all-to-all-start = ((bf16[8,48,768]{2,1,0:T(8,128)(2,1)}), bf16[8,48,768]{2,1,0:T(8,128)(2,1)S(1)}, u32[]{:S(2)}, u32[]{:S(2)}) async-start(bf16[8,48,768]{2,1,0:T(8,128)(2,1)} %select_select_fusion.1), calls=%async_computation | async-start | bytes 1179648 | tf_op jit(solution)/shard_map/all_to_all | solution.py:54
  144.1 208.3 %reduce-scatter.2.cloned.1.call-start = ((), (), s32[]{:S(2)}) async-start(), calls=%async_computation.8 | async-start | bytes 11796480 | tf_op jit(solution)/shard_map/reduce_scatter | solution.py:93
  162.3 0.8 copy-start.2
  162.3 1.0 copy-start.4
  175.8 57.8 %all-to-all-start.5 = ((bf16[2,8,96,768]{3,2,0,1:T(8,128)(2,1)}), bf16[2,8,96,768]{3,2,0,1:T(8,128)(2,1)}, u32[]{:S(2)}, u32[]{:S(2)}) async-start(bf16[2,8,96,768]{3,2,0,1:T(8,128)(2,1)} %copy.34), calls=%async_computation.6 | async-start | bytes 4718592 | tf_op jit(solution)/shard_map/all_to_all | solution.py:27
  184.0 53.9 %copy-start.3 = (bf16[384,1,768]{2,0,1:T(8,128)(2,1)S(1)}, bf16[384,1,768]{2,0,1:T(8,128)(2,1)}, u32[]{:S(2)}) copy-start(bf16[384,1,768]{2,0,1:T(8,128)(2,1)} %copy-done.2) | copy-start | bytes 1769476
  233.6 57.8 %all-to-all-start.4 = ((bf16[2,8,96,768]{3,2,0,1:T(8,128)(2,1)}), bf16[2,8,96,768]{3,2,0,1:T(8,128)(2,1)}, u32[]{:S(2)}, u32[]{:S(2)}) async-start(bf16[2,8,96,768]{3,2,0,1:T(8,128)(2,1)} %copy.31), calls=%async_computation.4 | async-start | bytes 4718592 | tf_op jit(solution)/shard_map/all_to_all | solution.py:26
  291.4 57.9 %all-to-all-start.3 = ((bf16[8,48,3072]{2,1,0:T(8,128)(2,1)}), bf16[8,48,3072]{2,1,0:T(8,128)(2,1)}, u32[]{:S(2)}, u32[]{:S(2)}) async-start(bf16[8,48,3072]{2,1,0:T(8,128)(2,1)} %bitcast.65), calls=%async_computation.3 | async-start | bytes 4718592 | tf_op jit(solution)/shard_map/all_to_all | solution.py:78
  352.4 9.3 %copy-start.1 = (bf16[128,3072]{1,0:T(8,128)(2,1)S(1)}, bf16[128,3072]{1,0:T(8,128)(2,1)}, u32[]{:S(2)}) copy-start(bf16[128,3072]{1,0:T(8,128)(2,1)} %param.7) | copy-start | bytes 2359300
Sparse Core Ops, SparseCore 0:
  71.8 63.2 all-gather.1
  172.7 77.4 reduce-scatter.1
where the time goes:
time: 369 us; the launch traced here: 368 us
  waiting for transfers between devices  188 us (51%)
  blocking collectives  60.9 us (17%)
  matrix products  31.1 us (8%)
  local copies, waits for them, and re-layouts  29.1 us (8%)
  other arithmetic  23 us (6%)
  starting transfers between devices  21.7 us (6%)
  between operations  14.2 us (4%)
    all_to_all x1, blocking collectives, per_device(): lax.all_to_all(weights, 'expert', split_axis=1, concat_axis=2, tiled=True)  60.9 us
    all_to_all x1, waiting for transfers between devices, per_device(): lax.all_to_all(second_moment, 'expert', split_axis=1, concat_axis=2, tile...  49.5 us
    all_to_all x1, waiting for transfers between devices, per_device(): lax.all_to_all(send_rows, 'expert', split_axis=0, concat_axis=0, tiled=True)  47.3 us
    all_to_all x1, waiting for transfers between devices, per_device(): lax.all_to_all(first_moment, 'expert', split_axis=1, concat_axis=2, tiled...  44.3 us
    all_to_all x1, waiting for transfers between devices, per_device(): lax.all_to_all(backward, 'expert', split_axis=0, concat_axis=0, tiled=True)  41.1 us
    unnamed x20, local copies, waits for them, and re-layouts  10.8 us
    dot_general x1, matrix products, per_device(): jnp.einsum('rd,ahd->rah', flat_rows, full_weights, preferred_element_type...  9.65 us
    convert_element_type x1, other arithmetic, per_device(): moment_two.astype(jnp.bfloat16)  9.25 us
  transfers between devices with their start and end apart: 7, of which 5 were waited for; matrix products, arithmetic and copies ran while one was open for 16% of the time, Pallas kernels for 0%

commit v1 on v0

v1 whole, which is shorter than its diff:
```python
import jax
import jax.numpy as jnp
from jax import lax
from jax.experimental import pallas as pl
from jax.experimental.pallas import tpu as pltpu
from jax.sharding import PartitionSpec as P

gate_unit = 32768.0
loss_scale = 16.0
beta_one = 0.9
beta_two = 0.95
step_size = 0.001
adam_eps = 1e-08


def slot_targets(flat_route, capacity):
    count = flat_route.shape[-1]
    order = jnp.arange(count, dtype=jnp.int32)
    earlier = order[None, :] < order[:, None]
    same = flat_route[:, None] == flat_route[None, :]
    position = jnp.sum((same & earlier).astype(jnp.int32), axis=-1)
    return flat_route * capacity + position


def after(value, *others):
    return lax.optimization_barrier((value, *others))[0]


def adam_step(summed, old, first_old, second_old, *refs):
    f32 = jnp.float32
    weights_out, first_out, second_out = refs[-3:]
    gradient = summed[...].astype(f32) / loss_scale
    moment_one = beta_one * first_old[...].astype(f32) + (1.0 - beta_one) * gradient
    moment_two = beta_two * second_old[0, 0].astype(f32) + (1.0 - beta_two) * gradient * gradient
    updated = old[...].astype(f32) - step_size * moment_one / (jnp.sqrt(moment_two) + adam_eps)
    weights_out[0, 0] = updated.astype(weights_out.dtype)
    first_out[0, 0] = moment_one.astype(first_out.dtype)
    second_out[0, 0] = moment_two.astype(second_out.dtype)


def adam(index, summed, old, first_old, second_old, *results):
    rows, width = old.shape
    sources, _, part, _ = second_old.shape
    flat = pl.BlockSpec((part, width), lambda i: (i, 0))
    second = pl.BlockSpec((1, 1, part, width), lambda i: (i, index, 0, 0))
    out = pl.BlockSpec((1, 1, part, width), lambda i: (index, 0, i, 0))
    shape = jax.ShapeDtypeStruct((2, 1, rows, width), old.dtype)
    return pl.pallas_call(
        adam_step,
        grid=(sources,),
        in_specs=[flat] * 3 + [second] + [pl.BlockSpec(memory_space=pl.ANY)] * len(results),
        out_specs=[out] * 3,
        out_shape=[shape] * 3,
        input_output_aliases={4 + i: i for i in range(len(results))},
        cost_estimate=pl.CostEstimate(
            flops=20 * old.size, bytes_accessed=14 * old.size, transcendentals=2 * old.size
        ),
        compiler_params=pltpu.CompilerParams(vmem_limit_bytes=60 * 1024 * 1024),
    )(summed, old, first_old, second_old, *results)


def per_device(
    tokens, routes, router_gates, hidden_cotangent, weights, first_moment, second_moment
):
    row_count, model_width = tokens.shape
    per_token = routes.shape[1]
    hidden_units = hidden_cotangent.shape[2]
    experts = weights.shape[1]
    capacity = 3 * row_count * per_token // (2 * experts)
    routings = row_count * per_token
    bf16 = jnp.bfloat16
    f32 = jnp.float32
    half = experts // 2
    mine = lax.axis_index("expert")
    side = mine // half
    local = mine % half
    swap = [(i, (i + half) % experts) for i in range(experts)]

    def shift(value, step):
        if step % half == 0:
            return value
        pairs = [(i, i // half * half + (i + step) % half) for i in range(experts)]
        return lax.ppermute(value, "expert", pairs)

    def slot_ids(of_side):
        expert = of_side * half + (local + jnp.arange(half, dtype=jnp.int32)) % half
        return expert[:, None] * capacity + jnp.arange(capacity, dtype=jnp.int32)[None, :]

    def to_owners(part):
        return lax.all_to_all(part, "expert", split_axis=0, concat_axis=1, tiled=True)[0]

    def over_dp(part):
        return lax.all_gather(part, "dp", axis=1, tiled=True)

    other_tokens = lax.ppermute(tokens, "expert", swap)
    other_routes = lax.ppermute(routes, "expert", swap)

    owned_gate = to_owners(weights[0])
    gate_factor = router_gates.astype(f32) / gate_unit
    scaled = (gate_factor[:, :, None] * hidden_cotangent.astype(f32)).astype(bf16)
    scaled = scaled.reshape(routings, hidden_units)
    target = slot_targets(routes.reshape(-1), capacity)
    other_target = slot_targets(other_routes.reshape(-1), capacity)
    near_ids = slot_ids(side)
    far_ids = slot_ids(1 - side)

    def pick_grads(ids, scaled):
        chosen = (target[None, :] == ids.reshape(-1)[:, None]).astype(bf16)
        picked = jnp.dot(chosen, scaled, preferred_element_type=f32).astype(bf16)
        return picked.reshape(half, capacity, hidden_units)

    far_grads = lax.ppermute(pick_grads(far_ids, after(scaled, owned_gate)), "expert", swap)
    grads_out = jnp.concatenate([far_grads, pick_grads(near_ids, scaled)], axis=1)
    grads_in = [shift(grads_out[s], s) for s in range(half)]
    upstream = jnp.swapaxes(jnp.stack(grads_in).reshape(half, 2, capacity, hidden_units), 0, 1)

    def pick_matrix(chosen_target):
        by_token = chosen_target.reshape(row_count, per_token)
        hit = by_token[None, :, :] == near_ids.reshape(-1)[:, None, None]
        return jnp.any(hit, axis=2).astype(bf16)

    near_pick = pick_matrix(target)
    other_pick = pick_matrix(other_target)

    def send_rows(picker, rows):
        picked = jnp.dot(picker, rows, preferred_element_type=f32).astype(bf16)
        picked = picked.reshape(half, capacity, model_width)
        return [shift(picked[s], s) for s in range(half)]

    near_rows = send_rows(near_pick, tokens)
    other_tokens = after(other_tokens, other_routes, *near_rows[1:])
    full_gate = over_dp(after(owned_gate, other_tokens))
    owned_up = to_owners(after(weights[1], owned_gate, other_tokens))
    far_rows = send_rows(other_pick, other_tokens)
    full_up = over_dp(after(owned_up, far_grads, *far_rows[1:]))
    flat_rows = jnp.concatenate(far_rows + near_rows, axis=0)

    first_gate = to_owners(after(first_moment[0], owned_up))
    first_up = to_owners(after(first_moment[1], first_gate))

    slots = flat_rows.shape[0]
    pre_gate = jnp.einsum("rd,hd->rh", flat_rows, full_gate, preferred_element_type=f32)
    pre_up = jnp.einsum("rd,hd->rh", flat_rows, full_up, preferred_element_type=f32)
    sigmoid_gate = jax.nn.sigmoid(pre_gate)
    upstream = upstream.reshape(slots, hidden_units).astype(f32)
    grad_up = (upstream * pre_gate * sigmoid_gate).astype(bf16)
    grad_gate = (upstream * pre_up * sigmoid_gate * (1.0 + pre_gate * (1.0 - sigmoid_gate))).astype(
        bf16
    )

    def weight_grad(grads, *earlier):
        total = jnp.einsum("rh,rd->hd", grads, flat_rows, preferred_element_type=f32)
        total = after(total.astype(bf16), *earlier)
        return lax.psum_scatter(total, "dp", scatter_dimension=1, tiled=True)

    up_sum = weight_grad(after(grad_up, first_gate))
    backward = (
        jnp.dot(grad_gate, full_gate, preferred_element_type=f32)
        + jnp.dot(grad_up, full_up, preferred_element_type=f32)
    ).astype(bf16)
    by_half = backward.reshape(2, half, capacity, model_width)
    far_back = [shift(by_half[0, s], -s) for s in range(half)]
    near_back = [shift(by_half[1, s], -s) for s in range(half)]
    gate_sum = weight_grad(after(grad_gate, backward), first_up, *far_back[1:])
    owned_second = lax.all_to_all(
        after(second_moment, first_up), "expert", split_axis=1, concat_axis=0
    )

    def combine(picker, rows):
        rows = jnp.concatenate(rows, axis=0)
        return jnp.einsum("st,sd->td", picker, rows, preferred_element_type=f32)

    far_sum = after(combine(other_pick, far_back).astype(bf16), owned_second)
    far_sum = lax.ppermute(far_sum, "expert", swap)
    results = adam(1, up_sum, owned_up, first_up, owned_second)
    results = adam(0, gate_sum, owned_gate, first_gate, owned_second, *results)
    near_back[1] = after(near_back[1], *results)
    token_grads = (combine(near_pick, near_back) + far_sum.astype(f32)).astype(bf16)
    return (token_grads, *results)


def solution(mesh):
    placed = (
        P(("dp", "expert"), None),
        P(("dp", "expert"), None),
        P(("dp", "expert"), None),
        P(("dp", "expert"), None, None),
        P(None, None, "expert", "dp"),
        P(None, None, "expert", "dp"),
        P(None, None, "expert", "dp"),
    )
    return jax.shard_map(
        per_device,
        mesh=mesh,
        in_specs=placed,
        out_specs=(
            P(("dp", "expert"), None),
            P(None, "expert", None, "dp"),
            P(None, "expert", None, "dp"),
            P(None, "expert", None, "dp"),
        ),
        check_vma=False,
    )
```

time: 369 us -> 317 us (0.86)
  blocking collectives: 60.9 us -> 0 us
  starting transfers between devices: 21.7 us -> 57.3 us
  waiting for transfers between devices: 188 us -> 165 us
  other arithmetic: 23 us -> 2.19 us
  Pallas kernels: 0 us -> 14.6 us
  matrix products: 31.1 us -> 37.6 us
  local copies, waits for them, and re-layouts: 29.1 us -> 23.7 us
    all_to_all x5, waiting for transfers between devices: 188 us -> 59.5 us  [the longest x1 49.3 us: per_device(): lax.all_to_all(after(second_moment, first_up), 'expert', split_axis=1, co...]
    ppermute x0 -> x19, waiting for transfers between devices: none -> 106 us  [the longest x15 98.2 us: shift(): return lax.ppermute(value, 'expert', pairs)]
    all_to_all x1 -> x0, blocking collectives: 60.9 us -> none  [per_device(): lax.all_to_all(weights, 'expert', split_axis=1, concat_axis=2, tiled=True)]
    ppermute x0 -> x19, starting transfers between devices: none -> 27.8 us  [the longest x15 21.2 us: shift(): return lax.ppermute(value, 'expert', pairs)]
    pallas_call x0 -> x2, Pallas kernels: none -> 14.6 us  [adam(): pl.pallas_call(adam_step, grid=(sources,), in_specs=[flat] * 3 + [second]...]
    convert_element_type x4 -> x2, other arithmetic: 11.8 us -> 0.48 us  [the longest x1 0.38 us: per_device(): (gate_factor[:, :, None] * hidden_cotangent.astype(f32)).astype(bf16)]
    all_to_all x5, starting transfers between devices: 21.5 us -> 29.1 us  [the longest x4 20.3 us: to_owners(): lax.all_to_all(part, 'expert', split_axis=0, concat_axis=1, tiled=True)[0]]
    squeeze x0 -> x3, local copies, waits for them, and re-layouts: none -> 7.6 us  [the longest x1 3.28 us: per_device(): first_gate = to_owners(after(first_moment[0], owned_up))]
  transfers between devices with their start and end apart: 7 -> 28, of which waited for: 5 -> 18; matrix products, arithmetic and copies ran while one was open for 16% -> 17% of each run, Pallas kernels for 0% -> 5%
where the time goes in v1:
time: 317 us; the launch traced here: 315 us
  waiting for transfers between devices  165 us (52%)
  starting transfers between devices  57.3 us (18%)
  matrix products  37.6 us (12%)
  local copies, waits for them, and re-layouts  23.7 us (7%)
  Pallas kernels  14.6 us (5%)
  between operations  14.2 us (4%)
    ppermute x15, waiting for transfers between devices, shift(): return lax.ppermute(value, 'expert', pairs)  98.2 us
    all_to_all x1, waiting for transfers between devices, per_device(): lax.all_to_all(after(second_moment, first_up), 'expert', split_axis=1, co...  49.3 us
    ppermute x15, starting transfers between devices, shift(): return lax.ppermute(value, 'expert', pairs)  21.2 us
    all_to_all x4, starting transfers between devices, to_owners(): lax.all_to_all(part, 'expert', split_axis=0, concat_axis=1, tiled=True)[0]  20.3 us
    pallas_call x2, Pallas kernels, adam(): pl.pallas_call(adam_step, grid=(sources,), in_specs=[flat] * 3 + [second]...  14.6 us
    unnamed x75, local copies, waits for them, and re-layouts  11.8 us
    dot_general x2, matrix products, weight_grad(): jnp.einsum('rh,rd->hd', grads, flat_rows, preferred_element_type=f32)  11 us
    all_to_all x4, waiting for transfers between devices, to_owners(): lax.all_to_all(part, 'expert', split_axis=0, concat_axis=1, tiled=True)[0]  10.2 us
  transfers between devices with their start and end apart: 28, of which 18 were waited for; matrix products, arithmetic and copies ran while one was open for 17% of the time, Pallas kernels for 5%

profile of v1, /device:TPU:0, one launch (start us, length us, event | category | flops | bytes accessed | tf_op | source)
XLA Modules:
  0.0 314.8 jit_solution(4895422167217542333)
XLA Ops:
  7.2 4.1 %collective-permute-start.4 = (s32[128,2]{0,1:T(2,128)}, s32[128,2]{0,1:T(2,128)S(1)}, u32[]{:S(2)}, u32[]{:S(2)}) collective-permute-start(s32[128,2]{0,1:T(2,128)} %param.8), channel_id=1, source_target_pairs={{0,4},{1,5},{2,6},{3,7},{4,0},{5,1},{6,2},{7,3},{8,12},{9,13},{10,... | collective-permute-start | bytes 3080 | tf_op jit(solution)/shard_map/ppermute | solution.py:96
  11.3 3.2 %slice_bitcast_fusion.2 = (bf16[8,96,768]{2,1,0:T(8,128)(2,1)}, bf16[8,96,768]{2,1,0:T(8,128)(2,1)}) fusion(bf16[2,8,96,768]{3,2,1,0:T(8,128)(2,1)} %param.11), kind=kLoop, calls=%fused_computation.35 | loop fusion | bytes 4718592 | tf_op jit(solution)/shard_map/squeeze | solution.py:133
  14.5 6.2 %all-to-all-start = ((bf16[8,96,768]{2,1,0:T(8,128)(2,1)}), bf16[8,96,768]{2,1,0:T(8,128)(2,1)S(1)}, u32[]{:S(2)}, u32[]{:S(2)}) async-start(bf16[8,96,768]{2,1,0:T(8,128)(2,1)} %get-tuple-element.55), calls=%async_computation | async-start | bytes 2359296 | tf_op jit(solution)/shard_map/all_to_all | solution.py:90
  23.6 2.9 collective-permute-start.8
  27.7 27.2 %collective-permute-done.8 = bf16[48,3072]{1,0:T(8,128)(2,1)S(1)} collective-permute-done((bf16[48,3072]{1,0:T(8,128)(2,1)S(1)}, bf16[48,3072]{1,0:T(8,128)(2,1)S(1)}, u32[]{:S(2)}, u32[]{:S(2)}) %collective-permute-start.8) | collective-permute-done | bytes 294944 | tf_op jit(solution)/shard_map/ppermute | solution.py:83
  54.9 8.7 %collective-permute-done.7 = bf16[48,3072]{1,0:T(8,128)(2,1)S(1)} collective-permute-done((bf16[48,3072]{1,0:T(8,128)(2,1)S(1)}, bf16[48,3072]{1,0:T(8,128)(2,1)S(1)}, u32[]{:S(2)}, u32[]{:S(2)}) %collective-permute-start.7) | collective-permute-done | bytes 294944 | tf_op jit(solution)/shard_map/ppermute | solution.py:83
  63.6 4.1 %collective-permute-done.6 = bf16[48,3072]{1,0:T(8,128)(2,1)} collective-permute-done((bf16[48,3072]{1,0:T(8,128)(2,1)S(1)}, bf16[48,3072]{1,0:T(8,128)(2,1)}, u32[]{:S(2)}, u32[]{:S(2)}) %collective-permute-start.6) | collective-permute-done | bytes 294944 | tf_op jit(solution)/shard_map/ppermute | solution.py:83
  67.7 5.9 %all-to-all-done = bf16[8,96,768]{2,1,0:T(8,128)(2,1)S(1)} async-done(((bf16[8,96,768]{2,1,0:T(8,128)(2,1)}), bf16[8,96,768]{2,1,0:T(8,128)(2,1)S(1)}, u32[]{:S(2)}, u32[]{:S(2)}) %all-to-all-start) | async-done | bytes 1179680 | tf_op jit(solution)/shard_map/all_to_all | solution.py:90
  73.6 1.1 copy-done.1
  74.8 3.6 %all-to-all-start.1 = ((bf16[8,96,768]{2,1,0:T(8,128)(2,1)}), bf16[8,96,768]{2,1,0:T(8,128)(2,1)S(1)}, u32[]{:S(2)}, u32[]{:S(2)}) async-start(bf16[8,96,768]{2,1,0:T(8,128)(2,1)} %get-tuple-element.25), calls=%async_computation.1 | async-start | bytes 2359296 | tf_op jit(solution)/shard_map/all_to_all | solution.py:90
  79.2 1.7 convolution_convert_fusion.2
  81.6 2.8 collective-permute-start.11
  85.8 2.4 collective-permute-start
  88.3 17.2 %collective-permute-done.11 = bf16[48,3072]{1,0:T(8,128)(2,1)S(1)} collective-permute-done((bf16[48,3072]{1,0:T(8,128)(2,1)S(1)}, bf16[48,3072]{1,0:T(8,128)(2,1)S(1)}, u32[]{:S(2)}, u32[]{:S(2)}) %collective-permute-start.11) | collective-permute-done | bytes 294944 | tf_op jit(solution)/shard_map/ppermute | solution.py:83
  105.5 13.3 %collective-permute-done.10 = bf16[48,3072]{1,0:T(8,128)(2,1)S(1)} collective-permute-done((bf16[48,3072]{1,0:T(8,128)(2,1)S(1)}, bf16[48,3072]{1,0:T(8,128)(2,1)S(1)}, u32[]{:S(2)}, u32[]{:S(2)}) %collective-permute-start.10) | collective-permute-done | bytes 294944 | tf_op jit(solution)/shard_map/ppermute | solution.py:83
  121.7 3.3 %slice_bitcast_fusion = (bf16[8,96,768]{2,1,0:T(8,128)(2,1)}, bf16[8,96,768]{2,1,0:T(8,128)(2,1)}) fusion(bf16[2,8,96,768]{3,2,1,0:T(8,128)(2,1)} %param.12), kind=kLoop, calls=%fused_computation.32 | loop fusion | bytes 4718592 | tf_op jit(solution)/shard_map/squeeze | solution.py:138
  127.2 3.7 %all-to-all-start.2 = ((bf16[8,96,768]{2,1,0:T(8,128)(2,1)}), bf16[8,96,768]{2,1,0:T(8,128)(2,1)S(1)}, u32[]{:S(2)}, u32[]{:S(2)}) async-start(bf16[8,96,768]{2,1,0:T(8,128)(2,1)} %get-tuple-element.29), calls=%async_computation.2 | async-start | bytes 2359296 | tf_op jit(solution)/shard_map/all_to_all | solution.py:90
  131.6 1.7 constant_dynamic-update-slice_fusion.2
  134.1 1.0 fusion.26
  135.1 2.0 collective-permute-start.1
  138.1 2.0 collective-permute-start.2
  140.8 13.1 %collective-permute-done.1 = bf16[96,768]{1,0:T(8,128)(2,1)S(1)} collective-permute-done((bf16[96,768]{1,0:T(8,128)(2,1)S(1)}, bf16[96,768]{1,0:T(8,128)(2,1)S(1)}, u32[]{:S(2)}, u32[]{:S(2)}) %collective-permute-start.1) | collective-permute-done | bytes 147488 | tf_op jit(solution)/shard_map/ppermute | solution.py:83
  154.3 1.7 collective-permute-done.2
  156.2 6.2 %fusion.19 = (bf16[384,768]{1,0:T(8,128)(2,1)S(1)}, f32[384,768]{1,0:T(8,128)}) fusion(f32[4,2,48,768]{3,2,0,1:T(8,128)S(1)} %maximum_convert_fusion, bf16[384,3072]{1,0:T(8,128)(2,1)} %constant_dynamic-update-slice_fusion, bf16[768,3072]{1,0:T(8,128)(2,1)} %all-gather.5.cloned.1.call-done), kind=kOutput, calls=%fused_computation.31 | convolution fusion | flops 1813708800 | bytes 10027008 | tf_op jit(solution)/shard_map/rd,hd->rh/dot_general | solution.py:142
  162.4 6.7 %convolution_convert_fusion = bf16[768,3072]{1,0:T(8,128)(2,1)} fusion(bf16[384,768]{1,0:T(8,128)(2,1)S(1)} %get-tuple-element.33, bf16[384,3072]{1,0:T(8,128)(2,1)} %constant_dynamic-update-slice_fusion), kind=kOutput, calls=%fused_computation | convolution fusion | flops 1814298624 | bytes 7667712 | tf_op jit(solution)/shard_map/rh,rd->hd/dot_general | solution.py:152
  169.1 6.9 %all-to-all-start.3 = ((bf16[8,96,768]{2,1,0:T(8,128)(2,1)}), bf16[8,96,768]{2,1,0:T(8,128)(2,1)S(1)}, u32[]{:S(2)}, u32[]{:S(2)}) async-start(bf16[8,96,768]{2,1,0:T(8,128)(2,1)} %get-tuple-element.30), calls=%async_computation.3 | async-start | bytes 2359296 | tf_op jit(solution)/shard_map/all_to_all | solution.py:90
  176.2 6.0 %fusion.3 = bf16[384,768]{1,0:T(8,128)(2,1)S(1)} fusion(f32[384,768]{1,0:T(8,128)S(1)} %bitcast.95, bf16[384,3072]{1,0:T(8,128)(2,1)} %constant_dynamic-update-slice_fusion, bf16[768,3072]{1,0:T(8,128)(2,1)} %all-gather.3.cloned.1.call-done, f32[384,768]{1,0:T(8,128)S(1)} %copy-done.33), kind=kOutput, calls=%fused_computation.12 | convolution fusion | flops 1814888448 | bytes 10027008 | tf_op jit(solution)/shard_map/rd,hd->rh/dot_general | solution.py:143
  182.2 4.6 %fusion.39 = f32[384,3072]{1,0:T(8,128)S(1)} fusion(bf16[384,768]{1,0:T(8,128)(2,1)S(1)} %fusion.3, bf16[768,3072]{1,0:T(8,128)(2,1)} %all-gather.5.cloned.1.call-done), kind=kOutput, calls=%fused_computation.97 | convolution fusion | flops 1811939328 | bytes 10027008 | tf_op jit(solution)/shard_map/dot_general | solution.py:158
  186.9 2.0 add_convert_fusion
  188.9 1.1 slice_bitcast_fusion.11
  190.0 1.9 collective-permute-start.15
  191.9 1.5 collective-permute-start.14
  193.4 1.4 collective-permute-start.13
  194.8 4.3 %convolution_convert_fusion.1 = bf16[768,3072]{1,0:T(8,128)(2,1)} fusion(bf16[384,768]{1,0:T(8,128)(2,1)S(1)} %fusion.3, bf16[384,3072]{1,0:T(8,128)(2,1)S(1)} %copy-done.24), kind=kOutput, calls=%fused_computation.1 | convolution fusion | flops 1814298624 | bytes 7667712 | tf_op jit(solution)/shard_map/rh,rd->hd/dot_general | solution.py:152
  199.2 4.3 %all-to-all-done.3 = bf16[8,96,768]{2,1,0:T(8,128)(2,1)S(1)} async-done(((bf16[8,96,768]{2,1,0:T(8,128)(2,1)}), bf16[8,96,768]{2,1,0:T(8,128)(2,1)S(1)}, u32[]{:S(2)}, u32[]{:S(2)}) %all-to-all-start.3) | async-done | bytes 1179680 | tf_op jit(solution)/shard_map/all_to_all | solution.py:90
  203.5 2.2 collective-permute-done.15
  207.9 1.6 copy-done.5
  209.5 1.6 copy.65
  211.1 8.8 %all-to-all-start.4 = ((bf16[1,2,8,96,768]{4,3,1,0,2:T(8,128)(2,1)}), bf16[1,2,8,96,768]{4,3,1,0,2:T(8,128)(2,1)S(1)}, u32[]{:S(2)}, u32[]{:S(2)}) async-start(bf16[1,2,8,96,768]{4,3,1,0,2:T(8,128)(2,1)} %bitcast.91), calls=%async_computation.5 | async-start | bytes 4718592 | tf_op jit(solution)/shard_map/all_to_all | solution.py:165
  219.9 2.5 convolution_convert_fusion.4
  222.5 49.3 %all-to-all-done.4 = bf16[1,2,8,96,768]{4,3,1,0,2:T(8,128)(2,1)S(1)} async-done(((bf16[1,2,8,96,768]{4,3,1,0,2:T(8,128)(2,1)}), bf16[1,2,8,96,768]{4,3,1,0,2:T(8,128)(2,1)S(1)}, u32[]{:S(2)}, u32[]{:S(2)}) %all-to-all-start.4) | async-done | bytes 2359328 | tf_op jit(solution)/shard_map/all_to_all | solution.py:165
  271.8 2.7 collective-permute-start.12
  275.3 7.3 %shard_map.102 = (bf16[2,1,768,768]{3,2,1,0:T(8,128)(2,1)}, bf16[2,1,768,768]{3,2,1,0:T(8,128)(2,1)}, bf16[2,1,768,768]{3,2,1,0:T(8,128)(2,1)}) custom-call(bf16[768,768]{1,0:T(8,128)(2,1)} %reduce-scatter.5.cloned.1.call-done.summed, bf16[768,768]{1,0:T(8,128)(2,1)} %bitcast.90, bf16[768,768]{1,0:T(8,128)(2,1)} %bitcast.93, bf16[8,2,96,768]{3,2,1,0:T(8,128)(2,1)} %bitcast.85), custom_call_target="tpu_custom_call" | custom-call | flops 11796480 | bytes 8257536 | tf_op jit(solution)/shard_map/pallas_call | solution.py:48
  282.6 7.3 %shard_map.103 = (bf16[2,1,768,768]{3,2,1,0:T(8,128)(2,1)}, bf16[2,1,768,768]{3,2,1,0:T(8,128)(2,1)}, bf16[2,1,768,768]{3,2,1,0:T(8,128)(2,1)}) custom-call(bf16[768,768]{1,0:T(8,128)(2,1)} %reduce-scatter.3.cloned.1.call-done.summed, bf16[768,768]{1,0:T(8,128)(2,1)} %bitcast.88, ...), custom_call_target="tpu_custom_call", output_to_operand_aliasing={{0}: (4, {}), {1}: (5, {}), {2}: (6, {})} | custom-call | flops 11796480 | bytes 8257536 | tf_op jit(solution)/shard_map/pallas_call | solution.py:48
  289.9 5.3 %collective-permute-done.12 = bf16[48,3072]{1,0:T(8,128)(2,1)S(1)} collective-permute-done((bf16[48,3072]{1,0:T(8,128)(2,1)S(1)}, bf16[48,3072]{1,0:T(8,128)(2,1)S(1)}, u32[]{:S(2)}, u32[]{:S(2)}) %collective-permute-start.12) | collective-permute-done | bytes 294944 | tf_op jit(solution)/shard_map/ppermute | solution.py:83
  295.2 3.2 %collective-permute-done.16 = bf16[48,3072]{1,0:T(8,128)(2,1)} collective-permute-done((bf16[48,3072]{1,0:T(8,128)(2,1)S(1)}, bf16[48,3072]{1,0:T(8,128)(2,1)}, u32[]{:S(2)}, u32[]{:S(2)}) %collective-permute-start.16) | collective-permute-done | bytes 294944 | tf_op jit(solution)/shard_map/ppermute | solution.py:83
  298.3 7.4 %collective-permute-done.18 = bf16[128,3072]{1,0:T(8,128)(2,1)} collective-permute-done((bf16[128,3072]{1,0:T(8,128)(2,1)}, bf16[128,3072]{1,0:T(8,128)(2,1)}, u32[]{:S(2)}, u32[]{:S(2)}) %collective-permute-start.18) | collective-permute-done | bytes 786464 | tf_op jit(solution)/shard_map/ppermute | solution.py:174
  305.7 2.6 fusion
  (132 shorter events, 19.3 us)
Async XLA Ops:
  7.2 14.5 %collective-permute-start.4 = (s32[128,2]{0,1:T(2,128)}, s32[128,2]{0,1:T(2,128)S(1)}, u32[]{:S(2)}, u32[]{:S(2)}) collective-permute-start(s32[128,2]{0,1:T(2,128)} %param.8), channel_id=1, source_target_pairs={{0,4},{1,5},{2,6},{3,7},{4,0},{5,1},{6,2},{7,3},{8,12},{9,13},{10,... | collective-permute-start | bytes 3080 | tf_op jit(solution)/shard_map/ppermute | solution.py:96
  11.3 56.5 %collective-permute-start.5 = (bf16[128,3072]{1,0:T(8,128)(2,1)}, bf16[128,3072]{1,0:T(8,128)(2,1)}, u32[]{:S(2)}, u32[]{:S(2)}) collective-permute-start(bf16[128,3072]{1,0:T(8,128)(2,1)} %param.7), channel_id=1, source_target_pairs={{0,4},{1,5},{2,6},{3,7},{4,0},{5,1},{6,2},{7,3},{8,12},{9,13},{10,... | collective-permute-start | bytes 2359304 | tf_op jit(solution)/shard_map/ppermute | solution.py:95
  14.5 6.3 %copy-start.25 = (s32[128,2]{0,1:T(2,128)S(1)}, s32[128,2]{0,1:T(2,128)}, u32[]{:S(2)}) copy-start(s32[128,2]{0,1:T(2,128)} %param.8) | copy-start | bytes 3076
  14.5 8.6 %copy-start.6 = (bf16[128,3072]{1,0:T(8,128)(2,1)S(1)}, bf16[128,3072]{1,0:T(8,128)(2,1)}, u32[]{:S(2)}) copy-start(bf16[128,3072]{1,0:T(8,128)(2,1)} %param.7) | copy-start | bytes 2359300
  14.5 59.1 %all-to-all-start = ((bf16[8,96,768]{2,1,0:T(8,128)(2,1)}), bf16[8,96,768]{2,1,0:T(8,128)(2,1)S(1)}, u32[]{:S(2)}, u32[]{:S(2)}) async-start(bf16[8,96,768]{2,1,0:T(8,128)(2,1)} %get-tuple-element.55), calls=%async_computation | async-start | bytes 2359296 | tf_op jit(solution)/shard_map/all_to_all | solution.py:90
  20.8 135.4 %all-gather.5.cloned.1.call-start = ((), (), s32[]{:S(2)}) async-start(), calls=%async_computation.8 | async-start | bytes 5898240 | tf_op jit(solution)/shard_map/all_gather | solution.py:93
  22.5 98.9 %copy-start.23 = (pred[192,128]{1,0:T(8,128)(4,1)}, pred[192,128]{1,0:T(8,128)(4,1)S(1)}, u32[]{:S(2)}) copy-start(pred[192,128]{1,0:T(8,128)(4,1)S(1)} %get-tuple-element.42) | copy-start | bytes 73732
  23.5 54.8 %copy-start.26 = (s32[128,2]{0,1:T(2,128)S(1)}, s32[128,2]{0,1:T(2,128)}, u32[]{:S(2)}) copy-start(s32[128,2]{0,1:T(2,128)} %param.9) | copy-start | bytes 3076
  23.6 55.0 %copy-start.7 = (bf16[128,2,768]{2,1,0:T(2,128)(2,1)S(1)}, bf16[128,2,768]{2,1,0:T(2,128)(2,1)}, u32[]{:S(2)}) copy-start(bf16[128,2,768]{2,1,0:T(2,128)(2,1)} %param.10) | copy-start | bytes 1179652
  23.6 31.2 %collective-permute-start.8 = (bf16[48,3072]{1,0:T(8,128)(2,1)S(1)}, bf16[48,3072]{1,0:T(8,128)(2,1)S(1)}, u32[]{:S(2)}, u32[]{:S(2)}) collective-permute-start(bf16[48,3072]{1,0:T(8,128)(2,1)S(1)} %get-tuple-element.60), channel_id=1, source_target_pairs={{0,3},{1,0},{2,1},{3,2},{4,7},{5,4},{6,5},{7,6},{8,11},{9,8},{10,9... | collective-permute-start | bytes 884744 | tf_op jit(solution)/shard_map/ppermute | solution.py:83
  26.5 37.1 %collective-permute-start.7 = (bf16[48,3072]{1,0:T(8,128)(2,1)S(1)}, bf16[48,3072]{1,0:T(8,128)(2,1)S(1)}, u32[]{:S(2)}, u32[]{:S(2)}) collective-permute-start(bf16[48,3072]{1,0:T(8,128)(2,1)S(1)} %get-tuple-element.61), channel_id=1, source_target_pairs={{0,2},{1,3},{2,0},{3,1},{4,6},{5,7},{6,4},{7,5},{8,10},{9,11},{10,... | collective-permute-start | bytes 884744 | tf_op jit(solution)/shard_map/ppermute | solution.py:83
  27.1 40.6 %collective-permute-start.6 = (bf16[48,3072]{1,0:T(8,128)(2,1)S(1)}, bf16[48,3072]{1,0:T(8,128)(2,1)}, u32[]{:S(2)}, u32[]{:S(2)}) collective-permute-start(bf16[48,3072]{1,0:T(8,128)(2,1)S(1)} %get-tuple-element.62), channel_id=1, source_target_pairs={{0,1},{1,2},{2,3},{3,0},{4,5},{5,6},{6,7},{7,4},{8,9},{9,10},{10,1... | collective-permute-start | bytes 884744 | tf_op jit(solution)/shard_map/ppermute | solution.py:83
  63.6 14.9 %copy-start.13 = (bf16[48,3072]{1,0:T(8,128)(2,1)}, bf16[48,3072]{1,0:T(8,128)(2,1)S(1)}, u32[]{:S(2)}) copy-start(bf16[48,3072]{1,0:T(8,128)(2,1)S(1)} %collective-permute-done.7) | copy-start | bytes 884740
  74.8 45.6 %all-to-all-start.1 = ((bf16[8,96,768]{2,1,0:T(8,128)(2,1)}), bf16[8,96,768]{2,1,0:T(8,128)(2,1)S(1)}, u32[]{:S(2)}, u32[]{:S(2)}) async-start(bf16[8,96,768]{2,1,0:T(8,128)(2,1)} %get-tuple-element.25), calls=%async_computation.1 | async-start | bytes 2359296 | tf_op jit(solution)/shard_map/all_to_all | solution.py:90
  78.3 97.9 %all-gather.3.cloned.1.call-start = ((), (), s32[]{:S(2)}) async-start(), calls=%async_computation.7 | async-start | bytes 5898240 | tf_op jit(solution)/shard_map/all_gather | solution.py:93
  81.6 23.8 %collective-permute-start.11 = (bf16[48,3072]{1,0:T(8,128)(2,1)S(1)}, bf16[48,3072]{1,0:T(8,128)(2,1)S(1)}, u32[]{:S(2)}, u32[]{:S(2)}) collective-permute-start(bf16[48,3072]{1,0:T(8,128)(2,1)S(1)} %get-tuple-element.56), channel_id=1, source_target_pairs={{0,3},{1,0},{2,1},{3,2},{4,7},{5,4},{6,5},{7,6},{8,11},{9,8},{10,9... | collective-permute-start | bytes 884744 | tf_op jit(solution)/shard_map/ppermute | solution.py:83
  84.4 34.4 %collective-permute-start.10 = (bf16[48,3072]{1,0:T(8,128)(2,1)S(1)}, bf16[48,3072]{1,0:T(8,128)(2,1)S(1)}, u32[]{:S(2)}, u32[]{:S(2)}) collective-permute-start(bf16[48,3072]{1,0:T(8,128)(2,1)S(1)} %get-tuple-element.57), channel_id=1, source_target_pairs={{0,2},{1,3},{2,0},{3,1},{4,6},{5,7},{6,4},{7,5},{8,10},{9,11},{10,... | collective-permute-start | bytes 884744 | tf_op jit(solution)/shard_map/ppermute | solution.py:83
  85.0 34.6 %collective-permute-start.9 = (bf16[48,3072]{1,0:T(8,128)(2,1)S(1)}, bf16[48,3072]{1,0:T(8,128)(2,1)S(1)}, u32[]{:S(2)}, u32[]{:S(2)}) collective-permute-start(bf16[48,3072]{1,0:T(8,128)(2,1)S(1)} %get-tuple-element.58), channel_id=1, source_target_pairs={{0,1},{1,2},{2,3},{3,0},{4,5},{5,6},{6,7},{7,4},{8,9},{9,10},{10,1... | collective-permute-start | bytes 884744 | tf_op jit(solution)/shard_map/ppermute | solution.py:83
  85.8 34.5 %collective-permute-start = (bf16[4,48,768]{2,1,0:T(8,128)(2,1)S(1)}, bf16[4,48,768]{2,1,0:T(8,128)(2,1)}, u32[]{:S(2)}, u32[]{:S(2)}) collective-permute-start(bf16[4,48,768]{2,1,0:T(8,128)(2,1)S(1)} %bitcast.98), channel_id=1, source_target_pairs={{0,4},{1,5},{2,6},{3,7},{4,0},{5,1},{6,2},{7,3},{8,12},{9,13},{10,... | collective-permute-start | bytes 884744 | tf_op jit(solution)/shard_map/ppermute | solution.py:112
  105.5 14.9 %copy-start.15 = (bf16[48,3072]{1,0:T(8,128)(2,1)}, bf16[48,3072]{1,0:T(8,128)(2,1)S(1)}, u32[]{:S(2)}) copy-start(bf16[48,3072]{1,0:T(8,128)(2,1)S(1)} %collective-permute-done.11) | copy-start | bytes 884740
  121.7 4.8 %copy-start.16 = (bf16[48,3072]{1,0:T(8,128)(2,1)S(1)}, bf16[48,3072]{1,0:T(8,128)(2,1)}, u32[]{:S(2)}) copy-start(bf16[48,3072]{1,0:T(8,128)(2,1)} %copy-done.15) | copy-start | bytes 884740
  125.7 7.6 %copy-start.14 = (bf16[48,3072]{1,0:T(8,128)(2,1)S(1)}, bf16[48,3072]{1,0:T(8,128)(2,1)}, u32[]{:S(2)}) copy-start(bf16[48,3072]{1,0:T(8,128)(2,1)} %copy-done.13) | copy-start | bytes 884740
  127.2 35.2 %all-to-all-start.2 = ((bf16[8,96,768]{2,1,0:T(8,128)(2,1)}), bf16[8,96,768]{2,1,0:T(8,128)(2,1)S(1)}, u32[]{:S(2)}, u32[]{:S(2)}) async-start(bf16[8,96,768]{2,1,0:T(8,128)(2,1)} %get-tuple-element.29), calls=%async_computation.2 | async-start | bytes 2359296 | tf_op jit(solution)/shard_map/all_to_all | solution.py:90
  130.9 144.4 %reduce-scatter.5.cloned.1.call-start = ((), (), s32[]{:S(2)}) async-start(), calls=%async_computation.10 | async-start | bytes 5898240 | tf_op jit(solution)/shard_map/reduce_scatter | solution.py:154
  135.1 18.8 %collective-permute-start.1 = (bf16[96,768]{1,0:T(8,128)(2,1)S(1)}, bf16[96,768]{1,0:T(8,128)(2,1)S(1)}, u32[]{:S(2)}, u32[]{:S(2)}) collective-permute-start(bf16[96,768]{1,0:T(8,128)(2,1)S(1)} %get-tuple-element.64), channel_id=1, source_target_pairs={{0,1},{1,2},{2,3},{3,0},{4,5},{5,6},{6,7},{7,4},{8,9},{9,10},{10,1... | collective-permute-start | bytes 442376 | tf_op jit(solution)/shard_map/ppermute | solution.py:83
  137.1 17.2 %collective-permute-start.3 = (bf16[96,768]{1,0:T(8,128)(2,1)S(1)}, bf16[96,768]{1,0:T(8,128)(2,1)S(1)}, u32[]{:S(2)}, u32[]{:S(2)}) collective-permute-start(bf16[96,768]{1,0:T(8,128)(2,1)S(1)} %get-tuple-element.65), channel_id=1, source_target_pairs={{0,3},{1,0},{2,1},{3,2},{4,7},{5,4},{6,5},{7,6},{8,11},{9,8},{10,9... | collective-permute-start | bytes 442376 | tf_op jit(solution)/shard_map/ppermute | solution.py:83
  138.1 17.9 %collective-permute-start.2 = (bf16[96,768]{1,0:T(8,128)(2,1)S(1)}, bf16[96,768]{1,0:T(8,128)(2,1)S(1)}, u32[]{:S(2)}, u32[]{:S(2)}) collective-permute-start(bf16[96,768]{1,0:T(8,128)(2,1)S(1)} %get-tuple-element.66), channel_id=1, source_target_pairs={{0,2},{1,3},{2,0},{3,1},{4,6},{5,7},{6,4},{7,5},{8,10},{9,11},{10,... | collective-permute-start | bytes 442376 | tf_op jit(solution)/shard_map/ppermute | solution.py:83
  162.4 6.7 %copy-start.31 = (bf16[384,768]{1,0:T(8,128)(2,1)}, bf16[384,768]{1,0:T(8,128)(2,1)S(1)}, u32[]{:S(2)}) copy-start(bf16[384,768]{1,0:T(8,128)(2,1)S(1)} %get-tuple-element.33) | copy-start | bytes 1769476
  162.4 6.7 %copy-start.3 = (bf16[8,96,768]{2,1,0:T(8,128)(2,1)}, bf16[8,96,768]{2,1,0:T(8,128)(2,1)S(1)}, u32[]{:S(2)}) copy-start(bf16[8,96,768]{2,1,0:T(8,128)(2,1)S(1)} %all-to-all-done.2) | copy-start | bytes 3538948
  169.1 7.1 %copy-start.33 = (f32[384,768]{1,0:T(8,128)S(1)}, f32[384,768]{1,0:T(8,128)}, u32[]{:S(2)}) copy-start(f32[384,768]{1,0:T(8,128)} %get-tuple-element.68) | copy-start | bytes 3538948
  169.1 34.4 %all-to-all-start.3 = ((bf16[8,96,768]{2,1,0:T(8,128)(2,1)}), bf16[8,96,768]{2,1,0:T(8,128)(2,1)S(1)}, u32[]{:S(2)}, u32[]{:S(2)}) async-start(bf16[8,96,768]{2,1,0:T(8,128)(2,1)} %get-tuple-element.30), calls=%async_computation.3 | async-start | bytes 2359296 | tf_op jit(solution)/shard_map/all_to_all | solution.py:90
  176.0 106.6 %reduce-scatter.3.cloned.1.call-start = ((), (), s32[]{:S(2)}) async-start(), calls=%async_computation.9 | async-start | bytes 5898240 | tf_op jit(solution)/shard_map/reduce_scatter | solution.py:154
  182.2 4.6 %copy-start.27 = (bf16[768,3072]{1,0:T(8,128)(2,1)S(1)}, bf16[768,3072]{1,0:T(8,128)(2,1)}, u32[]{:S(2)}) copy-start(bf16[768,3072]{1,0:T(8,128)(2,1)} %all-gather.3.cloned.1.call-done) | copy-start | bytes 14155780
  188.9 6.0 %copy-start.24 = (bf16[384,3072]{1,0:T(8,128)(2,1)S(1)}, bf16[384,3072]{1,0:T(8,128)(2,1)}, u32[]{:S(2)}) copy-start(bf16[384,3072]{1,0:T(8,128)(2,1)} %constant_dynamic-update-slice_fusion) | copy-start | bytes 7077892
  190.0 15.6 %collective-permute-start.15 = (bf16[48,3072]{1,0:T(8,128)(2,1)S(1)}, bf16[48,3072]{1,0:T(8,128)(2,1)S(1)}, u32[]{:S(2)}, u32[]{:S(2)}) collective-permute-start(bf16[48,3072]{1,0:T(8,128)(2,1)S(1)} %get-tuple-element.48), channel_id=1, source_target_pairs={{0,1},{1,2},{2,3},{3,0},{4,5},{5,6},{6,7},{7,4},{8,9},{9,10},{10,1... | collective-permute-start | bytes 884744 | tf_op jit(solution)/shard_map/ppermute | solution.py:83
  191.9 14.5 %collective-permute-start.14 = (bf16[48,3072]{1,0:T(8,128)(2,1)S(1)}, bf16[48,3072]{1,0:T(8,128)(2,1)S(1)}, u32[]{:S(2)}, u32[]{:S(2)}) collective-permute-start(bf16[48,3072]{1,0:T(8,128)(2,1)S(1)} %get-tuple-element.49), channel_id=1, source_target_pairs={{0,2},{1,3},{2,0},{3,1},{4,6},{5,7},{6,4},{7,5},{8,10},{9,11},{10,... | collective-permute-start | bytes 884744 | tf_op jit(solution)/shard_map/ppermute | solution.py:83
  193.4 13.3 %collective-permute-start.13 = (bf16[48,3072]{1,0:T(8,128)(2,1)S(1)}, bf16[48,3072]{1,0:T(8,128)(2,1)S(1)}, u32[]{:S(2)}, u32[]{:S(2)}) collective-permute-start(bf16[48,3072]{1,0:T(8,128)(2,1)S(1)} %get-tuple-element.50), channel_id=1, source_target_pairs={{0,3},{1,0},{2,1},{3,2},{4,7},{5,4},{6,5},{7,6},{8,11},{9,8},{10,9... | collective-permute-start | bytes 884744 | tf_op jit(solution)/shard_map/ppermute | solution.py:83
  211.1 8.8 %copy-start.12 = (bf16[48,3072]{1,0:T(8,128)(2,1)S(1)}, bf16[48,3072]{1,0:T(8,128)(2,1)}, u32[]{:S(2)}) copy-start(bf16[48,3072]{1,0:T(8,128)(2,1)} %get-tuple-element.45) | copy-start | bytes 884740
  211.1 60.7 %all-to-all-start.4 = ((bf16[1,2,8,96,768]{4,3,1,0,2:T(8,128)(2,1)}), bf16[1,2,8,96,768]{4,3,1,0,2:T(8,128)(2,1)S(1)}, u32[]{:S(2)}, u32[]{:S(2)}) async-start(bf16[1,2,8,96,768]{4,3,1,0,2:T(8,128)(2,1)} %bitcast.91), calls=%async_computation.5 | async-start | bytes 4718592 | tf_op jit(solution)/shard_map/all_to_all | solution.py:165
  219.9 51.9 %copy-start.11 = (bf16[48,3072]{1,0:T(8,128)(2,1)S(1)}, bf16[48,3072]{1,0:T(8,128)(2,1)}, u32[]{:S(2)}) copy-start(bf16[48,3072]{1,0:T(8,128)(2,1)} %get-tuple-element.51) | copy-start | bytes 884740
  219.9 54.5 %copy-start.10 = (bf16[48,3072]{1,0:T(8,128)(2,1)S(1)}, bf16[48,3072]{1,0:T(8,128)(2,1)}, u32[]{:S(2)}) copy-start(bf16[48,3072]{1,0:T(8,128)(2,1)} %get-tuple-element.46) | copy-start | bytes 884740
  219.9 54.5 %copy-start.9 = (bf16[48,3072]{1,0:T(8,128)(2,1)S(1)}, bf16[48,3072]{1,0:T(8,128)(2,1)}, u32[]{:S(2)}) copy-start(bf16[48,3072]{1,0:T(8,128)(2,1)} %get-tuple-element.47) | copy-start | bytes 884740
  271.8 33.9 %collective-permute-start.18 = (bf16[128,3072]{1,0:T(8,128)(2,1)}, bf16[128,3072]{1,0:T(8,128)(2,1)}, u32[]{:S(2)}, u32[]{:S(2)}) collective-permute-start(bf16[128,3072]{1,0:T(8,128)(2,1)} %convolution_convert_fusion.4), channel_id=1, source_target_pairs={{0,4},{1,5},{2,6},{3,7},{4,0},{5,1},{6,2},{7,3},{8,12},{9,13},{10,... | collective-permute-start | bytes 2359304 | tf_op jit(solution)/shard_map/ppermute | solution.py:174
  271.8 23.4 %collective-permute-start.12 = (bf16[48,3072]{1,0:T(8,128)(2,1)S(1)}, bf16[48,3072]{1,0:T(8,128)(2,1)S(1)}, u32[]{:S(2)}, u32[]{:S(2)}) collective-permute-start(bf16[48,3072]{1,0:T(8,128)(2,1)S(1)} %copy-done.11), channel_id=1, source_target_pairs={{0,3},{1,0},{2,1},{3,2},{4,7},{5,4},{6,5},{7,6},{8,11},{9,8},{10,9... | collective-permute-start | bytes 884744 | tf_op jit(solution)/shard_map/ppermute | solution.py:83
  274.4 20.7 %collective-permute-start.17 = (bf16[48,3072]{1,0:T(8,128)(2,1)S(1)}, bf16[48,3072]{1,0:T(8,128)(2,1)}, u32[]{:S(2)}, u32[]{:S(2)}) collective-permute-start(bf16[48,3072]{1,0:T(8,128)(2,1)S(1)} %copy-done.10), channel_id=1, source_target_pairs={{0,1},{1,2},{2,3},{3,0},{4,5},{5,6},{6,7},{7,4},{8,9},{9,10},{10,1... | collective-permute-start | bytes 884744 | tf_op jit(solution)/shard_map/ppermute | solution.py:83
  274.5 23.9 %collective-permute-start.16 = (bf16[48,3072]{1,0:T(8,128)(2,1)S(1)}, bf16[48,3072]{1,0:T(8,128)(2,1)}, u32[]{:S(2)}, u32[]{:S(2)}) collective-permute-start(bf16[48,3072]{1,0:T(8,128)(2,1)S(1)} %copy-done.9), channel_id=1, source_target_pairs={{0,2},{1,3},{2,0},{3,1},{4,6},{5,7},{6,4},{7,5},{8,10},{9,11},{10,... | collective-permute-start | bytes 884744 | tf_op jit(solution)/shard_map/ppermute | solution.py:83
  282.6 23.1 %copy-start.8 = (bf16[48,3072]{1,0:T(8,128)(2,1)S(1)}, bf16[48,3072]{1,0:T(8,128)(2,1)}, u32[]{:S(2)}) copy-start(bf16[48,3072]{1,0:T(8,128)(2,1)} %get-tuple-element.44) | copy-start | bytes 884740
  282.6 23.1 %copy-start.22 = (pred[192,128]{1,0:T(8,128)(4,1)S(1)}, pred[192,128]{1,0:T(8,128)(4,1)}, u32[]{:S(2)}) copy-start(pred[192,128]{1,0:T(8,128)(4,1)} %copy-done.21) | copy-start | bytes 73732
  (14 other events, 28.3 us)
Sparse Core Ops, SparseCore 0:
  74.8 36.3 all-gather.4
  121.5 36.5 all-gather.2
  169.2 49.9 reduce-scatter.4
  221.8 47.8 reduce-scatter.2

commit v2 on v1

v2 whole, which is shorter than its diff:
```python
import jax
import jax.numpy as jnp
from jax import lax
from jax.experimental import pallas as pl
from jax.experimental.pallas import tpu as pltpu
from jax.sharding import PartitionSpec as P

gate_unit = 32768.0
loss_scale = 16.0
beta_one = 0.9
beta_two = 0.95
step_size = 0.001
adam_eps = 1e-08
bf16 = jnp.bfloat16
f32 = jnp.float32
vmem_bytes = 32 * 1024 * 1024


def after(value, *others):
    return lax.optimization_barrier((value, *others))[0]


def tile_of(extent):
    return 256 if extent % 256 == 0 else extent


def whole(shape):
    return pl.BlockSpec(shape, lambda *_: (0,) * len(shape))


def run(body, place, grid, in_specs, out_specs, out_shape, *operands):
    return pl.pallas_call(
        body,
        grid_spec=pltpu.PrefetchScalarGridSpec(
            num_scalar_prefetch=1, grid=grid, in_specs=in_specs, out_specs=out_specs
        ),
        out_shape=out_shape,
        compiler_params=pltpu.CompilerParams(vmem_limit_bytes=vmem_bytes),
    )(place, *operands)


def columns(place, k, width, start=0, size=None):
    first = pl.multiple_of((place[0] ^ k) * width + start, 128)
    return pl.ds(first, width if size is None else size)


def project(place, rows, weights):
    total = None
    for k, piece in enumerate(weights):
        term = lax.dot_general(
            rows[:, columns(place, k, piece.shape[1])],
            piece[...],
            (((1,), (1,)), ((), ())),
            preferred_element_type=f32,
        )
        total = term if total is None else total + term
    return total


def forward_gate(place, blocks, upstream, gate):
    pieces, hidden = len(gate), gate[0].shape[0]
    width = gate[0].shape[1] * pieces
    count = sum(block.shape[0] for block in blocks)
    tile = tile_of(hidden)

    def body(place, *refs):
        block_refs, refs = refs[: len(blocks)], refs[len(blocks) :]
        up_ref, gate_refs = refs[0], refs[1 : 1 + pieces]
        rows, grad_up, factor = refs[1 + pieces :]

        @pl.when(pl.program_id(0) == 0)
        def _():
            first = 0
            for block in block_refs:
                rows[first : first + block.shape[0], :] = block[...]
                first += block.shape[0]

        pre_gate = project(place, rows, gate_refs)
        sigmoid_gate = jax.nn.sigmoid(pre_gate)
        upstream = up_ref[...].astype(f32) * sigmoid_gate
        grad_up[...] = (upstream * pre_gate).astype(bf16)
        factor[...] = upstream * (1.0 + pre_gate * (1.0 - sigmoid_gate))

    part = pl.BlockSpec((count, tile), lambda i, _: (0, i))
    return run(
        body,
        place,
        (hidden // tile,),
        [whole(block.shape) for block in blocks]
        + [part]
        + [pl.BlockSpec((tile, width // pieces), lambda i, _: (i, 0))] * pieces,
        [whole((count, width)), part, part],
        [
            jax.ShapeDtypeStruct((count, width), bf16),
            jax.ShapeDtypeStruct((count, hidden), bf16),
            jax.ShapeDtypeStruct((count, hidden), f32),
        ],
        *blocks,
        upstream,
        *gate,
    )


def forward_up(place, rows, factor, up):
    pieces, hidden = len(up), up[0].shape[0]
    count, width = rows.shape
    tile = tile_of(hidden)

    def body(place, rows, factor, *refs):
        refs[-1][...] = (factor[...] * project(place, rows, refs[:-1])).astype(bf16)

    part = pl.BlockSpec((count, tile), lambda i, _: (0, i))
    return run(
        body,
        place,
        (hidden // tile,),
        [whole((count, width)), part]
        + [pl.BlockSpec((tile, width // pieces), lambda i, _: (i, 0))] * pieces,
        part,
        jax.ShapeDtypeStruct((count, hidden), bf16),
        rows,
        factor,
        *up,
    )


def weight_grads(place, grads, rows, pieces):
    count, hidden = grads.shape
    width = rows.shape[1] // pieces
    tile = tile_of(hidden)

    def body(place, grads, rows, *outs):
        for k, out in enumerate(outs):
            out[...] = lax.dot_general(
                grads[...],
                rows[:, columns(place, k, width)],
                (((0,), (0,)), ((), ())),
                preferred_element_type=f32,
            ).astype(bf16)

    return run(
        body,
        place,
        (hidden // tile,),
        [pl.BlockSpec((count, tile), lambda i, _: (0, i)), whole(rows.shape)],
        [pl.BlockSpec((tile, width), lambda i, _: (i, 0))] * pieces,
        [jax.ShapeDtypeStruct((hidden, width), bf16)] * pieces,
        grads,
        rows,
    )


def input_grads(place, grad_gate, grad_up, gate, up, block_rows):
    count, hidden = grad_gate.shape
    pieces, width = len(gate), gate[0].shape[1]
    tile = tile_of(width)
    blocks = count // block_rows

    def body(place, grad_gate, grad_up, *refs):
        start = pl.program_id(0) * tile
        for k in range(pieces):
            total = jnp.dot(grad_gate[...], refs[k][...], preferred_element_type=f32)
            total += jnp.dot(grad_up[...], refs[pieces + k][...], preferred_element_type=f32)
            total = total.astype(bf16)
            for b, out in enumerate(refs[2 * pieces :]):
                out[:, columns(place, k, width, start, tile)] = total[
                    b * block_rows : (b + 1) * block_rows
                ]

    return run(
        body,
        place,
        (width // tile,),
        [whole((count, hidden))] * 2
        + [pl.BlockSpec((hidden, tile), lambda i, _: (0, i))] * (2 * pieces),
        [whole((block_rows, width * pieces))] * blocks,
        [jax.ShapeDtypeStruct((block_rows, width * pieces), bf16)] * blocks,
        grad_gate,
        grad_up,
        *gate,
        *up,
    )


def adam(index, parts, old, first_old, second_old, *results):
    rows, width = old.shape
    sources, _, part, _ = second_old.shape
    flat = pl.BlockSpec((part, width), lambda i: (i, 0))
    moment = pl.BlockSpec((1, 1, part, width), lambda i: (i, index, 0, 0))
    out = pl.BlockSpec((1, 1, part, width), lambda i: (index, 0, i, 0))
    shape = jax.ShapeDtypeStruct((2, 1, rows, width), old.dtype)
    count = len(parts)

    def body(*refs):
        old_ref, first_ref, second_ref = refs[count : count + 3]
        weights_out, first_out, second_out = refs[-3:]
        gradient = refs[0][...].astype(f32)
        for ref in refs[1:count]:
            gradient += ref[...].astype(f32)
        gradient = gradient / loss_scale
        moment_one = beta_one * first_ref[0, 0].astype(f32) + (1.0 - beta_one) * gradient
        moment_two = (
            beta_two * second_ref[0, 0].astype(f32) + (1.0 - beta_two) * gradient * gradient
        )
        updated = old_ref[...].astype(f32) - step_size * moment_one / (
            jnp.sqrt(moment_two) + adam_eps
        )
        weights_out[0, 0] = updated.astype(bf16)
        first_out[0, 0] = moment_one.astype(bf16)
        second_out[0, 0] = moment_two.astype(bf16)

    return pl.pallas_call(
        body,
        grid=(sources,),
        in_specs=[flat] * (count + 1)
        + [moment] * 2
        + [pl.BlockSpec(memory_space=pl.ANY)] * len(results),
        out_specs=[out] * 3,
        out_shape=[shape] * 3,
        input_output_aliases={count + 3 + i: i for i in range(len(results))},
        compiler_params=pltpu.CompilerParams(vmem_limit_bytes=vmem_bytes),
    )(*parts, old, first_old, second_old, *results)


def slot_targets(flat_route, capacity):
    count = flat_route.shape[-1]
    order = jnp.arange(count, dtype=jnp.int32)
    earlier = order[None, :] < order[:, None]
    same = flat_route[:, None] == flat_route[None, :]
    position = jnp.sum((same & earlier).astype(jnp.int32), axis=-1)
    return flat_route * capacity + position


def per_device(
    tokens, routes, router_gates, hidden_cotangent, weights, first_moment, second_moment
):
    row_count, model_width = tokens.shape
    per_token = routes.shape[1]
    hidden_units = hidden_cotangent.shape[2]
    experts = weights.shape[1]
    pieces = model_width // weights.shape[3]
    capacity = 3 * row_count * per_token // (2 * experts)
    routings = row_count * per_token
    half = experts // 2
    mine = lax.axis_index("expert")
    side = mine // half
    local = mine % half
    place = lax.axis_index("dp").astype(jnp.int32).reshape(1)
    swap = [(i, (i + half) % experts) for i in range(experts)]

    def shift(value, step):
        if step % half == 0:
            return value
        pairs = [(i, i // half * half + (i + step) % half) for i in range(experts)]
        return lax.ppermute(value, "expert", pairs)

    def across(value, k):
        return lax.ppermute(value, "dp", [(i, i ^ k) for i in range(pieces)])

    def slot_ids(of_side):
        expert = of_side * half + (local + jnp.arange(half, dtype=jnp.int32)) % half
        return expert[:, None] * capacity + jnp.arange(capacity, dtype=jnp.int32)[None, :]

    def to_owners(part, *earlier):
        by_owner = after(jnp.swapaxes(part, 0, 1), *earlier) if earlier else jnp.swapaxes(part, 0, 1)
        return lax.all_to_all(by_owner, "expert", split_axis=0, concat_axis=0, tiled=True)

    def along_x(part):
        return [across(part, k) for k in range(2, pieces, 2)]

    def both_cores(parts):
        return [piece for one in parts for piece in (one, across(one, 1))]

    def scatter(totals, *earlier):
        terms = [totals[0], across(totals[1], 1)]
        for k in range(2, pieces, 2):
            pair = totals[k].astype(f32) + across(totals[k + 1], 1).astype(f32)
            terms.append(across(after(pair.astype(bf16), *earlier), k))
        return terms

    other_tokens = lax.ppermute(tokens, "expert", swap)
    other_routes = lax.ppermute(routes, "expert", swap)

    gate_factor = router_gates.astype(f32) / gate_unit
    scaled = (gate_factor[:, :, None] * hidden_cotangent.astype(f32)).astype(bf16)
    scaled = scaled.reshape(routings, hidden_units)
    target = slot_targets(routes.reshape(-1), capacity)
    near_ids = slot_ids(side)
    far_ids = slot_ids(1 - side)

    def pick_grads(ids):
        chosen = (target[None, :] == ids.reshape(-1)[:, None]).astype(bf16)
        picked = jnp.dot(chosen, scaled, preferred_element_type=f32).astype(bf16)
        return picked.reshape(half, capacity, hidden_units)

    far_grads = lax.ppermute(pick_grads(far_ids), "expert", swap)

    def pick_matrix(chosen_target):
        by_token = chosen_target.reshape(row_count, per_token)
        hit = by_token[None, :, :] == near_ids.reshape(-1)[:, None, None]
        return jnp.any(hit, axis=2).astype(bf16)

    def send_rows(picker, rows):
        picked = jnp.dot(picker, rows, preferred_element_type=f32).astype(bf16)
        picked = picked.reshape(half, capacity, model_width)
        return [shift(picked[s], s) for s in range(half)]

    near_pick = pick_matrix(target)
    near_rows = send_rows(near_pick, tokens)
    other_tokens = after(other_tokens, other_routes, far_grads, *near_rows[1:])
    other_pick = pick_matrix(slot_targets(other_routes.reshape(-1), capacity))
    far_rows = send_rows(other_pick, other_tokens)
    grads_out = jnp.concatenate([far_grads, pick_grads(near_ids)], axis=1)
    grads_in = [shift(grads_out[s], s) for s in range(half)]

    owned = after(to_owners(weights, other_tokens), *far_rows[1:], *grads_in[1:])
    owned_gate = owned[:, 0].reshape(hidden_units, -1)
    owned_up = owned[:, 1].reshape(hidden_units, -1)
    owned_first = to_owners(first_moment, owned)

    gate_x = along_x(owned_gate)
    up_x = along_x(after(owned_up, *gate_x))
    gate = both_cores([owned_gate] + gate_x)
    up = both_cores([owned_up] + up_x)
    upstream = jnp.swapaxes(jnp.stack(grads_in).reshape(half, 2, capacity, hidden_units), 0, 1)
    upstream = upstream.reshape(2 * half * capacity, hidden_units)

    blocks = far_rows + near_rows
    joined = capacity % 16 != 0
    if joined:
        blocks = [jnp.concatenate(blocks, axis=0)]
    rows, grad_up, factor = forward_gate(place, blocks, upstream, gate)
    up_totals = weight_grads(place, grad_up, rows, pieces)
    up_terms = scatter(up_totals)
    owned_second = to_owners(second_moment, owned_first, up_totals[0])
    grad_gate = forward_up(place, rows, after(factor, owned_first), up)
    back = input_grads(
        place, grad_gate, grad_up, gate, up, rows.shape[0] if joined else capacity
    )
    if joined:
        back = [back[0][i * capacity : (i + 1) * capacity] for i in range(2 * half)]
    far_back = [shift(back[s], -s) for s in range(half)]
    near_back = [shift(after(back[half + s], *far_back[1:]), -s) for s in range(half)]
    gate_totals = weight_grads(place, after(grad_gate, *back), rows, pieces)
    gate_terms = scatter(gate_totals, *up_terms)

    def combine(picker, parts):
        parts = jnp.concatenate(parts, axis=0)
        return jnp.einsum("st,sd->td", picker, parts, preferred_element_type=f32)

    far_sum = after(combine(other_pick, far_back).astype(bf16), owned_second, *up_terms)
    far_sum = lax.ppermute(far_sum, "expert", swap)
    results = adam(1, up_terms, owned_up, owned_first, owned_second)
    results = adam(0, gate_terms, owned_gate, owned_first, owned_second, *results)
    near_back[1:] = [after(block, *results) for block in near_back[1:]]
    near_sum = combine(near_pick, near_back)
    token_grads = (near_sum + far_sum.astype(f32)).astype(bf16)
    return (token_grads, *results)


def solution(mesh):
    placed = (
        P(("dp", "expert"), None),
        P(("dp", "expert"), None),
        P(("dp", "expert"), None),
        P(("dp", "expert"), None, None),
        P(None, None, "expert", "dp"),
        P(None, None, "expert", "dp"),
        P(None, None, "expert", "dp"),
    )
    return jax.shard_map(
        per_device,
        mesh=mesh,
        in_specs=placed,
        out_specs=(
            P(("dp", "expert"), None),
            P(None, "expert", None, "dp"),
            P(None, "expert", None, "dp"),
            P(None, "expert", None, "dp"),
        ),
        check_vma=False,
    )
```

time: 317 us -> 279 us (0.88)
  matrix products: 37.6 us -> 4.07 us
  waiting for transfers between devices: 165 us -> 143 us
  Pallas kernels: 14.6 us -> 34.9 us
  between operations: 14.2 us -> 1.26 us
  local copies, waits for them, and re-layouts: 23.7 us -> 31 us
  other arithmetic: 2.19 us -> 6.85 us
    ppermute x1 -> x13, waiting for transfers between devices: 0.01 us -> 82.7 us  [the longest x12 60.2 us: across(): return lax.ppermute(value, 'dp', [(i, i ^ k) for i in range(pieces)])]
    ppermute x15, waiting for transfers between devices: 98.2 us -> 39.5 us  [shift(): return lax.ppermute(value, 'expert', pairs)]
    all_to_all x5 -> x3, waiting for transfers between devices: 59.5 us -> 4.21 us  [to_owners(): lax.all_to_all(by_owner, 'expert', split_axis=0, concat_axis=0, tiled=True)]
    dot_general x8 -> x2, matrix products: 34.9 us -> 2.61 us  [combine(): return jnp.einsum('st,sd->td', picker, parts, preferred_element_type=f32)]
    pallas_call x2 -> x7, Pallas kernels: 14.6 us -> 34.9 us  [the longest x5 20.5 us: run(): pl.pallas_call(body, grid_spec=pltpu.PrefetchScalarGridSpec(num_scalar_pr...]
    all_to_all x5 -> x3, starting transfers between devices: 29.1 us -> 12.6 us  [to_owners(): lax.all_to_all(by_owner, 'expert', split_axis=0, concat_axis=0, tiled=True)]
    unnamed x75 -> x122, local copies, waits for them, and re-layouts: 11.8 us -> 26.4 us
    ppermute x1, waiting for transfers between devices: 0.01 us -> 12.1 us  [per_device(): other_tokens = lax.ppermute(tokens, 'expert', swap)]
  transfers between devices with their start and end apart: 28 -> 34, of which waited for: 18 -> 13; matrix products, arithmetic and copies ran while one was open for 17% -> 8% of each run, Pallas kernels for 5% -> 13%
where the time goes in v2:
time: 279 us; the launch traced here: 278 us
  waiting for transfers between devices  143 us (51%)
  starting transfers between devices  57.2 us (21%)
  Pallas kernels  34.9 us (13%)
  local copies, waits for them, and re-layouts  31 us (11%)
  other arithmetic  6.85 us (2%)
  matrix products  4.07 us (1%)
    ppermute x12, waiting for transfers between devices, across(): return lax.ppermute(value, 'dp', [(i, i ^ k) for i in range(pieces)])  60.2 us
    ppermute x15, waiting for transfers between devices, shift(): return lax.ppermute(value, 'expert', pairs)  39.5 us
    ppermute x15, starting transfers between devices, shift(): return lax.ppermute(value, 'expert', pairs)  27 us
    unnamed x122, local copies, waits for them, and re-layouts  26.4 us
    ppermute x1, waiting for transfers between devices, per_device(): far_grads = lax.ppermute(pick_grads(far_ids), 'expert', swap)  22.5 us
    pallas_call x5, Pallas kernels, run(): pl.pallas_call(body, grid_spec=pltpu.PrefetchScalarGridSpec(num_scalar_pr...  20.5 us
    pallas_call x2, Pallas kernels, adam(): pl.pallas_call(body, grid=(sources,), in_specs=[flat] * (count + 1) + [mo...  14.5 us
    all_to_all x3, starting transfers between devices, to_owners(): lax.all_to_all(by_owner, 'expert', split_axis=0, concat_axis=0, tiled=True)  12.6 us
  transfers between devices with their start and end apart: 34, of which 13 were waited for; matrix products, arithmetic and copies ran while one was open for 8% of the time, Pallas kernels for 13%

profile of v2, /device:TPU:0, one launch (start us, length us, event | category | flops | bytes accessed | tf_op | source)
XLA Modules:
  0.0 278.1 jit_solution(8222646321747038810)
XLA Ops:
  0.6 4.1 %collective-permute-start = (s32[128,2]{0,1:T(2,128)}, s32[128,2]{0,1:T(2,128)S(1)}, u32[]{:S(2)}, u32[]{:S(2)}) collective-permute-start(s32[128,2]{0,1:T(2,128)} %param.8), channel_id=1, source_target_pairs={{0,4},{1,5},{2,6},{3,7},{4,0},{5,1},{6,2},{7,3},{8,12},{9,13},{10,... | collective-permute-start | bytes 3080 | tf_op jit(solution)/shard_map/ppermute | solution.py:282
  6.9 1.4 multiply_convert_fusion
  8.8 2.9 %collective-permute-start.1 = (bf16[128,3072]{1,0:T(8,128)(2,1)S(1)}, bf16[128,3072]{1,0:T(8,128)(2,1)S(1)}, u32[]{:S(2)}, u32[]{:S(2)}) collective-permute-start(bf16[128,3072]{1,0:T(8,128)(2,1)S(1)} %copy-done.45), channel_id=1, source_target_pairs={{0,4},{1,5},{2,6},{3,7},{4,0},{5,1},{6,2},{7,3},{8,12},{9,13},{10,... | collective-permute-start | bytes 2359304 | tf_op jit(solution)/shard_map/ppermute | solution.py:281
  14.8 2.5 collective-permute-start.5
  18.4 1.6 copy.57
  20.0 22.5 %collective-permute-done.2 = bf16[4,48,768]{2,1,0:T(8,128)(2,1)S(1)} collective-permute-done((bf16[4,48,768]{2,1,0:T(8,128)(2,1)S(1)}, bf16[4,48,768]{2,1,0:T(8,128)(2,1)S(1)}, u32[]{:S(2)}, u32[]{:S(2)}) %collective-permute-start.2) | collective-permute-done | bytes 294944 | tf_op jit(solution)/shard_map/ppermute | solution.py:296
  43.3 1.3 collective-permute-done.4.refs_6_
  46.1 12.1 %collective-permute-done.1 = bf16[128,3072]{1,0:T(8,128)(2,1)S(1)} collective-permute-done((bf16[128,3072]{1,0:T(8,128)(2,1)S(1)}, bf16[128,3072]{1,0:T(8,128)(2,1)S(1)}, u32[]{:S(2)}, u32[]{:S(2)}) %collective-permute-start.1) | collective-permute-done | bytes 786464 | tf_op jit(solution)/shard_map/ppermute | solution.py:281
  58.2 3.6 %all-to-all-start = ((bf16[8,2,96,768]{3,2,1,0:T(8,128)(2,1)}), bf16[8,2,96,768]{3,2,1,0:T(8,128)(2,1)S(1)}, u32[]{:S(2)}, u32[]{:S(2)}) async-start(bf16[8,2,96,768]{3,2,1,0:T(8,128)(2,1)} %bitcast.34), calls=%async_computation | async-start | bytes 4718592 | tf_op jit(solution)/shard_map/all_to_all | solution.py:266
  62.1 1.7 fusion.23
  63.8 1.9 collective-permute-start.9
  68.0 1.9 collective-permute-start.7
  70.5 2.4 collective-permute-start.11
  72.9 28.1 %collective-permute-done.9 = bf16[96,768]{1,0:T(8,128)(2,1)S(1)} collective-permute-done((bf16[96,768]{1,0:T(8,128)(2,1)S(1)}, bf16[96,768]{1,0:T(8,128)(2,1)S(1)}, u32[]{:S(2)}, u32[]{:S(2)}) %collective-permute-start.9) | collective-permute-done | bytes 147488 | tf_op jit(solution)/shard_map/ppermute | solution.py:255
  100.9 8.5 %collective-permute-start.10 = (bf16[96,768]{1,0:T(8,128)(2,1)S(1)}, bf16[96,768]{1,0:T(8,128)(2,1)S(1)}, u32[]{:S(2)}, u32[]{:S(2)}) collective-permute-start(bf16[96,768]{1,0:T(8,128)(2,1)S(1)} %get-tuple-element.103), channel_id=1, source_target_pairs={{0,2},{1,3},{2,0},{3,1},{4,6},{5,7},{6,4},{7,5},{8,10},{9,11},{10,... | collective-permute-start | bytes 442376 | tf_op jit(solution)/shard_map/ppermute | solution.py:255
  109.5 1.6 copy.56
  111.0 6.9 %collective-permute-done.11 = bf16[96,768]{1,0:T(8,128)(2,1)S(1)} collective-permute-done((bf16[96,768]{1,0:T(8,128)(2,1)S(1)}, bf16[96,768]{1,0:T(8,128)(2,1)S(1)}, u32[]{:S(2)}, u32[]{:S(2)}) %collective-permute-start.11) | collective-permute-done | bytes 147488 | tf_op jit(solution)/shard_map/ppermute | solution.py:255
  118.0 3.2 %collective-permute-done.10 = bf16[96,768]{1,0:T(8,128)(2,1)S(1)} collective-permute-done((bf16[96,768]{1,0:T(8,128)(2,1)S(1)}, bf16[96,768]{1,0:T(8,128)(2,1)S(1)}, u32[]{:S(2)}, u32[]{:S(2)}) %collective-permute-start.10) | collective-permute-done | bytes 147488 | tf_op jit(solution)/shard_map/ppermute | solution.py:255
  123.4 1.4 copy-done.42
  124.8 4.6 %all-to-all-start.1 = ((bf16[8,2,96,768]{3,2,1,0:T(8,128)(2,1)}), bf16[8,2,96,768]{3,2,1,0:T(8,128)(2,1)}, u32[]{:S(2)}, u32[]{:S(2)}) async-start(bf16[8,2,96,768]{3,2,1,0:T(8,128)(2,1)} %bitcast.33), calls=%async_computation.1 | async-start | bytes 4718592 | tf_op jit(solution)/shard_map/all_to_all | solution.py:266
  129.4 1.8 fusion.34
  131.2 1.6 collective-permute-start.13
  132.8 25.0 %collective-permute-done.13.refs_11_.refs_2_ = bf16[768,768]{1,0:T(8,128)(2,1)S(1)} collective-permute-done((bf16[768,768]{1,0:T(8,128)(2,1)S(1)}, bf16[768,768]{1,0:T(8,128)(2,1)S(1)}, u32[]{:S(2)}, u32[]{:S(2)}) %collective-permute-start.13) | collective-permute-done | bytes 1179680 | tf_op jit(solution)/shard_map/ppermute | solution.py:258
  157.8 3.8 %copy.55 = bf16[2,8,96,768]{3,2,0,1:T(8,128)(2,1)} copy(bf16[2,8,96,768]{3,2,1,0:T(8,128)(2,1)} %param.13) | data formatting | bytes 4718592 | tf_op args[6]
  161.7 1.6 collective-permute-start.16
  164.7 4.3 %shard_map.102 = (bf16[384,3072]{1,0:T(8,128)(2,1)S(1)}, bf16[384,768]{1,0:T(8,128)(2,1)S(1)}, f32[384,768]{1,0:T(8,128)S(1)}) custom-call(s32[1]{0:T(128)} %bitcast.place, bf16[48,3072]{1,0:T(8,128)(2,1)S(1)} %copy-done.20, bf16[48,3072]{1,0:T(8,128)(2,1)S(1)} %copy-done.34, bf16[48,3072]{1,0:T(8,128)(2,1)S(1)} %copy-done.32, ...), custom_call_target="tpu_custom_call" | custom-call | tf_op jit(solution)/shard_map/pallas_call | solution.py:32
  170.0 3.1 %shard_map.106 = (bf16[768,768]{1,0:T(8,128)(2,1)S(1)}, bf16[768,768]{1,0:T(8,128)(2,1)S(1)}, bf16[768,768]{1,0:T(8,128)(2,1)S(1)}, bf16[768,768]{1,0:T(8,128)(2,1)S(1)}) custom-call(s32[1]{0:T(128)} %bitcast.place, bf16[384,768]{1,0:T(8,128)(2,1)S(1)} %get-tuple-element.54.grad_up.grads, bf16[384,3072]{1,0:T(8,128)(2,1)S(1)} %get-tuple-element.49.rows), custom_call_target="tpu_custom_call" | custom-call | tf_op jit(solution)/shard_map/pallas_call | solution.py:32
  178.1 4.2 %all-to-all-done.1.refs_4_ = bf16[8,2,96,768]{3,2,1,0:T(8,128)(2,1)} async-done(((bf16[8,2,96,768]{3,2,1,0:T(8,128)(2,1)}), bf16[8,2,96,768]{3,2,1,0:T(8,128)(2,1)}, u32[]{:S(2)}, u32[]{:S(2)}) %all-to-all-start.1) | async-done | bytes 2359328 | tf_op jit(solution)/shard_map/all_to_all | solution.py:266
  182.3 4.4 %all-to-all-start.2 = ((bf16[8,2,96,768]{3,2,1,0:T(8,128)(2,1)}), bf16[8,2,96,768]{3,2,1,0:T(8,128)(2,1)}, u32[]{:S(2)}, u32[]{:S(2)}) async-start(bf16[8,2,96,768]{3,2,1,0:T(8,128)(2,1)} %bitcast.46), calls=%async_computation.2 | async-start | bytes 4718592 | tf_op jit(solution)/shard_map/all_to_all | solution.py:266
  186.8 3.0 %collective-permute-done.16.refs_2_.refs_6_ = bf16[768,768]{1,0:T(8,128)(2,1)} collective-permute-done((bf16[768,768]{1,0:T(8,128)(2,1)S(1)}, bf16[768,768]{1,0:T(8,128)(2,1)}, u32[]{:S(2)}, u32[]{:S(2)}) %collective-permute-start.16) | collective-permute-done | bytes 1179680 | tf_op jit(solution)/shard_map/ppermute | solution.py:258
  190.3 2.5 collective-permute-done.17.refs_3_.refs_7_
  194.1 3.7 %shard_map.103.grad_gate.grads = bf16[384,768]{1,0:T(8,128)(2,1)S(1)} custom-call(s32[1]{0:T(128)} %bitcast.place, bf16[384,3072]{1,0:T(8,128)(2,1)S(1)} %get-tuple-element.49.rows, f32[384,768]{1,0:T(8,128)S(1)} %copy-done.18, bf16[768,768]{1,0:T(8,128)(2,1)S(1)} %bitcast.37, bf16[768,768]{1,0:T(8,128)(2,1)S(1)} %collective-permute-done.15.refs_1_.refs_5_, ...), custom_call_target="tpu_custom_call" | custom-call | tf_op jit(solution)/shard_map/pallas_call | solution.py:32
  197.9 5.7 %shard_map.104 = (bf16[48,3072]{1,0:T(8,128)(2,1)S(1)}, bf16[48,3072]{1,0:T(8,128)(2,1)S(1)}, bf16[48,3072]{1,0:T(8,128)(2,1)S(1)}, bf16[48,3072]{1,0:T(8,128)(2...) custom-call(s32[1]{0:T(128)} %bitcast.place, ...), custom_call_target="tpu_custom_call" | custom-call | tf_op jit(solution)/shard_map/pallas_call | solution.py:32
  203.6 3.6 %shard_map.105 = (bf16[768,768]{1,0:T(8,128)(2,1)S(1)}, bf16[768,768]{1,0:T(8,128)(2,1)}, bf16[768,768]{1,0:T(8,128)(2,1)S(1)}, bf16[768,768]{1,0:T(8,128)(2,1)S(1)}) custom-call(s32[1]{0:T(128)} %bitcast.place, bf16[384,768]{1,0:T(8,128)(2,1)S(1)} %shard_map.103.grad_gate.grads, bf16[384,3072]{1,0:T(8,128)(2,1)S(1)} %get-tuple-element.49.rows), custom_call_target="tpu_custom_call" | custom-call | tf_op jit(solution)/shard_map/pallas_call | solution.py:32
  208.4 1.5 collective-permute-start.26
  209.9 2.6 collective-permute-start.18
  213.6 1.4 add_convert_fusion.1
  215.0 21.4 %collective-permute-done.26.refs_2_ = bf16[768,768]{1,0:T(8,128)(2,1)S(1)} collective-permute-done((bf16[768,768]{1,0:T(8,128)(2,1)S(1)}, bf16[768,768]{1,0:T(8,128)(2,1)S(1)}, u32[]{:S(2)}, u32[]{:S(2)}) %collective-permute-start.26) | collective-permute-done | bytes 1179680 | tf_op jit(solution)/shard_map/ppermute | solution.py:258
  237.4 1.5 collective-permute-start.27
  238.9 1.3 convolution_convert_fusion.2
  240.2 3.5 %collective-permute-start.30 = (bf16[128,3072]{1,0:T(8,128)(2,1)}, bf16[128,3072]{1,0:T(8,128)(2,1)S(1)}, u32[]{:S(2)}, u32[]{:S(2)}) collective-permute-start(bf16[128,3072]{1,0:T(8,128)(2,1)} %convolution_convert_fusion.2), channel_id=1, source_target_pairs={{0,4},{1,5},{2,6},{3,7},{4,0},{5,1},{6,2},{7,3},{8,12},{9,13},{10,... | collective-permute-start | bytes 2359304 | tf_op jit(solution)/shard_map/ppermute | solution.py:352
  244.3 1.5 collective-permute-start.28
  245.7 1.5 collective-permute-start.21
  249.8 7.0 %shard_map.107 = (bf16[2,1,768,768]{3,2,1,0:T(8,128)(2,1)}, bf16[2,1,768,768]{3,2,1,0:T(8,128)(2,1)}, bf16[2,1,768,768]{3,2,1,0:T(8,128)(2,1)}) custom-call(bf16[768,768]{1,0:T(8,128)(2,1)S(1)} %copy-done.10, bf16[768,768]{1,0:T(8,128)(2,1)S(1)} %copy-done.12, bf16[768,768]{1,0:T(8,128)(2,1)S(1)} %copy-done.16, bf16[768,768]{1,0:T(8,128)(2,1)S(1)} %bitcast.39, ...), custom_call_target="tpu_custom_call" | custom-call | tf_op jit(solution)/shard_map/pallas_call | solution.py:212
  256.7 8.3 %collective-permute-done.27.refs_2_ = bf16[768,768]{1,0:T(8,128)(2,1)} collective-permute-done((bf16[768,768]{1,0:T(8,128)(2,1)}, bf16[768,768]{1,0:T(8,128)(2,1)}, u32[]{:S(2)}, u32[]{:S(2)}) %collective-permute-start.27) | collective-permute-done | bytes 1179680 | tf_op jit(solution)/shard_map/ppermute | solution.py:258
  265.0 7.5 %shard_map.108 = (bf16[2,1,768,768]{3,2,1,0:T(8,128)(2,1)}, bf16[2,1,768,768]{3,2,1,0:T(8,128)(2,1)}, bf16[2,1,768,768]{3,2,1,0:T(8,128)(2,1)}) custom-call(bf16[768,768]{1,0:T(8,128)(2,1)S(1)} %copy-done.14, bf16[768,768]{1,0:T(8,128)(2,1)} %collective-permute-done.22.refs_1_, ...), custom_call_target="tpu_custom_call", output_to_operand_aliasing={{0}: (6, {}), {1}: (7, {}), {2}: (8, {})} | custom-call | tf_op jit(solution)/shard_map/pallas_call | solution.py:212
  272.6 4.2 %collective-permute-done.30 = bf16[128,3072]{1,0:T(8,128)(2,1)S(1)} collective-permute-done((bf16[128,3072]{1,0:T(8,128)(2,1)}, bf16[128,3072]{1,0:T(8,128)(2,1)S(1)}, u32[]{:S(2)}, u32[]{:S(2)}) %collective-permute-start.30) | collective-permute-done | bytes 786464 | tf_op jit(solution)/shard_map/ppermute | solution.py:352
  276.8 1.3 add_convert_fusion.2
  (184 shorter events, 29.9 us)
Async XLA Ops:
  0.6 11.5 %collective-permute-start = (s32[128,2]{0,1:T(2,128)}, s32[128,2]{0,1:T(2,128)S(1)}, u32[]{:S(2)}, u32[]{:S(2)}) collective-permute-start(s32[128,2]{0,1:T(2,128)} %param.8), channel_id=1, source_target_pairs={{0,4},{1,5},{2,6},{3,7},{4,0},{5,1},{6,2},{7,3},{8,12},{9,13},{10,... | collective-permute-start | bytes 3080 | tf_op jit(solution)/shard_map/ppermute | solution.py:282
  8.7 33.8 %collective-permute-start.2 = (bf16[4,48,768]{2,1,0:T(8,128)(2,1)S(1)}, bf16[4,48,768]{2,1,0:T(8,128)(2,1)S(1)}, u32[]{:S(2)}, u32[]{:S(2)}) collective-permute-start(bf16[4,48,768]{2,1,0:T(8,128)(2,1)S(1)} %bitcast.49), channel_id=1, source_target_pairs={{0,4},{1,5},{2,6},{3,7},{4,0},{5,1},{6,2},{7,3},{8,12},{9,13},{10,... | collective-permute-start | bytes 884744 | tf_op jit(solution)/shard_map/ppermute | solution.py:296
  8.8 49.4 %collective-permute-start.1 = (bf16[128,3072]{1,0:T(8,128)(2,1)S(1)}, bf16[128,3072]{1,0:T(8,128)(2,1)S(1)}, u32[]{:S(2)}, u32[]{:S(2)}) collective-permute-start(bf16[128,3072]{1,0:T(8,128)(2,1)S(1)} %copy-done.45), channel_id=1, source_target_pairs={{0,4},{1,5},{2,6},{3,7},{4,0},{5,1},{6,2},{7,3},{8,12},{9,13},{10,... | collective-permute-start | bytes 2359304 | tf_op jit(solution)/shard_map/ppermute | solution.py:281
  14.8 27.7 %collective-permute-start.5 = (bf16[48,3072]{1,0:T(8,128)(2,1)S(1)}, bf16[48,3072]{1,0:T(8,128)(2,1)S(1)}, u32[]{:S(2)}, u32[]{:S(2)}) collective-permute-start(bf16[48,3072]{1,0:T(8,128)(2,1)S(1)} %get-tuple-element.93), channel_id=1, source_target_pairs={{0,3},{1,0},{2,1},{3,2},{4,7},{5,4},{6,5},{7,6},{8,11},{9,8},{10,9... | collective-permute-start | bytes 884744 | tf_op jit(solution)/shard_map/ppermute | solution.py:255
  17.3 27.3 %collective-permute-start.4 = (bf16[48,3072]{1,0:T(8,128)(2,1)S(1)}, bf16[48,3072]{1,0:T(8,128)(2,1)S(1)}, u32[]{:S(2)}, u32[]{:S(2)}) collective-permute-start(bf16[48,3072]{1,0:T(8,128)(2,1)S(1)} %get-tuple-element.94), channel_id=1, source_target_pairs={{0,2},{1,3},{2,0},{3,1},{4,6},{5,7},{6,4},{7,5},{8,10},{9,11},{10,... | collective-permute-start | bytes 884744 | tf_op jit(solution)/shard_map/ppermute | solution.py:255
  17.8 27.6 %collective-permute-start.3 = (bf16[48,3072]{1,0:T(8,128)(2,1)S(1)}, bf16[48,3072]{1,0:T(8,128)(2,1)S(1)}, u32[]{:S(2)}, u32[]{:S(2)}) collective-permute-start(bf16[48,3072]{1,0:T(8,128)(2,1)S(1)} %get-tuple-element.95), channel_id=1, source_target_pairs={{0,1},{1,2},{2,3},{3,0},{4,5},{5,6},{6,7},{7,4},{8,9},{9,10},{10,1... | collective-permute-start | bytes 884744 | tf_op jit(solution)/shard_map/ppermute | solution.py:255
  42.5 15.7 %copy-start.47 = (bf16[4,48,768]{2,1,0:T(8,128)(2,1)}, bf16[4,48,768]{2,1,0:T(8,128)(2,1)S(1)}, u32[]{:S(2)}) copy-start(bf16[4,48,768]{2,1,0:T(8,128)(2,1)S(1)} %collective-permute-done.2) | copy-start | bytes 884740
  58.2 65.2 %all-to-all-start = ((bf16[8,2,96,768]{3,2,1,0:T(8,128)(2,1)}), bf16[8,2,96,768]{3,2,1,0:T(8,128)(2,1)S(1)}, u32[]{:S(2)}, u32[]{:S(2)}) async-start(bf16[8,2,96,768]{3,2,1,0:T(8,128)(2,1)} %bitcast.34), calls=%async_computation | async-start | bytes 4718592 | tf_op jit(solution)/shard_map/all_to_all | solution.py:266
  63.8 37.1 %collective-permute-start.9 = (bf16[96,768]{1,0:T(8,128)(2,1)S(1)}, bf16[96,768]{1,0:T(8,128)(2,1)S(1)}, u32[]{:S(2)}, u32[]{:S(2)}) collective-permute-start(bf16[96,768]{1,0:T(8,128)(2,1)S(1)} %get-tuple-element.101), channel_id=1, source_target_pairs={{0,1},{1,2},{2,3},{3,0},{4,5},{5,6},{6,7},{7,4},{8,9},{9,10},{10,1... | collective-permute-start | bytes 442376 | tf_op jit(solution)/shard_map/ppermute | solution.py:255
  66.2 43.3 %copy-start.44 = (bf16[2,8,96,768]{3,2,1,0:T(8,128)(2,1)S(1)}, bf16[2,8,96,768]{3,2,1,0:T(8,128)(2,1)}, u32[]{:S(2)}) copy-start(bf16[2,8,96,768]{3,2,1,0:T(8,128)(2,1)} %param.12) | copy-start | bytes 7077892
  67.0 54.2 %collective-permute-start.8 = (bf16[48,3072]{1,0:T(8,128)(2,1)S(1)}, bf16[48,3072]{1,0:T(8,128)(2,1)S(1)}, u32[]{:S(2)}, u32[]{:S(2)}) collective-permute-start(bf16[48,3072]{1,0:T(8,128)(2,1)S(1)} %get-tuple-element.96), channel_id=1, source_target_pairs={{0,3},{1,0},{2,1},{3,2},{4,7},{5,4},{6,5},{7,6},{8,11},{9,8},{10,9... | collective-permute-start | bytes 884744 | tf_op jit(solution)/shard_map/ppermute | solution.py:255
  68.0 53.9 %collective-permute-start.7 = (bf16[48,3072]{1,0:T(8,128)(2,1)S(1)}, bf16[48,3072]{1,0:T(8,128)(2,1)S(1)}, u32[]{:S(2)}, u32[]{:S(2)}) collective-permute-start(bf16[48,3072]{1,0:T(8,128)(2,1)S(1)} %get-tuple-element.97), channel_id=1, source_target_pairs={{0,2},{1,3},{2,0},{3,1},{4,6},{5,7},{6,4},{7,5},{8,10},{9,11},{10,... | collective-permute-start | bytes 884744 | tf_op jit(solution)/shard_map/ppermute | solution.py:255
  69.9 52.7 %collective-permute-start.6 = (bf16[48,3072]{1,0:T(8,128)(2,1)S(1)}, bf16[48,3072]{1,0:T(8,128)(2,1)S(1)}, u32[]{:S(2)}, u32[]{:S(2)}) collective-permute-start(bf16[48,3072]{1,0:T(8,128)(2,1)S(1)} %get-tuple-element.98), channel_id=1, source_target_pairs={{0,1},{1,2},{2,3},{3,0},{4,5},{5,6},{6,7},{7,4},{8,9},{9,10},{10,1... | collective-permute-start | bytes 884744 | tf_op jit(solution)/shard_map/ppermute | solution.py:255
  70.5 47.4 %collective-permute-start.11 = (bf16[96,768]{1,0:T(8,128)(2,1)S(1)}, bf16[96,768]{1,0:T(8,128)(2,1)S(1)}, u32[]{:S(2)}, u32[]{:S(2)}) collective-permute-start(bf16[96,768]{1,0:T(8,128)(2,1)S(1)} %get-tuple-element.102), channel_id=1, source_target_pairs={{0,3},{1,0},{2,1},{3,2},{4,7},{5,4},{6,5},{7,6},{8,11},{9,8},{10,9... | collective-permute-start | bytes 442376 | tf_op jit(solution)/shard_map/ppermute | solution.py:255
  100.9 10.1 %copy-start.48 = (bf16[96,768]{1,0:T(8,128)(2,1)}, bf16[96,768]{1,0:T(8,128)(2,1)S(1)}, u32[]{:S(2)}) copy-start(bf16[96,768]{1,0:T(8,128)(2,1)S(1)} %collective-permute-done.9) | copy-start | bytes 442372
  100.9 20.2 %collective-permute-start.10 = (bf16[96,768]{1,0:T(8,128)(2,1)S(1)}, bf16[96,768]{1,0:T(8,128)(2,1)S(1)}, u32[]{:S(2)}, u32[]{:S(2)}) collective-permute-start(bf16[96,768]{1,0:T(8,128)(2,1)S(1)} %get-tuple-element.103), channel_id=1, source_target_pairs={{0,2},{1,3},{2,0},{3,1},{4,6},{5,7},{6,4},{7,5},{8,10},{9,11},{10,... | collective-permute-start | bytes 442376 | tf_op jit(solution)/shard_map/ppermute | solution.py:255
  124.8 57.5 %all-to-all-start.1 = ((bf16[8,2,96,768]{3,2,1,0:T(8,128)(2,1)}), bf16[8,2,96,768]{3,2,1,0:T(8,128)(2,1)}, u32[]{:S(2)}, u32[]{:S(2)}) async-start(bf16[8,2,96,768]{3,2,1,0:T(8,128)(2,1)} %bitcast.33), calls=%async_computation.1 | async-start | bytes 4718592 | tf_op jit(solution)/shard_map/all_to_all | solution.py:266
  131.2 30.5 %copy-start = (bf16[8,1,96,768]{3,2,1,0:T(8,128)(2,1)}, bf16[8,1,96,768]{3,2,1,0:T(8,128)(2,1)S(1)}, u32[]{:S(2)}) copy-start(bf16[8,1,96,768]{3,2,1,0:T(8,128)(2,1)S(1)} %get-tuple-element.91) | copy-start | bytes 3538948
  131.2 26.5 %collective-permute-start.13 = (bf16[768,768]{1,0:T(8,128)(2,1)S(1)}, bf16[768,768]{1,0:T(8,128)(2,1)S(1)}, u32[]{:S(2)}, u32[]{:S(2)}) collective-permute-start(bf16[768,768]{1,0:T(8,128)(2,1)S(1)} %bitcast.40), channel_id=1, source_target_pairs={{0,16},{8,24},{16,0},{24,8},{1,17},{9,25},{17,1},{25,9},{2,18},{10... | collective-permute-start | bytes 3538952 | tf_op jit(solution)/shard_map/ppermute | solution.py:258
  132.8 30.5 %collective-permute-start.12 = (bf16[768,768]{1,0:T(8,128)(2,1)S(1)}, bf16[768,768]{1,0:T(8,128)(2,1)}, u32[]{:S(2)}, u32[]{:S(2)}) collective-permute-start(bf16[768,768]{1,0:T(8,128)(2,1)S(1)} %bitcast.41), channel_id=1, source_target_pairs={{0,8},{8,0},{16,24},{24,16},{1,9},{9,1},{17,25},{25,17},{2,10},{10... | collective-permute-start | bytes 3538952 | tf_op jit(solution)/shard_map/ppermute | solution.py:258
  157.7 5.6 %collective-permute-start.14 = (bf16[768,768]{1,0:T(8,128)(2,1)S(1)}, bf16[768,768]{1,0:T(8,128)(2,1)}, u32[]{:S(2)}, u32[]{:S(2)}) collective-permute-start(bf16[768,768]{1,0:T(8,128)(2,1)S(1)} %collective-permute-done.13.refs_11_.refs_2_), channel_id=1, source_target_pairs={{0,8},{8,0},{16,24},{24,16},{1,9},{9,1},{17,25},{25,17},{2,10},{10... | collective-permute-start | bytes 3538952 | tf_op jit(solution)/shard_map/ppermute | solution.py:258
  157.8 5.6 %copy-start.19 = (bf16[48,3072]{1,0:T(8,128)(2,1)S(1)}, bf16[48,3072]{1,0:T(8,128)(2,1)}, u32[]{:S(2)}) copy-start(bf16[48,3072]{1,0:T(8,128)(2,1)} %get-tuple-element.92.refs_4_) | copy-start | bytes 884740
  161.7 28.1 %collective-permute-start.16 = (bf16[768,768]{1,0:T(8,128)(2,1)S(1)}, bf16[768,768]{1,0:T(8,128)(2,1)}, u32[]{:S(2)}, u32[]{:S(2)}) collective-permute-start(bf16[768,768]{1,0:T(8,128)(2,1)S(1)} %bitcast.35), channel_id=1, source_target_pairs={{0,16},{8,24},{16,0},{24,8},{1,17},{9,25},{17,1},{25,9},{2,18},{10... | collective-permute-start | bytes 3538952 | tf_op jit(solution)/shard_map/ppermute | solution.py:258
  182.3 57.9 %all-to-all-start.2 = ((bf16[8,2,96,768]{3,2,1,0:T(8,128)(2,1)}), bf16[8,2,96,768]{3,2,1,0:T(8,128)(2,1)}, u32[]{:S(2)}, u32[]{:S(2)}) async-start(bf16[8,2,96,768]{3,2,1,0:T(8,128)(2,1)} %bitcast.46), calls=%async_computation.2 | async-start | bytes 4718592 | tf_op jit(solution)/shard_map/all_to_all | solution.py:266
  186.7 3.6 %collective-permute-start.15 = (bf16[768,768]{1,0:T(8,128)(2,1)S(1)}, bf16[768,768]{1,0:T(8,128)(2,1)S(1)}, u32[]{:S(2)}, u32[]{:S(2)}) collective-permute-start(bf16[768,768]{1,0:T(8,128)(2,1)S(1)} %bitcast.36), channel_id=1, source_target_pairs={{0,8},{8,0},{16,24},{24,16},{1,9},{9,1},{17,25},{25,17},{2,10},{10... | collective-permute-start | bytes 3538952 | tf_op jit(solution)/shard_map/ppermute | solution.py:258
  189.8 3.1 %collective-permute-start.17 = (bf16[768,768]{1,0:T(8,128)(2,1)}, bf16[768,768]{1,0:T(8,128)(2,1)S(1)}, u32[]{:S(2)}, u32[]{:S(2)}) collective-permute-start(bf16[768,768]{1,0:T(8,128)(2,1)} %collective-permute-done.16.refs_2_.refs_6_), channel_id=1, source_target_pairs={{0,8},{8,0},{16,24},{24,16},{1,9},{9,1},{17,25},{25,17},{2,10},{10... | collective-permute-start | bytes 3538952 | tf_op jit(solution)/shard_map/ppermute | solution.py:258
  189.8 17.7 %collective-permute-start.25 = (bf16[768,768]{1,0:T(8,128)(2,1)}, bf16[768,768]{1,0:T(8,128)(2,1)S(1)}, u32[]{:S(2)}, u32[]{:S(2)}) collective-permute-start(bf16[768,768]{1,0:T(8,128)(2,1)} %copy-done.36), channel_id=1, source_target_pairs={{0,8},{8,0},{16,24},{24,16},{1,9},{9,1},{17,25},{25,17},{2,10},{10... | collective-permute-start | bytes 3538952 | tf_op jit(solution)/shard_map/ppermute | solution.py:258
  190.3 22.8 %collective-permute-start.24 = (bf16[768,768]{1,0:T(8,128)(2,1)}, bf16[768,768]{1,0:T(8,128)(2,1)S(1)}, u32[]{:S(2)}, u32[]{:S(2)}) collective-permute-start(bf16[768,768]{1,0:T(8,128)(2,1)} %copy-done.35), channel_id=1, source_target_pairs={{0,8},{8,0},{16,24},{24,16},{1,9},{9,1},{17,25},{25,17},{2,10},{10... | collective-permute-start | bytes 3538952 | tf_op jit(solution)/shard_map/ppermute | solution.py:258
  190.3 7.6 %copy-start.2 = (bf16[8,1,96,768]{3,2,1,0:T(8,128)(2,1)S(1)}, bf16[8,1,96,768]{3,2,1,0:T(8,128)(2,1)}, u32[]{:S(2)}) copy-start(bf16[8,1,96,768]{3,2,1,0:T(8,128)(2,1)} %copy-done) | copy-start | bytes 3538948
  190.3 7.6 %copy-start.6 = (bf16[768,768]{1,0:T(8,128)(2,1)S(1)}, bf16[768,768]{1,0:T(8,128)(2,1)}, u32[]{:S(2)}) copy-start(bf16[768,768]{1,0:T(8,128)(2,1)} %copy-done.4) | copy-start | bytes 3538948
  190.3 7.6 %copy-start.8 = (bf16[384,768]{1,0:T(8,128)(2,1)S(1)}, bf16[384,768]{1,0:T(8,128)(2,1)}, u32[]{:S(2)}) copy-start(bf16[384,768]{1,0:T(8,128)(2,1)} %copy-done.7) | copy-start | bytes 1769476
  207.3 6.3 %collective-permute-start.23 = (bf16[768,768]{1,0:T(8,128)(2,1)S(1)}, bf16[768,768]{1,0:T(8,128)(2,1)S(1)}, u32[]{:S(2)}, u32[]{:S(2)}) collective-permute-start(bf16[768,768]{1,0:T(8,128)(2,1)S(1)} %get-tuple-element.69), channel_id=1, source_target_pairs={{0,8},{8,0},{16,24},{24,16},{1,9},{9,1},{17,25},{25,17},{2,10},{10... | collective-permute-start | bytes 3538952 | tf_op jit(solution)/shard_map/ppermute | solution.py:258
  208.4 28.0 %collective-permute-start.26 = (bf16[768,768]{1,0:T(8,128)(2,1)S(1)}, bf16[768,768]{1,0:T(8,128)(2,1)S(1)}, u32[]{:S(2)}, u32[]{:S(2)}) collective-permute-start(bf16[768,768]{1,0:T(8,128)(2,1)S(1)} %add_convert_fusion), channel_id=1, source_target_pairs={{0,16},{8,24},{16,0},{24,8},{1,17},{9,25},{17,1},{25,9},{2,18},{10... | collective-permute-start | bytes 3538952 | tf_op jit(solution)/shard_map/ppermute | solution.py:258
  209.9 29.0 %collective-permute-start.18 = (bf16[48,3072]{1,0:T(8,128)(2,1)S(1)}, bf16[48,3072]{1,0:T(8,128)(2,1)S(1)}, u32[]{:S(2)}, u32[]{:S(2)}) collective-permute-start(bf16[48,3072]{1,0:T(8,128)(2,1)S(1)} %get-tuple-element.56), channel_id=1, source_target_pairs={{0,3},{1,0},{2,1},{3,2},{4,7},{5,4},{6,5},{7,6},{8,11},{9,8},{10,9... | collective-permute-start | bytes 884744 | tf_op jit(solution)/shard_map/ppermute | solution.py:255
  212.5 26.5 %collective-permute-start.19 = (bf16[48,3072]{1,0:T(8,128)(2,1)S(1)}, bf16[48,3072]{1,0:T(8,128)(2,1)S(1)}, u32[]{:S(2)}, u32[]{:S(2)}) collective-permute-start(bf16[48,3072]{1,0:T(8,128)(2,1)S(1)} %get-tuple-element.57), channel_id=1, source_target_pairs={{0,2},{1,3},{2,0},{3,1},{4,6},{5,7},{6,4},{7,5},{8,10},{9,11},{10,... | collective-permute-start | bytes 884744 | tf_op jit(solution)/shard_map/ppermute | solution.py:255
  213.0 25.9 %collective-permute-start.20 = (bf16[48,3072]{1,0:T(8,128)(2,1)S(1)}, bf16[48,3072]{1,0:T(8,128)(2,1)S(1)}, u32[]{:S(2)}, u32[]{:S(2)}) collective-permute-start(bf16[48,3072]{1,0:T(8,128)(2,1)S(1)} %get-tuple-element.58), channel_id=1, source_target_pairs={{0,1},{1,2},{2,3},{3,0},{4,5},{5,6},{6,7},{7,4},{8,9},{9,10},{10,1... | collective-permute-start | bytes 884744 | tf_op jit(solution)/shard_map/ppermute | solution.py:255
  213.6 32.1 %collective-permute-start.22 = (bf16[768,768]{1,0:T(8,128)(2,1)}, bf16[768,768]{1,0:T(8,128)(2,1)}, u32[]{:S(2)}, u32[]{:S(2)}) collective-permute-start(bf16[768,768]{1,0:T(8,128)(2,1)} %get-tuple-element.67), channel_id=1, source_target_pairs={{0,8},{8,0},{16,24},{24,16},{1,9},{9,1},{17,25},{25,17},{2,10},{10... | collective-permute-start | bytes 3538952 | tf_op jit(solution)/shard_map/ppermute | solution.py:258
  213.6 25.3 %copy-start.57 = (pred[192,128]{1,0:T(8,128)(4,1)S(1)}, pred[192,128]{1,0:T(8,128)(4,1)}, u32[]{:S(2)}) copy-start(pred[192,128]{1,0:T(8,128)(4,1)} %get-tuple-element.89) | copy-start | bytes 73732
  215.0 32.2 %copy-start.10 = (bf16[768,768]{1,0:T(8,128)(2,1)S(1)}, bf16[768,768]{1,0:T(8,128)(2,1)}, u32[]{:S(2)}) copy-start(bf16[768,768]{1,0:T(8,128)(2,1)} %copy-done.9) | copy-start | bytes 3538948
  237.4 27.6 %collective-permute-start.27 = (bf16[768,768]{1,0:T(8,128)(2,1)}, bf16[768,768]{1,0:T(8,128)(2,1)}, u32[]{:S(2)}, u32[]{:S(2)}) collective-permute-start(bf16[768,768]{1,0:T(8,128)(2,1)} %add_convert_fusion.1), channel_id=1, source_target_pairs={{0,16},{8,24},{16,0},{24,8},{1,17},{9,25},{17,1},{25,9},{2,18},{10... | collective-permute-start | bytes 3538952 | tf_op jit(solution)/shard_map/ppermute | solution.py:258
  240.2 24.8 %copy-start.3 = (bf16[8,1,96,768]{3,2,1,0:T(8,128)(2,1)S(1)}, bf16[8,1,96,768]{3,2,1,0:T(8,128)(2,1)}, u32[]{:S(2)}) copy-start(bf16[8,1,96,768]{3,2,1,0:T(8,128)(2,1)} %copy-done) | copy-start | bytes 3538948
  240.2 36.5 %collective-permute-start.30 = (bf16[128,3072]{1,0:T(8,128)(2,1)}, bf16[128,3072]{1,0:T(8,128)(2,1)S(1)}, u32[]{:S(2)}, u32[]{:S(2)}) collective-permute-start(bf16[128,3072]{1,0:T(8,128)(2,1)} %convolution_convert_fusion.2), channel_id=1, source_target_pairs={{0,4},{1,5},{2,6},{3,7},{4,0},{5,1},{6,2},{7,3},{8,12},{9,13},{10,... | collective-permute-start | bytes 2359304 | tf_op jit(solution)/shard_map/ppermute | solution.py:352
  243.8 28.8 %collective-permute-start.29 = (bf16[48,3072]{1,0:T(8,128)(2,1)}, bf16[48,3072]{1,0:T(8,128)(2,1)S(1)}, u32[]{:S(2)}, u32[]{:S(2)}) collective-permute-start(bf16[48,3072]{1,0:T(8,128)(2,1)} %copy-done.41), channel_id=1, source_target_pairs={{0,1},{1,2},{2,3},{3,0},{4,5},{5,6},{6,7},{7,4},{8,9},{9,10},{10,1... | collective-permute-start | bytes 884744 | tf_op jit(solution)/shard_map/ppermute | solution.py:255
  244.3 28.3 %collective-permute-start.28 = (bf16[48,3072]{1,0:T(8,128)(2,1)}, bf16[48,3072]{1,0:T(8,128)(2,1)S(1)}, u32[]{:S(2)}, u32[]{:S(2)}) collective-permute-start(bf16[48,3072]{1,0:T(8,128)(2,1)} %copy-done.40), channel_id=1, source_target_pairs={{0,2},{1,3},{2,0},{3,1},{4,6},{5,7},{6,4},{7,5},{8,10},{9,11},{10,... | collective-permute-start | bytes 884744 | tf_op jit(solution)/shard_map/ppermute | solution.py:255
  245.7 26.8 %collective-permute-start.21 = (bf16[48,3072]{1,0:T(8,128)(2,1)}, bf16[48,3072]{1,0:T(8,128)(2,1)S(1)}, u32[]{:S(2)}, u32[]{:S(2)}) collective-permute-start(bf16[48,3072]{1,0:T(8,128)(2,1)} %copy-done.39), channel_id=1, source_target_pairs={{0,3},{1,0},{2,1},{3,2},{4,7},{5,4},{6,5},{7,6},{8,11},{9,8},{10,9... | collective-permute-start | bytes 884744 | tf_op jit(solution)/shard_map/ppermute | solution.py:255
  249.8 15.3 %copy-start.14 = (bf16[768,768]{1,0:T(8,128)(2,1)S(1)}, bf16[768,768]{1,0:T(8,128)(2,1)}, u32[]{:S(2)}) copy-start(bf16[768,768]{1,0:T(8,128)(2,1)} %copy-done.13) | copy-start | bytes 3538948
  265.0 11.7 %copy-start.38 = (bf16[48,3072]{1,0:T(8,128)(2,1)S(1)}, bf16[48,3072]{1,0:T(8,128)(2,1)}, u32[]{:S(2)}) copy-start(bf16[48,3072]{1,0:T(8,128)(2,1)} %copy-done.37) | copy-start | bytes 884740
  265.0 11.7 %copy-start.55 = (pred[192,128]{1,0:T(8,128)(4,1)S(1)}, pred[192,128]{1,0:T(8,128)(4,1)}, u32[]{:S(2)}) copy-start(pred[192,128]{1,0:T(8,128)(4,1)} %copy-done.54) | copy-start | bytes 73732
  (45 other events, 127.8 us)

commit v3 on v2

--- a/solution.py
+++ b/solution.py
@@ -182,25 +182,25 @@
     )
 
 
-def adam(index, parts, old, first_old, second_old, *results):
+def adam(index, parts, old, moments, *results):
     rows, width = old.shape
-    sources, _, part, _ = second_old.shape
+    sources, _, _, part, _ = moments.shape
     flat = pl.BlockSpec((part, width), lambda i: (i, 0))
-    moment = pl.BlockSpec((1, 1, part, width), lambda i: (i, index, 0, 0))
+    moment = pl.BlockSpec((1, 2, 1, part, width), lambda i: (i, 0, index, 0, 0))
     out = pl.BlockSpec((1, 1, part, width), lambda i: (index, 0, i, 0))
     shape = jax.ShapeDtypeStruct((2, 1, rows, width), old.dtype)
     count = len(parts)
 
     def body(*refs):
-        old_ref, first_ref, second_ref = refs[count : count + 3]
+        old_ref, moments_ref = refs[count : count + 2]
         weights_out, first_out, second_out = refs[-3:]
         gradient = refs[0][...].astype(f32)
         for ref in refs[1:count]:
             gradient += ref[...].astype(f32)
         gradient = gradient / loss_scale
-        moment_one = beta_one * first_ref[0, 0].astype(f32) + (1.0 - beta_one) * gradient
+        moment_one = beta_one * moments_ref[0, 0, 0].astype(f32) + (1.0 - beta_one) * gradient
         moment_two = (
-            beta_two * second_ref[0, 0].astype(f32) + (1.0 - beta_two) * gradient * gradient
+            beta_two * moments_ref[0, 1, 0].astype(f32) + (1.0 - beta_two) * gradient * gradient
         )
         updated = old_ref[...].astype(f32) - step_size * moment_one / (
             jnp.sqrt(moment_two) + adam_eps
@@ -213,13 +213,13 @@
         body,
         grid=(sources,),
         in_specs=[flat] * (count + 1)
-        + [moment] * 2
+        + [moment]
         + [pl.BlockSpec(memory_space=pl.ANY)] * len(results),
         out_specs=[out] * 3,
         out_shape=[shape] * 3,
-        input_output_aliases={count + 3 + i: i for i in range(len(results))},
+        input_output_aliases={count + 2 + i: i for i in range(len(results))},
         compiler_params=pltpu.CompilerParams(vmem_limit_bytes=vmem_bytes),
-    )(*parts, old, first_old, second_old, *results)
+    )(*parts, old, moments, *results)
 
 
 def slot_targets(flat_route, capacity):
@@ -261,8 +261,8 @@
         expert = of_side * half + (local + jnp.arange(half, dtype=jnp.int32)) % half
         return expert[:, None] * capacity + jnp.arange(capacity, dtype=jnp.int32)[None, :]
 
-    def to_owners(part, *earlier):
-        by_owner = after(jnp.swapaxes(part, 0, 1), *earlier) if earlier else jnp.swapaxes(part, 0, 1)
+    def to_owners(by_owner, *earlier):
+        by_owner = after(by_owner, *earlier)
         return lax.all_to_all(by_owner, "expert", split_axis=0, concat_axis=0, tiled=True)
 
     def along_x(part):
@@ -271,12 +271,16 @@
     def both_cores(parts):
         return [piece for one in parts for piece in (one, across(one, 1))]
 
-    def scatter(totals, *earlier):
-        terms = [totals[0], across(totals[1], 1)]
+    def core_sums(totals):
+        sums = []
         for k in range(2, pieces, 2):
             pair = totals[k].astype(f32) + across(totals[k + 1], 1).astype(f32)
-            terms.append(across(after(pair.astype(bf16), *earlier), k))
-        return terms
+            sums.append(pair.astype(bf16))
+        return sums
+
+    def scatter(totals, sums):
+        sums = [across(pair, 2 * (k + 1)) for k, pair in enumerate(sums)]
+        return [totals[0], across(totals[1], 1)] + sums
 
     other_tokens = lax.ppermute(tokens, "expert", swap)
     other_routes = lax.ppermute(routes, "expert", swap)
@@ -307,16 +311,17 @@
 
     near_pick = pick_matrix(target)
     near_rows = send_rows(near_pick, tokens)
-    other_tokens = after(other_tokens, other_routes, far_grads, *near_rows[1:])
+    grads_out = jnp.concatenate([far_grads, pick_grads(near_ids)], axis=1)
+    grads_in = [shift(grads_out[s], s) for s in range(half)]
+    other_tokens = after(other_tokens, other_routes, *grads_in[1:], *near_rows[1:])
     other_pick = pick_matrix(slot_targets(other_routes.reshape(-1), capacity))
     far_rows = send_rows(other_pick, other_tokens)
-    grads_out = jnp.concatenate([far_grads, pick_grads(near_ids)], axis=1)
-    grads_in = [shift(grads_out[s], s) for s in range(half)]
-
-    owned = after(to_owners(weights, other_tokens), *far_rows[1:], *grads_in[1:])
+
+    owned = after(to_owners(jnp.swapaxes(weights, 0, 1), other_tokens), *far_rows[1:])
     owned_gate = owned[:, 0].reshape(hidden_units, -1)
     owned_up = owned[:, 1].reshape(hidden_units, -1)
-    owned_first = to_owners(first_moment, owned)
+    moments = [jnp.swapaxes(moment, 0, 1) for moment in (first_moment, second_moment)]
+    moments = to_owners(jnp.stack(moments, axis=1), owned)
 
     gate_x = along_x(owned_gate)
     up_x = along_x(after(owned_up, *gate_x))
@@ -331,9 +336,9 @@
         blocks = [jnp.concatenate(blocks, axis=0)]
     rows, grad_up, factor = forward_gate(place, blocks, upstream, gate)
     up_totals = weight_grads(place, grad_up, rows, pieces)
-    up_terms = scatter(up_totals)
-    owned_second = to_owners(second_moment, owned_first, up_totals[0])
-    grad_gate = forward_up(place, rows, after(factor, owned_first), up)
+    up_sums = core_sums(up_totals)
+    up_terms = scatter(up_totals, up_sums)
+    grad_gate = forward_up(place, rows, after(factor, *up_sums), up)
     back = input_grads(
         place, grad_gate, grad_up, gate, up, rows.shape[0] if joined else capacity
     )
@@ -342,16 +347,17 @@
     far_back = [shift(back[s], -s) for s in range(half)]
     near_back = [shift(after(back[half + s], *far_back[1:]), -s) for s in range(half)]
     gate_totals = weight_grads(place, after(grad_gate, *back), rows, pieces)
-    gate_terms = scatter(gate_totals, *up_terms)
+    gate_sums = [after(pair, *up_terms) for pair in core_sums(gate_totals)]
+    gate_terms = scatter(gate_totals, gate_sums)
 
     def combine(picker, parts):
         parts = jnp.concatenate(parts, axis=0)
         return jnp.einsum("st,sd->td", picker, parts, preferred_element_type=f32)
 
-    far_sum = after(combine(other_pick, far_back).astype(bf16), owned_second, *up_terms)
+    far_sum = after(combine(other_pick, far_back).astype(bf16), moments, *up_terms)
     far_sum = lax.ppermute(far_sum, "expert", swap)
-    results = adam(1, up_terms, owned_up, owned_first, owned_second)
-    results = adam(0, gate_terms, owned_gate, owned_first, owned_second, *results)
+    results = adam(1, up_terms, owned_up, moments)
+    results = adam(0, gate_terms, owned_gate, moments, *results)
     near_back[1:] = [after(block, *results) for block in near_back[1:]]
     near_sum = combine(near_pick, near_back)
     token_grads = (near_sum + far_sum.astype(f32)).astype(bf16)

time: 279 us -> 285 us (1.022)
  waiting for transfers between devices: 143 us -> 160 us
  starting transfers between devices: 57.2 us -> 46.2 us
    ppermute x15, waiting for transfers between devices: 39.5 us -> 73.3 us  [shift(): return lax.ppermute(value, 'expert', pairs)]
    ppermute x1, waiting for transfers between devices: 12.1 us -> 0.01 us  [per_device(): other_tokens = lax.ppermute(tokens, 'expert', swap)]
    ppermute x15, starting transfers between devices: 27 us -> 19.9 us  [shift(): return lax.ppermute(value, 'expert', pairs)]
    unnamed x122 -> x80, local copies, waits for them, and re-layouts: 26.4 us -> 22.5 us
    all_to_all x3 -> x2, waiting for transfers between devices: 4.21 us -> 0.5 us  [to_owners(): lax.all_to_all(by_owner, 'expert', split_axis=0, concat_axis=0, tiled=True)]
    all_to_all x3 -> x2, starting transfers between devices: 12.6 us -> 10.2 us  [to_owners(): lax.all_to_all(by_owner, 'expert', split_axis=0, concat_axis=0, tiled=True)]
  transfers between devices with their start and end apart: 34 -> 33, of which waited for: 13 -> 15; matrix products, arithmetic and copies ran while one was open for 8% -> 8% of each run, Pallas kernels for 13% -> 12%
where the time goes in v3:
time: 285 us; the launch traced here: 284 us
  waiting for transfers between devices  160 us (56%)
  starting transfers between devices  46.2 us (16%)
  Pallas kernels  33.9 us (12%)
  local copies, waits for them, and re-layouts  29.1 us (10%)
  other arithmetic  8.86 us (3%)
  matrix products  4.79 us (2%)
    ppermute x15, waiting for transfers between devices, shift(): return lax.ppermute(value, 'expert', pairs)  73.3 us
    ppermute x12, waiting for transfers between devices, across(): return lax.ppermute(value, 'dp', [(i, i ^ k) for i in range(pieces)])  57.4 us
    ppermute x1, waiting for transfers between devices, per_device(): far_grads = lax.ppermute(pick_grads(far_ids), 'expert', swap)  24 us
    unnamed x80, local copies, waits for them, and re-layouts  22.5 us
    ppermute x15, starting transfers between devices, shift(): return lax.ppermute(value, 'expert', pairs)  19.9 us
    pallas_call x5, Pallas kernels, run(): pl.pallas_call(body, grid_spec=pltpu.PrefetchScalarGridSpec(num_scalar_pr...  19.6 us
    pallas_call x2, Pallas kernels, adam(): pl.pallas_call(body, grid=(sources,), in_specs=[flat] * (count + 1) + [mo...  14.3 us
    all_to_all x2, starting transfers between devices, to_owners(): lax.all_to_all(by_owner, 'expert', split_axis=0, concat_axis=0, tiled=True)  10.2 us
  transfers between devices with their start and end apart: 33, of which 15 were waited for; matrix products, arithmetic and copies ran while one was open for 8% of the time, Pallas kernels for 12%

profile of v3, /device:TPU:0, one launch (start us, length us, event | category | flops | bytes accessed | tf_op | source)
XLA Modules:
  0.0 284.0 jit_solution(3659560097100771739)
XLA Ops:
  0.7 4.1 %collective-permute-start = (s32[128,2]{0,1:T(2,128)}, s32[128,2]{0,1:T(2,128)S(1)}, u32[]{:S(2)}, u32[]{:S(2)}) collective-permute-start(s32[128,2]{0,1:T(2,128)} %param.8), channel_id=1, source_target_pairs={{0,4},{1,5},{2,6},{3,7},{4,0},{5,1},{6,2},{7,3},{8,12},{9,13},{10,... | collective-permute-start | bytes 3080 | tf_op jit(solution)/shard_map/ppermute | solution.py:286
  6.9 1.4 multiply_convert_fusion
  9.5 2.9 %collective-permute-start.1 = (bf16[128,3072]{1,0:T(8,128)(2,1)S(1)}, bf16[128,3072]{1,0:T(8,128)(2,1)S(1)}, u32[]{:S(2)}, u32[]{:S(2)}) collective-permute-start(bf16[128,3072]{1,0:T(8,128)(2,1)S(1)} %copy-done.30), channel_id=1, source_target_pairs={{0,4},{1,5},{2,6},{3,7},{4,0},{5,1},{6,2},{7,3},{8,12},{9,13},{10,... | collective-permute-start | bytes 2359304 | tf_op jit(solution)/shard_map/ppermute | solution.py:285
  15.4 2.5 collective-permute-start.8
  19.3 24.0 %collective-permute-done.2 = bf16[4,48,768]{2,1,0:T(8,128)(2,1)S(1)} collective-permute-done((bf16[4,48,768]{2,1,0:T(8,128)(2,1)}, bf16[4,48,768]{2,1,0:T(8,128)(2,1)S(1)}, u32[]{:S(2)}, u32[]{:S(2)}) %collective-permute-start.2) | collective-permute-done | bytes 294944 | tf_op jit(solution)/shard_map/ppermute | solution.py:300
  44.0 1.5 collective-permute-start.3
  47.4 1.1 collective-permute-start.5
  48.5 1.6 copy.55
  50.7 12.5 %collective-permute-done.3 = bf16[96,768]{1,0:T(8,128)(2,1)S(1)} collective-permute-done((bf16[96,768]{1,0:T(8,128)(2,1)S(1)}, bf16[96,768]{1,0:T(8,128)(2,1)S(1)}, u32[]{:S(2)}, u32[]{:S(2)}) %collective-permute-start.3) | collective-permute-done | bytes 147488 | tf_op jit(solution)/shard_map/ppermute | solution.py:255
  64.0 5.6 %all-to-all-start = ((bf16[8,2,96,768]{3,2,1,0:T(8,128)(2,1)}), bf16[8,2,96,768]{3,2,1,0:T(8,128)(2,1)S(1)}, u32[]{:S(2)}, u32[]{:S(2)}) async-start(bf16[8,2,96,768]{3,2,1,0:T(8,128)(2,1)} %bitcast.36), calls=%async_computation | async-start | bytes 4718592 | tf_op jit(solution)/shard_map/all_to_all | solution.py:266
  70.9 2.9 %collective-permute-start.11 = (bf16[48,3072]{1,0:T(8,128)(2,1)S(1)}, bf16[48,3072]{1,0:T(8,128)(2,1)S(1)}, u32[]{:S(2)}, u32[]{:S(2)}) collective-permute-start(bf16[48,3072]{1,0:T(8,128)(2,1)S(1)} %get-tuple-element.94), channel_id=1, source_target_pairs={{0,3},{1,0},{2,1},{3,2},{4,7},{5,4},{6,5},{7,6},{8,11},{9,8},{10,9... | collective-permute-start | bytes 884744 | tf_op jit(solution)/shard_map/ppermute | solution.py:255
  74.9 2.0 copy_bitcast_fusion
  76.9 2.6 pad_maximum_fusion
  79.5 36.8 %collective-permute-done.11.refs_3_ = bf16[48,3072]{1,0:T(8,128)(2,1)S(1)} collective-permute-done((bf16[48,3072]{1,0:T(8,128)(2,1)S(1)}, bf16[48,3072]{1,0:T(8,128)(2,1)S(1)}, u32[]{:S(2)}, u32[]{:S(2)}) %collective-permute-start.11) | collective-permute-done | bytes 294944 | tf_op jit(solution)/shard_map/ppermute | solution.py:255
  117.0 4.7 %collective-permute-done.10.refs_2_ = bf16[48,3072]{1,0:T(8,128)(2,1)S(1)} collective-permute-done((bf16[48,3072]{1,0:T(8,128)(2,1)S(1)}, bf16[48,3072]{1,0:T(8,128)(2,1)S(1)}, u32[]{:S(2)}, u32[]{:S(2)}) %collective-permute-start.10) | collective-permute-done | bytes 294944 | tf_op jit(solution)/shard_map/ppermute | solution.py:255
  123.6 1.4 copy-done.27
  125.0 4.6 %all-to-all-start.1 = ((bf16[8,2,2,96,768]{4,3,2,1,0:T(8,128)(2,1)}), bf16[8,2,2,96,768]{4,3,2,1,0:T(8,128)(2,1)}, u32[]{:S(2)}, u32[]{:S(2)}) async-start(bf16[8,2,2,96,768]{4,3,2,1,0:T(8,128)(2,1)} %pad_maximum_fusion), calls=%async_computation.1 | async-start | bytes 9437184 | tf_op jit(solution)/shard_map/all_to_all | solution.py:266
  129.7 1.8 fusion.34
  131.5 1.6 collective-permute-start.13
  133.0 25.4 %collective-permute-done.13.refs_11_.refs_2_ = bf16[768,768]{1,0:T(8,128)(2,1)} collective-permute-done((bf16[768,768]{1,0:T(8,128)(2,1)S(1)}, bf16[768,768]{1,0:T(8,128)(2,1)}, u32[]{:S(2)}, u32[]{:S(2)}) %collective-permute-start.13) | collective-permute-done | bytes 1179680 | tf_op jit(solution)/shard_map/ppermute | solution.py:258
  158.4 1.5 collective-permute-start.17
  159.9 1.2 pad_maximum_fusion.1
  169.3 4.5 %shard_map.102 = (bf16[384,3072]{1,0:T(8,128)(2,1)S(1)}, bf16[384,768]{1,0:T(8,128)(2,1)S(1)}, f32[384,768]{1,0:T(8,128)S(1)}) custom-call(s32[1]{0:T(128)} %bitcast.place, bf16[48,3072]{1,0:T(8,128)(2,1)S(1)} %copy-done.9, bf16[48,3072]{1,0:T(8,128)(2,1)S(1)} %copy-done.21, bf16[48,3072]{1,0:T(8,128)(2,1)S(1)} %copy-done.19, ...), custom_call_target="tpu_custom_call" | custom-call | tf_op jit(solution)/shard_map/pallas_call | solution.py:32
  173.8 3.1 %shard_map.103 = (bf16[768,768]{1,0:T(8,128)(2,1)S(1)}, bf16[768,768]{1,0:T(8,128)(2,1)S(1)}, bf16[768,768]{1,0:T(8,128)(2,1)S(1)}, bf16[768,768]{1,0:T(8,128)(2,1)S(1)}) custom-call(s32[1]{0:T(128)} %bitcast.place, bf16[384,768]{1,0:T(8,128)(2,1)S(1)} %get-tuple-element.50.grads.grad_up, bf16[384,3072]{1,0:T(8,128)(2,1)S(1)} %get-tuple-element.48.rows), custom_call_target="tpu_custom_call" | custom-call | tf_op jit(solution)/shard_map/pallas_call | solution.py:32
  178.5 8.3 %collective-permute-done.17.refs_2_.refs_6_ = bf16[768,768]{1,0:T(8,128)(2,1)S(1)} collective-permute-done((bf16[768,768]{1,0:T(8,128)(2,1)S(1)}, bf16[768,768]{1,0:T(8,128)(2,1)S(1)}, u32[]{:S(2)}, u32[]{:S(2)}) %collective-permute-start.17) | collective-permute-done | bytes 1179680 | tf_op jit(solution)/shard_map/ppermute | solution.py:258
  187.6 2.0 collective-permute-done.18.refs_3_.refs_7_
  189.6 2.6 shard_map.104.grad_gate.grads
  192.3 5.7 %shard_map.105 = (bf16[48,3072]{1,0:T(8,128)(2,1)S(1)}, bf16[48,3072]{1,0:T(8,128)(2,1)S(1)}, bf16[48,3072]{1,0:T(8,128)(2,1)S(1)}, bf16[48,3072]{1,0:T(8,128)(2...) custom-call(s32[1]{0:T(128)} %bitcast.place, ...), custom_call_target="tpu_custom_call" | custom-call | tf_op jit(solution)/shard_map/pallas_call | solution.py:32
  198.7 3.6 %shard_map.106 = (bf16[768,768]{1,0:T(8,128)(2,1)S(1)}, bf16[768,768]{1,0:T(8,128)(2,1)}, bf16[768,768]{1,0:T(8,128)(2,1)S(1)}, bf16[768,768]{1,0:T(8,128)(2,1)S(1)}) custom-call(s32[1]{0:T(128)} %bitcast.place, bf16[384,768]{1,0:T(8,128)(2,1)S(1)} %shard_map.104.grad_gate.grads, bf16[384,3072]{1,0:T(8,128)(2,1)S(1)} %get-tuple-element.48.rows), custom_call_target="tpu_custom_call" | custom-call | tf_op jit(solution)/shard_map/pallas_call | solution.py:32
  202.5 1.5 collective-permute-start.26
  204.0 2.5 collective-permute-start.19
  207.1 1.1 collective-permute-start.21
  208.2 1.3 add_convert_fusion
  209.5 21.2 %collective-permute-done.26.refs_2_ = bf16[768,768]{1,0:T(8,128)(2,1)S(1)} collective-permute-done((bf16[768,768]{1,0:T(8,128)(2,1)S(1)}, bf16[768,768]{1,0:T(8,128)(2,1)S(1)}, u32[]{:S(2)}, u32[]{:S(2)}) %collective-permute-start.26) | collective-permute-done | bytes 1179680 | tf_op jit(solution)/shard_map/ppermute | solution.py:258
  231.7 1.5 collective-permute-start.27
  233.2 11.3 %collective-permute-done.20 = bf16[48,3072]{1,0:T(8,128)(2,1)S(1)} collective-permute-done((bf16[48,3072]{1,0:T(8,128)(2,1)S(1)}, bf16[48,3072]{1,0:T(8,128)(2,1)S(1)}, u32[]{:S(2)}, u32[]{:S(2)}) %collective-permute-start.20) | collective-permute-done | bytes 294944 | tf_op jit(solution)/shard_map/ppermute | solution.py:255
  244.6 1.3 convolution_convert_fusion.2
  245.9 1.8 collective-permute-start.30
  247.7 2.5 collective-permute-start.28
  250.2 2.9 %collective-permute-start.22 = (bf16[48,3072]{1,0:T(8,128)(2,1)}, bf16[48,3072]{1,0:T(8,128)(2,1)S(1)}, u32[]{:S(2)}, u32[]{:S(2)}) collective-permute-start(bf16[48,3072]{1,0:T(8,128)(2,1)} %copy-done.24), channel_id=1, source_target_pairs={{0,3},{1,0},{2,1},{3,2},{4,7},{5,4},{6,5},{7,6},{8,11},{9,8},{10,9... | collective-permute-start | bytes 884744 | tf_op jit(solution)/shard_map/ppermute | solution.py:255
  253.1 1.3 copy-done.3
  254.4 1.3 copy-done.7
  255.7 6.8 %shard_map.107 = (bf16[2,1,768,768]{3,2,1,0:T(8,128)(2,1)}, bf16[2,1,768,768]{3,2,1,0:T(8,128)(2,1)}, bf16[2,1,768,768]{3,2,1,0:T(8,128)(2,1)}) custom-call(bf16[768,768]{1,0:T(8,128)(2,1)S(1)} %copy-done.1, bf16[768,768]{1,0:T(8,128)(2,1)S(1)} %copy-done.3, bf16[768,768]{1,0:T(8,128)(2,1)S(1)} %copy-done.7, bf16[768,768]{1,0:T(8,128)(2,1)S(1)} %bitcast.41, ...), custom_call_target="tpu_custom_call" | custom-call | tf_op jit(solution)/shard_map/pallas_call | solution.py:212
  262.6 7.5 %shard_map.108 = (bf16[2,1,768,768]{3,2,1,0:T(8,128)(2,1)}, bf16[2,1,768,768]{3,2,1,0:T(8,128)(2,1)}, bf16[2,1,768,768]{3,2,1,0:T(8,128)(2,1)}) custom-call(bf16[768,768]{1,0:T(8,128)(2,1)S(1)} %copy-done.5, bf16[768,768]{1,0:T(8,128)(2,1)} %collective-permute-done.23.refs_1_, ...), custom_call_target="tpu_custom_call", output_to_operand_aliasing={{0}: (5, {}), {1}: (6, {}), {2}: (7, {})} | custom-call | tf_op jit(solution)/shard_map/pallas_call | solution.py:212
  270.0 2.3 collective-permute-done.28
  272.3 5.4 %collective-permute-done.22 = bf16[48,3072]{1,0:T(8,128)(2,1)S(1)} collective-permute-done((bf16[48,3072]{1,0:T(8,128)(2,1)}, bf16[48,3072]{1,0:T(8,128)(2,1)S(1)}, u32[]{:S(2)}, u32[]{:S(2)}) %collective-permute-start.22) | collective-permute-done | bytes 294944 | tf_op jit(solution)/shard_map/ppermute | solution.py:255
  277.7 4.9 %collective-permute-done.30 = bf16[128,3072]{1,0:T(8,128)(2,1)S(1)} collective-permute-done((bf16[128,3072]{1,0:T(8,128)(2,1)}, bf16[128,3072]{1,0:T(8,128)(2,1)S(1)}, u32[]{:S(2)}, u32[]{:S(2)}) %collective-permute-start.30) | collective-permute-done | bytes 786464 | tf_op jit(solution)/shard_map/ppermute | solution.py:358
  282.7 1.3 add_convert_fusion.2
  (142 shorter events, 29.7 us)
Async XLA Ops:
  0.6 11.9 %copy-start.38 = (s32[128,2]{0,1:T(2,128)S(1)}, s32[128,2]{0,1:T(2,128)}, u32[]{:S(2)}) copy-start(s32[128,2]{0,1:T(2,128)} %param.8) | copy-start | bytes 3076
  0.6 8.8 %copy-start.30 = (bf16[128,3072]{1,0:T(8,128)(2,1)S(1)}, bf16[128,3072]{1,0:T(8,128)(2,1)}, u32[]{:S(2)}) copy-start(bf16[128,3072]{1,0:T(8,128)(2,1)} %param.7) | copy-start | bytes 2359300
  0.7 12.1 %collective-permute-start = (s32[128,2]{0,1:T(2,128)}, s32[128,2]{0,1:T(2,128)S(1)}, u32[]{:S(2)}, u32[]{:S(2)}) collective-permute-start(s32[128,2]{0,1:T(2,128)} %param.8), channel_id=1, source_target_pairs={{0,4},{1,5},{2,6},{3,7},{4,0},{5,1},{6,2},{7,3},{8,12},{9,13},{10,... | collective-permute-start | bytes 3080 | tf_op jit(solution)/shard_map/ppermute | solution.py:286
  9.4 33.9 %collective-permute-start.2 = (bf16[4,48,768]{2,1,0:T(8,128)(2,1)}, bf16[4,48,768]{2,1,0:T(8,128)(2,1)S(1)}, u32[]{:S(2)}, u32[]{:S(2)}) collective-permute-start(bf16[4,48,768]{2,1,0:T(8,128)(2,1)} %bitcast.1), channel_id=1, source_target_pairs={{0,4},{1,5},{2,6},{3,7},{4,0},{5,1},{6,2},{7,3},{8,12},{9,13},{10,... | collective-permute-start | bytes 884744 | tf_op jit(solution)/shard_map/ppermute | solution.py:300
  9.5 53.8 %collective-permute-start.1 = (bf16[128,3072]{1,0:T(8,128)(2,1)S(1)}, bf16[128,3072]{1,0:T(8,128)(2,1)S(1)}, u32[]{:S(2)}, u32[]{:S(2)}) collective-permute-start(bf16[128,3072]{1,0:T(8,128)(2,1)S(1)} %copy-done.30), channel_id=1, source_target_pairs={{0,4},{1,5},{2,6},{3,7},{4,0},{5,1},{6,2},{7,3},{8,12},{9,13},{10,... | collective-permute-start | bytes 2359304 | tf_op jit(solution)/shard_map/ppermute | solution.py:285
  13.5 56.1 %copy-start.36 = (pred[192,128]{1,0:T(8,128)(4,1)}, pred[192,128]{1,0:T(8,128)(4,1)S(1)}, u32[]{:S(2)}) copy-start(pred[192,128]{1,0:T(8,128)(4,1)S(1)} %get-tuple-element.87) | copy-start | bytes 73732
  14.6 33.9 %copy-start.28 = (bf16[2,8,96,768]{3,2,1,0:T(8,128)(2,1)S(1)}, bf16[2,8,96,768]{3,2,1,0:T(8,128)(2,1)}, u32[]{:S(2)}) copy-start(bf16[2,8,96,768]{3,2,1,0:T(8,128)(2,1)} %param.11) | copy-start | bytes 7077892
  15.4 30.2 %collective-permute-start.8 = (bf16[48,3072]{1,0:T(8,128)(2,1)S(1)}, bf16[48,3072]{1,0:T(8,128)(2,1)S(1)}, u32[]{:S(2)}, u32[]{:S(2)}) collective-permute-start(bf16[48,3072]{1,0:T(8,128)(2,1)S(1)} %get-tuple-element.91), channel_id=1, source_target_pairs={{0,3},{1,0},{2,1},{3,2},{4,7},{5,4},{6,5},{7,6},{8,11},{9,8},{10,9... | collective-permute-start | bytes 884744 | tf_op jit(solution)/shard_map/ppermute | solution.py:255
  17.9 28.7 %collective-permute-start.7 = (bf16[48,3072]{1,0:T(8,128)(2,1)S(1)}, bf16[48,3072]{1,0:T(8,128)(2,1)S(1)}, u32[]{:S(2)}, u32[]{:S(2)}) collective-permute-start(bf16[48,3072]{1,0:T(8,128)(2,1)S(1)} %get-tuple-element.92), channel_id=1, source_target_pairs={{0,2},{1,3},{2,0},{3,1},{4,6},{5,7},{6,4},{7,5},{8,10},{9,11},{10,... | collective-permute-start | bytes 884744 | tf_op jit(solution)/shard_map/ppermute | solution.py:255
  18.4 31.7 %collective-permute-start.6 = (bf16[48,3072]{1,0:T(8,128)(2,1)S(1)}, bf16[48,3072]{1,0:T(8,128)(2,1)S(1)}, u32[]{:S(2)}, u32[]{:S(2)}) collective-permute-start(bf16[48,3072]{1,0:T(8,128)(2,1)S(1)} %get-tuple-element.93), channel_id=1, source_target_pairs={{0,1},{1,2},{2,3},{3,0},{4,5},{5,6},{6,7},{7,4},{8,9},{9,10},{10,1... | collective-permute-start | bytes 884744 | tf_op jit(solution)/shard_map/ppermute | solution.py:255
  44.0 19.2 %collective-permute-start.3 = (bf16[96,768]{1,0:T(8,128)(2,1)S(1)}, bf16[96,768]{1,0:T(8,128)(2,1)S(1)}, u32[]{:S(2)}, u32[]{:S(2)}) collective-permute-start(bf16[96,768]{1,0:T(8,128)(2,1)S(1)} %get-tuple-element.99), channel_id=1, source_target_pairs={{0,1},{1,2},{2,3},{3,0},{4,5},{5,6},{6,7},{7,4},{8,9},{9,10},{10,1... | collective-permute-start | bytes 442376 | tf_op jit(solution)/shard_map/ppermute | solution.py:255
  46.3 17.0 %collective-permute-start.4 = (bf16[96,768]{1,0:T(8,128)(2,1)S(1)}, bf16[96,768]{1,0:T(8,128)(2,1)S(1)}, u32[]{:S(2)}, u32[]{:S(2)}) collective-permute-start(bf16[96,768]{1,0:T(8,128)(2,1)S(1)} %get-tuple-element.100), channel_id=1, source_target_pairs={{0,2},{1,3},{2,0},{3,1},{4,6},{5,7},{6,4},{7,5},{8,10},{9,11},{10,... | collective-permute-start | bytes 442376 | tf_op jit(solution)/shard_map/ppermute | solution.py:255
  47.4 15.9 %collective-permute-start.5 = (bf16[96,768]{1,0:T(8,128)(2,1)S(1)}, bf16[96,768]{1,0:T(8,128)(2,1)S(1)}, u32[]{:S(2)}, u32[]{:S(2)}) collective-permute-start(bf16[96,768]{1,0:T(8,128)(2,1)S(1)} %get-tuple-element.101), channel_id=1, source_target_pairs={{0,3},{1,0},{2,1},{3,2},{4,7},{5,4},{6,5},{7,6},{8,11},{9,8},{10,9... | collective-permute-start | bytes 442376 | tf_op jit(solution)/shard_map/ppermute | solution.py:255
  64.0 59.6 %all-to-all-start = ((bf16[8,2,96,768]{3,2,1,0:T(8,128)(2,1)}), bf16[8,2,96,768]{3,2,1,0:T(8,128)(2,1)S(1)}, u32[]{:S(2)}, u32[]{:S(2)}) async-start(bf16[8,2,96,768]{3,2,1,0:T(8,128)(2,1)} %bitcast.36), calls=%async_computation | async-start | bytes 4718592 | tf_op jit(solution)/shard_map/all_to_all | solution.py:266
  70.1 4.9 %copy-start.29 = (bf16[2,8,96,768]{3,2,1,0:T(8,128)(2,1)S(1)}, bf16[2,8,96,768]{3,2,1,0:T(8,128)(2,1)}, u32[]{:S(2)}) copy-start(bf16[2,8,96,768]{3,2,1,0:T(8,128)(2,1)} %param.13) | copy-start | bytes 7077892
  70.9 45.4 %collective-permute-start.11 = (bf16[48,3072]{1,0:T(8,128)(2,1)S(1)}, bf16[48,3072]{1,0:T(8,128)(2,1)S(1)}, u32[]{:S(2)}, u32[]{:S(2)}) collective-permute-start(bf16[48,3072]{1,0:T(8,128)(2,1)S(1)} %get-tuple-element.94), channel_id=1, source_target_pairs={{0,3},{1,0},{2,1},{3,2},{4,7},{5,4},{6,5},{7,6},{8,11},{9,8},{10,9... | collective-permute-start | bytes 884744 | tf_op jit(solution)/shard_map/ppermute | solution.py:255
  73.8 47.9 %collective-permute-start.10 = (bf16[48,3072]{1,0:T(8,128)(2,1)S(1)}, bf16[48,3072]{1,0:T(8,128)(2,1)S(1)}, u32[]{:S(2)}, u32[]{:S(2)}) collective-permute-start(bf16[48,3072]{1,0:T(8,128)(2,1)S(1)} %get-tuple-element.95), channel_id=1, source_target_pairs={{0,2},{1,3},{2,0},{3,1},{4,6},{5,7},{6,4},{7,5},{8,10},{9,11},{10,... | collective-permute-start | bytes 884744 | tf_op jit(solution)/shard_map/ppermute | solution.py:255
  74.4 48.0 %collective-permute-start.9 = (bf16[48,3072]{1,0:T(8,128)(2,1)S(1)}, bf16[48,3072]{1,0:T(8,128)(2,1)S(1)}, u32[]{:S(2)}, u32[]{:S(2)}) collective-permute-start(bf16[48,3072]{1,0:T(8,128)(2,1)S(1)} %get-tuple-element.96), channel_id=1, source_target_pairs={{0,1},{1,2},{2,3},{3,0},{4,5},{5,6},{6,7},{7,4},{8,9},{9,10},{10,1... | collective-permute-start | bytes 884744 | tf_op jit(solution)/shard_map/ppermute | solution.py:255
  125.0 120.9 %all-to-all-start.1 = ((bf16[8,2,2,96,768]{4,3,2,1,0:T(8,128)(2,1)}), bf16[8,2,2,96,768]{4,3,2,1,0:T(8,128)(2,1)}, u32[]{:S(2)}, u32[]{:S(2)}) async-start(bf16[8,2,2,96,768]{4,3,2,1,0:T(8,128)(2,1)} %pad_maximum_fusion), calls=%async_computation.1 | async-start | bytes 9437184 | tf_op jit(solution)/shard_map/all_to_all | solution.py:266
  131.5 26.9 %collective-permute-start.13 = (bf16[768,768]{1,0:T(8,128)(2,1)S(1)}, bf16[768,768]{1,0:T(8,128)(2,1)}, u32[]{:S(2)}, u32[]{:S(2)}) collective-permute-start(bf16[768,768]{1,0:T(8,128)(2,1)S(1)} %bitcast.42), channel_id=1, source_target_pairs={{0,16},{8,24},{16,0},{24,8},{1,17},{9,25},{17,1},{25,9},{2,18},{10... | collective-permute-start | bytes 3538952 | tf_op jit(solution)/shard_map/ppermute | solution.py:258
  133.0 28.1 %collective-permute-start.12 = (bf16[768,768]{1,0:T(8,128)(2,1)S(1)}, bf16[768,768]{1,0:T(8,128)(2,1)}, u32[]{:S(2)}, u32[]{:S(2)}) collective-permute-start(bf16[768,768]{1,0:T(8,128)(2,1)S(1)} %bitcast.43), channel_id=1, source_target_pairs={{0,8},{8,0},{16,24},{24,16},{1,9},{9,1},{17,25},{25,17},{2,10},{10... | collective-permute-start | bytes 3538952 | tf_op jit(solution)/shard_map/ppermute | solution.py:258
  158.4 3.2 %collective-permute-start.14 = (bf16[768,768]{1,0:T(8,128)(2,1)}, bf16[768,768]{1,0:T(8,128)(2,1)}, u32[]{:S(2)}, u32[]{:S(2)}) collective-permute-start(bf16[768,768]{1,0:T(8,128)(2,1)} %collective-permute-done.13.refs_11_.refs_2_), channel_id=1, source_target_pairs={{0,8},{8,0},{16,24},{24,16},{1,9},{9,1},{17,25},{25,17},{2,10},{10... | collective-permute-start | bytes 3538952 | tf_op jit(solution)/shard_map/ppermute | solution.py:258
  158.4 28.4 %collective-permute-start.17 = (bf16[768,768]{1,0:T(8,128)(2,1)S(1)}, bf16[768,768]{1,0:T(8,128)(2,1)S(1)}, u32[]{:S(2)}, u32[]{:S(2)}) collective-permute-start(bf16[768,768]{1,0:T(8,128)(2,1)S(1)} %bitcast.37), channel_id=1, source_target_pairs={{0,16},{8,24},{16,0},{24,8},{1,17},{9,25},{17,1},{25,9},{2,18},{10... | collective-permute-start | bytes 3538952 | tf_op jit(solution)/shard_map/ppermute | solution.py:258
  178.0 9.3 %collective-permute-start.15 = (bf16[768,768]{1,0:T(8,128)(2,1)S(1)}, bf16[768,768]{1,0:T(8,128)(2,1)S(1)}, u32[]{:S(2)}, u32[]{:S(2)}) collective-permute-start(bf16[768,768]{1,0:T(8,128)(2,1)S(1)} %get-tuple-element.52), channel_id=1, source_target_pairs={{0,8},{8,0},{16,24},{24,16},{1,9},{9,1},{17,25},{25,17},{2,10},{10... | collective-permute-start | bytes 3538952 | tf_op jit(solution)/shard_map/ppermute | solution.py:258
  178.1 9.5 %collective-permute-start.16 = (bf16[768,768]{1,0:T(8,128)(2,1)S(1)}, bf16[768,768]{1,0:T(8,128)(2,1)S(1)}, u32[]{:S(2)}, u32[]{:S(2)}) collective-permute-start(bf16[768,768]{1,0:T(8,128)(2,1)S(1)} %bitcast.38), channel_id=1, source_target_pairs={{0,8},{8,0},{16,24},{24,16},{1,9},{9,1},{17,25},{25,17},{2,10},{10... | collective-permute-start | bytes 3538952 | tf_op jit(solution)/shard_map/ppermute | solution.py:258
  186.8 2.8 %collective-permute-start.18 = (bf16[768,768]{1,0:T(8,128)(2,1)S(1)}, bf16[768,768]{1,0:T(8,128)(2,1)S(1)}, u32[]{:S(2)}, u32[]{:S(2)}) collective-permute-start(bf16[768,768]{1,0:T(8,128)(2,1)S(1)} %collective-permute-done.17.refs_2_.refs_6_), channel_id=1, source_target_pairs={{0,8},{8,0},{16,24},{24,16},{1,9},{9,1},{17,25},{25,17},{2,10},{10... | collective-permute-start | bytes 3538952 | tf_op jit(solution)/shard_map/ppermute | solution.py:258
  186.8 20.3 %collective-permute-start.25 = (bf16[768,768]{1,0:T(8,128)(2,1)S(1)}, bf16[768,768]{1,0:T(8,128)(2,1)S(1)}, u32[]{:S(2)}, u32[]{:S(2)}) collective-permute-start(bf16[768,768]{1,0:T(8,128)(2,1)S(1)} %get-tuple-element.71), channel_id=1, source_target_pairs={{0,8},{8,0},{16,24},{24,16},{1,9},{9,1},{17,25},{25,17},{2,10},{10... | collective-permute-start | bytes 3538952 | tf_op jit(solution)/shard_map/ppermute | solution.py:258
  198.7 10.8 %copy-start.24 = (bf16[48,3072]{1,0:T(8,128)(2,1)}, bf16[48,3072]{1,0:T(8,128)(2,1)S(1)}, u32[]{:S(2)}) copy-start(bf16[48,3072]{1,0:T(8,128)(2,1)S(1)} %get-tuple-element.61) | copy-start | bytes 884740
  198.7 10.8 %copy-start.25 = (bf16[48,3072]{1,0:T(8,128)(2,1)}, bf16[48,3072]{1,0:T(8,128)(2,1)S(1)}, u32[]{:S(2)}) copy-start(bf16[48,3072]{1,0:T(8,128)(2,1)S(1)} %get-tuple-element.81) | copy-start | bytes 884740
  198.7 10.8 %copy-start.26 = (bf16[48,3072]{1,0:T(8,128)(2,1)}, bf16[48,3072]{1,0:T(8,128)(2,1)S(1)}, u32[]{:S(2)}) copy-start(bf16[48,3072]{1,0:T(8,128)(2,1)S(1)} %get-tuple-element.83) | copy-start | bytes 884740
  202.3 7.2 %copy-start.4 = (bf16[768,768]{1,0:T(8,128)(2,1)}, bf16[768,768]{1,0:T(8,128)(2,1)S(1)}, u32[]{:S(2)}) copy-start(bf16[768,768]{1,0:T(8,128)(2,1)S(1)} %get-tuple-element.66.refs_0_) | copy-start | bytes 3538948
  202.3 5.9 %collective-permute-start.24 = (bf16[768,768]{1,0:T(8,128)(2,1)S(1)}, bf16[768,768]{1,0:T(8,128)(2,1)S(1)}, u32[]{:S(2)}, u32[]{:S(2)}) collective-permute-start(bf16[768,768]{1,0:T(8,128)(2,1)S(1)} %get-tuple-element.69), channel_id=1, source_target_pairs={{0,8},{8,0},{16,24},{24,16},{1,9},{9,1},{17,25},{25,17},{2,10},{10... | collective-permute-start | bytes 3538952 | tf_op jit(solution)/shard_map/ppermute | solution.py:258
  202.5 28.2 %collective-permute-start.26 = (bf16[768,768]{1,0:T(8,128)(2,1)S(1)}, bf16[768,768]{1,0:T(8,128)(2,1)S(1)}, u32[]{:S(2)}, u32[]{:S(2)}) collective-permute-start(bf16[768,768]{1,0:T(8,128)(2,1)S(1)} %add_convert_fusion.1), channel_id=1, source_target_pairs={{0,16},{8,24},{16,0},{24,8},{1,17},{9,25},{17,1},{25,9},{2,18},{10... | collective-permute-start | bytes 3538952 | tf_op jit(solution)/shard_map/ppermute | solution.py:258
  204.0 29.3 %collective-permute-start.19 = (bf16[48,3072]{1,0:T(8,128)(2,1)S(1)}, bf16[48,3072]{1,0:T(8,128)(2,1)S(1)}, u32[]{:S(2)}, u32[]{:S(2)}) collective-permute-start(bf16[48,3072]{1,0:T(8,128)(2,1)S(1)} %get-tuple-element.56), channel_id=1, source_target_pairs={{0,3},{1,0},{2,1},{3,2},{4,7},{5,4},{6,5},{7,6},{8,11},{9,8},{10,9... | collective-permute-start | bytes 884744 | tf_op jit(solution)/shard_map/ppermute | solution.py:255
  206.5 38.1 %collective-permute-start.20 = (bf16[48,3072]{1,0:T(8,128)(2,1)S(1)}, bf16[48,3072]{1,0:T(8,128)(2,1)S(1)}, u32[]{:S(2)}, u32[]{:S(2)}) collective-permute-start(bf16[48,3072]{1,0:T(8,128)(2,1)S(1)} %get-tuple-element.57), channel_id=1, source_target_pairs={{0,2},{1,3},{2,0},{3,1},{4,6},{5,7},{6,4},{7,5},{8,10},{9,11},{10,... | collective-permute-start | bytes 884744 | tf_op jit(solution)/shard_map/ppermute | solution.py:255
  207.1 2.5 copy-start.2
  207.1 37.5 %collective-permute-start.21 = (bf16[48,3072]{1,0:T(8,128)(2,1)S(1)}, bf16[48,3072]{1,0:T(8,128)(2,1)S(1)}, u32[]{:S(2)}, u32[]{:S(2)}) collective-permute-start(bf16[48,3072]{1,0:T(8,128)(2,1)S(1)} %get-tuple-element.58), channel_id=1, source_target_pairs={{0,1},{1,2},{2,3},{3,0},{4,5},{5,6},{6,7},{7,4},{8,9},{9,10},{10,1... | collective-permute-start | bytes 884744 | tf_op jit(solution)/shard_map/ppermute | solution.py:255
  208.2 42.0 %collective-permute-start.23 = (bf16[768,768]{1,0:T(8,128)(2,1)}, bf16[768,768]{1,0:T(8,128)(2,1)}, u32[]{:S(2)}, u32[]{:S(2)}) collective-permute-start(bf16[768,768]{1,0:T(8,128)(2,1)} %get-tuple-element.67), channel_id=1, source_target_pairs={{0,8},{8,0},{16,24},{24,16},{1,9},{9,1},{17,25},{25,17},{2,10},{10... | collective-permute-start | bytes 3538952 | tf_op jit(solution)/shard_map/ppermute | solution.py:258
  208.2 36.4 %copy-start.37 = (pred[192,128]{1,0:T(8,128)(4,1)S(1)}, pred[192,128]{1,0:T(8,128)(4,1)}, u32[]{:S(2)}) copy-start(pred[192,128]{1,0:T(8,128)(4,1)} %copy-done.36) | copy-start | bytes 73732
  231.7 21.4 %copy-start.1 = (bf16[768,768]{1,0:T(8,128)(2,1)S(1)}, bf16[768,768]{1,0:T(8,128)(2,1)}, u32[]{:S(2)}) copy-start(bf16[768,768]{1,0:T(8,128)(2,1)} %copy-done) | copy-start | bytes 3538948
  231.7 30.8 %collective-permute-start.27 = (bf16[768,768]{1,0:T(8,128)(2,1)}, bf16[768,768]{1,0:T(8,128)(2,1)}, u32[]{:S(2)}, u32[]{:S(2)}) collective-permute-start(bf16[768,768]{1,0:T(8,128)(2,1)} %add_convert_fusion), channel_id=1, source_target_pairs={{0,16},{8,24},{16,0},{24,8},{1,17},{9,25},{17,1},{25,9},{2,18},{10... | collective-permute-start | bytes 3538952 | tf_op jit(solution)/shard_map/ppermute | solution.py:258
  245.9 36.7 %collective-permute-start.30 = (bf16[128,3072]{1,0:T(8,128)(2,1)}, bf16[128,3072]{1,0:T(8,128)(2,1)S(1)}, u32[]{:S(2)}, u32[]{:S(2)}) collective-permute-start(bf16[128,3072]{1,0:T(8,128)(2,1)} %convolution_convert_fusion.2), channel_id=1, source_target_pairs={{0,4},{1,5},{2,6},{3,7},{4,0},{5,1},{6,2},{7,3},{8,12},{9,13},{10,... | collective-permute-start | bytes 2359304 | tf_op jit(solution)/shard_map/ppermute | solution.py:358
  247.7 22.3 %collective-permute-start.29 = (bf16[48,3072]{1,0:T(8,128)(2,1)}, bf16[48,3072]{1,0:T(8,128)(2,1)S(1)}, u32[]{:S(2)}, u32[]{:S(2)}) collective-permute-start(bf16[48,3072]{1,0:T(8,128)(2,1)} %copy-done.26), channel_id=1, source_target_pairs={{0,1},{1,2},{2,3},{3,0},{4,5},{5,6},{6,7},{7,4},{8,9},{9,10},{10,1... | collective-permute-start | bytes 884744 | tf_op jit(solution)/shard_map/ppermute | solution.py:255
  247.7 24.6 %collective-permute-start.28 = (bf16[48,3072]{1,0:T(8,128)(2,1)}, bf16[48,3072]{1,0:T(8,128)(2,1)S(1)}, u32[]{:S(2)}, u32[]{:S(2)}) collective-permute-start(bf16[48,3072]{1,0:T(8,128)(2,1)} %copy-done.25), channel_id=1, source_target_pairs={{0,2},{1,3},{2,0},{3,1},{4,6},{5,7},{6,4},{7,5},{8,10},{9,11},{10,... | collective-permute-start | bytes 884744 | tf_op jit(solution)/shard_map/ppermute | solution.py:255
  250.2 27.5 %collective-permute-start.22 = (bf16[48,3072]{1,0:T(8,128)(2,1)}, bf16[48,3072]{1,0:T(8,128)(2,1)S(1)}, u32[]{:S(2)}, u32[]{:S(2)}) collective-permute-start(bf16[48,3072]{1,0:T(8,128)(2,1)} %copy-done.24), channel_id=1, source_target_pairs={{0,3},{1,0},{2,1},{3,2},{4,7},{5,4},{6,5},{7,6},{8,11},{9,8},{10,9... | collective-permute-start | bytes 884744 | tf_op jit(solution)/shard_map/ppermute | solution.py:255
  255.7 6.8 %copy-start.5 = (bf16[768,768]{1,0:T(8,128)(2,1)S(1)}, bf16[768,768]{1,0:T(8,128)(2,1)}, u32[]{:S(2)}) copy-start(bf16[768,768]{1,0:T(8,128)(2,1)} %copy-done.4) | copy-start | bytes 3538948
  262.5 20.1 %copy-start.23 = (bf16[48,3072]{1,0:T(8,128)(2,1)S(1)}, bf16[48,3072]{1,0:T(8,128)(2,1)}, u32[]{:S(2)}) copy-start(bf16[48,3072]{1,0:T(8,128)(2,1)} %copy-done.22) | copy-start | bytes 884740
  262.5 20.1 %copy-start.35 = (pred[192,128]{1,0:T(8,128)(4,1)S(1)}, pred[192,128]{1,0:T(8,128)(4,1)}, u32[]{:S(2)}) copy-start(pred[192,128]{1,0:T(8,128)(4,1)} %copy-done.34) | copy-start | bytes 73732
  (24 other events, 21.4 us)

commit v4 on v3

--- a/solution.py
+++ b/solution.py
@@ -57,46 +57,156 @@
     return total
 
 
-def forward_gate(place, blocks, upstream, gate):
-    pieces, hidden = len(gate), gate[0].shape[0]
-    width = gate[0].shape[1] * pieces
+def chosen_by(info, which, route_rows, route_cols, capacity, half):
+    choices, count = route_rows.shape
+    slot = lax.broadcasted_iota(jnp.int32, (half * capacity, 1), 0)
+    number = jnp.zeros_like(slot)
+    for k in range(1, half):
+        number += (slot >= k * capacity).astype(jnp.int32)
+    expert = info[0] + number
+    expert = jnp.where(expert >= half, expert - half, expert) + which * half
+    slot = (expert * capacity + slot - number * capacity).astype(f32)
+    before = lax.broadcasted_iota(jnp.int32, (count, count), 0)
+    before = before < lax.broadcasted_iota(jnp.int32, (count, count), 1)
+    chosen = []
+    for k in range(choices):
+        row = route_rows[k : k + 1, :]
+        position = jnp.zeros((1, count), f32)
+        for other in range(k + 1):
+            same = route_cols[:, other : other + 1] == row
+            if other == k:
+                same = same & before
+            position += jnp.sum(jnp.where(same, 1.0, 0.0), axis=0, keepdims=True)
+        target = row.astype(f32) * capacity + position
+        chosen.append(jnp.where(target == slot, 1.0, 0.0).astype(bf16))
+    return chosen
+
+
+def store_blocks(refs, start, picked):
+    part = picked.shape[0] // len(refs)
+    for number, ref in enumerate(refs):
+        ref[:, start : start + picked.shape[1]] = picked[number * part : (number + 1) * part]
+
+
+def pick_near(info, routes, gates, cotangent, tokens, capacity, half):
+    count, width = tokens.shape
+    hidden = cotangent.shape[2]
+    slots = half * capacity
+    blocks = half if capacity % 16 == 0 else 1
+
+    def body(info, route_rows, route_cols, gates, cotangent, tokens, *outs):
+        for which, out in ((1 - info[1], outs[0]), (info[1], outs[1])):
+            chosen = chosen_by(info, which, route_rows, route_cols, capacity, half)
+            total = None
+            for k, pick in enumerate(chosen):
+                factor = gates[:, k : k + 1].astype(f32) / gate_unit
+                scaled = (factor * cotangent[:, k, :].astype(f32)).astype(bf16)
+                term = jnp.dot(pick, scaled, preferred_element_type=f32)
+                total = term if total is None else total + term
+            out[...] = total.astype(bf16)
+        pick = sum(chosen[1:], chosen[0])
+        outs[2][...] = pick
+        store_blocks(
+            outs[3:], 0, jnp.dot(pick, tokens[...], preferred_element_type=f32).astype(bf16)
+        )
+
+    operands = (routes.T, routes, gates, cotangent, tokens)
+    shapes = [(slots, hidden)] * 2 + [(slots, count)] + [(slots // blocks, width)] * blocks
+    return run(
+        body,
+        info,
+        (1,),
+        [whole(operand.shape) for operand in operands],
+        [whole(shape) for shape in shapes],
+        [jax.ShapeDtypeStruct(shape, bf16) for shape in shapes],
+        *operands,
+    )
+
+
+def pick_far(info, routes, tokens, far_grads, near_grads, capacity, half):
+    count, width = tokens.shape
+    hidden = far_grads.shape[1]
+    slots = half * capacity
+    blocks = half if capacity % 16 == 0 else 1
+
+    def body(info, route_rows, route_cols, tokens, far_grads, near_grads, pick_out, *outs):
+        chosen = chosen_by(info, info[1], route_rows, route_cols, capacity, half)
+        pick = sum(chosen[1:], chosen[0])
+        pick_out[...] = pick
+        store_blocks(outs, 0, jnp.dot(pick, tokens[...], preferred_element_type=f32).astype(bf16))
+        store_blocks(outs, width, far_grads[...])
+        store_blocks(outs, width + hidden, near_grads[...])
+
+    operands = (routes.T, routes, tokens, far_grads, near_grads)
+    shapes = [(slots, count)] + [(slots // blocks, width + 2 * hidden)] * blocks
+    return run(
+        body,
+        info,
+        (1,),
+        [whole(operand.shape) for operand in operands],
+        [whole(shape) for shape in shapes],
+        [jax.ShapeDtypeStruct(shape, bf16) for shape in shapes],
+        *operands,
+    )
+
+
+def join(place, far, near):
+    blocks = far + near
+    width = near[0].shape[1]
+    hidden = (far[0].shape[1] - width) // 2
     count = sum(block.shape[0] for block in blocks)
-    tile = tile_of(hidden)
 
     def body(place, *refs):
-        block_refs, refs = refs[: len(blocks)], refs[len(blocks) :]
-        up_ref, gate_refs = refs[0], refs[1 : 1 + pieces]
-        rows, grad_up, factor = refs[1 + pieces :]
-
-        @pl.when(pl.program_id(0) == 0)
-        def _():
-            first = 0
-            for block in block_refs:
-                rows[first : first + block.shape[0], :] = block[...]
-                first += block.shape[0]
-
-        pre_gate = project(place, rows, gate_refs)
-        sigmoid_gate = jax.nn.sigmoid(pre_gate)
-        upstream = up_ref[...].astype(f32) * sigmoid_gate
-        grad_up[...] = (upstream * pre_gate).astype(bf16)
-        factor[...] = upstream * (1.0 + pre_gate * (1.0 - sigmoid_gate))
-
-    part = pl.BlockSpec((count, tile), lambda i, _: (0, i))
+        rows, grads = refs[len(blocks) :]
+        first = 0
+        for number, block in enumerate(refs[: len(blocks)]):
+            held = pl.ds(first, block.shape[0])
+            start = width if number < len(far) else width + hidden
+            rows[held, :] = block[:, :width]
+            grads[held, :] = refs[number % len(far)][:, start : start + hidden]
+            first += block.shape[0]
+
     return run(
         body,
         place,
-        (hidden // tile,),
-        [whole(block.shape) for block in blocks]
-        + [part]
-        + [pl.BlockSpec((tile, width // pieces), lambda i, _: (i, 0))] * pieces,
-        [whole((count, width)), part, part],
+        (1,),
+        [whole(block.shape) for block in blocks],
+        [whole((count, width)), whole((count, hidden))],
         [
             jax.ShapeDtypeStruct((count, width), bf16),
             jax.ShapeDtypeStruct((count, hidden), bf16),
+        ],
+        *blocks,
+    )
+
+
+def forward_gate(place, rows, grads, gate):
+    pieces, hidden = len(gate), gate[0].shape[0]
+    count, width = rows.shape
+    tile = tile_of(hidden)
+
+    def body(place, rows, grads, *refs):
+        grad_up, factor = refs[pieces:]
+        pre_gate = project(place, rows, refs[:pieces])
+        sigmoid_gate = jax.nn.sigmoid(pre_gate)
+        upstream = grads[...].astype(f32) * sigmoid_gate
+        grad_up[...] = (upstream * pre_gate).astype(bf16)
+        factor[...] = upstream * (1.0 + pre_gate * (1.0 - sigmoid_gate))
+
+    part = pl.BlockSpec((count, tile), lambda i, _: (0, i))
+    return run(
+        body,
+        place,
+        (hidden // tile,),
+        [whole((count, width)), part]
+        + [pl.BlockSpec((tile, width // pieces), lambda i, _: (i, 0))] * pieces,
+        [part, part],
+        [
+            jax.ShapeDtypeStruct((count, hidden), bf16),
             jax.ShapeDtypeStruct((count, hidden), f32),
         ],
-        *blocks,
-        upstream,
+        rows,
+        grads,
         *gate,
     )
 
@@ -182,25 +292,25 @@
     )
 
 
-def adam(index, parts, old, moments, *results):
+def adam(index, parts, old, first, second, *results):
     rows, width = old.shape
-    sources, _, _, part, _ = moments.shape
+    sources, _, part, _ = first.shape
     flat = pl.BlockSpec((part, width), lambda i: (i, 0))
-    moment = pl.BlockSpec((1, 2, 1, part, width), lambda i: (i, 0, index, 0, 0))
+    moment = pl.BlockSpec((1, 1, part, width), lambda i: (i, index, 0, 0))
     out = pl.BlockSpec((1, 1, part, width), lambda i: (index, 0, i, 0))
     shape = jax.ShapeDtypeStruct((2, 1, rows, width), old.dtype)
     count = len(parts)
 
     def body(*refs):
-        old_ref, moments_ref = refs[count : count + 2]
+        old_ref, first_ref, second_ref = refs[count : count + 3]
         weights_out, first_out, second_out = refs[-3:]
         gradient = refs[0][...].astype(f32)
         for ref in refs[1:count]:
             gradient += ref[...].astype(f32)
         gradient = gradient / loss_scale
-        moment_one = beta_one * moments_ref[0, 0, 0].astype(f32) + (1.0 - beta_one) * gradient
+        moment_one = beta_one * first_ref[0, 0].astype(f32) + (1.0 - beta_one) * gradient
         moment_two = (
-            beta_two * moments_ref[0, 1, 0].astype(f32) + (1.0 - beta_two) * gradient * gradient
+            beta_two * second_ref[0, 0].astype(f32) + (1.0 - beta_two) * gradient * gradient
         )
         updated = old_ref[...].astype(f32) - step_size * moment_one / (
             jnp.sqrt(moment_two) + adam_eps
@@ -213,22 +323,13 @@
         body,
         grid=(sources,),
         in_specs=[flat] * (count + 1)
-        + [moment]
+        + [moment] * 2
         + [pl.BlockSpec(memory_space=pl.ANY)] * len(results),
         out_specs=[out] * 3,
         out_shape=[shape] * 3,
-        input_output_aliases={count + 2 + i: i for i in range(len(results))},
+        input_output_aliases={count + 3 + i: i for i in range(len(results))},
         compiler_params=pltpu.CompilerParams(vmem_limit_bytes=vmem_bytes),
-    )(*parts, old, moments, *results)
-
-
-def slot_targets(flat_route, capacity):
-    count = flat_route.shape[-1]
-    order = jnp.arange(count, dtype=jnp.int32)
-    earlier = order[None, :] < order[:, None]
-    same = flat_route[:, None] == flat_route[None, :]
-    position = jnp.sum((same & earlier).astype(jnp.int32), axis=-1)
-    return flat_route * capacity + position
+    )(*parts, old, first, second, *results)
 
 
 def per_device(
@@ -240,11 +341,10 @@
     experts = weights.shape[1]
     pieces = model_width // weights.shape[3]
     capacity = 3 * row_count * per_token // (2 * experts)
-    routings = row_count * per_token
     half = experts // 2
     mine = lax.axis_index("expert")
     side = mine // half
-    local = mine % half
+    info = jnp.stack([mine % half, side]).astype(jnp.int32)
     place = lax.axis_index("dp").astype(jnp.int32).reshape(1)
     swap = [(i, (i + half) % experts) for i in range(experts)]
 
@@ -256,10 +356,6 @@
 
     def across(value, k):
         return lax.ppermute(value, "dp", [(i, i ^ k) for i in range(pieces)])
-
-    def slot_ids(of_side):
-        expert = of_side * half + (local + jnp.arange(half, dtype=jnp.int32)) % half
-        return expert[:, None] * capacity + jnp.arange(capacity, dtype=jnp.int32)[None, :]
 
     def to_owners(by_owner, *earlier):
         by_owner = after(by_owner, *earlier)
@@ -285,67 +381,47 @@
     other_tokens = lax.ppermute(tokens, "expert", swap)
     other_routes = lax.ppermute(routes, "expert", swap)
 
-    gate_factor = router_gates.astype(f32) / gate_unit
-    scaled = (gate_factor[:, :, None] * hidden_cotangent.astype(f32)).astype(bf16)
-    scaled = scaled.reshape(routings, hidden_units)
-    target = slot_targets(routes.reshape(-1), capacity)
-    near_ids = slot_ids(side)
-    far_ids = slot_ids(1 - side)
-
-    def pick_grads(ids):
-        chosen = (target[None, :] == ids.reshape(-1)[:, None]).astype(bf16)
-        picked = jnp.dot(chosen, scaled, preferred_element_type=f32).astype(bf16)
-        return picked.reshape(half, capacity, hidden_units)
-
-    far_grads = lax.ppermute(pick_grads(far_ids), "expert", swap)
-
-    def pick_matrix(chosen_target):
-        by_token = chosen_target.reshape(row_count, per_token)
-        hit = by_token[None, :, :] == near_ids.reshape(-1)[:, None, None]
-        return jnp.any(hit, axis=2).astype(bf16)
-
-    def send_rows(picker, rows):
-        picked = jnp.dot(picker, rows, preferred_element_type=f32).astype(bf16)
-        picked = picked.reshape(half, capacity, model_width)
-        return [shift(picked[s], s) for s in range(half)]
-
-    near_pick = pick_matrix(target)
-    near_rows = send_rows(near_pick, tokens)
-    grads_out = jnp.concatenate([far_grads, pick_grads(near_ids)], axis=1)
-    grads_in = [shift(grads_out[s], s) for s in range(half)]
-    other_tokens = after(other_tokens, other_routes, *grads_in[1:], *near_rows[1:])
-    other_pick = pick_matrix(slot_targets(other_routes.reshape(-1), capacity))
-    far_rows = send_rows(other_pick, other_tokens)
-
-    owned = after(to_owners(jnp.swapaxes(weights, 0, 1), other_tokens), *far_rows[1:])
+    grads_away, near_grads, near_pick, *near_rows = pick_near(
+        info, routes, router_gates, hidden_cotangent, tokens, capacity, half
+    )
+    far_grads = lax.ppermute(grads_away, "expert", swap)
+
+    def send(blocks, direction=1):
+        if len(blocks) == 1:
+            blocks = [blocks[0][s * capacity : (s + 1) * capacity] for s in range(half)]
+        return [shift(block, direction * s) for s, block in enumerate(blocks)]
+
+    def unsplit(blocks):
+        return blocks if capacity % 16 == 0 else [jnp.concatenate(blocks, axis=0)]
+
+    near_rows = send(near_rows)
+    other_tokens = after(other_tokens, other_routes, far_grads, *near_rows[1:])
+    owned = to_owners(jnp.swapaxes(weights, 0, 1), other_tokens)
+    other_pick, *far_rows = pick_far(
+        info, other_routes, other_tokens, far_grads, near_grads, capacity, half
+    )
+    far_rows = send(far_rows)
+    owned = after(owned, *far_rows[1:])
     owned_gate = owned[:, 0].reshape(hidden_units, -1)
     owned_up = owned[:, 1].reshape(hidden_units, -1)
-    moments = [jnp.swapaxes(moment, 0, 1) for moment in (first_moment, second_moment)]
-    moments = to_owners(jnp.stack(moments, axis=1), owned)
+    owned_first = to_owners(jnp.swapaxes(first_moment, 0, 1), owned)
 
     gate_x = along_x(owned_gate)
     up_x = along_x(after(owned_up, *gate_x))
-    gate = both_cores([owned_gate] + gate_x)
+    rows, grads = join(place, unsplit(far_rows), unsplit(near_rows))
+    gate = both_cores([owned_gate] + [after(piece, rows) for piece in gate_x])
     up = both_cores([owned_up] + up_x)
-    upstream = jnp.swapaxes(jnp.stack(grads_in).reshape(half, 2, capacity, hidden_units), 0, 1)
-    upstream = upstream.reshape(2 * half * capacity, hidden_units)
-
-    blocks = far_rows + near_rows
-    joined = capacity % 16 != 0
-    if joined:
-        blocks = [jnp.concatenate(blocks, axis=0)]
-    rows, grad_up, factor = forward_gate(place, blocks, upstream, gate)
+    grad_up, factor = forward_gate(place, rows, grads, gate)
     up_totals = weight_grads(place, grad_up, rows, pieces)
     up_sums = core_sums(up_totals)
     up_terms = scatter(up_totals, up_sums)
-    grad_gate = forward_up(place, rows, after(factor, *up_sums), up)
-    back = input_grads(
-        place, grad_gate, grad_up, gate, up, rows.shape[0] if joined else capacity
-    )
-    if joined:
-        back = [back[0][i * capacity : (i + 1) * capacity] for i in range(2 * half)]
-    far_back = [shift(back[s], -s) for s in range(half)]
-    near_back = [shift(after(back[half + s], *far_back[1:]), -s) for s in range(half)]
+    grad_gate = forward_up(place, rows, after(factor, owned_first, *up_sums), up)
+    block_rows = capacity if capacity % 16 == 0 else half * capacity
+    back = input_grads(place, grad_gate, grad_up, gate, up, block_rows)
+    far_back = send(back[: len(back) // 2], -1)
+    near_back = [after(block, *far_back[1:]) for block in back[len(back) // 2 :]]
+    near_back = send(near_back, -1)
+    owned_second = to_owners(jnp.swapaxes(second_moment, 0, 1), owned_first, up_totals[0])
     gate_totals = weight_grads(place, after(grad_gate, *back), rows, pieces)
     gate_sums = [after(pair, *up_terms) for pair in core_sums(gate_totals)]
     gate_terms = scatter(gate_totals, gate_sums)
@@ -354,10 +430,10 @@
         parts = jnp.concatenate(parts, axis=0)
         return jnp.einsum("st,sd->td", picker, parts, preferred_element_type=f32)
 
-    far_sum = after(combine(other_pick, far_back).astype(bf16), moments, *up_terms)
+    far_sum = after(combine(other_pick, far_back).astype(bf16), owned_second)
     far_sum = lax.ppermute(far_sum, "expert", swap)
-    results = adam(1, up_terms, owned_up, moments)
-    results = adam(0, gate_terms, owned_gate, moments, *results)
+    results = adam(1, up_terms, owned_up, owned_first, owned_second)
+    results = adam(0, gate_terms, owned_gate, owned_first, owned_second, *results)
     near_back[1:] = [after(block, *results) for block in near_back[1:]]
     near_sum = combine(near_pick, near_back)
     token_grads = (near_sum + far_sum.astype(f32)).astype(bf16)

time: 285 us -> 288 us (1.011)
  waiting for transfers between devices: 160 us -> 145 us
  starting transfers between devices: 46.2 us -> 59.4 us
  local copies, waits for them, and re-layouts: 29.1 us -> 35.9 us
  other arithmetic: 8.86 us -> 3.07 us
  Pallas kernels: 33.9 us -> 39.1 us
    ppermute x1, waiting for transfers between devices: 0.01 us -> 31.8 us  [per_device(): other_routes = lax.ppermute(routes, 'expert', swap)]
    ppermute x15 -> x12, waiting for transfers between devices: 73.3 us -> 48.5 us  [shift(): return lax.ppermute(value, 'expert', pairs)]
    ppermute x1, waiting for transfers between devices: 24 us -> 1.41 us  [per_device(): far_grads = lax.ppermute(grads_away, 'expert', swap)]
    all_to_all x2 -> x3, starting transfers between devices: 10.2 us -> 25.3 us  [to_owners(): lax.all_to_all(by_owner, 'expert', split_axis=0, concat_axis=0, tiled=True)]
    unnamed x80 -> x101, local copies, waits for them, and re-layouts: 22.5 us -> 33 us
    all_to_all x2 -> x3, waiting for transfers between devices: 0.5 us -> 7.63 us  [to_owners(): lax.all_to_all(by_owner, 'expert', split_axis=0, concat_axis=0, tiled=True)]
    ppermute x12, waiting for transfers between devices: 57.4 us -> 51.1 us  [across(): return lax.ppermute(value, 'dp', [(i, i ^ k) for i in range(pieces)])]
    pallas_call x5 -> x8, Pallas kernels: 19.6 us -> 24.3 us  [run(): pl.pallas_call(body, grid_spec=pltpu.PrefetchScalarGridSpec(num_scalar_pr...]
  transfers between devices with their start and end apart: 33 -> 31, of which waited for: 15 -> 18; matrix products, arithmetic and copies ran while one was open for 8% -> 6% of each run, Pallas kernels for 12% -> 14%
where the time goes in v4:
time: 288 us; the launch traced here: 286 us
  waiting for transfers between devices  145 us (50%)
  starting transfers between devices  59.4 us (21%)
  Pallas kernels  39.1 us (14%)
  local copies, waits for them, and re-layouts  35.9 us (12%)
  other arithmetic  3.07 us (1%)
    ppermute x12, waiting for transfers between devices, across(): return lax.ppermute(value, 'dp', [(i, i ^ k) for i in range(pieces)])  51.1 us
    ppermute x12, waiting for transfers between devices, shift(): return lax.ppermute(value, 'expert', pairs)  48.5 us
    unnamed x101, local copies, waits for them, and re-layouts  33 us
    ppermute x1, waiting for transfers between devices, per_device(): other_routes = lax.ppermute(routes, 'expert', swap)  31.8 us
    all_to_all x3, starting transfers between devices, to_owners(): lax.all_to_all(by_owner, 'expert', split_axis=0, concat_axis=0, tiled=True)  25.3 us
    pallas_call x8, Pallas kernels, run(): pl.pallas_call(body, grid_spec=pltpu.PrefetchScalarGridSpec(num_scalar_pr...  24.3 us
    ppermute x12, starting transfers between devices, shift(): return lax.ppermute(value, 'expert', pairs)  15.9 us
    pallas_call x2, Pallas kernels, adam(): pl.pallas_call(body, grid=(sources,), in_specs=[flat] * (count + 1) + [mo...  14.7 us
  transfers between devices with their start and end apart: 31, of which 18 were waited for; matrix products, arithmetic and copies ran while one was open for 6% of the time, Pallas kernels for 14%

profile of v4, /device:TPU:0, one launch (start us, length us, event | category | flops | bytes accessed | tf_op | source)
XLA Modules:
  0.0 286.2 jit_solution(10297230668025611149)
XLA Ops:
  0.6 4.1 %collective-permute-start.1 = (bf16[128,3072]{1,0:T(8,128)(2,1)}, bf16[128,3072]{1,0:T(8,128)(2,1)S(1)}, u32[]{:S(2)}, u32[]{:S(2)}) collective-permute-start(bf16[128,3072]{1,0:T(8,128)(2,1)} %tokens.1), channel_id=1, source_target_pairs={{0,4},{1,5},{2,6},{3,7},{4,0},{5,1},{6,2},{7,3},{8,12},{9,13},{10,... | collective-permute-start | bytes 2359304 | tf_op jit(solution)/shard_map/ppermute | solution.py:381
  6.5 1.1 copy-done.17
  9.3 2.1 shard_map.102
  11.4 3.0 %collective-permute-start.2 = (bf16[192,768]{1,0:T(8,128)(2,1)S(1)}, bf16[192,768]{1,0:T(8,128)(2,1)S(1)}, u32[]{:S(2)}, u32[]{:S(2)}) collective-permute-start(bf16[192,768]{1,0:T(8,128)(2,1)S(1)} %get-tuple-element.61), channel_id=1, source_target_pairs={{0,4},{1,5},{2,6},{3,7},{4,0},{5,1},{6,2},{7,3},{8,12},{9,13},{10,... | collective-permute-start | bytes 884744 | tf_op jit(solution)/shard_map/ppermute | solution.py:387
  14.4 1.5 collective-permute-start.3
  15.9 1.6 collective-permute-start.4
  17.5 31.8 %collective-permute-done.route_cols = s32[128,2]{1,0:T(8,128)S(1)} collective-permute-done((s32[128,2]{1,0:T(8,128)S(1)}, s32[128,2]{1,0:T(8,128)S(1)}, u32[]{:S(2)}, u32[]{:S(2)}) %collective-permute-start) | collective-permute-done | bytes 1056 | tf_op jit(solution)/shard_map/ppermute | solution.py:382
  50.2 3.2 %copy.32 = bf16[2,8,96,768]{3,2,0,1:T(8,128)(2,1)} copy(bf16[2,8,96,768]{3,2,1,0:T(8,128)(2,1)} %param.11) | data formatting | bytes 4718592 | tf_op args[4]
  53.5 1.4 collective-permute-done.2.far_grads
  57.4 10.2 %all-to-all-start = ((bf16[8,2,96,768]{3,2,1,0:T(8,128)(2,1)}), bf16[8,2,96,768]{3,2,1,0:T(8,128)(2,1)}, u32[]{:S(2)}, u32[]{:S(2)}) async-start(bf16[8,2,96,768]{3,2,1,0:T(8,128)(2,1)} %bitcast.26), calls=%async_computation | async-start | bytes 4718592 | tf_op jit(solution)/shard_map/all_to_all | solution.py:362
  67.6 1.1 shard_map.103
  68.7 2.1 collective-permute-start.6
  70.8 1.5 collective-permute-start.7
  72.3 1.5 collective-permute-start.8
  73.7 3.2 %copy.31 = bf16[2,8,96,768]{3,2,0,1:T(8,128)(2,1)} copy(bf16[2,8,96,768]{3,2,1,0:T(8,128)(2,1)} %param.12) | data formatting | bytes 4718592 | tf_op args[5]
  77.0 36.2 %collective-permute-done.6.refs_1_ = bf16[48,4608]{1,0:T(8,128)(2,1)S(1)} collective-permute-done((bf16[48,4608]{1,0:T(8,128)(2,1)S(1)}, bf16[48,4608]{1,0:T(8,128)(2,1)S(1)}, u32[]{:S(2)}, u32[]{:S(2)}) %collective-permute-start.6) | collective-permute-done | bytes 442400 | tf_op jit(solution)/shard_map/ppermute | solution.py:355
  113.9 3.5 %collective-permute-done.7.refs_2_ = bf16[48,4608]{1,0:T(8,128)(2,1)S(1)} collective-permute-done((bf16[48,4608]{1,0:T(8,128)(2,1)S(1)}, bf16[48,4608]{1,0:T(8,128)(2,1)S(1)}, u32[]{:S(2)}, u32[]{:S(2)}) %collective-permute-start.7) | collective-permute-done | bytes 442400 | tf_op jit(solution)/shard_map/ppermute | solution.py:355
  118.2 7.8 %collective-permute-done.8.refs_3_ = bf16[48,4608]{1,0:T(8,128)(2,1)S(1)} collective-permute-done((bf16[48,4608]{1,0:T(8,128)(2,1)S(1)}, bf16[48,4608]{1,0:T(8,128)(2,1)S(1)}, u32[]{:S(2)}, u32[]{:S(2)}) %collective-permute-start.8) | collective-permute-done | bytes 442400 | tf_op jit(solution)/shard_map/ppermute | solution.py:355
  126.7 10.7 %all-to-all-start.1 = ((bf16[8,2,96,768]{3,2,1,0:T(8,128)(2,1)}), bf16[8,2,96,768]{3,2,1,0:T(8,128)(2,1)}, u32[]{:S(2)}, u32[]{:S(2)}) async-start(bf16[8,2,96,768]{3,2,1,0:T(8,128)(2,1)} %bitcast.16), calls=%async_computation.1 | async-start | bytes 4718592 | tf_op jit(solution)/shard_map/all_to_all | solution.py:362
  137.5 2.8 fusion.19
  140.3 1.5 collective-permute-start.10
  150.0 17.1 %collective-permute-done.10.refs_2_ = bf16[768,768]{1,0:T(8,128)(2,1)} collective-permute-done((bf16[768,768]{1,0:T(8,128)(2,1)}, bf16[768,768]{1,0:T(8,128)(2,1)}, u32[]{:S(2)}, u32[]{:S(2)}) %collective-permute-start.10) | collective-permute-done | bytes 1179680 | tf_op jit(solution)/shard_map/ppermute | solution.py:358
  167.1 1.5 collective-permute-start.14
  168.6 1.6 copy.30
  170.2 4.7 %shard_map.105 = (bf16[384,768]{1,0:T(8,128)(2,1)S(1)}, f32[384,768]{1,0:T(8,128)S(1)}) custom-call(s32[1]{0:T(128)} %bitcast.3.place, bf16[384,3072]{1,0:T(8,128)(2,1)S(1)} %get-tuple-element.72.rows, bf16[384,768]{1,0:T(8,128)(2,1)S(1)} %get-tuple-element.73.grads, bf16[768,768]{1,0:T(8,128)(2,1)} %bitcast.6.refs_0_.refs_3_, ...), custom_call_target="tpu_custom_call" | custom-call | tf_op jit(solution)/shard_map/pallas_call | solution.py:32
  175.9 3.1 %shard_map.106 = (bf16[768,768]{1,0:T(8,128)(2,1)S(1)}, bf16[768,768]{1,0:T(8,128)(2,1)S(1)}, bf16[768,768]{1,0:T(8,128)(2,1)S(1)}, bf16[768,768]{1,0:T(8,128)(2,1)S(1)}) custom-call(s32[1]{0:T(128)} %bitcast.3.place, bf16[384,768]{1,0:T(8,128)(2,1)S(1)} %get-tuple-element.79.grads.grad_up, bf16[384,3072]{1,0:T(8,128)(2,1)S(1)} %get-tuple-element.72.rows), custom_call_target="tpu_custom_call" | custom-call | tf_op jit(solution)/shard_map/pallas_call | solution.py:32
  184.0 6.5 %all-to-all-done.1.refs_4_ = bf16[8,2,96,768]{3,2,1,0:T(8,128)(2,1)} async-done(((bf16[8,2,96,768]{3,2,1,0:T(8,128)(2,1)}), bf16[8,2,96,768]{3,2,1,0:T(8,128)(2,1)}, u32[]{:S(2)}, u32[]{:S(2)}) %all-to-all-start.1) | async-done | bytes 2359328 | tf_op jit(solution)/shard_map/all_to_all | solution.py:362
  190.5 4.4 %all-to-all-start.2 = ((bf16[8,2,96,768]{3,2,1,0:T(8,128)(2,1)}), bf16[8,2,96,768]{3,2,1,0:T(8,128)(2,1)}, u32[]{:S(2)}, u32[]{:S(2)}) async-start(bf16[8,2,96,768]{3,2,1,0:T(8,128)(2,1)} %bitcast.25), calls=%async_computation.2 | async-start | bytes 4718592 | tf_op jit(solution)/shard_map/all_to_all | solution.py:362
  196.1 2.8 collective-permute-done.12
  198.9 1.6 add_convert_fusion.1
  201.4 3.8 %shard_map.107.grad_gate.grads = bf16[384,768]{1,0:T(8,128)(2,1)S(1)} custom-call(s32[1]{0:T(128)} %bitcast.3.place, bf16[384,3072]{1,0:T(8,128)(2,1)S(1)} %get-tuple-element.72.rows, f32[384,768]{1,0:T(8,128)S(1)} %copy-done.15, bf16[768,768]{1,0:T(8,128)(2,1)S(1)} %bitcast.20, bf16[768,768]{1,0:T(8,128)(2,1)S(1)} %collective-permute-done.13.refs_1_.refs_5_, ...), custom_call_target="tpu_custom_call" | custom-call | tf_op jit(solution)/shard_map/pallas_call | solution.py:32
  205.2 5.7 %shard_map.108 = (bf16[48,3072]{1,0:T(8,128)(2,1)S(1)}, bf16[48,3072]{1,0:T(8,128)(2,1)S(1)}, bf16[48,3072]{1,0:T(8,128)(2,1)S(1)}, bf16[48,3072]{1,0:T(8,128)(2...) custom-call(s32[1]{0:T(128)} %bitcast.3.place, ...), custom_call_target="tpu_custom_call" | custom-call | tf_op jit(solution)/shard_map/pallas_call | solution.py:32
  210.9 3.6 %shard_map.109 = (bf16[768,768]{1,0:T(8,128)(2,1)S(1)}, bf16[768,768]{1,0:T(8,128)(2,1)}, bf16[768,768]{1,0:T(8,128)(2,1)S(1)}, bf16[768,768]{1,0:T(8,128)(2,1)S(1)}) custom-call(s32[1]{0:T(128)} %bitcast.3.place, bf16[384,768]{1,0:T(8,128)(2,1)S(1)} %shard_map.107.grad_gate.grads, bf16[384,3072]{1,0:T(8,128)(2,1)S(1)} %get-tuple-element.72.rows), custom_call_target="tpu_custom_call" | custom-call | tf_op jit(solution)/shard_map/pallas_call | solution.py:32
  214.8 1.5 collective-permute-start.23
  216.3 2.9 %collective-permute-start.16 = (bf16[48,3072]{1,0:T(8,128)(2,1)S(1)}, bf16[48,3072]{1,0:T(8,128)(2,1)S(1)}, u32[]{:S(2)}, u32[]{:S(2)}) collective-permute-start(bf16[48,3072]{1,0:T(8,128)(2,1)S(1)} %get-tuple-element.85), channel_id=1, source_target_pairs={{0,3},{1,0},{2,1},{3,2},{4,7},{5,4},{6,5},{7,6},{8,11},{9,8},{10,9... | collective-permute-start | bytes 884744 | tf_op jit(solution)/shard_map/ppermute | solution.py:355
  220.3 1.3 add_convert_fusion
  221.7 21.4 %collective-permute-done.23.refs_2_ = bf16[768,768]{1,0:T(8,128)(2,1)S(1)} collective-permute-done((bf16[768,768]{1,0:T(8,128)(2,1)S(1)}, bf16[768,768]{1,0:T(8,128)(2,1)S(1)}, u32[]{:S(2)}, u32[]{:S(2)}) %collective-permute-start.23) | collective-permute-done | bytes 1179680 | tf_op jit(solution)/shard_map/ppermute | solution.py:358
  244.1 1.5 collective-permute-start.24
  245.9 1.3 convolution_convert_fusion
  247.1 1.1 all-to-all-done.2.refs_5_
  248.3 3.6 %collective-permute-start.27 = (bf16[128,3072]{1,0:T(8,128)(2,1)}, bf16[128,3072]{1,0:T(8,128)(2,1)S(1)}, u32[]{:S(2)}, u32[]{:S(2)}) collective-permute-start(bf16[128,3072]{1,0:T(8,128)(2,1)} %convolution_convert_fusion), channel_id=1, source_target_pairs={{0,4},{1,5},{2,6},{3,7},{4,0},{5,1},{6,2},{7,3},{8,12},{9,13},{10,... | collective-permute-start | bytes 2359304 | tf_op jit(solution)/shard_map/ppermute | solution.py:434
  252.7 2.1 collective-permute-start.19
  254.9 1.3 copy-done.13
  256.1 6.9 %shard_map.110 = (bf16[2,1,768,768]{3,2,1,0:T(8,128)(2,1)}, bf16[2,1,768,768]{3,2,1,0:T(8,128)(2,1)}, bf16[2,1,768,768]{3,2,1,0:T(8,128)(2,1)}) custom-call(bf16[768,768]{1,0:T(8,128)(2,1)S(1)} %copy-done.7, bf16[768,768]{1,0:T(8,128)(2,1)S(1)} %copy-done.9, bf16[768,768]{1,0:T(8,128)(2,1)S(1)} %copy-done.13, bf16[768,768]{1,0:T(8,128)(2,1)S(1)} %bitcast.22, ...), custom_call_target="tpu_custom_call" | custom-call | tf_op jit(solution)/shard_map/pallas_call | solution.py:322
  263.0 8.8 %collective-permute-done.24.refs_2_ = bf16[768,768]{1,0:T(8,128)(2,1)} collective-permute-done((bf16[768,768]{1,0:T(8,128)(2,1)}, bf16[768,768]{1,0:T(8,128)(2,1)}, u32[]{:S(2)}, u32[]{:S(2)}) %collective-permute-start.24) | collective-permute-done | bytes 1179680 | tf_op jit(solution)/shard_map/ppermute | solution.py:358
  271.8 7.9 %shard_map.111 = (bf16[2,1,768,768]{3,2,1,0:T(8,128)(2,1)}, bf16[2,1,768,768]{3,2,1,0:T(8,128)(2,1)}, bf16[2,1,768,768]{3,2,1,0:T(8,128)(2,1)}) custom-call(bf16[768,768]{1,0:T(8,128)(2,1)S(1)} %copy-done.11, bf16[768,768]{1,0:T(8,128)(2,1)} %collective-permute-done.20.refs_1_, ...), custom_call_target="tpu_custom_call", output_to_operand_aliasing={{0}: (6, {}), {1}: (7, {}), {2}: (8, {})} | custom-call | tf_op jit(solution)/shard_map/pallas_call | solution.py:322
  280.1 4.8 %collective-permute-done.27 = bf16[128,3072]{1,0:T(8,128)(2,1)S(1)} collective-permute-done((bf16[128,3072]{1,0:T(8,128)(2,1)}, bf16[128,3072]{1,0:T(8,128)(2,1)S(1)}, u32[]{:S(2)}, u32[]{:S(2)}) %collective-permute-start.27) | collective-permute-done | bytes 786464 | tf_op jit(solution)/shard_map/ppermute | solution.py:434
  284.9 1.3 add_convert_fusion.2
  (132 shorter events, 29.2 us)
Async XLA Ops:
  0.6 56.8 %collective-permute-start.1 = (bf16[128,3072]{1,0:T(8,128)(2,1)}, bf16[128,3072]{1,0:T(8,128)(2,1)S(1)}, u32[]{:S(2)}, u32[]{:S(2)}) collective-permute-start(bf16[128,3072]{1,0:T(8,128)(2,1)} %tokens.1), channel_id=1, source_target_pairs={{0,4},{1,5},{2,6},{3,7},{4,0},{5,1},{6,2},{7,3},{8,12},{9,13},{10,... | collective-permute-start | bytes 2359304 | tf_op jit(solution)/shard_map/ppermute | solution.py:381
  5.5 43.8 %collective-permute-start = (s32[128,2]{1,0:T(8,128)S(1)}, s32[128,2]{1,0:T(8,128)S(1)}, u32[]{:S(2)}, u32[]{:S(2)}) collective-permute-start(s32[128,2]{1,0:T(8,128)S(1)} %copy.20.route_cols), channel_id=1, source_target_pairs={{0,4},{1,5},{2,6},{3,7},{4,0},{5,1},{6,2},{7,3},{8,12},{9,13},{10,... | collective-permute-start | bytes 3080 | tf_op jit(solution)/shard_map/ppermute | solution.py:382
  11.4 42.1 %copy-start.27 = (bf16[48,3072]{1,0:T(8,128)(2,1)}, bf16[48,3072]{1,0:T(8,128)(2,1)S(1)}, u32[]{:S(2)}) copy-start(bf16[48,3072]{1,0:T(8,128)(2,1)S(1)} %get-tuple-element.71.refs_4_) | copy-start | bytes 884740
  11.4 42.1 %copy-start.43 = (bf16[192,128]{1,0:T(8,128)(2,1)}, bf16[192,128]{1,0:T(8,128)(2,1)S(1)}, u32[]{:S(2)}) copy-start(bf16[192,128]{1,0:T(8,128)(2,1)S(1)} %get-tuple-element.60) | copy-start | bytes 147460
  11.4 43.5 %collective-permute-start.2 = (bf16[192,768]{1,0:T(8,128)(2,1)S(1)}, bf16[192,768]{1,0:T(8,128)(2,1)S(1)}, u32[]{:S(2)}, u32[]{:S(2)}) collective-permute-start(bf16[192,768]{1,0:T(8,128)(2,1)S(1)} %get-tuple-element.61), channel_id=1, source_target_pairs={{0,4},{1,5},{2,6},{3,7},{4,0},{5,1},{6,2},{7,3},{8,12},{9,13},{10,... | collective-permute-start | bytes 884744 | tf_op jit(solution)/shard_map/ppermute | solution.py:387
  14.4 40.5 %collective-permute-start.3 = (bf16[48,3072]{1,0:T(8,128)(2,1)S(1)}, bf16[48,3072]{1,0:T(8,128)(2,1)S(1)}, u32[]{:S(2)}, u32[]{:S(2)}) collective-permute-start(bf16[48,3072]{1,0:T(8,128)(2,1)S(1)} %get-tuple-element.62), channel_id=1, source_target_pairs={{0,1},{1,2},{2,3},{3,0},{4,5},{5,6},{6,7},{7,4},{8,9},{9,10},{10,1... | collective-permute-start | bytes 884744 | tf_op jit(solution)/shard_map/ppermute | solution.py:355
  15.9 39.7 %collective-permute-start.4 = (bf16[48,3072]{1,0:T(8,128)(2,1)S(1)}, bf16[48,3072]{1,0:T(8,128)(2,1)S(1)}, u32[]{:S(2)}, u32[]{:S(2)}) collective-permute-start(bf16[48,3072]{1,0:T(8,128)(2,1)S(1)} %get-tuple-element.63), channel_id=1, source_target_pairs={{0,2},{1,3},{2,0},{3,1},{4,6},{5,7},{6,4},{7,5},{8,10},{9,11},{10,... | collective-permute-start | bytes 884744 | tf_op jit(solution)/shard_map/ppermute | solution.py:355
  49.3 7.4 %collective-permute-start.5 = (bf16[48,3072]{1,0:T(8,128)(2,1)S(1)}, bf16[48,3072]{1,0:T(8,128)(2,1)S(1)}, u32[]{:S(2)}, u32[]{:S(2)}) collective-permute-start(bf16[48,3072]{1,0:T(8,128)(2,1)S(1)} %get-tuple-element.64), channel_id=1, source_target_pairs={{0,3},{1,0},{2,1},{3,2},{4,7},{5,4},{6,5},{7,6},{8,11},{9,8},{10,9... | collective-permute-start | bytes 884744 | tf_op jit(solution)/shard_map/ppermute | solution.py:355
  57.4 69.3 %all-to-all-start = ((bf16[8,2,96,768]{3,2,1,0:T(8,128)(2,1)}), bf16[8,2,96,768]{3,2,1,0:T(8,128)(2,1)}, u32[]{:S(2)}, u32[]{:S(2)}) async-start(bf16[8,2,96,768]{3,2,1,0:T(8,128)(2,1)} %bitcast.26), calls=%async_computation | async-start | bytes 4718592 | tf_op jit(solution)/shard_map/all_to_all | solution.py:362
  68.7 8.3 %copy-start.18 = (bf16[48,4608]{1,0:T(8,128)(2,1)}, bf16[48,4608]{1,0:T(8,128)(2,1)S(1)}, u32[]{:S(2)}) copy-start(bf16[48,4608]{1,0:T(8,128)(2,1)S(1)} %get-tuple-element.67.refs_0_) | copy-start | bytes 1327108
  68.7 8.2 %copy-start.45 = (bf16[192,128]{1,0:T(8,128)(2,1)}, bf16[192,128]{1,0:T(8,128)(2,1)S(1)}, u32[]{:S(2)}) copy-start(bf16[192,128]{1,0:T(8,128)(2,1)S(1)} %get-tuple-element.114) | copy-start | bytes 147460
  68.7 44.4 %collective-permute-start.6 = (bf16[48,4608]{1,0:T(8,128)(2,1)S(1)}, bf16[48,4608]{1,0:T(8,128)(2,1)S(1)}, u32[]{:S(2)}, u32[]{:S(2)}) collective-permute-start(bf16[48,4608]{1,0:T(8,128)(2,1)S(1)} %get-tuple-element.68), channel_id=1, source_target_pairs={{0,1},{1,2},{2,3},{3,0},{4,5},{5,6},{6,7},{7,4},{8,9},{9,10},{10,1... | collective-permute-start | bytes 1327112 | tf_op jit(solution)/shard_map/ppermute | solution.py:355
  70.8 46.6 %collective-permute-start.7 = (bf16[48,4608]{1,0:T(8,128)(2,1)S(1)}, bf16[48,4608]{1,0:T(8,128)(2,1)S(1)}, u32[]{:S(2)}, u32[]{:S(2)}) collective-permute-start(bf16[48,4608]{1,0:T(8,128)(2,1)S(1)} %get-tuple-element.69), channel_id=1, source_target_pairs={{0,2},{1,3},{2,0},{3,1},{4,6},{5,7},{6,4},{7,5},{8,10},{9,11},{10,... | collective-permute-start | bytes 1327112 | tf_op jit(solution)/shard_map/ppermute | solution.py:355
  72.3 53.7 %collective-permute-start.8 = (bf16[48,4608]{1,0:T(8,128)(2,1)S(1)}, bf16[48,4608]{1,0:T(8,128)(2,1)S(1)}, u32[]{:S(2)}, u32[]{:S(2)}) collective-permute-start(bf16[48,4608]{1,0:T(8,128)(2,1)S(1)} %get-tuple-element.70), channel_id=1, source_target_pairs={{0,3},{1,0},{2,1},{3,2},{4,7},{5,4},{6,5},{7,6},{8,11},{9,8},{10,9... | collective-permute-start | bytes 1327112 | tf_op jit(solution)/shard_map/ppermute | solution.py:355
  126.7 63.8 %all-to-all-start.1 = ((bf16[8,2,96,768]{3,2,1,0:T(8,128)(2,1)}), bf16[8,2,96,768]{3,2,1,0:T(8,128)(2,1)}, u32[]{:S(2)}, u32[]{:S(2)}) async-start(bf16[8,2,96,768]{3,2,1,0:T(8,128)(2,1)} %bitcast.16), calls=%async_computation.1 | async-start | bytes 4718592 | tf_op jit(solution)/shard_map/all_to_all | solution.py:362
  140.3 26.8 %collective-permute-start.10 = (bf16[768,768]{1,0:T(8,128)(2,1)}, bf16[768,768]{1,0:T(8,128)(2,1)}, u32[]{:S(2)}, u32[]{:S(2)}) collective-permute-start(bf16[768,768]{1,0:T(8,128)(2,1)} %bitcast.6.refs_0_.refs_3_), channel_id=1, source_target_pairs={{0,16},{8,24},{16,0},{24,8},{1,17},{9,25},{17,1},{25,9},{2,18},{10... | collective-permute-start | bytes 3538952 | tf_op jit(solution)/shard_map/ppermute | solution.py:358
  149.7 18.9 %copy-start.47 = (bf16[2,8,96,768]{3,2,1,0:T(8,128)(2,1)S(1)}, bf16[2,8,96,768]{3,2,1,0:T(8,128)(2,1)}, u32[]{:S(2)}) copy-start(bf16[2,8,96,768]{3,2,1,0:T(8,128)(2,1)} %param.13) | copy-start | bytes 7077892
  149.9 20.3 %collective-permute-start.9 = (bf16[768,768]{1,0:T(8,128)(2,1)}, bf16[768,768]{1,0:T(8,128)(2,1)S(1)}, u32[]{:S(2)}, u32[]{:S(2)}) collective-permute-start(bf16[768,768]{1,0:T(8,128)(2,1)} %bitcast.6.refs_0_.refs_3_), channel_id=1, source_target_pairs={{0,8},{8,0},{16,24},{24,16},{1,9},{9,1},{17,25},{25,17},{2,10},{10... | collective-permute-start | bytes 3538952 | tf_op jit(solution)/shard_map/ppermute | solution.py:358
  167.1 3.1 %collective-permute-start.11 = (bf16[768,768]{1,0:T(8,128)(2,1)}, bf16[768,768]{1,0:T(8,128)(2,1)S(1)}, u32[]{:S(2)}, u32[]{:S(2)}) collective-permute-start(bf16[768,768]{1,0:T(8,128)(2,1)} %collective-permute-done.10.refs_2_), channel_id=1, source_target_pairs={{0,8},{8,0},{16,24},{24,16},{1,9},{9,1},{17,25},{25,17},{2,10},{10... | collective-permute-start | bytes 3538952 | tf_op jit(solution)/shard_map/ppermute | solution.py:358
  167.1 28.5 %collective-permute-start.14 = (bf16[768,768]{1,0:T(8,128)(2,1)S(1)}, bf16[768,768]{1,0:T(8,128)(2,1)}, u32[]{:S(2)}, u32[]{:S(2)}) collective-permute-start(bf16[768,768]{1,0:T(8,128)(2,1)S(1)} %bitcast.18), channel_id=1, source_target_pairs={{0,16},{8,24},{16,0},{24,8},{1,17},{9,25},{17,1},{25,9},{2,18},{10... | collective-permute-start | bytes 3538952 | tf_op jit(solution)/shard_map/ppermute | solution.py:358
  170.2 4.7 %copy-start = (bf16[768,768]{1,0:T(8,128)(2,1)}, bf16[768,768]{1,0:T(8,128)(2,1)S(1)}, u32[]{:S(2)}) copy-start(bf16[768,768]{1,0:T(8,128)(2,1)S(1)} %collective-permute-done.9.refs_1_) | copy-start | bytes 3538948
  170.2 4.7 %copy-start.2 = (bf16[768,768]{1,0:T(8,128)(2,1)}, bf16[768,768]{1,0:T(8,128)(2,1)S(1)}, u32[]{:S(2)}) copy-start(bf16[768,768]{1,0:T(8,128)(2,1)S(1)} %collective-permute-done.11.refs_3_) | copy-start | bytes 3538948
  190.5 57.8 %all-to-all-start.2 = ((bf16[8,2,96,768]{3,2,1,0:T(8,128)(2,1)}), bf16[8,2,96,768]{3,2,1,0:T(8,128)(2,1)}, u32[]{:S(2)}, u32[]{:S(2)}) async-start(bf16[8,2,96,768]{3,2,1,0:T(8,128)(2,1)} %bitcast.25), calls=%async_computation.2 | async-start | bytes 4718592 | tf_op jit(solution)/shard_map/all_to_all | solution.py:362
  194.9 4.0 %collective-permute-start.12 = (bf16[768,768]{1,0:T(8,128)(2,1)}, bf16[768,768]{1,0:T(8,128)(2,1)S(1)}, u32[]{:S(2)}, u32[]{:S(2)}) collective-permute-start(bf16[768,768]{1,0:T(8,128)(2,1)} %copy-done.37), channel_id=1, source_target_pairs={{0,8},{8,0},{16,24},{24,16},{1,9},{9,1},{17,25},{25,17},{2,10},{10... | collective-permute-start | bytes 3538952 | tf_op jit(solution)/shard_map/ppermute | solution.py:358
  195.0 5.8 %collective-permute-start.13 = (bf16[768,768]{1,0:T(8,128)(2,1)S(1)}, bf16[768,768]{1,0:T(8,128)(2,1)S(1)}, u32[]{:S(2)}, u32[]{:S(2)}) collective-permute-start(bf16[768,768]{1,0:T(8,128)(2,1)S(1)} %bitcast.19), channel_id=1, source_target_pairs={{0,8},{8,0},{16,24},{24,16},{1,9},{9,1},{17,25},{25,17},{2,10},{10... | collective-permute-start | bytes 3538952 | tf_op jit(solution)/shard_map/ppermute | solution.py:358
  195.6 5.8 %collective-permute-start.15 = (bf16[768,768]{1,0:T(8,128)(2,1)}, bf16[768,768]{1,0:T(8,128)(2,1)S(1)}, u32[]{:S(2)}, u32[]{:S(2)}) collective-permute-start(bf16[768,768]{1,0:T(8,128)(2,1)} %collective-permute-done.14.refs_2_.refs_6_), channel_id=1, source_target_pairs={{0,8},{8,0},{16,24},{24,16},{1,9},{9,1},{17,25},{25,17},{2,10},{10... | collective-permute-start | bytes 3538952 | tf_op jit(solution)/shard_map/ppermute | solution.py:358
  195.6 24.1 %collective-permute-start.22 = (bf16[768,768]{1,0:T(8,128)(2,1)}, bf16[768,768]{1,0:T(8,128)(2,1)S(1)}, u32[]{:S(2)}, u32[]{:S(2)}) collective-permute-start(bf16[768,768]{1,0:T(8,128)(2,1)} %copy-done.36), channel_id=1, source_target_pairs={{0,8},{8,0},{16,24},{24,16},{1,9},{9,1},{17,25},{25,17},{2,10},{10... | collective-permute-start | bytes 3538952 | tf_op jit(solution)/shard_map/ppermute | solution.py:358
  200.6 4.6 %copy-start.1 = (bf16[768,768]{1,0:T(8,128)(2,1)S(1)}, bf16[768,768]{1,0:T(8,128)(2,1)}, u32[]{:S(2)}) copy-start(bf16[768,768]{1,0:T(8,128)(2,1)} %copy-done) | copy-start | bytes 3538948
  200.6 4.6 %copy-start.3 = (bf16[768,768]{1,0:T(8,128)(2,1)S(1)}, bf16[768,768]{1,0:T(8,128)(2,1)}, u32[]{:S(2)}) copy-start(bf16[768,768]{1,0:T(8,128)(2,1)} %copy-done.2) | copy-start | bytes 3538948
  200.6 4.6 %copy-start.5 = (bf16[384,768]{1,0:T(8,128)(2,1)S(1)}, bf16[384,768]{1,0:T(8,128)(2,1)}, u32[]{:S(2)}) copy-start(bf16[384,768]{1,0:T(8,128)(2,1)} %copy-done.4) | copy-start | bytes 1769476
  214.6 7.1 %copy-start.10 = (bf16[768,768]{1,0:T(8,128)(2,1)}, bf16[768,768]{1,0:T(8,128)(2,1)S(1)}, u32[]{:S(2)}) copy-start(bf16[768,768]{1,0:T(8,128)(2,1)S(1)} %get-tuple-element.95.refs_0_) | copy-start | bytes 3538948
  214.6 5.7 %collective-permute-start.21 = (bf16[768,768]{1,0:T(8,128)(2,1)S(1)}, bf16[768,768]{1,0:T(8,128)(2,1)S(1)}, u32[]{:S(2)}, u32[]{:S(2)}) collective-permute-start(bf16[768,768]{1,0:T(8,128)(2,1)S(1)} %get-tuple-element.98), channel_id=1, source_target_pairs={{0,8},{8,0},{16,24},{24,16},{1,9},{9,1},{17,25},{25,17},{2,10},{10... | collective-permute-start | bytes 3538952 | tf_op jit(solution)/shard_map/ppermute | solution.py:358
  214.8 28.2 %collective-permute-start.23 = (bf16[768,768]{1,0:T(8,128)(2,1)S(1)}, bf16[768,768]{1,0:T(8,128)(2,1)S(1)}, u32[]{:S(2)}, u32[]{:S(2)}) collective-permute-start(bf16[768,768]{1,0:T(8,128)(2,1)S(1)} %add_convert_fusion.1), channel_id=1, source_target_pairs={{0,16},{8,24},{16,0},{24,8},{1,17},{9,25},{17,1},{25,9},{2,18},{10... | collective-permute-start | bytes 3538952 | tf_op jit(solution)/shard_map/ppermute | solution.py:358
  216.3 29.3 %collective-permute-start.16 = (bf16[48,3072]{1,0:T(8,128)(2,1)S(1)}, bf16[48,3072]{1,0:T(8,128)(2,1)S(1)}, u32[]{:S(2)}, u32[]{:S(2)}) collective-permute-start(bf16[48,3072]{1,0:T(8,128)(2,1)S(1)} %get-tuple-element.85), channel_id=1, source_target_pairs={{0,3},{1,0},{2,1},{3,2},{4,7},{5,4},{6,5},{7,6},{8,11},{9,8},{10,9... | collective-permute-start | bytes 884744 | tf_op jit(solution)/shard_map/ppermute | solution.py:355
  219.2 26.7 %collective-permute-start.17 = (bf16[48,3072]{1,0:T(8,128)(2,1)S(1)}, bf16[48,3072]{1,0:T(8,128)(2,1)S(1)}, u32[]{:S(2)}, u32[]{:S(2)}) collective-permute-start(bf16[48,3072]{1,0:T(8,128)(2,1)S(1)} %get-tuple-element.86), channel_id=1, source_target_pairs={{0,2},{1,3},{2,0},{3,1},{4,6},{5,7},{6,4},{7,5},{8,10},{9,11},{10,... | collective-permute-start | bytes 884744 | tf_op jit(solution)/shard_map/ppermute | solution.py:355
  219.7 26.1 %collective-permute-start.18 = (bf16[48,3072]{1,0:T(8,128)(2,1)S(1)}, bf16[48,3072]{1,0:T(8,128)(2,1)S(1)}, u32[]{:S(2)}, u32[]{:S(2)}) collective-permute-start(bf16[48,3072]{1,0:T(8,128)(2,1)S(1)} %get-tuple-element.87), channel_id=1, source_target_pairs={{0,1},{1,2},{2,3},{3,0},{4,5},{5,6},{6,7},{7,4},{8,9},{9,10},{10,1... | collective-permute-start | bytes 884744 | tf_op jit(solution)/shard_map/ppermute | solution.py:355
  220.3 32.4 %collective-permute-start.20 = (bf16[768,768]{1,0:T(8,128)(2,1)}, bf16[768,768]{1,0:T(8,128)(2,1)}, u32[]{:S(2)}, u32[]{:S(2)}) collective-permute-start(bf16[768,768]{1,0:T(8,128)(2,1)} %get-tuple-element.96), channel_id=1, source_target_pairs={{0,8},{8,0},{16,24},{24,16},{1,9},{9,1},{17,25},{25,17},{2,10},{10... | collective-permute-start | bytes 3538952 | tf_op jit(solution)/shard_map/ppermute | solution.py:358
  220.3 25.5 %copy-start.46 = (bf16[192,128]{1,0:T(8,128)(2,1)S(1)}, bf16[192,128]{1,0:T(8,128)(2,1)}, u32[]{:S(2)}) copy-start(bf16[192,128]{1,0:T(8,128)(2,1)} %copy-done.45) | copy-start | bytes 147460
  244.1 27.7 %collective-permute-start.24 = (bf16[768,768]{1,0:T(8,128)(2,1)}, bf16[768,768]{1,0:T(8,128)(2,1)}, u32[]{:S(2)}, u32[]{:S(2)}) collective-permute-start(bf16[768,768]{1,0:T(8,128)(2,1)} %add_convert_fusion), channel_id=1, source_target_pairs={{0,16},{8,24},{16,0},{24,8},{1,17},{9,25},{17,1},{25,9},{2,18},{10... | collective-permute-start | bytes 3538952 | tf_op jit(solution)/shard_map/ppermute | solution.py:358
  245.9 9.0 %copy-start.7 = (bf16[768,768]{1,0:T(8,128)(2,1)S(1)}, bf16[768,768]{1,0:T(8,128)(2,1)}, u32[]{:S(2)}) copy-start(bf16[768,768]{1,0:T(8,128)(2,1)} %copy-done.6) | copy-start | bytes 3538948
  245.9 9.0 %copy-start.9 = (bf16[768,768]{1,0:T(8,128)(2,1)S(1)}, bf16[768,768]{1,0:T(8,128)(2,1)}, u32[]{:S(2)}) copy-start(bf16[768,768]{1,0:T(8,128)(2,1)} %copy-done.8) | copy-start | bytes 3538948
  248.3 23.5 %copy-start.11 = (bf16[768,768]{1,0:T(8,128)(2,1)S(1)}, bf16[768,768]{1,0:T(8,128)(2,1)}, u32[]{:S(2)}) copy-start(bf16[768,768]{1,0:T(8,128)(2,1)} %copy-done.10) | copy-start | bytes 3538948
  248.3 36.6 %collective-permute-start.27 = (bf16[128,3072]{1,0:T(8,128)(2,1)}, bf16[128,3072]{1,0:T(8,128)(2,1)S(1)}, u32[]{:S(2)}, u32[]{:S(2)}) collective-permute-start(bf16[128,3072]{1,0:T(8,128)(2,1)} %convolution_convert_fusion), channel_id=1, source_target_pairs={{0,4},{1,5},{2,6},{3,7},{4,0},{5,1},{6,2},{7,3},{8,12},{9,13},{10,... | collective-permute-start | bytes 2359304 | tf_op jit(solution)/shard_map/ppermute | solution.py:434
  251.9 27.8 %collective-permute-start.26 = (bf16[48,3072]{1,0:T(8,128)(2,1)}, bf16[48,3072]{1,0:T(8,128)(2,1)S(1)}, u32[]{:S(2)}, u32[]{:S(2)}) collective-permute-start(bf16[48,3072]{1,0:T(8,128)(2,1)} %copy-done.42), channel_id=1, source_target_pairs={{0,1},{1,2},{2,3},{3,0},{4,5},{5,6},{6,7},{7,4},{8,9},{9,10},{10,1... | collective-permute-start | bytes 884744 | tf_op jit(solution)/shard_map/ppermute | solution.py:355
  251.9 27.8 %collective-permute-start.25 = (bf16[48,3072]{1,0:T(8,128)(2,1)}, bf16[48,3072]{1,0:T(8,128)(2,1)S(1)}, u32[]{:S(2)}, u32[]{:S(2)}) collective-permute-start(bf16[48,3072]{1,0:T(8,128)(2,1)} %copy-done.41), channel_id=1, source_target_pairs={{0,2},{1,3},{2,0},{3,1},{4,6},{5,7},{6,4},{7,5},{8,10},{9,11},{10,... | collective-permute-start | bytes 884744 | tf_op jit(solution)/shard_map/ppermute | solution.py:355
  252.7 27.4 %collective-permute-start.19 = (bf16[48,3072]{1,0:T(8,128)(2,1)}, bf16[48,3072]{1,0:T(8,128)(2,1)S(1)}, u32[]{:S(2)}, u32[]{:S(2)}) collective-permute-start(bf16[48,3072]{1,0:T(8,128)(2,1)} %copy-done.40), channel_id=1, source_target_pairs={{0,3},{1,0},{2,1},{3,2},{4,7},{5,4},{6,5},{7,6},{8,11},{9,8},{10,9... | collective-permute-start | bytes 884744 | tf_op jit(solution)/shard_map/ppermute | solution.py:355
  271.8 13.1 %copy-start.39 = (bf16[48,3072]{1,0:T(8,128)(2,1)S(1)}, bf16[48,3072]{1,0:T(8,128)(2,1)}, u32[]{:S(2)}) copy-start(bf16[48,3072]{1,0:T(8,128)(2,1)} %copy-done.38) | copy-start | bytes 884740
  271.8 13.1 %copy-start.44 = (bf16[192,128]{1,0:T(8,128)(2,1)S(1)}, bf16[192,128]{1,0:T(8,128)(2,1)}, u32[]{:S(2)}) copy-start(bf16[192,128]{1,0:T(8,128)(2,1)} %copy-done.43) | copy-start | bytes 147460
  (31 other events, 42.5 us)

commit v5 on v4

--- a/solution.py
+++ b/solution.py
@@ -92,6 +92,7 @@
     count, width = tokens.shape
     hidden = cotangent.shape[2]
     slots = half * capacity
+    extra = 16
     blocks = half if capacity % 16 == 0 else 1
 
     def body(info, route_rows, route_cols, gates, cotangent, tokens, *outs):
@@ -103,7 +104,11 @@
                 scaled = (factor * cotangent[:, k, :].astype(f32)).astype(bf16)
                 term = jnp.dot(pick, scaled, preferred_element_type=f32)
                 total = term if total is None else total + term
-            out[...] = total.astype(bf16)
+            out[:slots, :] = total.astype(bf16)
+        below = jnp.zeros((extra - routes.shape[1], count), f32)
+        numbers = jnp.concatenate([route_rows[...].astype(f32), below], axis=0)
+        beside = jnp.zeros((extra, hidden - count), f32)
+        outs[0][slots:, :] = jnp.concatenate([numbers, beside], axis=1).astype(bf16)
         pick = sum(chosen[1:], chosen[0])
         outs[2][...] = pick
         store_blocks(
@@ -111,7 +116,8 @@
         )
 
     operands = (routes.T, routes, gates, cotangent, tokens)
-    shapes = [(slots, hidden)] * 2 + [(slots, count)] + [(slots // blocks, width)] * blocks
+    shapes = [(slots + extra, hidden), (slots, hidden), (slots, count)]
+    shapes += [(slots // blocks, width)] * blocks
     return run(
         body,
         info,
@@ -123,22 +129,19 @@
     )
 
 
-def pick_far(info, routes, tokens, far_grads, near_grads, capacity, half):
+def pick_far(info, routes, tokens, capacity, half):
     count, width = tokens.shape
-    hidden = far_grads.shape[1]
     slots = half * capacity
     blocks = half if capacity % 16 == 0 else 1
 
-    def body(info, route_rows, route_cols, tokens, far_grads, near_grads, pick_out, *outs):
+    def body(info, route_rows, route_cols, tokens, pick_out, *outs):
         chosen = chosen_by(info, info[1], route_rows, route_cols, capacity, half)
         pick = sum(chosen[1:], chosen[0])
         pick_out[...] = pick
         store_blocks(outs, 0, jnp.dot(pick, tokens[...], preferred_element_type=f32).astype(bf16))
-        store_blocks(outs, width, far_grads[...])
-        store_blocks(outs, width + hidden, near_grads[...])
-
-    operands = (routes.T, routes, tokens, far_grads, near_grads)
-    shapes = [(slots, count)] + [(slots // blocks, width + 2 * hidden)] * blocks
+
+    operands = (routes.T, routes, tokens)
+    shapes = [(slots, count)] + [(slots // blocks, width)] * blocks
     return run(
         body,
         info,
@@ -150,20 +153,14 @@
     )
 
 
-def join(place, far, near):
-    blocks = far + near
-    width = near[0].shape[1]
-    hidden = (far[0].shape[1] - width) // 2
+def join(place, blocks):
+    width = blocks[0].shape[1]
     count = sum(block.shape[0] for block in blocks)
 
     def body(place, *refs):
-        rows, grads = refs[len(blocks) :]
         first = 0
-        for number, block in enumerate(refs[: len(blocks)]):
-            held = pl.ds(first, block.shape[0])
-            start = width if number < len(far) else width + hidden
-            rows[held, :] = block[:, :width]
-            grads[held, :] = refs[number % len(far)][:, start : start + hidden]
+        for block in refs[:-1]:
+            refs[-1][first : first + block.shape[0], :] = block[...]
             first += block.shape[0]
 
     return run(
@@ -171,11 +168,8 @@
         place,
         (1,),
         [whole(block.shape) for block in blocks],
-        [whole((count, width)), whole((count, hidden))],
-        [
-            jax.ShapeDtypeStruct((count, width), bf16),
-            jax.ShapeDtypeStruct((count, hidden), bf16),
-        ],
+        whole((count, width)),
+        jax.ShapeDtypeStruct((count, width), bf16),
         *blocks,
     )
 
@@ -379,12 +373,14 @@
         return [totals[0], across(totals[1], 1)] + sums
 
     other_tokens = lax.ppermute(tokens, "expert", swap)
-    other_routes = lax.ppermute(routes, "expert", swap)
 
     grads_away, near_grads, near_pick, *near_rows = pick_near(
         info, routes, router_gates, hidden_cotangent, tokens, capacity, half
     )
-    far_grads = lax.ppermute(grads_away, "expert", swap)
+    arrived = lax.ppermute(grads_away, "expert", swap)
+    far_grads = arrived[: half * capacity]
+    other_routes = arrived[half * capacity : half * capacity + per_token, :row_count]
+    other_routes = other_routes.astype(jnp.int32).T
 
     def send(blocks, direction=1):
         if len(blocks) == 1:
@@ -395,20 +391,23 @@
         return blocks if capacity % 16 == 0 else [jnp.concatenate(blocks, axis=0)]
 
     near_rows = send(near_rows)
-    other_tokens = after(other_tokens, other_routes, far_grads, *near_rows[1:])
+    other_tokens = after(other_tokens, arrived, *near_rows[1:])
     owned = to_owners(jnp.swapaxes(weights, 0, 1), other_tokens)
-    other_pick, *far_rows = pick_far(
-        info, other_routes, other_tokens, far_grads, near_grads, capacity, half
-    )
+    other_pick, *far_rows = pick_far(info, other_routes, other_tokens, capacity, half)
     far_rows = send(far_rows)
-    owned = after(owned, *far_rows[1:])
+    pairs = [part.reshape(half, capacity, hidden_units) for part in (far_grads, near_grads)]
+    pairs = jnp.concatenate(pairs, axis=1)
+    pairs = [shift(after(pairs[s], other_tokens), s) for s in range(half)]
+    owned = after(owned, *far_rows[1:], *pairs[1:])
     owned_gate = owned[:, 0].reshape(hidden_units, -1)
     owned_up = owned[:, 1].reshape(hidden_units, -1)
     owned_first = to_owners(jnp.swapaxes(first_moment, 0, 1), owned)
 
     gate_x = along_x(owned_gate)
     up_x = along_x(after(owned_up, *gate_x))
-    rows, grads = join(place, unsplit(far_rows), unsplit(near_rows))
+    rows = join(place, unsplit(far_rows) + unsplit(near_rows))
+    grads = jnp.stack(pairs).reshape(half, 2, capacity, hidden_units)
+    grads = jnp.swapaxes(grads, 0, 1).reshape(2 * half * capacity, hidden_units)
     gate = both_cores([owned_gate] + [after(piece, rows) for piece in gate_x])
     up = both_cores([owned_up] + up_x)
     grad_up, factor = forward_gate(place, rows, grads, gate)

time: 288 us -> 281 us (0.976)
  starting transfers between devices: 59.4 us -> 51.6 us
  waiting for transfers between devices: 145 us -> 140 us
  other arithmetic: 3.07 us -> 6.35 us
  local copies, waits for them, and re-layouts: 35.9 us -> 39.1 us
    ppermute x2 -> x1, waiting for transfers between devices: 33.2 us -> 12.6 us  [per_device(): arrived = lax.ppermute(grads_away, 'expert', swap)]
    ppermute x12 -> x15, waiting for transfers between devices: 48.5 us -> 62 us  [shift(): return lax.ppermute(value, 'expert', pairs)]
    all_to_all x3, starting transfers between devices: 25.3 us -> 16 us  [to_owners(): lax.all_to_all(by_owner, 'expert', split_axis=0, concat_axis=0, tiled=True)]
    ppermute x12 -> x15, starting transfers between devices: 15.9 us -> 20.4 us  [shift(): return lax.ppermute(value, 'expert', pairs)]
    ppermute x2 -> x1, starting transfers between devices: 3.03 us -> 0.1 us  [per_device(): arrived = lax.ppermute(grads_away, 'expert', swap)]
    unnamed x101 -> x117, local copies, waits for them, and re-layouts: 33 us -> 34.9 us
  transfers between devices with their start and end apart: 31 -> 33, of which waited for: 18 -> 16; matrix products, arithmetic and copies ran while one was open for 6% -> 8% of each run, Pallas kernels for 14% -> 14%
where the time goes in v5:
time: 281 us; the launch traced here: 280 us
  waiting for transfers between devices  140 us (50%)
  starting transfers between devices  51.6 us (18%)
  local copies, waits for them, and re-layouts  39.1 us (14%)
  Pallas kernels  39 us (14%)
  other arithmetic  6.35 us (2%)
    ppermute x15, waiting for transfers between devices, shift(): return lax.ppermute(value, 'expert', pairs)  62 us
    ppermute x12, waiting for transfers between devices, across(): return lax.ppermute(value, 'dp', [(i, i ^ k) for i in range(pieces)])  51.9 us
    unnamed x117, local copies, waits for them, and re-layouts  34.9 us
    pallas_call x8, Pallas kernels, run(): pl.pallas_call(body, grid_spec=pltpu.PrefetchScalarGridSpec(num_scalar_pr...  24.3 us
    ppermute x15, starting transfers between devices, shift(): return lax.ppermute(value, 'expert', pairs)  20.4 us
    all_to_all x3, starting transfers between devices, to_owners(): lax.all_to_all(by_owner, 'expert', split_axis=0, concat_axis=0, tiled=True)  16 us
    pallas_call x2, Pallas kernels, adam(): pl.pallas_call(body, grid=(sources,), in_specs=[flat] * (count + 1) + [mo...  14.7 us
    ppermute x1, waiting for transfers between devices, per_device(): arrived = lax.ppermute(grads_away, 'expert', swap)  12.6 us
  transfers between devices with their start and end apart: 33, of which 16 were waited for; matrix products, arithmetic and copies ran while one was open for 8% of the time, Pallas kernels for 14%

profile of v5, /device:TPU:0, one launch (start us, length us, event | category | flops | bytes accessed | tf_op | source)
XLA Modules:
  0.0 279.8 jit_solution(9328978394192098562)
XLA Ops:
  0.6 4.1 %collective-permute-start.1 = (bf16[128,3072]{1,0:T(8,128)(2,1)}, bf16[128,3072]{1,0:T(8,128)(2,1)S(1)}, u32[]{:S(2)}, u32[]{:S(2)}) collective-permute-start(bf16[128,3072]{1,0:T(8,128)(2,1)} %tokens.1), channel_id=1, source_target_pairs={{0,4},{1,5},{2,6},{3,7},{4,0},{5,1},{6,2},{7,3},{8,12},{9,13},{10,... | collective-permute-start | bytes 2359304 | tf_op jit(solution)/shard_map/ppermute | solution.py:375
  9.2 2.1 shard_map.102
  12.9 1.8 collective-permute-start.2
  14.7 1.6 collective-permute-start.3
  16.3 1.4 collective-permute-start.4
  17.7 3.2 %copy.53 = bf16[2,8,96,768]{3,2,0,1:T(8,128)(2,1)} copy(bf16[2,8,96,768]{3,2,1,0:T(8,128)(2,1)} %param.11) | data formatting | bytes 4718592 | tf_op args[4]
  20.9 2.9 %collective-permute-done.2.refs_5_ = bf16[48,3072]{1,0:T(8,128)(2,1)S(1)} collective-permute-done((bf16[48,3072]{1,0:T(8,128)(2,1)S(1)}, bf16[48,3072]{1,0:T(8,128)(2,1)S(1)}, u32[]{:S(2)}, u32[]{:S(2)}) %collective-permute-start.2) | collective-permute-done | bytes 294944 | tf_op jit(solution)/shard_map/ppermute | solution.py:349
  24.5 13.1 %collective-permute-done.3.refs_6_ = bf16[48,3072]{1,0:T(8,128)(2,1)S(1)} collective-permute-done((bf16[48,3072]{1,0:T(8,128)(2,1)S(1)}, bf16[48,3072]{1,0:T(8,128)(2,1)S(1)}, u32[]{:S(2)}, u32[]{:S(2)}) %collective-permute-start.3) | collective-permute-done | bytes 294944 | tf_op jit(solution)/shard_map/ppermute | solution.py:349
  38.4 4.5 %collective-permute-done.4.refs_7_ = bf16[48,3072]{1,0:T(8,128)(2,1)S(1)} collective-permute-done((bf16[48,3072]{1,0:T(8,128)(2,1)S(1)}, bf16[48,3072]{1,0:T(8,128)(2,1)S(1)}, u32[]{:S(2)}, u32[]{:S(2)}) %collective-permute-start.4) | collective-permute-done | bytes 294944 | tf_op jit(solution)/shard_map/ppermute | solution.py:349
  43.6 12.6 %collective-permute-done = bf16[208,768]{0,1:T(8,128)(2,1)S(1)} collective-permute-done((bf16[208,768]{0,1:T(8,128)(2,1)S(1)}, bf16[208,768]{0,1:T(8,128)(2,1)S(1)}, u32[]{:S(2)}, u32[]{:S(2)}) %collective-permute-start) | collective-permute-done | bytes 319520 | tf_op jit(solution)/shard_map/ppermute | solution.py:380
  56.9 5.8 %all-to-all-start = ((bf16[8,2,96,768]{3,2,1,0:T(8,128)(2,1)}), bf16[8,2,96,768]{3,2,1,0:T(8,128)(2,1)S(1)}, u32[]{:S(2)}, u32[]{:S(2)}) async-start(bf16[8,2,96,768]{3,2,1,0:T(8,128)(2,1)} %bitcast.54), calls=%async_computation | async-start | bytes 4718592 | tf_op jit(solution)/shard_map/all_to_all | solution.py:356
  62.7 1.5 fusion.24
  65.1 1.9 copy.40
  67.0 1.7 fusion.20
  68.7 2.0 collective-permute-start.9
  71.8 1.5 collective-permute-start.5
  74.9 1.9 collective-permute-start.10
  76.8 29.5 %collective-permute-done.9 = bf16[96,768]{1,0:T(8,128)(2,1)S(1)} collective-permute-done((bf16[96,768]{1,0:T(8,128)(2,1)S(1)}, bf16[96,768]{1,0:T(8,128)(2,1)S(1)}, u32[]{:S(2)}, u32[]{:S(2)}) %collective-permute-start.9) | collective-permute-done | bytes 147488 | tf_op jit(solution)/shard_map/ppermute | solution.py:349
  106.3 1.5 collective-permute-start.8
  107.8 3.2 %copy.52 = bf16[2,8,96,768]{3,2,0,1:T(8,128)(2,1)} copy(bf16[2,8,96,768]{3,2,1,0:T(8,128)(2,1)} %param.12) | data formatting | bytes 4718592 | tf_op args[5]
  111.0 10.1 %collective-permute-done.10 = bf16[96,768]{1,0:T(8,128)(2,1)S(1)} collective-permute-done((bf16[96,768]{1,0:T(8,128)(2,1)S(1)}, bf16[96,768]{1,0:T(8,128)(2,1)S(1)}, u32[]{:S(2)}, u32[]{:S(2)}) %collective-permute-start.10) | collective-permute-done | bytes 147488 | tf_op jit(solution)/shard_map/ppermute | solution.py:349
  121.1 1.9 collective-permute-done.8
  125.3 5.9 %all-to-all-start.1 = ((bf16[8,2,96,768]{3,2,1,0:T(8,128)(2,1)}), bf16[8,2,96,768]{3,2,1,0:T(8,128)(2,1)}, u32[]{:S(2)}, u32[]{:S(2)}) async-start(bf16[8,2,96,768]{3,2,1,0:T(8,128)(2,1)} %bitcast.42), calls=%async_computation.1 | async-start | bytes 4718592 | tf_op jit(solution)/shard_map/all_to_all | solution.py:356
  132.4 1.5 collective-permute-start.12
  141.9 17.3 %collective-permute-done.12.refs_2_ = bf16[768,768]{1,0:T(8,128)(2,1)} collective-permute-done((bf16[768,768]{1,0:T(8,128)(2,1)}, bf16[768,768]{1,0:T(8,128)(2,1)}, u32[]{:S(2)}, u32[]{:S(2)}) %collective-permute-start.12) | collective-permute-done | bytes 1179680 | tf_op jit(solution)/shard_map/ppermute | solution.py:352
  159.2 1.6 copy.51
  160.8 1.5 collective-permute-start.16
  162.4 4.7 %shard_map.105 = (bf16[384,768]{1,0:T(8,128)(2,1)S(1)}, f32[384,768]{1,0:T(8,128)S(1)}) custom-call(s32[1]{0:T(128)} %bitcast.3.place, bf16[384,3072]{1,0:T(8,128)(2,1)S(1)} %shard_map.104.rows, bf16[384,768]{1,0:T(8,128)(2,1)S(1)} %bitcast.50, bf16[768,768]{1,0:T(8,128)(2,1)} %bitcast.22.refs_0_.refs_3_, ...), custom_call_target="tpu_custom_call" | custom-call | tf_op jit(solution)/shard_map/pallas_call | solution.py:32
  168.2 3.1 %shard_map.106 = (bf16[768,768]{1,0:T(8,128)(2,1)S(1)}, bf16[768,768]{1,0:T(8,128)(2,1)S(1)}, bf16[768,768]{1,0:T(8,128)(2,1)S(1)}, bf16[768,768]{1,0:T(8,128)(2,1)S(1)}) custom-call(s32[1]{0:T(128)} %bitcast.3.place, bf16[384,768]{1,0:T(8,128)(2,1)S(1)} %get-tuple-element.83.grads.grad_up, bf16[384,3072]{1,0:T(8,128)(2,1)S(1)} %shard_map.104.rows), custom_call_target="tpu_custom_call" | custom-call | tf_op jit(solution)/shard_map/pallas_call | solution.py:32
  176.3 8.9 %all-to-all-done.1.refs_4_ = bf16[8,2,96,768]{3,2,1,0:T(8,128)(2,1)} async-done(((bf16[8,2,96,768]{3,2,1,0:T(8,128)(2,1)}), bf16[8,2,96,768]{3,2,1,0:T(8,128)(2,1)}, u32[]{:S(2)}, u32[]{:S(2)}) %all-to-all-start.1) | async-done | bytes 2359328 | tf_op jit(solution)/shard_map/all_to_all | solution.py:356
  185.3 4.4 %all-to-all-start.2 = ((bf16[8,2,96,768]{3,2,1,0:T(8,128)(2,1)}), bf16[8,2,96,768]{3,2,1,0:T(8,128)(2,1)}, u32[]{:S(2)}, u32[]{:S(2)}) async-start(bf16[8,2,96,768]{3,2,1,0:T(8,128)(2,1)} %bitcast.53), calls=%async_computation.2 | async-start | bytes 4718592 | tf_op jit(solution)/shard_map/all_to_all | solution.py:356
  190.7 2.9 %collective-permute-done.14 = bf16[768,768]{1,0:T(8,128)(2,1)S(1)} collective-permute-done((bf16[768,768]{1,0:T(8,128)(2,1)}, bf16[768,768]{1,0:T(8,128)(2,1)S(1)}, u32[]{:S(2)}, u32[]{:S(2)}) %collective-permute-start.14) | collective-permute-done | bytes 1179680 | tf_op jit(solution)/shard_map/ppermute | solution.py:352
  193.7 1.6 add_convert_fusion.1
  196.1 3.8 %shard_map.107.grad_gate.grads = bf16[384,768]{1,0:T(8,128)(2,1)S(1)} custom-call(s32[1]{0:T(128)} %bitcast.3.place, bf16[384,3072]{1,0:T(8,128)(2,1)S(1)} %shard_map.104.rows, f32[384,768]{1,0:T(8,128)S(1)} %copy-done.15, bf16[768,768]{1,0:T(8,128)(2,1)S(1)} %bitcast.47, bf16[768,768]{1,0:T(8,128)(2,1)S(1)} %collective-permute-done.15.refs_1_.refs_5_, ...), custom_call_target="tpu_custom_call" | custom-call | tf_op jit(solution)/shard_map/pallas_call | solution.py:32
  199.9 5.7 %shard_map.108 = (bf16[48,3072]{1,0:T(8,128)(2,1)S(1)}, bf16[48,3072]{1,0:T(8,128)(2,1)S(1)}, bf16[48,3072]{1,0:T(8,128)(2,1)S(1)}, bf16[48,3072]{1,0:T(8,128)(2...) custom-call(s32[1]{0:T(128)} %bitcast.3.place, ...), custom_call_target="tpu_custom_call" | custom-call | tf_op jit(solution)/shard_map/pallas_call | solution.py:32
  205.7 3.6 %shard_map.109 = (bf16[768,768]{1,0:T(8,128)(2,1)S(1)}, bf16[768,768]{1,0:T(8,128)(2,1)}, bf16[768,768]{1,0:T(8,128)(2,1)S(1)}, bf16[768,768]{1,0:T(8,128)(2,1)S(1)}) custom-call(s32[1]{0:T(128)} %bitcast.3.place, bf16[384,768]{1,0:T(8,128)(2,1)S(1)} %shard_map.107.grad_gate.grads, bf16[384,3072]{1,0:T(8,128)(2,1)S(1)} %shard_map.104.rows), custom_call_target="tpu_custom_call" | custom-call | tf_op jit(solution)/shard_map/pallas_call | solution.py:32
  209.5 1.5 collective-permute-start.25
  211.1 2.9 %collective-permute-start.18 = (bf16[48,3072]{1,0:T(8,128)(2,1)S(1)}, bf16[48,3072]{1,0:T(8,128)(2,1)S(1)}, u32[]{:S(2)}, u32[]{:S(2)}) collective-permute-start(bf16[48,3072]{1,0:T(8,128)(2,1)S(1)} %get-tuple-element.89), channel_id=1, source_target_pairs={{0,3},{1,0},{2,1},{3,2},{4,7},{5,4},{6,5},{7,6},{8,11},{9,8},{10,9... | collective-permute-start | bytes 884744 | tf_op jit(solution)/shard_map/ppermute | solution.py:349
  215.1 1.4 add_convert_fusion
  216.4 21.3 %collective-permute-done.25.refs_2_ = bf16[768,768]{1,0:T(8,128)(2,1)S(1)} collective-permute-done((bf16[768,768]{1,0:T(8,128)(2,1)S(1)}, bf16[768,768]{1,0:T(8,128)(2,1)S(1)}, u32[]{:S(2)}, u32[]{:S(2)}) %collective-permute-start.25) | collective-permute-done | bytes 1179680 | tf_op jit(solution)/shard_map/ppermute | solution.py:352
  238.8 1.5 collective-permute-start.26
  242.2 3.6 %collective-permute-start.29 = (bf16[128,3072]{1,0:T(8,128)(2,1)}, bf16[128,3072]{1,0:T(8,128)(2,1)S(1)}, u32[]{:S(2)}, u32[]{:S(2)}) collective-permute-start(bf16[128,3072]{1,0:T(8,128)(2,1)} %convolution_convert_fusion), channel_id=1, source_target_pairs={{0,4},{1,5},{2,6},{3,7},{4,0},{5,1},{6,2},{7,3},{8,12},{9,13},{10,... | collective-permute-start | bytes 2359304 | tf_op jit(solution)/shard_map/ppermute | solution.py:433
  246.0 1.5 collective-permute-start.27
  247.4 1.5 collective-permute-start.21
  250.2 6.9 %shard_map.110 = (bf16[2,1,768,768]{3,2,1,0:T(8,128)(2,1)}, bf16[2,1,768,768]{3,2,1,0:T(8,128)(2,1)}, bf16[2,1,768,768]{3,2,1,0:T(8,128)(2,1)}) custom-call(bf16[768,768]{1,0:T(8,128)(2,1)S(1)} %copy-done.7, bf16[768,768]{1,0:T(8,128)(2,1)S(1)} %copy-done.9, bf16[768,768]{1,0:T(8,128)(2,1)S(1)} %copy-done.13, bf16[768,768]{1,0:T(8,128)(2,1)S(1)} %bitcast.49, ...), custom_call_target="tpu_custom_call" | custom-call | tf_op jit(solution)/shard_map/pallas_call | solution.py:316
  257.0 9.5 %collective-permute-done.26.refs_2_ = bf16[768,768]{1,0:T(8,128)(2,1)} collective-permute-done((bf16[768,768]{1,0:T(8,128)(2,1)}, bf16[768,768]{1,0:T(8,128)(2,1)}, u32[]{:S(2)}, u32[]{:S(2)}) %collective-permute-start.26) | collective-permute-done | bytes 1179680 | tf_op jit(solution)/shard_map/ppermute | solution.py:352
  266.5 7.9 %shard_map.111 = (bf16[2,1,768,768]{3,2,1,0:T(8,128)(2,1)}, bf16[2,1,768,768]{3,2,1,0:T(8,128)(2,1)}, bf16[2,1,768,768]{3,2,1,0:T(8,128)(2,1)}) custom-call(bf16[768,768]{1,0:T(8,128)(2,1)S(1)} %copy-done.11, bf16[768,768]{1,0:T(8,128)(2,1)} %collective-permute-done.22.refs_1_, ...), custom_call_target="tpu_custom_call", output_to_operand_aliasing={{0}: (6, {}), {1}: (7, {}), {2}: (8, {})} | custom-call | tf_op jit(solution)/shard_map/pallas_call | solution.py:316
  274.4 4.1 %collective-permute-done.29 = bf16[128,3072]{1,0:T(8,128)(2,1)S(1)} collective-permute-done((bf16[128,3072]{1,0:T(8,128)(2,1)}, bf16[128,3072]{1,0:T(8,128)(2,1)S(1)}, u32[]{:S(2)}, u32[]{:S(2)}) %collective-permute-start.29) | collective-permute-done | bytes 786464 | tf_op jit(solution)/shard_map/ppermute | solution.py:433
  (157 shorter events, 38.8 us)
Async XLA Ops:
  0.6 55.6 %collective-permute-start.1 = (bf16[128,3072]{1,0:T(8,128)(2,1)}, bf16[128,3072]{1,0:T(8,128)(2,1)S(1)}, u32[]{:S(2)}, u32[]{:S(2)}) collective-permute-start(bf16[128,3072]{1,0:T(8,128)(2,1)} %tokens.1), channel_id=1, source_target_pairs={{0,4},{1,5},{2,6},{3,7},{4,0},{5,1},{6,2},{7,3},{8,12},{9,13},{10,... | collective-permute-start | bytes 2359304 | tf_op jit(solution)/shard_map/ppermute | solution.py:375
  12.8 43.4 %collective-permute-start = (bf16[208,768]{0,1:T(8,128)(2,1)S(1)}, bf16[208,768]{0,1:T(8,128)(2,1)S(1)}, u32[]{:S(2)}, u32[]{:S(2)}) collective-permute-start(bf16[208,768]{0,1:T(8,128)(2,1)S(1)} %copy.38), channel_id=1, source_target_pairs={{0,4},{1,5},{2,6},{3,7},{4,0},{5,1},{6,2},{7,3},{8,12},{9,13},{10,... | collective-permute-start | bytes 958472 | tf_op jit(solution)/shard_map/ppermute | solution.py:380
  12.9 10.9 %collective-permute-start.2 = (bf16[48,3072]{1,0:T(8,128)(2,1)S(1)}, bf16[48,3072]{1,0:T(8,128)(2,1)S(1)}, u32[]{:S(2)}, u32[]{:S(2)}) collective-permute-start(bf16[48,3072]{1,0:T(8,128)(2,1)S(1)} %get-tuple-element.64), channel_id=1, source_target_pairs={{0,1},{1,2},{2,3},{3,0},{4,5},{5,6},{6,7},{7,4},{8,9},{9,10},{10,1... | collective-permute-start | bytes 884744 | tf_op jit(solution)/shard_map/ppermute | solution.py:349
  14.7 22.9 %collective-permute-start.3 = (bf16[48,3072]{1,0:T(8,128)(2,1)S(1)}, bf16[48,3072]{1,0:T(8,128)(2,1)S(1)}, u32[]{:S(2)}, u32[]{:S(2)}) collective-permute-start(bf16[48,3072]{1,0:T(8,128)(2,1)S(1)} %get-tuple-element.65), channel_id=1, source_target_pairs={{0,2},{1,3},{2,0},{3,1},{4,6},{5,7},{6,4},{7,5},{8,10},{9,11},{10,... | collective-permute-start | bytes 884744 | tf_op jit(solution)/shard_map/ppermute | solution.py:349
  16.3 26.5 %collective-permute-start.4 = (bf16[48,3072]{1,0:T(8,128)(2,1)S(1)}, bf16[48,3072]{1,0:T(8,128)(2,1)S(1)}, u32[]{:S(2)}, u32[]{:S(2)}) collective-permute-start(bf16[48,3072]{1,0:T(8,128)(2,1)S(1)} %get-tuple-element.66), channel_id=1, source_target_pairs={{0,3},{1,0},{2,1},{3,2},{4,7},{5,4},{6,5},{7,6},{8,11},{9,8},{10,9... | collective-permute-start | bytes 884744 | tf_op jit(solution)/shard_map/ppermute | solution.py:349
  56.9 68.4 %all-to-all-start = ((bf16[8,2,96,768]{3,2,1,0:T(8,128)(2,1)}), bf16[8,2,96,768]{3,2,1,0:T(8,128)(2,1)S(1)}, u32[]{:S(2)}, u32[]{:S(2)}) async-start(bf16[8,2,96,768]{3,2,1,0:T(8,128)(2,1)} %bitcast.54), calls=%async_computation | async-start | bytes 4718592 | tf_op jit(solution)/shard_map/all_to_all | solution.py:356
  68.7 37.6 %collective-permute-start.9 = (bf16[96,768]{1,0:T(8,128)(2,1)S(1)}, bf16[96,768]{1,0:T(8,128)(2,1)S(1)}, u32[]{:S(2)}, u32[]{:S(2)}) collective-permute-start(bf16[96,768]{1,0:T(8,128)(2,1)S(1)} %get-tuple-element.76), channel_id=1, source_target_pairs={{0,2},{1,3},{2,0},{3,1},{4,6},{5,7},{6,4},{7,5},{8,10},{9,11},{10,... | collective-permute-start | bytes 442376 | tf_op jit(solution)/shard_map/ppermute | solution.py:349
  71.8 39.2 %copy-start.27 = (bf16[48,3072]{1,0:T(8,128)(2,1)}, bf16[48,3072]{1,0:T(8,128)(2,1)S(1)}, u32[]{:S(2)}) copy-start(bf16[48,3072]{1,0:T(8,128)(2,1)S(1)} %get-tuple-element.68.refs_0_) | copy-start | bytes 884740
  71.8 39.2 %copy-start.45 = (bf16[192,128]{1,0:T(8,128)(2,1)}, bf16[192,128]{1,0:T(8,128)(2,1)S(1)}, u32[]{:S(2)}) copy-start(bf16[192,128]{1,0:T(8,128)(2,1)S(1)} %get-tuple-element.118) | copy-start | bytes 147460
  71.8 51.3 %collective-permute-start.5 = (bf16[48,3072]{1,0:T(8,128)(2,1)S(1)}, bf16[48,3072]{1,0:T(8,128)(2,1)S(1)}, u32[]{:S(2)}, u32[]{:S(2)}) collective-permute-start(bf16[48,3072]{1,0:T(8,128)(2,1)S(1)} %get-tuple-element.69), channel_id=1, source_target_pairs={{0,1},{1,2},{2,3},{3,0},{4,5},{5,6},{6,7},{7,4},{8,9},{9,10},{10,1... | collective-permute-start | bytes 884744 | tf_op jit(solution)/shard_map/ppermute | solution.py:349
  73.3 50.5 %collective-permute-start.6 = (bf16[48,3072]{1,0:T(8,128)(2,1)S(1)}, bf16[48,3072]{1,0:T(8,128)(2,1)S(1)}, u32[]{:S(2)}, u32[]{:S(2)}) collective-permute-start(bf16[48,3072]{1,0:T(8,128)(2,1)S(1)} %get-tuple-element.70), channel_id=1, source_target_pairs={{0,2},{1,3},{2,0},{3,1},{4,6},{5,7},{6,4},{7,5},{8,10},{9,11},{10,... | collective-permute-start | bytes 884744 | tf_op jit(solution)/shard_map/ppermute | solution.py:349
  73.9 50.7 %collective-permute-start.7 = (bf16[48,3072]{1,0:T(8,128)(2,1)S(1)}, bf16[48,3072]{1,0:T(8,128)(2,1)S(1)}, u32[]{:S(2)}, u32[]{:S(2)}) collective-permute-start(bf16[48,3072]{1,0:T(8,128)(2,1)S(1)} %get-tuple-element.71), channel_id=1, source_target_pairs={{0,3},{1,0},{2,1},{3,2},{4,7},{5,4},{6,5},{7,6},{8,11},{9,8},{10,9... | collective-permute-start | bytes 884744 | tf_op jit(solution)/shard_map/ppermute | solution.py:349
  74.9 46.3 %collective-permute-start.10 = (bf16[96,768]{1,0:T(8,128)(2,1)S(1)}, bf16[96,768]{1,0:T(8,128)(2,1)S(1)}, u32[]{:S(2)}, u32[]{:S(2)}) collective-permute-start(bf16[96,768]{1,0:T(8,128)(2,1)S(1)} %get-tuple-element.77), channel_id=1, source_target_pairs={{0,3},{1,0},{2,1},{3,2},{4,7},{5,4},{6,5},{7,6},{8,11},{9,8},{10,9... | collective-permute-start | bytes 442376 | tf_op jit(solution)/shard_map/ppermute | solution.py:349
  106.3 16.8 %collective-permute-start.8 = (bf16[96,768]{1,0:T(8,128)(2,1)S(1)}, bf16[96,768]{1,0:T(8,128)(2,1)S(1)}, u32[]{:S(2)}, u32[]{:S(2)}) collective-permute-start(bf16[96,768]{1,0:T(8,128)(2,1)S(1)} %get-tuple-element.75), channel_id=1, source_target_pairs={{0,1},{1,2},{2,3},{3,0},{4,5},{5,6},{6,7},{7,4},{8,9},{9,10},{10,1... | collective-permute-start | bytes 442376 | tf_op jit(solution)/shard_map/ppermute | solution.py:349
  125.3 59.9 %all-to-all-start.1 = ((bf16[8,2,96,768]{3,2,1,0:T(8,128)(2,1)}), bf16[8,2,96,768]{3,2,1,0:T(8,128)(2,1)}, u32[]{:S(2)}, u32[]{:S(2)}) async-start(bf16[8,2,96,768]{3,2,1,0:T(8,128)(2,1)} %bitcast.42), calls=%async_computation.1 | async-start | bytes 4718592 | tf_op jit(solution)/shard_map/all_to_all | solution.py:356
  132.4 26.8 %collective-permute-start.12 = (bf16[768,768]{1,0:T(8,128)(2,1)}, bf16[768,768]{1,0:T(8,128)(2,1)}, u32[]{:S(2)}, u32[]{:S(2)}) collective-permute-start(bf16[768,768]{1,0:T(8,128)(2,1)} %bitcast.22.refs_0_.refs_3_), channel_id=1, source_target_pairs={{0,16},{8,24},{16,0},{24,8},{1,17},{9,25},{17,1},{25,9},{2,18},{10... | collective-permute-start | bytes 3538952 | tf_op jit(solution)/shard_map/ppermute | solution.py:352
  141.6 17.6 %copy-start.47 = (bf16[2,8,96,768]{3,2,1,0:T(8,128)(2,1)S(1)}, bf16[2,8,96,768]{3,2,1,0:T(8,128)(2,1)}, u32[]{:S(2)}) copy-start(bf16[2,8,96,768]{3,2,1,0:T(8,128)(2,1)} %param.13) | copy-start | bytes 7077892
  141.8 20.5 %copy-start.48 = (bf16[96,768]{1,0:T(8,128)(2,1)S(1)}, bf16[96,768]{1,0:T(8,128)(2,1)}, u32[]{:S(2)}) copy-start(bf16[96,768]{1,0:T(8,128)(2,1)} %get-tuple-element.74) | copy-start | bytes 442372
  141.8 20.5 %copy-start.51 = (bf16[96,768]{1,0:T(8,128)(2,1)S(1)}, bf16[96,768]{1,0:T(8,128)(2,1)}, u32[]{:S(2)}) copy-start(bf16[96,768]{1,0:T(8,128)(2,1)} %copy-done.50) | copy-start | bytes 442372
  141.8 20.5 %copy-start.53 = (bf16[96,768]{1,0:T(8,128)(2,1)S(1)}, bf16[96,768]{1,0:T(8,128)(2,1)}, u32[]{:S(2)}) copy-start(bf16[96,768]{1,0:T(8,128)(2,1)} %copy-done.52) | copy-start | bytes 442372
  141.8 20.5 %copy-start.55 = (bf16[96,768]{1,0:T(8,128)(2,1)S(1)}, bf16[96,768]{1,0:T(8,128)(2,1)}, u32[]{:S(2)}) copy-start(bf16[96,768]{1,0:T(8,128)(2,1)} %copy-done.54) | copy-start | bytes 442372
  141.8 20.6 %collective-permute-start.11 = (bf16[768,768]{1,0:T(8,128)(2,1)}, bf16[768,768]{1,0:T(8,128)(2,1)S(1)}, u32[]{:S(2)}, u32[]{:S(2)}) collective-permute-start(bf16[768,768]{1,0:T(8,128)(2,1)} %bitcast.22.refs_0_.refs_3_), channel_id=1, source_target_pairs={{0,8},{8,0},{16,24},{24,16},{1,9},{9,1},{17,25},{25,17},{2,10},{10... | collective-permute-start | bytes 3538952 | tf_op jit(solution)/shard_map/ppermute | solution.py:352
  159.2 3.2 %collective-permute-start.13 = (bf16[768,768]{1,0:T(8,128)(2,1)}, bf16[768,768]{1,0:T(8,128)(2,1)S(1)}, u32[]{:S(2)}, u32[]{:S(2)}) collective-permute-start(bf16[768,768]{1,0:T(8,128)(2,1)} %collective-permute-done.12.refs_2_), channel_id=1, source_target_pairs={{0,8},{8,0},{16,24},{24,16},{1,9},{9,1},{17,25},{25,17},{2,10},{10... | collective-permute-start | bytes 3538952 | tf_op jit(solution)/shard_map/ppermute | solution.py:352
  160.8 29.4 %collective-permute-start.16 = (bf16[768,768]{1,0:T(8,128)(2,1)S(1)}, bf16[768,768]{1,0:T(8,128)(2,1)}, u32[]{:S(2)}, u32[]{:S(2)}) collective-permute-start(bf16[768,768]{1,0:T(8,128)(2,1)S(1)} %bitcast.45), channel_id=1, source_target_pairs={{0,16},{8,24},{16,0},{24,8},{1,17},{9,25},{17,1},{25,9},{2,18},{10... | collective-permute-start | bytes 3538952 | tf_op jit(solution)/shard_map/ppermute | solution.py:352
  162.4 4.8 %copy-start = (bf16[768,768]{1,0:T(8,128)(2,1)}, bf16[768,768]{1,0:T(8,128)(2,1)S(1)}, u32[]{:S(2)}) copy-start(bf16[768,768]{1,0:T(8,128)(2,1)S(1)} %collective-permute-done.11.refs_1_) | copy-start | bytes 3538948
  185.3 57.0 %all-to-all-start.2 = ((bf16[8,2,96,768]{3,2,1,0:T(8,128)(2,1)}), bf16[8,2,96,768]{3,2,1,0:T(8,128)(2,1)}, u32[]{:S(2)}, u32[]{:S(2)}) async-start(bf16[8,2,96,768]{3,2,1,0:T(8,128)(2,1)} %bitcast.53), calls=%async_computation.2 | async-start | bytes 4718592 | tf_op jit(solution)/shard_map/all_to_all | solution.py:356
  189.6 4.0 %collective-permute-start.14 = (bf16[768,768]{1,0:T(8,128)(2,1)}, bf16[768,768]{1,0:T(8,128)(2,1)S(1)}, u32[]{:S(2)}, u32[]{:S(2)}) collective-permute-start(bf16[768,768]{1,0:T(8,128)(2,1)} %copy-done.37), channel_id=1, source_target_pairs={{0,8},{8,0},{16,24},{24,16},{1,9},{9,1},{17,25},{25,17},{2,10},{10... | collective-permute-start | bytes 3538952 | tf_op jit(solution)/shard_map/ppermute | solution.py:352
  189.7 5.8 %collective-permute-start.15 = (bf16[768,768]{1,0:T(8,128)(2,1)S(1)}, bf16[768,768]{1,0:T(8,128)(2,1)S(1)}, u32[]{:S(2)}, u32[]{:S(2)}) collective-permute-start(bf16[768,768]{1,0:T(8,128)(2,1)S(1)} %bitcast.46), channel_id=1, source_target_pairs={{0,8},{8,0},{16,24},{24,16},{1,9},{9,1},{17,25},{25,17},{2,10},{10... | collective-permute-start | bytes 3538952 | tf_op jit(solution)/shard_map/ppermute | solution.py:352
  190.2 5.9 %collective-permute-start.17 = (bf16[768,768]{1,0:T(8,128)(2,1)}, bf16[768,768]{1,0:T(8,128)(2,1)S(1)}, u32[]{:S(2)}, u32[]{:S(2)}) collective-permute-start(bf16[768,768]{1,0:T(8,128)(2,1)} %collective-permute-done.16.refs_2_.refs_6_), channel_id=1, source_target_pairs={{0,8},{8,0},{16,24},{24,16},{1,9},{9,1},{17,25},{25,17},{2,10},{10... | collective-permute-start | bytes 3538952 | tf_op jit(solution)/shard_map/ppermute | solution.py:352
  190.3 24.2 %collective-permute-start.24 = (bf16[768,768]{1,0:T(8,128)(2,1)}, bf16[768,768]{1,0:T(8,128)(2,1)S(1)}, u32[]{:S(2)}, u32[]{:S(2)}) collective-permute-start(bf16[768,768]{1,0:T(8,128)(2,1)} %copy-done.36), channel_id=1, source_target_pairs={{0,8},{8,0},{16,24},{24,16},{1,9},{9,1},{17,25},{25,17},{2,10},{10... | collective-permute-start | bytes 3538952 | tf_op jit(solution)/shard_map/ppermute | solution.py:352
  209.3 7.1 %copy-start.10 = (bf16[768,768]{1,0:T(8,128)(2,1)}, bf16[768,768]{1,0:T(8,128)(2,1)S(1)}, u32[]{:S(2)}) copy-start(bf16[768,768]{1,0:T(8,128)(2,1)S(1)} %get-tuple-element.99.refs_0_) | copy-start | bytes 3538948
  209.3 5.7 %collective-permute-start.23 = (bf16[768,768]{1,0:T(8,128)(2,1)S(1)}, bf16[768,768]{1,0:T(8,128)(2,1)S(1)}, u32[]{:S(2)}, u32[]{:S(2)}) collective-permute-start(bf16[768,768]{1,0:T(8,128)(2,1)S(1)} %get-tuple-element.102), channel_id=1, source_target_pairs={{0,8},{8,0},{16,24},{24,16},{1,9},{9,1},{17,25},{25,17},{2,10},{10... | collective-permute-start | bytes 3538952 | tf_op jit(solution)/shard_map/ppermute | solution.py:352
  209.5 28.2 %collective-permute-start.25 = (bf16[768,768]{1,0:T(8,128)(2,1)S(1)}, bf16[768,768]{1,0:T(8,128)(2,1)S(1)}, u32[]{:S(2)}, u32[]{:S(2)}) collective-permute-start(bf16[768,768]{1,0:T(8,128)(2,1)S(1)} %add_convert_fusion.1), channel_id=1, source_target_pairs={{0,16},{8,24},{16,0},{24,8},{1,17},{9,25},{17,1},{25,9},{2,18},{10... | collective-permute-start | bytes 3538952 | tf_op jit(solution)/shard_map/ppermute | solution.py:352
  211.1 29.2 %collective-permute-start.18 = (bf16[48,3072]{1,0:T(8,128)(2,1)S(1)}, bf16[48,3072]{1,0:T(8,128)(2,1)S(1)}, u32[]{:S(2)}, u32[]{:S(2)}) collective-permute-start(bf16[48,3072]{1,0:T(8,128)(2,1)S(1)} %get-tuple-element.89), channel_id=1, source_target_pairs={{0,3},{1,0},{2,1},{3,2},{4,7},{5,4},{6,5},{7,6},{8,11},{9,8},{10,9... | collective-permute-start | bytes 884744 | tf_op jit(solution)/shard_map/ppermute | solution.py:349
  213.9 26.4 %collective-permute-start.19 = (bf16[48,3072]{1,0:T(8,128)(2,1)S(1)}, bf16[48,3072]{1,0:T(8,128)(2,1)S(1)}, u32[]{:S(2)}, u32[]{:S(2)}) collective-permute-start(bf16[48,3072]{1,0:T(8,128)(2,1)S(1)} %get-tuple-element.90), channel_id=1, source_target_pairs={{0,2},{1,3},{2,0},{3,1},{4,6},{5,7},{6,4},{7,5},{8,10},{9,11},{10,... | collective-permute-start | bytes 884744 | tf_op jit(solution)/shard_map/ppermute | solution.py:349
  214.5 25.8 %collective-permute-start.20 = (bf16[48,3072]{1,0:T(8,128)(2,1)S(1)}, bf16[48,3072]{1,0:T(8,128)(2,1)S(1)}, u32[]{:S(2)}, u32[]{:S(2)}) collective-permute-start(bf16[48,3072]{1,0:T(8,128)(2,1)S(1)} %get-tuple-element.91), channel_id=1, source_target_pairs={{0,1},{1,2},{2,3},{3,0},{4,5},{5,6},{6,7},{7,4},{8,9},{9,10},{10,1... | collective-permute-start | bytes 884744 | tf_op jit(solution)/shard_map/ppermute | solution.py:349
  215.0 32.4 %collective-permute-start.22 = (bf16[768,768]{1,0:T(8,128)(2,1)}, bf16[768,768]{1,0:T(8,128)(2,1)}, u32[]{:S(2)}, u32[]{:S(2)}) collective-permute-start(bf16[768,768]{1,0:T(8,128)(2,1)} %get-tuple-element.100), channel_id=1, source_target_pairs={{0,8},{8,0},{16,24},{24,16},{1,9},{9,1},{17,25},{25,17},{2,10},{10... | collective-permute-start | bytes 3538952 | tf_op jit(solution)/shard_map/ppermute | solution.py:352
  215.1 25.3 %copy-start.46 = (bf16[192,128]{1,0:T(8,128)(2,1)S(1)}, bf16[192,128]{1,0:T(8,128)(2,1)}, u32[]{:S(2)}) copy-start(bf16[192,128]{1,0:T(8,128)(2,1)} %copy-done.45) | copy-start | bytes 147460
  238.8 27.7 %collective-permute-start.26 = (bf16[768,768]{1,0:T(8,128)(2,1)}, bf16[768,768]{1,0:T(8,128)(2,1)}, u32[]{:S(2)}, u32[]{:S(2)}) collective-permute-start(bf16[768,768]{1,0:T(8,128)(2,1)} %add_convert_fusion), channel_id=1, source_target_pairs={{0,16},{8,24},{16,0},{24,8},{1,17},{9,25},{17,1},{25,9},{2,18},{10... | collective-permute-start | bytes 3538952 | tf_op jit(solution)/shard_map/ppermute | solution.py:352
  240.3 8.6 %copy-start.7 = (bf16[768,768]{1,0:T(8,128)(2,1)S(1)}, bf16[768,768]{1,0:T(8,128)(2,1)}, u32[]{:S(2)}) copy-start(bf16[768,768]{1,0:T(8,128)(2,1)} %copy-done.6) | copy-start | bytes 3538948
  240.3 8.6 %copy-start.9 = (bf16[768,768]{1,0:T(8,128)(2,1)S(1)}, bf16[768,768]{1,0:T(8,128)(2,1)}, u32[]{:S(2)}) copy-start(bf16[768,768]{1,0:T(8,128)(2,1)} %copy-done.8) | copy-start | bytes 3538948
  242.2 24.3 %copy-start.11 = (bf16[768,768]{1,0:T(8,128)(2,1)S(1)}, bf16[768,768]{1,0:T(8,128)(2,1)}, u32[]{:S(2)}) copy-start(bf16[768,768]{1,0:T(8,128)(2,1)} %copy-done.10) | copy-start | bytes 3538948
  242.2 36.3 %collective-permute-start.29 = (bf16[128,3072]{1,0:T(8,128)(2,1)}, bf16[128,3072]{1,0:T(8,128)(2,1)S(1)}, u32[]{:S(2)}, u32[]{:S(2)}) collective-permute-start(bf16[128,3072]{1,0:T(8,128)(2,1)} %convolution_convert_fusion), channel_id=1, source_target_pairs={{0,4},{1,5},{2,6},{3,7},{4,0},{5,1},{6,2},{7,3},{8,12},{9,13},{10,... | collective-permute-start | bytes 2359304 | tf_op jit(solution)/shard_map/ppermute | solution.py:433
  245.8 28.6 %collective-permute-start.28 = (bf16[48,3072]{1,0:T(8,128)(2,1)}, bf16[48,3072]{1,0:T(8,128)(2,1)S(1)}, u32[]{:S(2)}, u32[]{:S(2)}) collective-permute-start(bf16[48,3072]{1,0:T(8,128)(2,1)} %copy-done.42), channel_id=1, source_target_pairs={{0,1},{1,2},{2,3},{3,0},{4,5},{5,6},{6,7},{7,4},{8,9},{9,10},{10,1... | collective-permute-start | bytes 884744 | tf_op jit(solution)/shard_map/ppermute | solution.py:349
  246.0 28.4 %collective-permute-start.27 = (bf16[48,3072]{1,0:T(8,128)(2,1)}, bf16[48,3072]{1,0:T(8,128)(2,1)S(1)}, u32[]{:S(2)}, u32[]{:S(2)}) collective-permute-start(bf16[48,3072]{1,0:T(8,128)(2,1)} %copy-done.41), channel_id=1, source_target_pairs={{0,2},{1,3},{2,0},{3,1},{4,6},{5,7},{6,4},{7,5},{8,10},{9,11},{10,... | collective-permute-start | bytes 884744 | tf_op jit(solution)/shard_map/ppermute | solution.py:349
  247.4 27.0 %collective-permute-start.21 = (bf16[48,3072]{1,0:T(8,128)(2,1)}, bf16[48,3072]{1,0:T(8,128)(2,1)S(1)}, u32[]{:S(2)}, u32[]{:S(2)}) collective-permute-start(bf16[48,3072]{1,0:T(8,128)(2,1)} %copy-done.40), channel_id=1, source_target_pairs={{0,3},{1,0},{2,1},{3,2},{4,7},{5,4},{6,5},{7,6},{8,11},{9,8},{10,9... | collective-permute-start | bytes 884744 | tf_op jit(solution)/shard_map/ppermute | solution.py:349
  266.5 12.0 %copy-start.39 = (bf16[48,3072]{1,0:T(8,128)(2,1)S(1)}, bf16[48,3072]{1,0:T(8,128)(2,1)}, u32[]{:S(2)}) copy-start(bf16[48,3072]{1,0:T(8,128)(2,1)} %copy-done.38) | copy-start | bytes 884740
  266.5 12.0 %copy-start.44 = (bf16[192,128]{1,0:T(8,128)(2,1)S(1)}, bf16[192,128]{1,0:T(8,128)(2,1)}, u32[]{:S(2)}) copy-start(bf16[192,128]{1,0:T(8,128)(2,1)} %copy-done.43) | copy-start | bytes 147460
  (41 other events, 71.2 us)

commit v6 on v5

--- a/solution.py
+++ b/solution.py
@@ -395,10 +395,10 @@
     owned = to_owners(jnp.swapaxes(weights, 0, 1), other_tokens)
     other_pick, *far_rows = pick_far(info, other_routes, other_tokens, capacity, half)
     far_rows = send(far_rows)
+    owned = after(owned, *far_rows[1:])
     pairs = [part.reshape(half, capacity, hidden_units) for part in (far_grads, near_grads)]
     pairs = jnp.concatenate(pairs, axis=1)
-    pairs = [shift(after(pairs[s], other_tokens), s) for s in range(half)]
-    owned = after(owned, *far_rows[1:], *pairs[1:])
+    pairs = [shift(after(pairs[s], owned), s) for s in range(half)]
     owned_gate = owned[:, 0].reshape(hidden_units, -1)
     owned_up = owned[:, 1].reshape(hidden_units, -1)
     owned_first = to_owners(jnp.swapaxes(first_moment, 0, 1), owned)
@@ -408,6 +408,7 @@
     rows = join(place, unsplit(far_rows) + unsplit(near_rows))
     grads = jnp.stack(pairs).reshape(half, 2, capacity, hidden_units)
     grads = jnp.swapaxes(grads, 0, 1).reshape(2 * half * capacity, hidden_units)
+    grads = after(grads, *up_x)
     gate = both_cores([owned_gate] + [after(piece, rows) for piece in gate_x])
     up = both_cores([owned_up] + up_x)
     grad_up, factor = forward_gate(place, rows, grads, gate)
@@ -420,7 +421,7 @@
     far_back = send(back[: len(back) // 2], -1)
     near_back = [after(block, *far_back[1:]) for block in back[len(back) // 2 :]]
     near_back = send(near_back, -1)
-    owned_second = to_owners(jnp.swapaxes(second_moment, 0, 1), owned_first, up_totals[0])
+    owned_second = to_owners(jnp.swapaxes(second_moment, 0, 1), owned_first, *pairs[1:])
     gate_totals = weight_grads(place, after(grad_gate, *back), rows, pieces)
     gate_sums = [after(pair, *up_terms) for pair in core_sums(gate_totals)]
     gate_terms = scatter(gate_totals, gate_sums)

time: 281 us -> 287 us (1.021)
  starting transfers between devices: 51.6 us -> 58.1 us
  waiting for transfers between devices: 140 us -> 145 us
  local copies, waits for them, and re-layouts: 39.1 us -> 34.3 us
    all_to_all x3, starting transfers between devices: 16 us -> 23.2 us  [to_owners(): lax.all_to_all(by_owner, 'expert', split_axis=0, concat_axis=0, tiled=True)]
    ppermute x15, waiting for transfers between devices: 62 us -> 66.8 us  [shift(): return lax.ppermute(value, 'expert', pairs)]
    unnamed x117 -> x81, local copies, waits for them, and re-layouts: 34.9 us -> 30.9 us
    ppermute x12, waiting for transfers between devices: 51.9 us -> 55.3 us  [across(): return lax.ppermute(value, 'dp', [(i, i ^ k) for i in range(pieces)])]
  transfers between devices with their start and end apart: 33 -> 33, of which waited for: 16 -> 18; matrix products, arithmetic and copies ran while one was open for 8% -> 7% of each run, Pallas kernels for 14% -> 14%
where the time goes in v6:
time: 287 us; the launch traced here: 286 us
  waiting for transfers between devices  145 us (51%)
  starting transfers between devices  58.1 us (20%)
  Pallas kernels  39.1 us (14%)
  local copies, waits for them, and re-layouts  34.3 us (12%)
  other arithmetic  5.53 us (2%)
    ppermute x15, waiting for transfers between devices, shift(): return lax.ppermute(value, 'expert', pairs)  66.8 us
    ppermute x12, waiting for transfers between devices, across(): return lax.ppermute(value, 'dp', [(i, i ^ k) for i in range(pieces)])  55.3 us
    unnamed x81, local copies, waits for them, and re-layouts  30.9 us
    pallas_call x8, Pallas kernels, run(): pl.pallas_call(body, grid_spec=pltpu.PrefetchScalarGridSpec(num_scalar_pr...  24.4 us
    all_to_all x3, starting transfers between devices, to_owners(): lax.all_to_all(by_owner, 'expert', split_axis=0, concat_axis=0, tiled=True)  23.2 us
    ppermute x15, starting transfers between devices, shift(): return lax.ppermute(value, 'expert', pairs)  21.9 us
    pallas_call x2, Pallas kernels, adam(): pl.pallas_call(body, grid=(sources,), in_specs=[flat] * (count + 1) + [mo...  14.7 us
    ppermute x1, waiting for transfers between devices, per_device(): arrived = lax.ppermute(grads_away, 'expert', swap)  12.6 us
  transfers between devices with their start and end apart: 33, of which 18 were waited for; matrix products, arithmetic and copies ran while one was open for 7% of the time, Pallas kernels for 14%

profile of v6, /device:TPU:0, one launch (start us, length us, event | category | flops | bytes accessed | tf_op | source)
XLA Modules:
  0.0 285.8 jit_solution(924364923305601356)
XLA Ops:
  0.6 4.1 %collective-permute-start.1 = (bf16[128,3072]{1,0:T(8,128)(2,1)}, bf16[128,3072]{1,0:T(8,128)(2,1)S(1)}, u32[]{:S(2)}, u32[]{:S(2)}) collective-permute-start(bf16[128,3072]{1,0:T(8,128)(2,1)} %tokens.1), channel_id=1, source_target_pairs={{0,4},{1,5},{2,6},{3,7},{4,0},{5,1},{6,2},{7,3},{8,12},{9,13},{10,... | collective-permute-start | bytes 2359304 | tf_op jit(solution)/shard_map/ppermute | solution.py:375
  9.2 2.1 shard_map.102
  13.4 1.5 collective-permute-start.2
  14.9 1.6 collective-permute-start.3
  16.4 1.4 collective-permute-start.4
  17.9 3.2 %copy.53 = bf16[2,8,96,768]{3,2,0,1:T(8,128)(2,1)} copy(bf16[2,8,96,768]{3,2,1,0:T(8,128)(2,1)} %param.11) | data formatting | bytes 4718592 | tf_op args[4]
  21.1 3.1 %collective-permute-done.2.refs_5_ = bf16[48,3072]{1,0:T(8,128)(2,1)S(1)} collective-permute-done((bf16[48,3072]{1,0:T(8,128)(2,1)S(1)}, bf16[48,3072]{1,0:T(8,128)(2,1)S(1)}, u32[]{:S(2)}, u32[]{:S(2)}) %collective-permute-start.2) | collective-permute-done | bytes 294944 | tf_op jit(solution)/shard_map/ppermute | solution.py:349
  24.9 12.7 %collective-permute-done.3.refs_6_ = bf16[48,3072]{1,0:T(8,128)(2,1)S(1)} collective-permute-done((bf16[48,3072]{1,0:T(8,128)(2,1)S(1)}, bf16[48,3072]{1,0:T(8,128)(2,1)S(1)}, u32[]{:S(2)}, u32[]{:S(2)}) %collective-permute-start.3) | collective-permute-done | bytes 294944 | tf_op jit(solution)/shard_map/ppermute | solution.py:349
  38.4 4.5 %collective-permute-done.4.refs_7_ = bf16[48,3072]{1,0:T(8,128)(2,1)S(1)} collective-permute-done((bf16[48,3072]{1,0:T(8,128)(2,1)S(1)}, bf16[48,3072]{1,0:T(8,128)(2,1)S(1)}, u32[]{:S(2)}, u32[]{:S(2)}) %collective-permute-start.4) | collective-permute-done | bytes 294944 | tf_op jit(solution)/shard_map/ppermute | solution.py:349
  43.6 12.6 %collective-permute-done = bf16[208,768]{0,1:T(8,128)(2,1)S(1)} collective-permute-done((bf16[208,768]{0,1:T(8,128)(2,1)S(1)}, bf16[208,768]{0,1:T(8,128)(2,1)S(1)}, u32[]{:S(2)}, u32[]{:S(2)}) %collective-permute-start) | collective-permute-done | bytes 319520 | tf_op jit(solution)/shard_map/ppermute | solution.py:380
  56.9 5.8 %all-to-all-start = ((bf16[8,2,96,768]{3,2,1,0:T(8,128)(2,1)}), bf16[8,2,96,768]{3,2,1,0:T(8,128)(2,1)S(1)}, u32[]{:S(2)}, u32[]{:S(2)}) async-start(bf16[8,2,96,768]{3,2,1,0:T(8,128)(2,1)} %bitcast.54), calls=%async_computation | async-start | bytes 4718592 | tf_op jit(solution)/shard_map/all_to_all | solution.py:356
  64.8 2.1 collective-permute-start.5
  66.8 1.5 collective-permute-start.6
  68.3 1.5 collective-permute-start.7
  69.8 3.2 %copy.52 = bf16[2,8,96,768]{3,2,0,1:T(8,128)(2,1)} copy(bf16[2,8,96,768]{3,2,1,0:T(8,128)(2,1)} %param.12) | data formatting | bytes 4718592 | tf_op args[5]
  73.0 32.1 %collective-permute-done.5.refs_1_ = bf16[48,3072]{1,0:T(8,128)(2,1)S(1)} collective-permute-done((bf16[48,3072]{1,0:T(8,128)(2,1)S(1)}, bf16[48,3072]{1,0:T(8,128)(2,1)S(1)}, u32[]{:S(2)}, u32[]{:S(2)}) %collective-permute-start.5) | collective-permute-done | bytes 294944 | tf_op jit(solution)/shard_map/ppermute | solution.py:349
  105.8 3.6 %collective-permute-done.6.refs_2_ = bf16[48,3072]{1,0:T(8,128)(2,1)S(1)} collective-permute-done((bf16[48,3072]{1,0:T(8,128)(2,1)S(1)}, bf16[48,3072]{1,0:T(8,128)(2,1)S(1)}, u32[]{:S(2)}, u32[]{:S(2)}) %collective-permute-start.6) | collective-permute-done | bytes 294944 | tf_op jit(solution)/shard_map/ppermute | solution.py:349
  110.2 4.6 %collective-permute-done.7.refs_3_ = bf16[48,3072]{1,0:T(8,128)(2,1)S(1)} collective-permute-done((bf16[48,3072]{1,0:T(8,128)(2,1)S(1)}, bf16[48,3072]{1,0:T(8,128)(2,1)S(1)}, u32[]{:S(2)}, u32[]{:S(2)}) %collective-permute-start.7) | collective-permute-done | bytes 294944 | tf_op jit(solution)/shard_map/ppermute | solution.py:349
  116.7 8.3 %all-to-all-start.1 = ((bf16[8,2,96,768]{3,2,1,0:T(8,128)(2,1)}), bf16[8,2,96,768]{3,2,1,0:T(8,128)(2,1)}, u32[]{:S(2)}, u32[]{:S(2)}) async-start(bf16[8,2,96,768]{3,2,1,0:T(8,128)(2,1)} %bitcast.42), calls=%async_computation.1 | async-start | bytes 4718592 | tf_op jit(solution)/shard_map/all_to_all | solution.py:356
  126.2 1.5 collective-permute-start.11
  135.6 17.5 %collective-permute-done.11.refs_2_ = bf16[768,768]{1,0:T(8,128)(2,1)} collective-permute-done((bf16[768,768]{1,0:T(8,128)(2,1)}, bf16[768,768]{1,0:T(8,128)(2,1)}, u32[]{:S(2)}, u32[]{:S(2)}) %collective-permute-start.11) | collective-permute-done | bytes 1179680 | tf_op jit(solution)/shard_map/ppermute | solution.py:352
  153.0 1.5 collective-permute-start.12
  155.0 1.9 copy.40
  156.9 1.8 fusion.20
  158.7 1.7 collective-permute-start.8
  160.5 1.5 collective-permute-start.9
  162.0 4.5 %collective-permute-done.8 = bf16[96,768]{1,0:T(8,128)(2,1)} collective-permute-done((bf16[96,768]{1,0:T(8,128)(2,1)S(1)}, bf16[96,768]{1,0:T(8,128)(2,1)}, u32[]{:S(2)}, u32[]{:S(2)}) %collective-permute-start.8) | collective-permute-done | bytes 147488 | tf_op jit(solution)/shard_map/ppermute | solution.py:349
  167.3 3.2 %copy.51 = bf16[2,8,96,768]{3,2,0,1:T(8,128)(2,1)} copy(bf16[2,8,96,768]{3,2,1,0:T(8,128)(2,1)} %param.13) | data formatting | bytes 4718592 | tf_op args[6]
  170.5 1.6 collective-permute-done.10
  172.1 6.0 %all-to-all-done.1.refs_4_ = bf16[8,2,96,768]{3,2,1,0:T(8,128)(2,1)} async-done(((bf16[8,2,96,768]{3,2,1,0:T(8,128)(2,1)}), bf16[8,2,96,768]{3,2,1,0:T(8,128)(2,1)}, u32[]{:S(2)}, u32[]{:S(2)}) %all-to-all-start.1) | async-done | bytes 2359328 | tf_op jit(solution)/shard_map/all_to_all | solution.py:356
  178.1 9.2 %all-to-all-start.2 = ((bf16[8,2,96,768]{3,2,1,0:T(8,128)(2,1)}), bf16[8,2,96,768]{3,2,1,0:T(8,128)(2,1)}, u32[]{:S(2)}, u32[]{:S(2)}) async-start(bf16[8,2,96,768]{3,2,1,0:T(8,128)(2,1)} %bitcast.53), calls=%async_computation.2 | async-start | bytes 4718592 | tf_op jit(solution)/shard_map/all_to_all | solution.py:356
  188.6 4.6 %shard_map.105 = (bf16[384,768]{1,0:T(8,128)(2,1)S(1)}, f32[384,768]{1,0:T(8,128)S(1)}) custom-call(s32[1]{0:T(128)} %bitcast.3.place, bf16[384,3072]{1,0:T(8,128)(2,1)S(1)} %shard_map.104.rows, bf16[384,768]{1,0:T(8,128)(2,1)S(1)} %bitcast.50, bf16[768,768]{1,0:T(8,128)(2,1)} %bitcast.23.refs_0_.refs_3_, bf16[768,768]{1,0:T(8,128)(2,1)} %collective-permute-done.13.refs_1_, ...), custom_call_target="tpu_custom_call" | custom-call | tf_op jit(solution)/shard_map/pallas_call | solution.py:32
  193.2 3.1 %shard_map.106 = (bf16[768,768]{1,0:T(8,128)(2,1)S(1)}, bf16[768,768]{1,0:T(8,128)(2,1)S(1)}, bf16[768,768]{1,0:T(8,128)(2,1)S(1)}, bf16[768,768]{1,0:T(8,128)(2,1)S(1)}) custom-call(s32[1]{0:T(128)} %bitcast.3.place, bf16[384,768]{1,0:T(8,128)(2,1)S(1)} %get-tuple-element.86.grads.grad_up, bf16[384,3072]{1,0:T(8,128)(2,1)S(1)} %shard_map.104.rows), custom_call_target="tpu_custom_call" | custom-call | tf_op jit(solution)/shard_map/pallas_call | solution.py:32
  197.4 1.8 collective-permute-done.15
  199.5 3.1 %collective-permute-done.16.refs_1_.refs_5_ = bf16[768,768]{1,0:T(8,128)(2,1)S(1)} collective-permute-done((bf16[768,768]{1,0:T(8,128)(2,1)S(1)}, bf16[768,768]{1,0:T(8,128)(2,1)S(1)}, u32[]{:S(2)}, u32[]{:S(2)}) %collective-permute-start.16) | collective-permute-done | bytes 1179680 | tf_op jit(solution)/shard_map/ppermute | solution.py:352
  202.8 3.7 %shard_map.107.grad_gate.grads = bf16[384,768]{1,0:T(8,128)(2,1)S(1)} custom-call(s32[1]{0:T(128)} %bitcast.3.place, bf16[384,3072]{1,0:T(8,128)(2,1)S(1)} %shard_map.104.rows, f32[384,768]{1,0:T(8,128)S(1)} %get-tuple-element.89.factor, bf16[768,768]{1,0:T(8,128)(2,1)S(1)} %bitcast.47, bf16[768,768]{1,0:T(8,128)(2,1)S(1)} %collective-permute-done.16.refs_1_.refs_5_, ...), custom_call_target="tpu_custom_call" | custom-call | tf_op jit(solution)/shard_map/pallas_call | solution.py:32
  206.6 5.8 %shard_map.108 = (bf16[48,3072]{1,0:T(8,128)(2,1)S(1)}, bf16[48,3072]{1,0:T(8,128)(2,1)S(1)}, bf16[48,3072]{1,0:T(8,128)(2,1)S(1)}, bf16[48,3072]{1,0:T(8,128)(2...) custom-call(s32[1]{0:T(128)} %bitcast.3.place, ...), custom_call_target="tpu_custom_call" | custom-call | tf_op jit(solution)/shard_map/pallas_call | solution.py:32
  212.5 3.6 %shard_map.109 = (bf16[768,768]{1,0:T(8,128)(2,1)S(1)}, bf16[768,768]{1,0:T(8,128)(2,1)}, bf16[768,768]{1,0:T(8,128)(2,1)S(1)}, bf16[768,768]{1,0:T(8,128)(2,1)S(1)}) custom-call(s32[1]{0:T(128)} %bitcast.3.place, bf16[384,768]{1,0:T(8,128)(2,1)S(1)} %shard_map.107.grad_gate.grads, bf16[384,3072]{1,0:T(8,128)(2,1)S(1)} %shard_map.104.rows), custom_call_target="tpu_custom_call" | custom-call | tf_op jit(solution)/shard_map/pallas_call | solution.py:32
  216.9 2.9 %collective-permute-start.18 = (bf16[48,3072]{1,0:T(8,128)(2,1)S(1)}, bf16[48,3072]{1,0:T(8,128)(2,1)S(1)}, u32[]{:S(2)}, u32[]{:S(2)}) collective-permute-start(bf16[48,3072]{1,0:T(8,128)(2,1)S(1)} %get-tuple-element.91), channel_id=1, source_target_pairs={{0,3},{1,0},{2,1},{3,2},{4,7},{5,4},{6,5},{7,6},{8,11},{9,8},{10,9... | collective-permute-start | bytes 884744 | tf_op jit(solution)/shard_map/ppermute | solution.py:349
  222.3 22.3 %collective-permute-done.25.refs_2_ = bf16[768,768]{1,0:T(8,128)(2,1)S(1)} collective-permute-done((bf16[768,768]{1,0:T(8,128)(2,1)S(1)}, bf16[768,768]{1,0:T(8,128)(2,1)S(1)}, u32[]{:S(2)}, u32[]{:S(2)}) %collective-permute-start.25) | collective-permute-done | bytes 1179680 | tf_op jit(solution)/shard_map/ppermute | solution.py:352
  247.5 2.9 %collective-permute-start.29 = (bf16[128,3072]{1,0:T(8,128)(2,1)}, bf16[128,3072]{1,0:T(8,128)(2,1)S(1)}, u32[]{:S(2)}, u32[]{:S(2)}) collective-permute-start(bf16[128,3072]{1,0:T(8,128)(2,1)} %convolution_convert_fusion), channel_id=1, source_target_pairs={{0,4},{1,5},{2,6},{3,7},{4,0},{5,1},{6,2},{7,3},{8,12},{9,13},{10,... | collective-permute-start | bytes 2359304 | tf_op jit(solution)/shard_map/ppermute | solution.py:434
  250.4 1.5 collective-permute-start.28
  251.9 1.4 collective-permute-start.27
  253.3 1.5 collective-permute-start.21
  256.1 6.9 %shard_map.110 = (bf16[2,1,768,768]{3,2,1,0:T(8,128)(2,1)}, bf16[2,1,768,768]{3,2,1,0:T(8,128)(2,1)}, bf16[2,1,768,768]{3,2,1,0:T(8,128)(2,1)}) custom-call(bf16[768,768]{1,0:T(8,128)(2,1)S(1)} %copy-done.1, bf16[768,768]{1,0:T(8,128)(2,1)S(1)} %copy-done.3, bf16[768,768]{1,0:T(8,128)(2,1)S(1)} %copy-done.7, bf16[768,768]{1,0:T(8,128)(2,1)S(1)} %bitcast.49, ...), custom_call_target="tpu_custom_call" | custom-call | tf_op jit(solution)/shard_map/pallas_call | solution.py:316
  263.0 10.4 %collective-permute-done.26.refs_2_ = bf16[768,768]{1,0:T(8,128)(2,1)} collective-permute-done((bf16[768,768]{1,0:T(8,128)(2,1)}, bf16[768,768]{1,0:T(8,128)(2,1)}, u32[]{:S(2)}, u32[]{:S(2)}) %collective-permute-start.26) | collective-permute-done | bytes 1179680 | tf_op jit(solution)/shard_map/ppermute | solution.py:352
  273.3 7.9 %shard_map.111 = (bf16[2,1,768,768]{3,2,1,0:T(8,128)(2,1)}, bf16[2,1,768,768]{3,2,1,0:T(8,128)(2,1)}, bf16[2,1,768,768]{3,2,1,0:T(8,128)(2,1)}) custom-call(bf16[768,768]{1,0:T(8,128)(2,1)S(1)} %copy-done.5, bf16[768,768]{1,0:T(8,128)(2,1)} %collective-permute-done.22.refs_1_, ...), custom_call_target="tpu_custom_call", output_to_operand_aliasing={{0}: (6, {}), {1}: (7, {}), {2}: (8, {})} | custom-call | tf_op jit(solution)/shard_map/pallas_call | solution.py:316
  281.2 3.2 %collective-permute-done.29 = bf16[128,3072]{1,0:T(8,128)(2,1)S(1)} collective-permute-done((bf16[128,3072]{1,0:T(8,128)(2,1)}, bf16[128,3072]{1,0:T(8,128)(2,1)S(1)}, u32[]{:S(2)}, u32[]{:S(2)}) %collective-permute-start.29) | collective-permute-done | bytes 786464 | tf_op jit(solution)/shard_map/ppermute | solution.py:434
  (121 shorter events, 36.6 us)
Async XLA Ops:
  0.6 55.6 %collective-permute-start.1 = (bf16[128,3072]{1,0:T(8,128)(2,1)}, bf16[128,3072]{1,0:T(8,128)(2,1)S(1)}, u32[]{:S(2)}, u32[]{:S(2)}) collective-permute-start(bf16[128,3072]{1,0:T(8,128)(2,1)} %tokens.1), channel_id=1, source_target_pairs={{0,4},{1,5},{2,6},{3,7},{4,0},{5,1},{6,2},{7,3},{8,12},{9,13},{10,... | collective-permute-start | bytes 2359304 | tf_op jit(solution)/shard_map/ppermute | solution.py:375
  12.9 43.3 %collective-permute-start = (bf16[208,768]{0,1:T(8,128)(2,1)S(1)}, bf16[208,768]{0,1:T(8,128)(2,1)S(1)}, u32[]{:S(2)}, u32[]{:S(2)}) collective-permute-start(bf16[208,768]{0,1:T(8,128)(2,1)S(1)} %copy.38), channel_id=1, source_target_pairs={{0,4},{1,5},{2,6},{3,7},{4,0},{5,1},{6,2},{7,3},{8,12},{9,13},{10,... | collective-permute-start | bytes 958472 | tf_op jit(solution)/shard_map/ppermute | solution.py:380
  13.4 10.9 %collective-permute-start.2 = (bf16[48,3072]{1,0:T(8,128)(2,1)S(1)}, bf16[48,3072]{1,0:T(8,128)(2,1)S(1)}, u32[]{:S(2)}, u32[]{:S(2)}) collective-permute-start(bf16[48,3072]{1,0:T(8,128)(2,1)S(1)} %get-tuple-element.65), channel_id=1, source_target_pairs={{0,1},{1,2},{2,3},{3,0},{4,5},{5,6},{6,7},{7,4},{8,9},{9,10},{10,1... | collective-permute-start | bytes 884744 | tf_op jit(solution)/shard_map/ppermute | solution.py:349
  14.9 22.8 %collective-permute-start.3 = (bf16[48,3072]{1,0:T(8,128)(2,1)S(1)}, bf16[48,3072]{1,0:T(8,128)(2,1)S(1)}, u32[]{:S(2)}, u32[]{:S(2)}) collective-permute-start(bf16[48,3072]{1,0:T(8,128)(2,1)S(1)} %get-tuple-element.66), channel_id=1, source_target_pairs={{0,2},{1,3},{2,0},{3,1},{4,6},{5,7},{6,4},{7,5},{8,10},{9,11},{10,... | collective-permute-start | bytes 884744 | tf_op jit(solution)/shard_map/ppermute | solution.py:349
  16.4 26.4 %collective-permute-start.4 = (bf16[48,3072]{1,0:T(8,128)(2,1)S(1)}, bf16[48,3072]{1,0:T(8,128)(2,1)S(1)}, u32[]{:S(2)}, u32[]{:S(2)}) collective-permute-start(bf16[48,3072]{1,0:T(8,128)(2,1)S(1)} %get-tuple-element.67), channel_id=1, source_target_pairs={{0,3},{1,0},{2,1},{3,2},{4,7},{5,4},{6,5},{7,6},{8,11},{9,8},{10,9... | collective-permute-start | bytes 884744 | tf_op jit(solution)/shard_map/ppermute | solution.py:349
  56.9 59.8 %all-to-all-start = ((bf16[8,2,96,768]{3,2,1,0:T(8,128)(2,1)}), bf16[8,2,96,768]{3,2,1,0:T(8,128)(2,1)S(1)}, u32[]{:S(2)}, u32[]{:S(2)}) async-start(bf16[8,2,96,768]{3,2,1,0:T(8,128)(2,1)} %bitcast.54), calls=%async_computation | async-start | bytes 4718592 | tf_op jit(solution)/shard_map/all_to_all | solution.py:356
  64.7 8.3 %copy-start.18 = (bf16[48,3072]{1,0:T(8,128)(2,1)}, bf16[48,3072]{1,0:T(8,128)(2,1)S(1)}, u32[]{:S(2)}) copy-start(bf16[48,3072]{1,0:T(8,128)(2,1)S(1)} %get-tuple-element.69.refs_0_) | copy-start | bytes 884740
  64.7 8.2 %copy-start.35 = (bf16[192,128]{1,0:T(8,128)(2,1)}, bf16[192,128]{1,0:T(8,128)(2,1)S(1)}, u32[]{:S(2)}) copy-start(bf16[192,128]{1,0:T(8,128)(2,1)S(1)} %get-tuple-element.120) | copy-start | bytes 147460
  64.8 40.3 %collective-permute-start.5 = (bf16[48,3072]{1,0:T(8,128)(2,1)S(1)}, bf16[48,3072]{1,0:T(8,128)(2,1)S(1)}, u32[]{:S(2)}, u32[]{:S(2)}) collective-permute-start(bf16[48,3072]{1,0:T(8,128)(2,1)S(1)} %get-tuple-element.70), channel_id=1, source_target_pairs={{0,1},{1,2},{2,3},{3,0},{4,5},{5,6},{6,7},{7,4},{8,9},{9,10},{10,1... | collective-permute-start | bytes 884744 | tf_op jit(solution)/shard_map/ppermute | solution.py:349
  66.8 42.6 %collective-permute-start.6 = (bf16[48,3072]{1,0:T(8,128)(2,1)S(1)}, bf16[48,3072]{1,0:T(8,128)(2,1)S(1)}, u32[]{:S(2)}, u32[]{:S(2)}) collective-permute-start(bf16[48,3072]{1,0:T(8,128)(2,1)S(1)} %get-tuple-element.71), channel_id=1, source_target_pairs={{0,2},{1,3},{2,0},{3,1},{4,6},{5,7},{6,4},{7,5},{8,10},{9,11},{10,... | collective-permute-start | bytes 884744 | tf_op jit(solution)/shard_map/ppermute | solution.py:349
  68.3 46.5 %collective-permute-start.7 = (bf16[48,3072]{1,0:T(8,128)(2,1)S(1)}, bf16[48,3072]{1,0:T(8,128)(2,1)S(1)}, u32[]{:S(2)}, u32[]{:S(2)}) collective-permute-start(bf16[48,3072]{1,0:T(8,128)(2,1)S(1)} %get-tuple-element.72), channel_id=1, source_target_pairs={{0,3},{1,0},{2,1},{3,2},{4,7},{5,4},{6,5},{7,6},{8,11},{9,8},{10,9... | collective-permute-start | bytes 884744 | tf_op jit(solution)/shard_map/ppermute | solution.py:349
  116.7 61.4 %all-to-all-start.1 = ((bf16[8,2,96,768]{3,2,1,0:T(8,128)(2,1)}), bf16[8,2,96,768]{3,2,1,0:T(8,128)(2,1)}, u32[]{:S(2)}, u32[]{:S(2)}) async-start(bf16[8,2,96,768]{3,2,1,0:T(8,128)(2,1)} %bitcast.42), calls=%async_computation.1 | async-start | bytes 4718592 | tf_op jit(solution)/shard_map/all_to_all | solution.py:356
  126.2 26.8 %collective-permute-start.11 = (bf16[768,768]{1,0:T(8,128)(2,1)}, bf16[768,768]{1,0:T(8,128)(2,1)}, u32[]{:S(2)}, u32[]{:S(2)}) collective-permute-start(bf16[768,768]{1,0:T(8,128)(2,1)} %bitcast.23.refs_0_.refs_3_), channel_id=1, source_target_pairs={{0,16},{8,24},{16,0},{24,8},{1,17},{9,25},{17,1},{25,9},{2,18},{10... | collective-permute-start | bytes 3538952 | tf_op jit(solution)/shard_map/ppermute | solution.py:352
  153.0 35.5 %collective-permute-start.12 = (bf16[768,768]{1,0:T(8,128)(2,1)S(1)}, bf16[768,768]{1,0:T(8,128)(2,1)}, u32[]{:S(2)}, u32[]{:S(2)}) collective-permute-start(bf16[768,768]{1,0:T(8,128)(2,1)S(1)} %bitcast.45), channel_id=1, source_target_pairs={{0,16},{8,24},{16,0},{24,8},{1,17},{9,25},{17,1},{25,9},{2,18},{10... | collective-permute-start | bytes 3538952 | tf_op jit(solution)/shard_map/ppermute | solution.py:352
  154.5 34.0 %collective-permute-start.13 = (bf16[768,768]{1,0:T(8,128)(2,1)}, bf16[768,768]{1,0:T(8,128)(2,1)}, u32[]{:S(2)}, u32[]{:S(2)}) collective-permute-start(bf16[768,768]{1,0:T(8,128)(2,1)} %bitcast.23.refs_0_.refs_3_), channel_id=1, source_target_pairs={{0,8},{8,0},{16,24},{24,16},{1,9},{9,1},{17,25},{25,17},{2,10},{10... | collective-permute-start | bytes 3538952 | tf_op jit(solution)/shard_map/ppermute | solution.py:352
  154.5 34.0 %collective-permute-start.14 = (bf16[768,768]{1,0:T(8,128)(2,1)}, bf16[768,768]{1,0:T(8,128)(2,1)}, u32[]{:S(2)}, u32[]{:S(2)}) collective-permute-start(bf16[768,768]{1,0:T(8,128)(2,1)} %collective-permute-done.11.refs_2_), channel_id=1, source_target_pairs={{0,8},{8,0},{16,24},{24,16},{1,9},{9,1},{17,25},{25,17},{2,10},{10... | collective-permute-start | bytes 3538952 | tf_op jit(solution)/shard_map/ppermute | solution.py:352
  158.7 7.8 %collective-permute-start.8 = (bf16[96,768]{1,0:T(8,128)(2,1)S(1)}, bf16[96,768]{1,0:T(8,128)(2,1)}, u32[]{:S(2)}, u32[]{:S(2)}) collective-permute-start(bf16[96,768]{1,0:T(8,128)(2,1)S(1)} %get-tuple-element.78), channel_id=1, source_target_pairs={{0,1},{1,2},{2,3},{3,0},{4,5},{5,6},{6,7},{7,4},{8,9},{9,10},{10,1... | collective-permute-start | bytes 442376 | tf_op jit(solution)/shard_map/ppermute | solution.py:349
  160.5 10.0 %collective-permute-start.9 = (bf16[96,768]{1,0:T(8,128)(2,1)S(1)}, bf16[96,768]{1,0:T(8,128)(2,1)}, u32[]{:S(2)}, u32[]{:S(2)}) collective-permute-start(bf16[96,768]{1,0:T(8,128)(2,1)S(1)} %get-tuple-element.79), channel_id=1, source_target_pairs={{0,2},{1,3},{2,0},{3,1},{4,6},{5,7},{6,4},{7,5},{8,10},{9,11},{10,... | collective-permute-start | bytes 442376 | tf_op jit(solution)/shard_map/ppermute | solution.py:349
  166.5 5.6 %collective-permute-start.10 = (bf16[96,768]{1,0:T(8,128)(2,1)S(1)}, bf16[96,768]{1,0:T(8,128)(2,1)}, u32[]{:S(2)}, u32[]{:S(2)}) collective-permute-start(bf16[96,768]{1,0:T(8,128)(2,1)S(1)} %get-tuple-element.80), channel_id=1, source_target_pairs={{0,3},{1,0},{2,1},{3,2},{4,7},{5,4},{6,5},{7,6},{8,11},{9,8},{10,9... | collective-permute-start | bytes 442376 | tf_op jit(solution)/shard_map/ppermute | solution.py:349
  178.1 69.4 %all-to-all-start.2 = ((bf16[8,2,96,768]{3,2,1,0:T(8,128)(2,1)}), bf16[8,2,96,768]{3,2,1,0:T(8,128)(2,1)}, u32[]{:S(2)}, u32[]{:S(2)}) async-start(bf16[8,2,96,768]{3,2,1,0:T(8,128)(2,1)} %bitcast.53), calls=%async_computation.2 | async-start | bytes 4718592 | tf_op jit(solution)/shard_map/all_to_all | solution.py:356
  196.3 3.2 %copy-start = (bf16[768,768]{1,0:T(8,128)(2,1)}, bf16[768,768]{1,0:T(8,128)(2,1)S(1)}, u32[]{:S(2)}) copy-start(bf16[768,768]{1,0:T(8,128)(2,1)S(1)} %get-tuple-element.105.refs_0_) | copy-start | bytes 3538948
  196.3 2.9 %collective-permute-start.15 = (bf16[768,768]{1,0:T(8,128)(2,1)S(1)}, bf16[768,768]{1,0:T(8,128)(2,1)S(1)}, u32[]{:S(2)}, u32[]{:S(2)}) collective-permute-start(bf16[768,768]{1,0:T(8,128)(2,1)S(1)} %get-tuple-element.88), channel_id=1, source_target_pairs={{0,8},{8,0},{16,24},{24,16},{1,9},{9,1},{17,25},{25,17},{2,10},{10... | collective-permute-start | bytes 3538952 | tf_op jit(solution)/shard_map/ppermute | solution.py:352
  196.4 6.2 %collective-permute-start.16 = (bf16[768,768]{1,0:T(8,128)(2,1)S(1)}, bf16[768,768]{1,0:T(8,128)(2,1)S(1)}, u32[]{:S(2)}, u32[]{:S(2)}) collective-permute-start(bf16[768,768]{1,0:T(8,128)(2,1)S(1)} %bitcast.46), channel_id=1, source_target_pairs={{0,8},{8,0},{16,24},{24,16},{1,9},{9,1},{17,25},{25,17},{2,10},{10... | collective-permute-start | bytes 3538952 | tf_op jit(solution)/shard_map/ppermute | solution.py:352
  196.9 5.9 %collective-permute-start.17 = (bf16[768,768]{1,0:T(8,128)(2,1)}, bf16[768,768]{1,0:T(8,128)(2,1)S(1)}, u32[]{:S(2)}, u32[]{:S(2)}) collective-permute-start(bf16[768,768]{1,0:T(8,128)(2,1)} %collective-permute-done.12.refs_2_.refs_6_), channel_id=1, source_target_pairs={{0,8},{8,0},{16,24},{24,16},{1,9},{9,1},{17,25},{25,17},{2,10},{10... | collective-permute-start | bytes 3538952 | tf_op jit(solution)/shard_map/ppermute | solution.py:352
  197.0 23.4 %collective-permute-start.24 = (bf16[768,768]{1,0:T(8,128)(2,1)S(1)}, bf16[768,768]{1,0:T(8,128)(2,1)S(1)}, u32[]{:S(2)}, u32[]{:S(2)}) collective-permute-start(bf16[768,768]{1,0:T(8,128)(2,1)S(1)} %get-tuple-element.106), channel_id=1, source_target_pairs={{0,8},{8,0},{16,24},{24,16},{1,9},{9,1},{17,25},{25,17},{2,10},{10... | collective-permute-start | bytes 3538952 | tf_op jit(solution)/shard_map/ppermute | solution.py:352
  212.4 3.7 %copy-start.28 = (bf16[48,3072]{1,0:T(8,128)(2,1)}, bf16[48,3072]{1,0:T(8,128)(2,1)S(1)}, u32[]{:S(2)}) copy-start(bf16[48,3072]{1,0:T(8,128)(2,1)S(1)} %get-tuple-element.94) | copy-start | bytes 884740
  212.4 3.7 %copy-start.30 = (bf16[48,3072]{1,0:T(8,128)(2,1)}, bf16[48,3072]{1,0:T(8,128)(2,1)S(1)}, u32[]{:S(2)}) copy-start(bf16[48,3072]{1,0:T(8,128)(2,1)S(1)} %get-tuple-element.96) | copy-start | bytes 884740
  212.4 3.7 %copy-start.31 = (bf16[48,3072]{1,0:T(8,128)(2,1)}, bf16[48,3072]{1,0:T(8,128)(2,1)S(1)}, u32[]{:S(2)}) copy-start(bf16[48,3072]{1,0:T(8,128)(2,1)S(1)} %get-tuple-element.116) | copy-start | bytes 884740
  212.5 3.7 %copy-start.32 = (bf16[48,3072]{1,0:T(8,128)(2,1)}, bf16[48,3072]{1,0:T(8,128)(2,1)S(1)}, u32[]{:S(2)}) copy-start(bf16[48,3072]{1,0:T(8,128)(2,1)S(1)} %get-tuple-element.118) | copy-start | bytes 884740
  216.1 6.2 %copy-start.4 = (bf16[768,768]{1,0:T(8,128)(2,1)}, bf16[768,768]{1,0:T(8,128)(2,1)S(1)}, u32[]{:S(2)}) copy-start(bf16[768,768]{1,0:T(8,128)(2,1)S(1)} %get-tuple-element.101.refs_0_) | copy-start | bytes 3538948
  216.1 4.8 %collective-permute-start.23 = (bf16[768,768]{1,0:T(8,128)(2,1)S(1)}, bf16[768,768]{1,0:T(8,128)(2,1)S(1)}, u32[]{:S(2)}, u32[]{:S(2)}) collective-permute-start(bf16[768,768]{1,0:T(8,128)(2,1)S(1)} %get-tuple-element.104), channel_id=1, source_target_pairs={{0,8},{8,0},{16,24},{24,16},{1,9},{9,1},{17,25},{25,17},{2,10},{10... | collective-permute-start | bytes 3538952 | tf_op jit(solution)/shard_map/ppermute | solution.py:352
  216.4 28.2 %collective-permute-start.25 = (bf16[768,768]{1,0:T(8,128)(2,1)S(1)}, bf16[768,768]{1,0:T(8,128)(2,1)S(1)}, u32[]{:S(2)}, u32[]{:S(2)}) collective-permute-start(bf16[768,768]{1,0:T(8,128)(2,1)S(1)} %add_convert_fusion.1), channel_id=1, source_target_pairs={{0,16},{8,24},{16,0},{24,8},{1,17},{9,25},{17,1},{25,9},{2,18},{10... | collective-permute-start | bytes 3538952 | tf_op jit(solution)/shard_map/ppermute | solution.py:352
  216.9 29.3 %collective-permute-start.18 = (bf16[48,3072]{1,0:T(8,128)(2,1)S(1)}, bf16[48,3072]{1,0:T(8,128)(2,1)S(1)}, u32[]{:S(2)}, u32[]{:S(2)}) collective-permute-start(bf16[48,3072]{1,0:T(8,128)(2,1)S(1)} %get-tuple-element.91), channel_id=1, source_target_pairs={{0,3},{1,0},{2,1},{3,2},{4,7},{5,4},{6,5},{7,6},{8,11},{9,8},{10,9... | collective-permute-start | bytes 884744 | tf_op jit(solution)/shard_map/ppermute | solution.py:349
  219.8 26.3 %collective-permute-start.19 = (bf16[48,3072]{1,0:T(8,128)(2,1)S(1)}, bf16[48,3072]{1,0:T(8,128)(2,1)S(1)}, u32[]{:S(2)}, u32[]{:S(2)}) collective-permute-start(bf16[48,3072]{1,0:T(8,128)(2,1)S(1)} %get-tuple-element.92), channel_id=1, source_target_pairs={{0,2},{1,3},{2,0},{3,1},{4,6},{5,7},{6,4},{7,5},{8,10},{9,11},{10,... | collective-permute-start | bytes 884744 | tf_op jit(solution)/shard_map/ppermute | solution.py:349
  220.4 1.9 copy-start.2
  220.4 25.8 %collective-permute-start.20 = (bf16[48,3072]{1,0:T(8,128)(2,1)S(1)}, bf16[48,3072]{1,0:T(8,128)(2,1)S(1)}, u32[]{:S(2)}, u32[]{:S(2)}) collective-permute-start(bf16[48,3072]{1,0:T(8,128)(2,1)S(1)} %get-tuple-element.93), channel_id=1, source_target_pairs={{0,1},{1,2},{2,3},{3,0},{4,5},{5,6},{6,7},{7,4},{8,9},{9,10},{10,1... | collective-permute-start | bytes 884744 | tf_op jit(solution)/shard_map/ppermute | solution.py:349
  221.0 32.4 %collective-permute-start.22 = (bf16[768,768]{1,0:T(8,128)(2,1)}, bf16[768,768]{1,0:T(8,128)(2,1)}, u32[]{:S(2)}, u32[]{:S(2)}) collective-permute-start(bf16[768,768]{1,0:T(8,128)(2,1)} %get-tuple-element.102), channel_id=1, source_target_pairs={{0,8},{8,0},{16,24},{24,16},{1,9},{9,1},{17,25},{25,17},{2,10},{10... | collective-permute-start | bytes 3538952 | tf_op jit(solution)/shard_map/ppermute | solution.py:352
  221.0 25.2 %copy-start.36 = (bf16[192,128]{1,0:T(8,128)(2,1)S(1)}, bf16[192,128]{1,0:T(8,128)(2,1)}, u32[]{:S(2)}) copy-start(bf16[192,128]{1,0:T(8,128)(2,1)} %copy-done.35) | copy-start | bytes 147460
  245.6 27.7 %collective-permute-start.26 = (bf16[768,768]{1,0:T(8,128)(2,1)}, bf16[768,768]{1,0:T(8,128)(2,1)}, u32[]{:S(2)}, u32[]{:S(2)}) collective-permute-start(bf16[768,768]{1,0:T(8,128)(2,1)} %add_convert_fusion), channel_id=1, source_target_pairs={{0,16},{8,24},{16,0},{24,8},{1,17},{9,25},{17,1},{25,9},{2,18},{10... | collective-permute-start | bytes 3538952 | tf_op jit(solution)/shard_map/ppermute | solution.py:352
  246.2 8.6 %copy-start.1 = (bf16[768,768]{1,0:T(8,128)(2,1)S(1)}, bf16[768,768]{1,0:T(8,128)(2,1)}, u32[]{:S(2)}) copy-start(bf16[768,768]{1,0:T(8,128)(2,1)} %copy-done) | copy-start | bytes 3538948
  246.2 8.6 %copy-start.3 = (bf16[768,768]{1,0:T(8,128)(2,1)S(1)}, bf16[768,768]{1,0:T(8,128)(2,1)}, u32[]{:S(2)}) copy-start(bf16[768,768]{1,0:T(8,128)(2,1)} %copy-done.2) | copy-start | bytes 3538948
  247.5 25.8 %copy-start.5 = (bf16[768,768]{1,0:T(8,128)(2,1)S(1)}, bf16[768,768]{1,0:T(8,128)(2,1)}, u32[]{:S(2)}) copy-start(bf16[768,768]{1,0:T(8,128)(2,1)} %copy-done.4) | copy-start | bytes 3538948
  247.5 37.0 %collective-permute-start.29 = (bf16[128,3072]{1,0:T(8,128)(2,1)}, bf16[128,3072]{1,0:T(8,128)(2,1)S(1)}, u32[]{:S(2)}, u32[]{:S(2)}) collective-permute-start(bf16[128,3072]{1,0:T(8,128)(2,1)} %convolution_convert_fusion), channel_id=1, source_target_pairs={{0,4},{1,5},{2,6},{3,7},{4,0},{5,1},{6,2},{7,3},{8,12},{9,13},{10,... | collective-permute-start | bytes 2359304 | tf_op jit(solution)/shard_map/ppermute | solution.py:434
  250.4 30.8 %collective-permute-start.28 = (bf16[48,3072]{1,0:T(8,128)(2,1)}, bf16[48,3072]{1,0:T(8,128)(2,1)S(1)}, u32[]{:S(2)}, u32[]{:S(2)}) collective-permute-start(bf16[48,3072]{1,0:T(8,128)(2,1)} %copy-done.32), channel_id=1, source_target_pairs={{0,1},{1,2},{2,3},{3,0},{4,5},{5,6},{6,7},{7,4},{8,9},{9,10},{10,1... | collective-permute-start | bytes 884744 | tf_op jit(solution)/shard_map/ppermute | solution.py:349
  251.9 29.3 %collective-permute-start.27 = (bf16[48,3072]{1,0:T(8,128)(2,1)}, bf16[48,3072]{1,0:T(8,128)(2,1)S(1)}, u32[]{:S(2)}, u32[]{:S(2)}) collective-permute-start(bf16[48,3072]{1,0:T(8,128)(2,1)} %copy-done.31), channel_id=1, source_target_pairs={{0,2},{1,3},{2,0},{3,1},{4,6},{5,7},{6,4},{7,5},{8,10},{9,11},{10,... | collective-permute-start | bytes 884744 | tf_op jit(solution)/shard_map/ppermute | solution.py:349
  253.3 27.9 %collective-permute-start.21 = (bf16[48,3072]{1,0:T(8,128)(2,1)}, bf16[48,3072]{1,0:T(8,128)(2,1)S(1)}, u32[]{:S(2)}, u32[]{:S(2)}) collective-permute-start(bf16[48,3072]{1,0:T(8,128)(2,1)} %copy-done.30), channel_id=1, source_target_pairs={{0,3},{1,0},{2,1},{3,2},{4,7},{5,4},{6,5},{7,6},{8,11},{9,8},{10,9... | collective-permute-start | bytes 884744 | tf_op jit(solution)/shard_map/ppermute | solution.py:349
  273.3 11.1 %copy-start.29 = (bf16[48,3072]{1,0:T(8,128)(2,1)S(1)}, bf16[48,3072]{1,0:T(8,128)(2,1)}, u32[]{:S(2)}) copy-start(bf16[48,3072]{1,0:T(8,128)(2,1)} %copy-done.28) | copy-start | bytes 884740
  273.3 11.1 %copy-start.34 = (bf16[192,128]{1,0:T(8,128)(2,1)S(1)}, bf16[192,128]{1,0:T(8,128)(2,1)}, u32[]{:S(2)}) copy-start(bf16[192,128]{1,0:T(8,128)(2,1)} %copy-done.33) | copy-start | bytes 147460
  (23 other events, 19.9 us)

commit v7 on v2

--- a/solution.py
+++ b/solution.py
@@ -333,7 +333,7 @@
     up_totals = weight_grads(place, grad_up, rows, pieces)
     up_terms = scatter(up_totals)
     owned_second = to_owners(second_moment, owned_first, up_totals[0])
-    grad_gate = forward_up(place, rows, after(factor, owned_first), up)
+    grad_gate = forward_up(place, rows, after(factor, owned_first, up_terms[1]), up)
     back = input_grads(
         place, grad_gate, grad_up, gate, up, rows.shape[0] if joined else capacity
     )
@@ -342,13 +342,13 @@
     far_back = [shift(back[s], -s) for s in range(half)]
     near_back = [shift(after(back[half + s], *far_back[1:]), -s) for s in range(half)]
     gate_totals = weight_grads(place, after(grad_gate, *back), rows, pieces)
-    gate_terms = scatter(gate_totals, *up_terms)
+    gate_terms = scatter(gate_totals)
 
     def combine(picker, parts):
         parts = jnp.concatenate(parts, axis=0)
         return jnp.einsum("st,sd->td", picker, parts, preferred_element_type=f32)
 
-    far_sum = after(combine(other_pick, far_back).astype(bf16), owned_second, *up_terms)
+    far_sum = combine(other_pick, far_back).astype(bf16)
     far_sum = lax.ppermute(far_sum, "expert", swap)
     results = adam(1, up_terms, owned_up, owned_first, owned_second)
     results = adam(0, gate_terms, owned_gate, owned_first, owned_second, *results)

time: 279 us -> 281 us (level)
  waiting for transfers between devices: 143 us -> 139 us
    ppermute x12, waiting for transfers between devices: 60.2 us -> 33.5 us  [across(): return lax.ppermute(value, 'dp', [(i, i ^ k) for i in range(pieces)])]
    ppermute x15, waiting for transfers between devices: 39.5 us -> 62.3 us  [shift(): return lax.ppermute(value, 'expert', pairs)]
    unnamed x122 -> x120, local copies, waits for them, and re-layouts: 26.4 us -> 27.9 us
  transfers between devices with their start and end apart: 34 -> 34, of which waited for: 13 -> 16; matrix products, arithmetic and copies ran while one was open for 8% -> 8% of each run, Pallas kernels for 13% -> 13%
where the time goes in v7:
time: 281 us; the launch traced here: 280 us
  waiting for transfers between devices  139 us (49%)
  starting transfers between devices  59.4 us (21%)
  Pallas kernels  35.1 us (12%)
  local copies, waits for them, and re-layouts  32.5 us (12%)
  other arithmetic  6.83 us (2%)
  matrix products  5.47 us (2%)
    ppermute x15, waiting for transfers between devices, shift(): return lax.ppermute(value, 'expert', pairs)  62.3 us
    ppermute x12, waiting for transfers between devices, across(): return lax.ppermute(value, 'dp', [(i, i ^ k) for i in range(pieces)])  33.5 us
    unnamed x120, local copies, waits for them, and re-layouts  27.9 us
    ppermute x15, starting transfers between devices, shift(): return lax.ppermute(value, 'expert', pairs)  27.7 us
    ppermute x1, waiting for transfers between devices, per_device(): far_grads = lax.ppermute(pick_grads(far_ids), 'expert', swap)  22.5 us
    pallas_call x5, Pallas kernels, run(): pl.pallas_call(body, grid_spec=pltpu.PrefetchScalarGridSpec(num_scalar_pr...  20.8 us
    pallas_call x2, Pallas kernels, adam(): pl.pallas_call(body, grid=(sources,), in_specs=[flat] * (count + 1) + [mo...  14.3 us
    all_to_all x3, starting transfers between devices, to_owners(): lax.all_to_all(by_owner, 'expert', split_axis=0, concat_axis=0, tiled=True)  12.6 us
  transfers between devices with their start and end apart: 34, of which 16 were waited for; matrix products, arithmetic and copies ran while one was open for 8% of the time, Pallas kernels for 13%

profile of v7, /device:TPU:0, one launch (start us, length us, event | category | flops | bytes accessed | tf_op | source)
XLA Modules:
  0.0 279.6 jit_solution(10532387320157941761)
XLA Ops:
  0.6 4.1 %collective-permute-start = (s32[128,2]{0,1:T(2,128)}, s32[128,2]{0,1:T(2,128)S(1)}, u32[]{:S(2)}, u32[]{:S(2)}) collective-permute-start(s32[128,2]{0,1:T(2,128)} %param.8), channel_id=1, source_target_pairs={{0,4},{1,5},{2,6},{3,7},{4,0},{5,1},{6,2},{7,3},{8,12},{9,13},{10,... | collective-permute-start | bytes 3080 | tf_op jit(solution)/shard_map/ppermute | solution.py:282
  6.9 1.4 multiply_convert_fusion
  8.8 2.9 %collective-permute-start.1 = (bf16[128,3072]{1,0:T(8,128)(2,1)S(1)}, bf16[128,3072]{1,0:T(8,128)(2,1)S(1)}, u32[]{:S(2)}, u32[]{:S(2)}) collective-permute-start(bf16[128,3072]{1,0:T(8,128)(2,1)S(1)} %copy-done.44), channel_id=1, source_target_pairs={{0,4},{1,5},{2,6},{3,7},{4,0},{5,1},{6,2},{7,3},{8,12},{9,13},{10,... | collective-permute-start | bytes 2359304 | tf_op jit(solution)/shard_map/ppermute | solution.py:281
  14.8 2.5 collective-permute-start.5
  18.4 1.6 copy.57
  20.0 22.5 %collective-permute-done.2 = bf16[4,48,768]{2,1,0:T(8,128)(2,1)S(1)} collective-permute-done((bf16[4,48,768]{2,1,0:T(8,128)(2,1)S(1)}, bf16[4,48,768]{2,1,0:T(8,128)(2,1)S(1)}, u32[]{:S(2)}, u32[]{:S(2)}) %collective-permute-start.2) | collective-permute-done | bytes 294944 | tf_op jit(solution)/shard_map/ppermute | solution.py:296
  43.3 1.3 collective-permute-done.4.refs_6_
  46.1 12.1 %collective-permute-done.1 = bf16[128,3072]{1,0:T(8,128)(2,1)S(1)} collective-permute-done((bf16[128,3072]{1,0:T(8,128)(2,1)S(1)}, bf16[128,3072]{1,0:T(8,128)(2,1)S(1)}, u32[]{:S(2)}, u32[]{:S(2)}) %collective-permute-start.1) | collective-permute-done | bytes 786464 | tf_op jit(solution)/shard_map/ppermute | solution.py:281
  58.2 3.6 %all-to-all-start = ((bf16[8,2,96,768]{3,2,1,0:T(8,128)(2,1)}), bf16[8,2,96,768]{3,2,1,0:T(8,128)(2,1)S(1)}, u32[]{:S(2)}, u32[]{:S(2)}) async-start(bf16[8,2,96,768]{3,2,1,0:T(8,128)(2,1)} %bitcast.34), calls=%async_computation | async-start | bytes 4718592 | tf_op jit(solution)/shard_map/all_to_all | solution.py:266
  62.1 1.7 fusion.23
  63.8 1.9 collective-permute-start.9
  68.0 1.9 collective-permute-start.7
  70.5 2.4 collective-permute-start.11
  72.9 28.1 %collective-permute-done.9 = bf16[96,768]{1,0:T(8,128)(2,1)S(1)} collective-permute-done((bf16[96,768]{1,0:T(8,128)(2,1)S(1)}, bf16[96,768]{1,0:T(8,128)(2,1)S(1)}, u32[]{:S(2)}, u32[]{:S(2)}) %collective-permute-start.9) | collective-permute-done | bytes 147488 | tf_op jit(solution)/shard_map/ppermute | solution.py:255
  100.9 8.5 %collective-permute-start.10 = (bf16[96,768]{1,0:T(8,128)(2,1)S(1)}, bf16[96,768]{1,0:T(8,128)(2,1)S(1)}, u32[]{:S(2)}, u32[]{:S(2)}) collective-permute-start(bf16[96,768]{1,0:T(8,128)(2,1)S(1)} %get-tuple-element.99), channel_id=1, source_target_pairs={{0,2},{1,3},{2,0},{3,1},{4,6},{5,7},{6,4},{7,5},{8,10},{9,11},{10,... | collective-permute-start | bytes 442376 | tf_op jit(solution)/shard_map/ppermute | solution.py:255
  109.5 1.6 copy.56
  111.0 6.9 %collective-permute-done.11 = bf16[96,768]{1,0:T(8,128)(2,1)S(1)} collective-permute-done((bf16[96,768]{1,0:T(8,128)(2,1)S(1)}, bf16[96,768]{1,0:T(8,128)(2,1)S(1)}, u32[]{:S(2)}, u32[]{:S(2)}) %collective-permute-start.11) | collective-permute-done | bytes 147488 | tf_op jit(solution)/shard_map/ppermute | solution.py:255
  118.0 3.2 %collective-permute-done.10 = bf16[96,768]{1,0:T(8,128)(2,1)S(1)} collective-permute-done((bf16[96,768]{1,0:T(8,128)(2,1)S(1)}, bf16[96,768]{1,0:T(8,128)(2,1)S(1)}, u32[]{:S(2)}, u32[]{:S(2)}) %collective-permute-start.10) | collective-permute-done | bytes 147488 | tf_op jit(solution)/shard_map/ppermute | solution.py:255
  123.4 1.4 copy-done.41
  124.8 4.6 %all-to-all-start.1 = ((bf16[8,2,96,768]{3,2,1,0:T(8,128)(2,1)}), bf16[8,2,96,768]{3,2,1,0:T(8,128)(2,1)}, u32[]{:S(2)}, u32[]{:S(2)}) async-start(bf16[8,2,96,768]{3,2,1,0:T(8,128)(2,1)} %bitcast.33), calls=%async_computation.1 | async-start | bytes 4718592 | tf_op jit(solution)/shard_map/all_to_all | solution.py:266
  129.4 1.8 fusion.34
  131.2 1.6 collective-permute-start.13
  132.8 25.0 %collective-permute-done.13.refs_11_.refs_2_ = bf16[768,768]{1,0:T(8,128)(2,1)S(1)} collective-permute-done((bf16[768,768]{1,0:T(8,128)(2,1)S(1)}, bf16[768,768]{1,0:T(8,128)(2,1)S(1)}, u32[]{:S(2)}, u32[]{:S(2)}) %collective-permute-start.13) | collective-permute-done | bytes 1179680 | tf_op jit(solution)/shard_map/ppermute | solution.py:258
  157.7 1.5 collective-permute-start.17
  159.3 3.4 %copy.55 = bf16[2,8,96,768]{3,2,0,1:T(8,128)(2,1)} copy(bf16[2,8,96,768]{3,2,1,0:T(8,128)(2,1)} %param.13) | data formatting | bytes 4718592 | tf_op args[6]
  165.2 4.3 %shard_map.102 = (bf16[384,3072]{1,0:T(8,128)(2,1)S(1)}, bf16[384,768]{1,0:T(8,128)(2,1)S(1)}, f32[384,768]{1,0:T(8,128)S(1)}) custom-call(s32[1]{0:T(128)} %bitcast.place, bf16[48,3072]{1,0:T(8,128)(2,1)S(1)} %copy-done.22, bf16[48,3072]{1,0:T(8,128)(2,1)S(1)} %copy-done.36, bf16[48,3072]{1,0:T(8,128)(2,1)S(1)} %copy-done.34, ...), custom_call_target="tpu_custom_call" | custom-call | tf_op jit(solution)/shard_map/pallas_call | solution.py:32
  170.5 3.1 %shard_map.103 = (bf16[768,768]{1,0:T(8,128)(2,1)S(1)}, bf16[768,768]{1,0:T(8,128)(2,1)S(1)}, bf16[768,768]{1,0:T(8,128)(2,1)S(1)}, bf16[768,768]{1,0:T(8,128)(2,1)S(1)}) custom-call(s32[1]{0:T(128)} %bitcast.place, bf16[384,768]{1,0:T(8,128)(2,1)S(1)} %get-tuple-element.50.grads.grad_up, bf16[384,3072]{1,0:T(8,128)(2,1)S(1)} %get-tuple-element.47.rows), custom_call_target="tpu_custom_call" | custom-call | tf_op jit(solution)/shard_map/pallas_call | solution.py:32
  178.6 3.7 %all-to-all-done.1.refs_4_ = bf16[8,2,96,768]{3,2,1,0:T(8,128)(2,1)} async-done(((bf16[8,2,96,768]{3,2,1,0:T(8,128)(2,1)}), bf16[8,2,96,768]{3,2,1,0:T(8,128)(2,1)}, u32[]{:S(2)}, u32[]{:S(2)}) %all-to-all-start.1) | async-done | bytes 2359328 | tf_op jit(solution)/shard_map/all_to_all | solution.py:266
  182.3 4.4 %all-to-all-start.2 = ((bf16[8,2,96,768]{3,2,1,0:T(8,128)(2,1)}), bf16[8,2,96,768]{3,2,1,0:T(8,128)(2,1)}, u32[]{:S(2)}, u32[]{:S(2)}) async-start(bf16[8,2,96,768]{3,2,1,0:T(8,128)(2,1)} %bitcast.46), calls=%async_computation.2 | async-start | bytes 4718592 | tf_op jit(solution)/shard_map/all_to_all | solution.py:266
  187.8 2.9 %collective-permute-done.15.refs_1_ = bf16[768,768]{1,0:T(8,128)(2,1)S(1)} collective-permute-done((bf16[768,768]{1,0:T(8,128)(2,1)}, bf16[768,768]{1,0:T(8,128)(2,1)S(1)}, u32[]{:S(2)}, u32[]{:S(2)}) %collective-permute-start.15) | collective-permute-done | bytes 1179680 | tf_op jit(solution)/shard_map/ppermute | solution.py:258
  190.7 1.9 collective-permute-done.16.refs_1_.refs_5_
  194.5 3.7 %shard_map.104.grad_gate.grads = bf16[384,768]{1,0:T(8,128)(2,1)S(1)} custom-call(s32[1]{0:T(128)} %bitcast.place, bf16[384,3072]{1,0:T(8,128)(2,1)S(1)} %get-tuple-element.47.rows, f32[384,768]{1,0:T(8,128)S(1)} %copy-done.20, bf16[768,768]{1,0:T(8,128)(2,1)S(1)} %bitcast.37, bf16[768,768]{1,0:T(8,128)(2,1)S(1)} %collective-permute-done.16.refs_1_.refs_5_, ...), custom_call_target="tpu_custom_call" | custom-call | tf_op jit(solution)/shard_map/pallas_call | solution.py:32
  198.3 6.6 %shard_map.105 = (bf16[48,3072]{1,0:T(8,128)(2,1)S(1)}, bf16[48,3072]{1,0:T(8,128)(2,1)S(1)}, bf16[48,3072]{1,0:T(8,128)(2,1)S(1)}, bf16[48,3072]{1,0:T(8,128)(2...) custom-call(s32[1]{0:T(128)} %bitcast.place, ...), custom_call_target="tpu_custom_call" | custom-call | tf_op jit(solution)/shard_map/pallas_call | solution.py:32
  204.8 3.1 %shard_map.106 = (bf16[768,768]{1,0:T(8,128)(2,1)S(1)}, bf16[768,768]{1,0:T(8,128)(2,1)S(1)}, bf16[768,768]{1,0:T(8,128)(2,1)S(1)}, bf16[768,768]{1,0:T(8,128)(2,1)S(1)}) custom-call(s32[1]{0:T(128)} %bitcast.place, bf16[384,768]{1,0:T(8,128)(2,1)S(1)} %shard_map.104.grad_gate.grads, bf16[384,3072]{1,0:T(8,128)(2,1)S(1)} %get-tuple-element.47.rows), custom_call_target="tpu_custom_call" | custom-call | tf_op jit(solution)/shard_map/pallas_call | solution.py:32
  209.0 1.5 collective-permute-start.27
  210.5 2.7 collective-permute-start.19
  214.4 1.3 add_convert_fusion.1
  215.7 17.4 %collective-permute-done.19 = bf16[48,3072]{1,0:T(8,128)(2,1)S(1)} collective-permute-done((bf16[48,3072]{1,0:T(8,128)(2,1)S(1)}, bf16[48,3072]{1,0:T(8,128)(2,1)S(1)}, u32[]{:S(2)}, u32[]{:S(2)}) %collective-permute-start.19) | collective-permute-done | bytes 294944 | tf_op jit(solution)/shard_map/ppermute | solution.py:255
  233.1 1.4 collective-permute-start.25
  234.6 3.2 %collective-permute-done.20 = bf16[48,3072]{1,0:T(8,128)(2,1)S(1)} collective-permute-done((bf16[48,3072]{1,0:T(8,128)(2,1)S(1)}, bf16[48,3072]{1,0:T(8,128)(2,1)S(1)}, u32[]{:S(2)}, u32[]{:S(2)}) %collective-permute-start.20) | collective-permute-done | bytes 294944 | tf_op jit(solution)/shard_map/ppermute | solution.py:255
  239.1 4.7 %collective-permute-start.30 = (bf16[128,3072]{1,0:T(8,128)(2,1)}, bf16[128,3072]{1,0:T(8,128)(2,1)}, u32[]{:S(2)}, u32[]{:S(2)}) collective-permute-start(bf16[128,3072]{1,0:T(8,128)(2,1)} %convolution_convert_fusion.2), channel_id=1, source_target_pairs={{0,4},{1,5},{2,6},{3,7},{4,0},{5,1},{6,2},{7,3},{8,12},{9,13},{10,... | collective-permute-start | bytes 2359304 | tf_op jit(solution)/shard_map/ppermute | solution.py:352
  246.8 2.9 %collective-permute-start.22 = (bf16[48,3072]{1,0:T(8,128)(2,1)}, bf16[48,3072]{1,0:T(8,128)(2,1)}, u32[]{:S(2)}, u32[]{:S(2)}) collective-permute-start(bf16[48,3072]{1,0:T(8,128)(2,1)} %get-tuple-element.60), channel_id=1, source_target_pairs={{0,3},{1,0},{2,1},{3,2},{4,7},{5,4},{6,5},{7,6},{8,11},{9,8},{10,9... | collective-permute-start | bytes 884744 | tf_op jit(solution)/shard_map/ppermute | solution.py:255
  252.3 7.0 %shard_map.107 = (bf16[2,1,768,768]{3,2,1,0:T(8,128)(2,1)}, bf16[2,1,768,768]{3,2,1,0:T(8,128)(2,1)}, bf16[2,1,768,768]{3,2,1,0:T(8,128)(2,1)}) custom-call(bf16[768,768]{1,0:T(8,128)(2,1)S(1)} %copy-done.10, bf16[768,768]{1,0:T(8,128)(2,1)S(1)} %copy-done.12, bf16[768,768]{1,0:T(8,128)(2,1)S(1)} %copy-done.16, bf16[768,768]{1,0:T(8,128)(2,1)S(1)} %bitcast.39, ...), custom_call_target="tpu_custom_call" | custom-call | tf_op jit(solution)/shard_map/pallas_call | solution.py:212
  259.3 3.1 %collective-permute-done.25.refs_2_ = bf16[768,768]{1,0:T(8,128)(2,1)} collective-permute-done((bf16[768,768]{1,0:T(8,128)(2,1)}, bf16[768,768]{1,0:T(8,128)(2,1)}, u32[]{:S(2)}, u32[]{:S(2)}) %collective-permute-start.25) | collective-permute-done | bytes 1179680 | tf_op jit(solution)/shard_map/ppermute | solution.py:258
  262.5 7.2 %shard_map.108 = (bf16[2,1,768,768]{3,2,1,0:T(8,128)(2,1)}, bf16[2,1,768,768]{3,2,1,0:T(8,128)(2,1)}, bf16[2,1,768,768]{3,2,1,0:T(8,128)(2,1)}) custom-call(bf16[768,768]{1,0:T(8,128)(2,1)S(1)} %copy-done.14, bf16[768,768]{1,0:T(8,128)(2,1)S(1)} %copy-done.18, ...), custom_call_target="tpu_custom_call", output_to_operand_aliasing={{0}: (6, {}), {1}: (7, {}), {2}: (8, {})} | custom-call | tf_op jit(solution)/shard_map/pallas_call | solution.py:212
  269.7 2.2 collective-permute-done.22
  271.9 4.9 %collective-permute-done.30 = bf16[128,3072]{1,0:T(8,128)(2,1)} collective-permute-done((bf16[128,3072]{1,0:T(8,128)(2,1)}, bf16[128,3072]{1,0:T(8,128)(2,1)}, u32[]{:S(2)}, u32[]{:S(2)}) %collective-permute-start.30) | collective-permute-done | bytes 786464 | tf_op jit(solution)/shard_map/ppermute | solution.py:352
  276.9 2.7 add_convert_fusion.2
  (182 shorter events, 34.7 us)
Async XLA Ops:
  0.6 11.5 %collective-permute-start = (s32[128,2]{0,1:T(2,128)}, s32[128,2]{0,1:T(2,128)S(1)}, u32[]{:S(2)}, u32[]{:S(2)}) collective-permute-start(s32[128,2]{0,1:T(2,128)} %param.8), channel_id=1, source_target_pairs={{0,4},{1,5},{2,6},{3,7},{4,0},{5,1},{6,2},{7,3},{8,12},{9,13},{10,... | collective-permute-start | bytes 3080 | tf_op jit(solution)/shard_map/ppermute | solution.py:282
  8.7 33.8 %collective-permute-start.2 = (bf16[4,48,768]{2,1,0:T(8,128)(2,1)S(1)}, bf16[4,48,768]{2,1,0:T(8,128)(2,1)S(1)}, u32[]{:S(2)}, u32[]{:S(2)}) collective-permute-start(bf16[4,48,768]{2,1,0:T(8,128)(2,1)S(1)} %bitcast.49), channel_id=1, source_target_pairs={{0,4},{1,5},{2,6},{3,7},{4,0},{5,1},{6,2},{7,3},{8,12},{9,13},{10,... | collective-permute-start | bytes 884744 | tf_op jit(solution)/shard_map/ppermute | solution.py:296
  8.8 49.4 %collective-permute-start.1 = (bf16[128,3072]{1,0:T(8,128)(2,1)S(1)}, bf16[128,3072]{1,0:T(8,128)(2,1)S(1)}, u32[]{:S(2)}, u32[]{:S(2)}) collective-permute-start(bf16[128,3072]{1,0:T(8,128)(2,1)S(1)} %copy-done.44), channel_id=1, source_target_pairs={{0,4},{1,5},{2,6},{3,7},{4,0},{5,1},{6,2},{7,3},{8,12},{9,13},{10,... | collective-permute-start | bytes 2359304 | tf_op jit(solution)/shard_map/ppermute | solution.py:281
  14.8 27.7 %collective-permute-start.5 = (bf16[48,3072]{1,0:T(8,128)(2,1)S(1)}, bf16[48,3072]{1,0:T(8,128)(2,1)S(1)}, u32[]{:S(2)}, u32[]{:S(2)}) collective-permute-start(bf16[48,3072]{1,0:T(8,128)(2,1)S(1)} %get-tuple-element.89), channel_id=1, source_target_pairs={{0,3},{1,0},{2,1},{3,2},{4,7},{5,4},{6,5},{7,6},{8,11},{9,8},{10,9... | collective-permute-start | bytes 884744 | tf_op jit(solution)/shard_map/ppermute | solution.py:255
  17.3 27.3 %collective-permute-start.4 = (bf16[48,3072]{1,0:T(8,128)(2,1)S(1)}, bf16[48,3072]{1,0:T(8,128)(2,1)S(1)}, u32[]{:S(2)}, u32[]{:S(2)}) collective-permute-start(bf16[48,3072]{1,0:T(8,128)(2,1)S(1)} %get-tuple-element.90), channel_id=1, source_target_pairs={{0,2},{1,3},{2,0},{3,1},{4,6},{5,7},{6,4},{7,5},{8,10},{9,11},{10,... | collective-permute-start | bytes 884744 | tf_op jit(solution)/shard_map/ppermute | solution.py:255
  17.8 27.6 %collective-permute-start.3 = (bf16[48,3072]{1,0:T(8,128)(2,1)S(1)}, bf16[48,3072]{1,0:T(8,128)(2,1)S(1)}, u32[]{:S(2)}, u32[]{:S(2)}) collective-permute-start(bf16[48,3072]{1,0:T(8,128)(2,1)S(1)} %get-tuple-element.91), channel_id=1, source_target_pairs={{0,1},{1,2},{2,3},{3,0},{4,5},{5,6},{6,7},{7,4},{8,9},{9,10},{10,1... | collective-permute-start | bytes 884744 | tf_op jit(solution)/shard_map/ppermute | solution.py:255
  42.5 15.7 %copy-start.46 = (bf16[4,48,768]{2,1,0:T(8,128)(2,1)}, bf16[4,48,768]{2,1,0:T(8,128)(2,1)S(1)}, u32[]{:S(2)}) copy-start(bf16[4,48,768]{2,1,0:T(8,128)(2,1)S(1)} %collective-permute-done.2) | copy-start | bytes 884740
  58.2 65.2 %all-to-all-start = ((bf16[8,2,96,768]{3,2,1,0:T(8,128)(2,1)}), bf16[8,2,96,768]{3,2,1,0:T(8,128)(2,1)S(1)}, u32[]{:S(2)}, u32[]{:S(2)}) async-start(bf16[8,2,96,768]{3,2,1,0:T(8,128)(2,1)} %bitcast.34), calls=%async_computation | async-start | bytes 4718592 | tf_op jit(solution)/shard_map/all_to_all | solution.py:266
  63.8 37.1 %collective-permute-start.9 = (bf16[96,768]{1,0:T(8,128)(2,1)S(1)}, bf16[96,768]{1,0:T(8,128)(2,1)S(1)}, u32[]{:S(2)}, u32[]{:S(2)}) collective-permute-start(bf16[96,768]{1,0:T(8,128)(2,1)S(1)} %get-tuple-element.97), channel_id=1, source_target_pairs={{0,1},{1,2},{2,3},{3,0},{4,5},{5,6},{6,7},{7,4},{8,9},{9,10},{10,1... | collective-permute-start | bytes 442376 | tf_op jit(solution)/shard_map/ppermute | solution.py:255
  66.2 43.3 %copy-start.43 = (bf16[2,8,96,768]{3,2,1,0:T(8,128)(2,1)S(1)}, bf16[2,8,96,768]{3,2,1,0:T(8,128)(2,1)}, u32[]{:S(2)}) copy-start(bf16[2,8,96,768]{3,2,1,0:T(8,128)(2,1)} %param.12) | copy-start | bytes 7077892
  67.0 54.2 %collective-permute-start.8 = (bf16[48,3072]{1,0:T(8,128)(2,1)S(1)}, bf16[48,3072]{1,0:T(8,128)(2,1)S(1)}, u32[]{:S(2)}, u32[]{:S(2)}) collective-permute-start(bf16[48,3072]{1,0:T(8,128)(2,1)S(1)} %get-tuple-element.92), channel_id=1, source_target_pairs={{0,3},{1,0},{2,1},{3,2},{4,7},{5,4},{6,5},{7,6},{8,11},{9,8},{10,9... | collective-permute-start | bytes 884744 | tf_op jit(solution)/shard_map/ppermute | solution.py:255
  68.0 53.9 %collective-permute-start.7 = (bf16[48,3072]{1,0:T(8,128)(2,1)S(1)}, bf16[48,3072]{1,0:T(8,128)(2,1)S(1)}, u32[]{:S(2)}, u32[]{:S(2)}) collective-permute-start(bf16[48,3072]{1,0:T(8,128)(2,1)S(1)} %get-tuple-element.93), channel_id=1, source_target_pairs={{0,2},{1,3},{2,0},{3,1},{4,6},{5,7},{6,4},{7,5},{8,10},{9,11},{10,... | collective-permute-start | bytes 884744 | tf_op jit(solution)/shard_map/ppermute | solution.py:255
  69.9 52.7 %collective-permute-start.6 = (bf16[48,3072]{1,0:T(8,128)(2,1)S(1)}, bf16[48,3072]{1,0:T(8,128)(2,1)S(1)}, u32[]{:S(2)}, u32[]{:S(2)}) collective-permute-start(bf16[48,3072]{1,0:T(8,128)(2,1)S(1)} %get-tuple-element.94), channel_id=1, source_target_pairs={{0,1},{1,2},{2,3},{3,0},{4,5},{5,6},{6,7},{7,4},{8,9},{9,10},{10,1... | collective-permute-start | bytes 884744 | tf_op jit(solution)/shard_map/ppermute | solution.py:255
  70.5 47.4 %collective-permute-start.11 = (bf16[96,768]{1,0:T(8,128)(2,1)S(1)}, bf16[96,768]{1,0:T(8,128)(2,1)S(1)}, u32[]{:S(2)}, u32[]{:S(2)}) collective-permute-start(bf16[96,768]{1,0:T(8,128)(2,1)S(1)} %get-tuple-element.98), channel_id=1, source_target_pairs={{0,3},{1,0},{2,1},{3,2},{4,7},{5,4},{6,5},{7,6},{8,11},{9,8},{10,9... | collective-permute-start | bytes 442376 | tf_op jit(solution)/shard_map/ppermute | solution.py:255
  100.9 10.1 %copy-start.47 = (bf16[96,768]{1,0:T(8,128)(2,1)}, bf16[96,768]{1,0:T(8,128)(2,1)S(1)}, u32[]{:S(2)}) copy-start(bf16[96,768]{1,0:T(8,128)(2,1)S(1)} %collective-permute-done.9) | copy-start | bytes 442372
  100.9 20.2 %collective-permute-start.10 = (bf16[96,768]{1,0:T(8,128)(2,1)S(1)}, bf16[96,768]{1,0:T(8,128)(2,1)S(1)}, u32[]{:S(2)}, u32[]{:S(2)}) collective-permute-start(bf16[96,768]{1,0:T(8,128)(2,1)S(1)} %get-tuple-element.99), channel_id=1, source_target_pairs={{0,2},{1,3},{2,0},{3,1},{4,6},{5,7},{6,4},{7,5},{8,10},{9,11},{10,... | collective-permute-start | bytes 442376 | tf_op jit(solution)/shard_map/ppermute | solution.py:255
  124.8 57.5 %all-to-all-start.1 = ((bf16[8,2,96,768]{3,2,1,0:T(8,128)(2,1)}), bf16[8,2,96,768]{3,2,1,0:T(8,128)(2,1)}, u32[]{:S(2)}, u32[]{:S(2)}) async-start(bf16[8,2,96,768]{3,2,1,0:T(8,128)(2,1)} %bitcast.33), calls=%async_computation.1 | async-start | bytes 4718592 | tf_op jit(solution)/shard_map/all_to_all | solution.py:266
  131.2 31.5 %copy-start = (bf16[8,1,96,768]{3,2,1,0:T(8,128)(2,1)}, bf16[8,1,96,768]{3,2,1,0:T(8,128)(2,1)S(1)}, u32[]{:S(2)}) copy-start(bf16[8,1,96,768]{3,2,1,0:T(8,128)(2,1)S(1)} %get-tuple-element.87) | copy-start | bytes 3538948
  131.2 26.5 %collective-permute-start.13 = (bf16[768,768]{1,0:T(8,128)(2,1)S(1)}, bf16[768,768]{1,0:T(8,128)(2,1)S(1)}, u32[]{:S(2)}, u32[]{:S(2)}) collective-permute-start(bf16[768,768]{1,0:T(8,128)(2,1)S(1)} %bitcast.40), channel_id=1, source_target_pairs={{0,16},{8,24},{16,0},{24,8},{1,17},{9,25},{17,1},{25,9},{2,18},{10... | collective-permute-start | bytes 3538952 | tf_op jit(solution)/shard_map/ppermute | solution.py:258
  132.8 30.1 %collective-permute-start.12 = (bf16[768,768]{1,0:T(8,128)(2,1)S(1)}, bf16[768,768]{1,0:T(8,128)(2,1)}, u32[]{:S(2)}, u32[]{:S(2)}) collective-permute-start(bf16[768,768]{1,0:T(8,128)(2,1)S(1)} %bitcast.41), channel_id=1, source_target_pairs={{0,8},{8,0},{16,24},{24,16},{1,9},{9,1},{17,25},{25,17},{2,10},{10... | collective-permute-start | bytes 3538952 | tf_op jit(solution)/shard_map/ppermute | solution.py:258
  157.7 5.1 %collective-permute-start.14 = (bf16[768,768]{1,0:T(8,128)(2,1)S(1)}, bf16[768,768]{1,0:T(8,128)(2,1)}, u32[]{:S(2)}, u32[]{:S(2)}) collective-permute-start(bf16[768,768]{1,0:T(8,128)(2,1)S(1)} %collective-permute-done.13.refs_11_.refs_2_), channel_id=1, source_target_pairs={{0,8},{8,0},{16,24},{24,16},{1,9},{9,1},{17,25},{25,17},{2,10},{10... | collective-permute-start | bytes 3538952 | tf_op jit(solution)/shard_map/ppermute | solution.py:258
  157.7 29.6 %collective-permute-start.17 = (bf16[768,768]{1,0:T(8,128)(2,1)S(1)}, bf16[768,768]{1,0:T(8,128)(2,1)}, u32[]{:S(2)}, u32[]{:S(2)}) collective-permute-start(bf16[768,768]{1,0:T(8,128)(2,1)S(1)} %bitcast.35), channel_id=1, source_target_pairs={{0,16},{8,24},{16,0},{24,8},{1,17},{9,25},{17,1},{25,9},{2,18},{10... | collective-permute-start | bytes 3538952 | tf_op jit(solution)/shard_map/ppermute | solution.py:258
  182.3 67.4 %all-to-all-start.2 = ((bf16[8,2,96,768]{3,2,1,0:T(8,128)(2,1)}), bf16[8,2,96,768]{3,2,1,0:T(8,128)(2,1)}, u32[]{:S(2)}, u32[]{:S(2)}) async-start(bf16[8,2,96,768]{3,2,1,0:T(8,128)(2,1)} %bitcast.46), calls=%async_computation.2 | async-start | bytes 4718592 | tf_op jit(solution)/shard_map/all_to_all | solution.py:266
  186.7 4.0 %collective-permute-start.15 = (bf16[768,768]{1,0:T(8,128)(2,1)}, bf16[768,768]{1,0:T(8,128)(2,1)S(1)}, u32[]{:S(2)}, u32[]{:S(2)}) collective-permute-start(bf16[768,768]{1,0:T(8,128)(2,1)} %copy-done.38), channel_id=1, source_target_pairs={{0,8},{8,0},{16,24},{24,16},{1,9},{9,1},{17,25},{25,17},{2,10},{10... | collective-permute-start | bytes 3538952 | tf_op jit(solution)/shard_map/ppermute | solution.py:258
  186.8 5.8 %collective-permute-start.16 = (bf16[768,768]{1,0:T(8,128)(2,1)S(1)}, bf16[768,768]{1,0:T(8,128)(2,1)S(1)}, u32[]{:S(2)}, u32[]{:S(2)}) collective-permute-start(bf16[768,768]{1,0:T(8,128)(2,1)S(1)} %bitcast.36), channel_id=1, source_target_pairs={{0,8},{8,0},{16,24},{24,16},{1,9},{9,1},{17,25},{25,17},{2,10},{10... | collective-permute-start | bytes 3538952 | tf_op jit(solution)/shard_map/ppermute | solution.py:258
  187.3 5.9 %collective-permute-start.18 = (bf16[768,768]{1,0:T(8,128)(2,1)}, bf16[768,768]{1,0:T(8,128)(2,1)S(1)}, u32[]{:S(2)}, u32[]{:S(2)}) collective-permute-start(bf16[768,768]{1,0:T(8,128)(2,1)} %collective-permute-done.17.refs_2_.refs_6_), channel_id=1, source_target_pairs={{0,8},{8,0},{16,24},{24,16},{1,9},{9,1},{17,25},{25,17},{2,10},{10... | collective-permute-start | bytes 3538952 | tf_op jit(solution)/shard_map/ppermute | solution.py:258
  187.4 20.8 %collective-permute-start.26 = (bf16[768,768]{1,0:T(8,128)(2,1)}, bf16[768,768]{1,0:T(8,128)(2,1)S(1)}, u32[]{:S(2)}, u32[]{:S(2)}) collective-permute-start(bf16[768,768]{1,0:T(8,128)(2,1)} %copy-done.37), channel_id=1, source_target_pairs={{0,8},{8,0},{16,24},{24,16},{1,9},{9,1},{17,25},{25,17},{2,10},{10... | collective-permute-start | bytes 3538952 | tf_op jit(solution)/shard_map/ppermute | solution.py:258
  190.7 7.5 %copy-start.2 = (bf16[8,1,96,768]{3,2,1,0:T(8,128)(2,1)S(1)}, bf16[8,1,96,768]{3,2,1,0:T(8,128)(2,1)}, u32[]{:S(2)}) copy-start(bf16[8,1,96,768]{3,2,1,0:T(8,128)(2,1)} %copy-done) | copy-start | bytes 3538948
  190.7 7.5 %copy-start.6 = (bf16[768,768]{1,0:T(8,128)(2,1)S(1)}, bf16[768,768]{1,0:T(8,128)(2,1)}, u32[]{:S(2)}) copy-start(bf16[768,768]{1,0:T(8,128)(2,1)} %copy-done.4) | copy-start | bytes 3538948
  190.7 7.5 %copy-start.8 = (bf16[384,768]{1,0:T(8,128)(2,1)S(1)}, bf16[384,768]{1,0:T(8,128)(2,1)}, u32[]{:S(2)}) copy-start(bf16[384,768]{1,0:T(8,128)(2,1)} %copy-done.7) | copy-start | bytes 1769476
  208.0 6.4 %collective-permute-start.24 = (bf16[768,768]{1,0:T(8,128)(2,1)S(1)}, bf16[768,768]{1,0:T(8,128)(2,1)S(1)}, u32[]{:S(2)}, u32[]{:S(2)}) collective-permute-start(bf16[768,768]{1,0:T(8,128)(2,1)S(1)} %get-tuple-element.68), channel_id=1, source_target_pairs={{0,8},{8,0},{16,24},{24,16},{1,9},{9,1},{17,25},{25,17},{2,10},{10... | collective-permute-start | bytes 3538952 | tf_op jit(solution)/shard_map/ppermute | solution.py:258
  209.0 34.7 %collective-permute-start.27 = (bf16[768,768]{1,0:T(8,128)(2,1)S(1)}, bf16[768,768]{1,0:T(8,128)(2,1)S(1)}, u32[]{:S(2)}, u32[]{:S(2)}) collective-permute-start(bf16[768,768]{1,0:T(8,128)(2,1)S(1)} %add_convert_fusion), channel_id=1, source_target_pairs={{0,16},{8,24},{16,0},{24,8},{1,17},{9,25},{17,1},{25,9},{2,18},{10... | collective-permute-start | bytes 3538952 | tf_op jit(solution)/shard_map/ppermute | solution.py:258
  210.5 22.6 %collective-permute-start.19 = (bf16[48,3072]{1,0:T(8,128)(2,1)S(1)}, bf16[48,3072]{1,0:T(8,128)(2,1)S(1)}, u32[]{:S(2)}, u32[]{:S(2)}) collective-permute-start(bf16[48,3072]{1,0:T(8,128)(2,1)S(1)} %get-tuple-element.55), channel_id=1, source_target_pairs={{0,3},{1,0},{2,1},{3,2},{4,7},{5,4},{6,5},{7,6},{8,11},{9,8},{10,9... | collective-permute-start | bytes 884744 | tf_op jit(solution)/shard_map/ppermute | solution.py:255
  213.3 24.5 %collective-permute-start.20 = (bf16[48,3072]{1,0:T(8,128)(2,1)S(1)}, bf16[48,3072]{1,0:T(8,128)(2,1)S(1)}, u32[]{:S(2)}, u32[]{:S(2)}) collective-permute-start(bf16[48,3072]{1,0:T(8,128)(2,1)S(1)} %get-tuple-element.56), channel_id=1, source_target_pairs={{0,2},{1,3},{2,0},{3,1},{4,6},{5,7},{6,4},{7,5},{8,10},{9,11},{10,... | collective-permute-start | bytes 884744 | tf_op jit(solution)/shard_map/ppermute | solution.py:255
  213.8 24.0 %collective-permute-start.21 = (bf16[48,3072]{1,0:T(8,128)(2,1)S(1)}, bf16[48,3072]{1,0:T(8,128)(2,1)S(1)}, u32[]{:S(2)}, u32[]{:S(2)}) collective-permute-start(bf16[48,3072]{1,0:T(8,128)(2,1)S(1)} %get-tuple-element.57), channel_id=1, source_target_pairs={{0,1},{1,2},{2,3},{3,0},{4,5},{5,6},{6,7},{7,4},{8,9},{9,10},{10,1... | collective-permute-start | bytes 884744 | tf_op jit(solution)/shard_map/ppermute | solution.py:255
  214.4 31.4 %collective-permute-start.23 = (bf16[768,768]{1,0:T(8,128)(2,1)S(1)}, bf16[768,768]{1,0:T(8,128)(2,1)S(1)}, u32[]{:S(2)}, u32[]{:S(2)}) collective-permute-start(bf16[768,768]{1,0:T(8,128)(2,1)S(1)} %get-tuple-element.66), channel_id=1, source_target_pairs={{0,8},{8,0},{16,24},{24,16},{1,9},{9,1},{17,25},{25,17},{2,10},{10... | collective-permute-start | bytes 3538952 | tf_op jit(solution)/shard_map/ppermute | solution.py:258
  214.4 23.4 %copy-start.56 = (pred[192,128]{1,0:T(8,128)(4,1)S(1)}, pred[192,128]{1,0:T(8,128)(4,1)}, u32[]{:S(2)}) copy-start(pred[192,128]{1,0:T(8,128)(4,1)} %get-tuple-element.85) | copy-start | bytes 73732
  215.7 34.0 %copy-start.10 = (bf16[768,768]{1,0:T(8,128)(2,1)S(1)}, bf16[768,768]{1,0:T(8,128)(2,1)}, u32[]{:S(2)}) copy-start(bf16[768,768]{1,0:T(8,128)(2,1)} %copy-done.9) | copy-start | bytes 3538948
  233.1 29.3 %collective-permute-start.25 = (bf16[768,768]{1,0:T(8,128)(2,1)}, bf16[768,768]{1,0:T(8,128)(2,1)}, u32[]{:S(2)}, u32[]{:S(2)}) collective-permute-start(bf16[768,768]{1,0:T(8,128)(2,1)} %add_convert_fusion.1), channel_id=1, source_target_pairs={{0,16},{8,24},{16,0},{24,8},{1,17},{9,25},{17,1},{25,9},{2,18},{10... | collective-permute-start | bytes 3538952 | tf_op jit(solution)/shard_map/ppermute | solution.py:258
  239.1 23.4 %copy-start.3 = (bf16[8,1,96,768]{3,2,1,0:T(8,128)(2,1)S(1)}, bf16[8,1,96,768]{3,2,1,0:T(8,128)(2,1)}, u32[]{:S(2)}) copy-start(bf16[8,1,96,768]{3,2,1,0:T(8,128)(2,1)} %copy-done) | copy-start | bytes 3538948
  239.1 37.8 %collective-permute-start.30 = (bf16[128,3072]{1,0:T(8,128)(2,1)}, bf16[128,3072]{1,0:T(8,128)(2,1)}, u32[]{:S(2)}, u32[]{:S(2)}) collective-permute-start(bf16[128,3072]{1,0:T(8,128)(2,1)} %convolution_convert_fusion.2), channel_id=1, source_target_pairs={{0,4},{1,5},{2,6},{3,7},{4,0},{5,1},{6,2},{7,3},{8,12},{9,13},{10,... | collective-permute-start | bytes 2359304 | tf_op jit(solution)/shard_map/ppermute | solution.py:352
  243.8 26.0 %collective-permute-start.29 = (bf16[48,3072]{1,0:T(8,128)(2,1)}, bf16[48,3072]{1,0:T(8,128)(2,1)}, u32[]{:S(2)}, u32[]{:S(2)}) collective-permute-start(bf16[48,3072]{1,0:T(8,128)(2,1)} %get-tuple-element.82), channel_id=1, source_target_pairs={{0,1},{1,2},{2,3},{3,0},{4,5},{5,6},{6,7},{7,4},{8,9},{9,10},{10,1... | collective-permute-start | bytes 884744 | tf_op jit(solution)/shard_map/ppermute | solution.py:255
  244.8 24.9 %collective-permute-start.28 = (bf16[48,3072]{1,0:T(8,128)(2,1)}, bf16[48,3072]{1,0:T(8,128)(2,1)}, u32[]{:S(2)}, u32[]{:S(2)}) collective-permute-start(bf16[48,3072]{1,0:T(8,128)(2,1)} %get-tuple-element.80), channel_id=1, source_target_pairs={{0,2},{1,3},{2,0},{3,1},{4,6},{5,7},{6,4},{7,5},{8,10},{9,11},{10,... | collective-permute-start | bytes 884744 | tf_op jit(solution)/shard_map/ppermute | solution.py:255
  246.8 25.1 %collective-permute-start.22 = (bf16[48,3072]{1,0:T(8,128)(2,1)}, bf16[48,3072]{1,0:T(8,128)(2,1)}, u32[]{:S(2)}, u32[]{:S(2)}) collective-permute-start(bf16[48,3072]{1,0:T(8,128)(2,1)} %get-tuple-element.60), channel_id=1, source_target_pairs={{0,3},{1,0},{2,1},{3,2},{4,7},{5,4},{6,5},{7,6},{8,11},{9,8},{10,9... | collective-permute-start | bytes 884744 | tf_op jit(solution)/shard_map/ppermute | solution.py:255
  252.3 10.1 %copy-start.14 = (bf16[768,768]{1,0:T(8,128)(2,1)S(1)}, bf16[768,768]{1,0:T(8,128)(2,1)}, u32[]{:S(2)}) copy-start(bf16[768,768]{1,0:T(8,128)(2,1)} %copy-done.13) | copy-start | bytes 3538948
  252.3 10.1 %copy-start.18 = (bf16[768,768]{1,0:T(8,128)(2,1)S(1)}, bf16[768,768]{1,0:T(8,128)(2,1)}, u32[]{:S(2)}) copy-start(bf16[768,768]{1,0:T(8,128)(2,1)} %copy-done.17) | copy-start | bytes 3538948
  262.4 14.4 %copy-start.40 = (bf16[48,3072]{1,0:T(8,128)(2,1)S(1)}, bf16[48,3072]{1,0:T(8,128)(2,1)}, u32[]{:S(2)}) copy-start(bf16[48,3072]{1,0:T(8,128)(2,1)} %copy-done.39) | copy-start | bytes 884740
  262.5 14.4 %copy-start.54 = (pred[192,128]{1,0:T(8,128)(4,1)S(1)}, pred[192,128]{1,0:T(8,128)(4,1)}, u32[]{:S(2)}) copy-start(pred[192,128]{1,0:T(8,128)(4,1)} %copy-done.53) | copy-start | bytes 73732
  (44 other events, 104.7 us)

commit v8 on v2

--- a/solution.py
+++ b/solution.py
@@ -72,7 +72,7 @@
         def _():
             first = 0
             for block in block_refs:
-                rows[first : first + block.shape[0], :] = block[...]
+                rows[first : first + block.shape[0], :] = block[:, :width]
                 first += block.shape[0]
 
         pre_gate = project(place, rows, gate_refs)
@@ -300,20 +300,18 @@
         hit = by_token[None, :, :] == near_ids.reshape(-1)[:, None, None]
         return jnp.any(hit, axis=2).astype(bf16)
 
-    def send_rows(picker, rows):
+    def send_rows(picker, rows, grads):
         picked = jnp.dot(picker, rows, preferred_element_type=f32).astype(bf16)
         picked = picked.reshape(half, capacity, model_width)
+        picked = jnp.concatenate([picked, grads], axis=2)
         return [shift(picked[s], s) for s in range(half)]
 
     near_pick = pick_matrix(target)
-    near_rows = send_rows(near_pick, tokens)
+    near_rows = send_rows(near_pick, tokens, pick_grads(near_ids))
     other_tokens = after(other_tokens, other_routes, far_grads, *near_rows[1:])
     other_pick = pick_matrix(slot_targets(other_routes.reshape(-1), capacity))
-    far_rows = send_rows(other_pick, other_tokens)
-    grads_out = jnp.concatenate([far_grads, pick_grads(near_ids)], axis=1)
-    grads_in = [shift(grads_out[s], s) for s in range(half)]
-
-    owned = after(to_owners(weights, other_tokens), *far_rows[1:], *grads_in[1:])
+    far_rows = send_rows(other_pick, other_tokens, far_grads)
+    owned = after(to_owners(weights, other_tokens), *far_rows[1:])
     owned_gate = owned[:, 0].reshape(hidden_units, -1)
     owned_up = owned[:, 1].reshape(hidden_units, -1)
     owned_first = to_owners(first_moment, owned)
@@ -322,10 +320,8 @@
     up_x = along_x(after(owned_up, *gate_x))
     gate = both_cores([owned_gate] + gate_x)
     up = both_cores([owned_up] + up_x)
-    upstream = jnp.swapaxes(jnp.stack(grads_in).reshape(half, 2, capacity, hidden_units), 0, 1)
-    upstream = upstream.reshape(2 * half * capacity, hidden_units)
-
     blocks = far_rows + near_rows
+    upstream = jnp.concatenate([block[:, model_width:] for block in blocks], axis=0)
     joined = capacity % 16 != 0
     if joined:
         blocks = [jnp.concatenate(blocks, axis=0)]

time: 279 us -> 273 us (0.978)
  waiting for transfers between devices: 143 us -> 131 us
  starting transfers between devices: 57.2 us -> 60.4 us
    ppermute x1, starting transfers between devices: 0.08 us -> 14.1 us  [per_device(): far_grads = lax.ppermute(pick_grads(far_ids), 'expert', swap)]
    ppermute x1, waiting for transfers between devices: 12.1 us -> 0.01 us  [per_device(): other_tokens = lax.ppermute(tokens, 'expert', swap)]
    ppermute x15 -> x12, starting transfers between devices: 27 us -> 15.5 us  [shift(): return lax.ppermute(value, 'expert', pairs)]
    ppermute x15 -> x12, waiting for transfers between devices: 39.5 us -> 48.5 us  [shift(): return lax.ppermute(value, 'expert', pairs)]
    ppermute x12, waiting for transfers between devices: 60.2 us -> 55.2 us  [across(): return lax.ppermute(value, 'dp', [(i, i ^ k) for i in range(pieces)])]
    all_to_all x3, starting transfers between devices: 12.6 us -> 16.1 us  [to_owners(): lax.all_to_all(by_owner, 'expert', split_axis=0, concat_axis=0, tiled=True)]
    all_to_all x3, waiting for transfers between devices: 4.21 us -> 1.22 us  [to_owners(): lax.all_to_all(by_owner, 'expert', split_axis=0, concat_axis=0, tiled=True)]
    ppermute x1, starting transfers between devices: 2.9 us -> 0.08 us  [per_device(): other_tokens = lax.ppermute(tokens, 'expert', swap)]
  transfers between devices with their start and end apart: 34 -> 31, of which waited for: 13 -> 12; matrix products, arithmetic and copies ran while one was open for 8% -> 9% of each run, Pallas kernels for 13% -> 13%
where the time goes in v8:
time: 273 us; the launch traced here: 272 us
  waiting for transfers between devices  131 us (48%)
  starting transfers between devices  60.4 us (22%)
  Pallas kernels  35.1 us (13%)
  local copies, waits for them, and re-layouts  33 us (12%)
  other arithmetic  6.77 us (2%)
  matrix products  4.07 us (1%)
    ppermute x12, waiting for transfers between devices, across(): return lax.ppermute(value, 'dp', [(i, i ^ k) for i in range(pieces)])  55.2 us
    ppermute x12, waiting for transfers between devices, shift(): return lax.ppermute(value, 'expert', pairs)  48.5 us
    unnamed x95, local copies, waits for them, and re-layouts  29.1 us
    ppermute x1, waiting for transfers between devices, per_device(): far_grads = lax.ppermute(pick_grads(far_ids), 'expert', swap)  21.6 us
    pallas_call x5, Pallas kernels, run(): pl.pallas_call(body, grid_spec=pltpu.PrefetchScalarGridSpec(num_scalar_pr...  20.7 us
    all_to_all x3, starting transfers between devices, to_owners(): lax.all_to_all(by_owner, 'expert', split_axis=0, concat_axis=0, tiled=True)  16.1 us
    ppermute x12, starting transfers between devices, shift(): return lax.ppermute(value, 'expert', pairs)  15.5 us
    pallas_call x2, Pallas kernels, adam(): pl.pallas_call(body, grid=(sources,), in_specs=[flat] * (count + 1) + [mo...  14.5 us
  transfers between devices with their start and end apart: 31, of which 12 were waited for; matrix products, arithmetic and copies ran while one was open for 9% of the time, Pallas kernels for 13%

profile of v8, /device:TPU:0, one launch (start us, length us, event | category | flops | bytes accessed | tf_op | source)
XLA Modules:
  0.0 271.8 jit_solution(8484862879101398285)
XLA Ops:
  0.6 4.1 %collective-permute-start = (s32[128,2]{0,1:T(2,128)}, s32[128,2]{0,1:T(2,128)S(1)}, u32[]{:S(2)}, u32[]{:S(2)}) collective-permute-start(s32[128,2]{0,1:T(2,128)} %param.8), channel_id=1, source_target_pairs={{0,4},{1,5},{2,6},{3,7},{4,0},{5,1},{6,2},{7,3},{8,12},{9,13},{10,... | collective-permute-start | bytes 3080 | tf_op jit(solution)/shard_map/ppermute | solution.py:282
  7.8 1.4 multiply_convert_fusion
  12.1 1.8 collective-permute-start.3
  13.8 1.6 collective-permute-start.4
  15.4 1.4 collective-permute-start.5
  17.1 14.1 %collective-permute-start.2 = (bf16[4,48,768]{2,1,0:T(8,128)(2,1)S(1)}, bf16[4,48,768]{2,1,0:T(8,128)(2,1)S(1)}, u32[]{:S(2)}, u32[]{:S(2)}) collective-permute-start(bf16[4,48,768]{2,1,0:T(8,128)(2,1)S(1)} %bitcast.54), channel_id=1, source_target_pairs={{0,4},{1,5},{2,6},{3,7},{4,0},{5,1},{6,2},{7,3},{8,12},{9,13},{10,... | collective-permute-start | bytes 884744 | tf_op jit(solution)/shard_map/ppermute | solution.py:296
  31.2 1.6 copy.57
  32.8 21.6 %collective-permute-done.2 = bf16[4,48,768]{2,1,0:T(8,128)(2,1)S(1)} collective-permute-done((bf16[4,48,768]{2,1,0:T(8,128)(2,1)S(1)}, bf16[4,48,768]{2,1,0:T(8,128)(2,1)S(1)}, u32[]{:S(2)}, u32[]{:S(2)}) %collective-permute-start.2) | collective-permute-done | bytes 294944 | tf_op jit(solution)/shard_map/ppermute | solution.py:296
  54.4 5.8 %all-to-all-start = ((bf16[8,2,96,768]{3,2,1,0:T(8,128)(2,1)}), bf16[8,2,96,768]{3,2,1,0:T(8,128)(2,1)S(1)}, u32[]{:S(2)}, u32[]{:S(2)}) async-start(bf16[8,2,96,768]{3,2,1,0:T(8,128)(2,1)} %bitcast.39), calls=%async_computation | async-start | bytes 4718592 | tf_op jit(solution)/shard_map/all_to_all | solution.py:266
  61.5 2.9 %collective-permute-start.8 = (bf16[48,3840]{1,0:T(8,128)(2,1)S(1)}, bf16[48,3840]{1,0:T(8,128)(2,1)}, u32[]{:S(2)}, u32[]{:S(2)}) collective-permute-start(bf16[48,3840]{1,0:T(8,128)(2,1)S(1)} %get-tuple-element.96), channel_id=1, source_target_pairs={{0,3},{1,0},{2,1},{3,2},{4,7},{5,4},{6,5},{7,6},{8,11},{9,8},{10,9... | collective-permute-start | bytes 1105928 | tf_op jit(solution)/shard_map/ppermute | solution.py:255
  64.4 1.1 collective-permute-start.7
  65.6 1.6 copy.56
  67.1 40.2 %collective-permute-done.8.refs_3_ = bf16[48,3840]{1,0:T(8,128)(2,1)} collective-permute-done((bf16[48,3840]{1,0:T(8,128)(2,1)S(1)}, bf16[48,3840]{1,0:T(8,128)(2,1)}, u32[]{:S(2)}, u32[]{:S(2)}) %collective-permute-start.8) | collective-permute-done | bytes 368672 | tf_op jit(solution)/shard_map/ppermute | solution.py:255
  107.4 7.1 %collective-permute-done.7.refs_2_ = bf16[48,3840]{1,0:T(8,128)(2,1)} collective-permute-done((bf16[48,3840]{1,0:T(8,128)(2,1)S(1)}, bf16[48,3840]{1,0:T(8,128)(2,1)}, u32[]{:S(2)}, u32[]{:S(2)}) %collective-permute-start.7) | collective-permute-done | bytes 368672 | tf_op jit(solution)/shard_map/ppermute | solution.py:255
  114.5 1.4 copy-done.34
  115.9 5.2 %all-to-all-start.1 = ((bf16[8,2,96,768]{3,2,1,0:T(8,128)(2,1)}), bf16[8,2,96,768]{3,2,1,0:T(8,128)(2,1)}, u32[]{:S(2)}, u32[]{:S(2)}) async-start(bf16[8,2,96,768]{3,2,1,0:T(8,128)(2,1)} %bitcast.38), calls=%async_computation.1 | async-start | bytes 4718592 | tf_op jit(solution)/shard_map/all_to_all | solution.py:266
  121.1 1.8 fusion.42
  122.9 1.6 collective-permute-start.10
  124.4 3.3 %copy.55 = bf16[2,8,96,768]{3,2,0,1:T(8,128)(2,1)} copy(bf16[2,8,96,768]{3,2,1,0:T(8,128)(2,1)} %param.13) | data formatting | bytes 4718592 | tf_op args[6]
  128.6 20.1 %collective-permute-done.10.refs_11_.refs_2_ = bf16[768,768]{1,0:T(8,128)(2,1)S(1)} collective-permute-done((bf16[768,768]{1,0:T(8,128)(2,1)S(1)}, bf16[768,768]{1,0:T(8,128)(2,1)S(1)}, u32[]{:S(2)}, u32[]{:S(2)}) %collective-permute-start.10) | collective-permute-done | bytes 1179680 | tf_op jit(solution)/shard_map/ppermute | solution.py:258
  153.3 1.5 collective-permute-start.13
  155.7 2.1 copy-done.1
  157.8 1.3 copy-done.5
  159.1 4.6 %shard_map.102 = (bf16[384,3072]{1,0:T(8,128)(2,1)S(1)}, bf16[384,768]{1,0:T(8,128)(2,1)S(1)}, f32[384,768]{1,0:T(8,128)S(1)}) custom-call(s32[1]{0:T(128)} %bitcast.place, bf16[48,3840]{1,0:T(8,128)(2,1)S(1)} %copy-done.14, bf16[48,3840]{1,0:T(8,128)(2,1)} %collective-permute-done.6.refs_1_, bf16[48,3840]{1,0:T(8,128)(2,1)} %collective-permute-done.7.refs_2_, ...), custom_call_target="tpu_custom_call" | custom-call | tf_op jit(solution)/shard_map/pallas_call | solution.py:32
  164.7 3.1 %shard_map.106 = (bf16[768,768]{1,0:T(8,128)(2,1)S(1)}, bf16[768,768]{1,0:T(8,128)(2,1)S(1)}, bf16[768,768]{1,0:T(8,128)(2,1)S(1)}, bf16[768,768]{1,0:T(8,128)(2,1)S(1)}) custom-call(s32[1]{0:T(128)} %bitcast.place, bf16[384,768]{1,0:T(8,128)(2,1)S(1)} %get-tuple-element.54.grad_up.grads, bf16[384,3072]{1,0:T(8,128)(2,1)S(1)} %get-tuple-element.49.rows), custom_call_target="tpu_custom_call" | custom-call | tf_op jit(solution)/shard_map/pallas_call | solution.py:32
  173.4 5.2 %all-to-all-start.2 = ((bf16[8,2,96,768]{3,2,1,0:T(8,128)(2,1)}), bf16[8,2,96,768]{3,2,1,0:T(8,128)(2,1)}, u32[]{:S(2)}, u32[]{:S(2)}) async-start(bf16[8,2,96,768]{3,2,1,0:T(8,128)(2,1)} %bitcast.50), calls=%async_computation.2 | async-start | bytes 4718592 | tf_op jit(solution)/shard_map/all_to_all | solution.py:266
  178.5 3.2 %collective-permute-done.13.refs_2_.refs_6_ = bf16[768,768]{1,0:T(8,128)(2,1)} collective-permute-done((bf16[768,768]{1,0:T(8,128)(2,1)S(1)}, bf16[768,768]{1,0:T(8,128)(2,1)}, u32[]{:S(2)}, u32[]{:S(2)}) %collective-permute-start.13) | collective-permute-done | bytes 1179680 | tf_op jit(solution)/shard_map/ppermute | solution.py:258
  182.3 2.5 collective-permute-done.14.refs_3_.refs_7_
  184.8 1.3 copy-done.24
  186.1 3.7 %shard_map.103.grad_gate.grads = bf16[384,768]{1,0:T(8,128)(2,1)S(1)} custom-call(s32[1]{0:T(128)} %bitcast.place, bf16[384,3072]{1,0:T(8,128)(2,1)S(1)} %get-tuple-element.49.rows, f32[384,768]{1,0:T(8,128)S(1)} %copy-done.24, bf16[768,768]{1,0:T(8,128)(2,1)S(1)} %bitcast.42, bf16[768,768]{1,0:T(8,128)(2,1)S(1)} %collective-permute-done.12.refs_1_.refs_5_, ...), custom_call_target="tpu_custom_call" | custom-call | tf_op jit(solution)/shard_map/pallas_call | solution.py:32
  189.9 5.6 %shard_map.104 = (bf16[48,3072]{1,0:T(8,128)(2,1)S(1)}, bf16[48,3072]{1,0:T(8,128)(2,1)S(1)}, bf16[48,3072]{1,0:T(8,128)(2,1)S(1)}, bf16[48,3072]{1,0:T(8,128)(2...) custom-call(s32[1]{0:T(128)} %bitcast.place, ...), custom_call_target="tpu_custom_call" | custom-call | tf_op jit(solution)/shard_map/pallas_call | solution.py:32
  195.6 3.6 %shard_map.105 = (bf16[768,768]{1,0:T(8,128)(2,1)S(1)}, bf16[768,768]{1,0:T(8,128)(2,1)}, bf16[768,768]{1,0:T(8,128)(2,1)S(1)}, bf16[768,768]{1,0:T(8,128)(2,1)S(1)}) custom-call(s32[1]{0:T(128)} %bitcast.place, bf16[384,768]{1,0:T(8,128)(2,1)S(1)} %shard_map.103.grad_gate.grads, bf16[384,3072]{1,0:T(8,128)(2,1)S(1)} %get-tuple-element.49.rows), custom_call_target="tpu_custom_call" | custom-call | tf_op jit(solution)/shard_map/pallas_call | solution.py:32
  200.4 1.5 collective-permute-start.23
  201.9 2.6 collective-permute-start.15
  205.7 1.3 add_convert_fusion.1
  207.0 21.4 %collective-permute-done.23.refs_2_ = bf16[768,768]{1,0:T(8,128)(2,1)S(1)} collective-permute-done((bf16[768,768]{1,0:T(8,128)(2,1)S(1)}, bf16[768,768]{1,0:T(8,128)(2,1)S(1)}, u32[]{:S(2)}, u32[]{:S(2)}) %collective-permute-start.23) | collective-permute-done | bytes 1179680 | tf_op jit(solution)/shard_map/ppermute | solution.py:258
  229.4 1.5 collective-permute-start.24
  231.0 1.3 convolution_convert_fusion.2
  232.9 3.7 %collective-permute-start.27 = (bf16[128,3072]{1,0:T(8,128)(2,1)}, bf16[128,3072]{1,0:T(8,128)(2,1)S(1)}, u32[]{:S(2)}, u32[]{:S(2)}) collective-permute-start(bf16[128,3072]{1,0:T(8,128)(2,1)} %convolution_convert_fusion.2), channel_id=1, source_target_pairs={{0,4},{1,5},{2,6},{3,7},{4,0},{5,1},{6,2},{7,3},{8,12},{9,13},{10,... | collective-permute-start | bytes 2359304 | tf_op jit(solution)/shard_map/ppermute | solution.py:348
  236.6 1.2 collective-permute-start.25
  237.8 1.7 collective-permute-start.18
  239.5 1.3 copy-done.18
  240.8 1.3 copy-done.22
  242.1 7.0 %shard_map.107 = (bf16[2,1,768,768]{3,2,1,0:T(8,128)(2,1)}, bf16[2,1,768,768]{3,2,1,0:T(8,128)(2,1)}, bf16[2,1,768,768]{3,2,1,0:T(8,128)(2,1)}) custom-call(bf16[768,768]{1,0:T(8,128)(2,1)S(1)} %copy-done.16, bf16[768,768]{1,0:T(8,128)(2,1)S(1)} %copy-done.18, bf16[768,768]{1,0:T(8,128)(2,1)S(1)} %copy-done.22, bf16[768,768]{1,0:T(8,128)(2,1)S(1)} %bitcast.44, ...), custom_call_target="tpu_custom_call" | custom-call | tf_op jit(solution)/shard_map/pallas_call | solution.py:212
  249.0 8.0 %collective-permute-done.24.refs_2_ = bf16[768,768]{1,0:T(8,128)(2,1)} collective-permute-done((bf16[768,768]{1,0:T(8,128)(2,1)}, bf16[768,768]{1,0:T(8,128)(2,1)}, u32[]{:S(2)}, u32[]{:S(2)}) %collective-permute-start.24) | collective-permute-done | bytes 1179680 | tf_op jit(solution)/shard_map/ppermute | solution.py:258
  257.1 7.5 %shard_map.108 = (bf16[2,1,768,768]{3,2,1,0:T(8,128)(2,1)}, bf16[2,1,768,768]{3,2,1,0:T(8,128)(2,1)}, bf16[2,1,768,768]{3,2,1,0:T(8,128)(2,1)}) custom-call(bf16[768,768]{1,0:T(8,128)(2,1)S(1)} %copy-done.20, bf16[768,768]{1,0:T(8,128)(2,1)} %collective-permute-done.19.refs_1_, ...), custom_call_target="tpu_custom_call", output_to_operand_aliasing={{0}: (6, {}), {1}: (7, {}), {2}: (8, {})} | custom-call | tf_op jit(solution)/shard_map/pallas_call | solution.py:212
  265.7 4.8 %collective-permute-done.27 = bf16[128,3072]{1,0:T(8,128)(2,1)S(1)} collective-permute-done((bf16[128,3072]{1,0:T(8,128)(2,1)}, bf16[128,3072]{1,0:T(8,128)(2,1)S(1)}, u32[]{:S(2)}, u32[]{:S(2)}) %collective-permute-start.27) | collective-permute-done | bytes 786464 | tf_op jit(solution)/shard_map/ppermute | solution.py:348
  270.5 1.3 add_convert_fusion.2
  (150 shorter events, 26.1 us)
Async XLA Ops:
  0.6 9.2 %collective-permute-start = (s32[128,2]{0,1:T(2,128)}, s32[128,2]{0,1:T(2,128)S(1)}, u32[]{:S(2)}, u32[]{:S(2)}) collective-permute-start(s32[128,2]{0,1:T(2,128)} %param.8), channel_id=1, source_target_pairs={{0,4},{1,5},{2,6},{3,7},{4,0},{5,1},{6,2},{7,3},{8,12},{9,13},{10,... | collective-permute-start | bytes 3080 | tf_op jit(solution)/shard_map/ppermute | solution.py:282
  4.7 49.7 %collective-permute-start.1 = (bf16[128,3072]{1,0:T(8,128)(2,1)}, bf16[128,3072]{1,0:T(8,128)(2,1)S(1)}, u32[]{:S(2)}, u32[]{:S(2)}) collective-permute-start(bf16[128,3072]{1,0:T(8,128)(2,1)} %param.7), channel_id=1, source_target_pairs={{0,4},{1,5},{2,6},{3,7},{4,0},{5,1},{6,2},{7,3},{8,12},{9,13},{10,... | collective-permute-start | bytes 2359304 | tf_op jit(solution)/shard_map/ppermute | solution.py:281
  10.6 49.6 %copy-start.40 = (pred[192,128]{1,0:T(8,128)(4,1)}, pred[192,128]{1,0:T(8,128)(4,1)S(1)}, u32[]{:S(2)}) copy-start(pred[192,128]{1,0:T(8,128)(4,1)S(1)} %get-tuple-element.89) | copy-start | bytes 73732
  11.2 20.0 %copy-start.35 = (bf16[2,8,96,768]{3,2,1,0:T(8,128)(2,1)S(1)}, bf16[2,8,96,768]{3,2,1,0:T(8,128)(2,1)}, u32[]{:S(2)}) copy-start(bf16[2,8,96,768]{3,2,1,0:T(8,128)(2,1)} %param.11) | copy-start | bytes 7077892
  12.1 42.3 %collective-permute-start.3 = (bf16[48,3840]{1,0:T(8,128)(2,1)S(1)}, bf16[48,3840]{1,0:T(8,128)(2,1)}, u32[]{:S(2)}, u32[]{:S(2)}) collective-permute-start(bf16[48,3840]{1,0:T(8,128)(2,1)S(1)} %get-tuple-element.93), channel_id=1, source_target_pairs={{0,1},{1,2},{2,3},{3,0},{4,5},{5,6},{6,7},{7,4},{8,9},{9,10},{10,1... | collective-permute-start | bytes 1105928 | tf_op jit(solution)/shard_map/ppermute | solution.py:255
  13.8 40.6 %collective-permute-start.4 = (bf16[48,3840]{1,0:T(8,128)(2,1)S(1)}, bf16[48,3840]{1,0:T(8,128)(2,1)}, u32[]{:S(2)}, u32[]{:S(2)}) collective-permute-start(bf16[48,3840]{1,0:T(8,128)(2,1)S(1)} %get-tuple-element.94), channel_id=1, source_target_pairs={{0,2},{1,3},{2,0},{3,1},{4,6},{5,7},{6,4},{7,5},{8,10},{9,11},{10,... | collective-permute-start | bytes 1105928 | tf_op jit(solution)/shard_map/ppermute | solution.py:255
  15.4 39.0 %collective-permute-start.5 = (bf16[48,3840]{1,0:T(8,128)(2,1)S(1)}, bf16[48,3840]{1,0:T(8,128)(2,1)}, u32[]{:S(2)}, u32[]{:S(2)}) collective-permute-start(bf16[48,3840]{1,0:T(8,128)(2,1)S(1)} %get-tuple-element.95), channel_id=1, source_target_pairs={{0,3},{1,0},{2,1},{3,2},{4,7},{5,4},{6,5},{7,6},{8,11},{9,8},{10,9... | collective-permute-start | bytes 1105928 | tf_op jit(solution)/shard_map/ppermute | solution.py:255
  17.1 37.3 %collective-permute-start.2 = (bf16[4,48,768]{2,1,0:T(8,128)(2,1)S(1)}, bf16[4,48,768]{2,1,0:T(8,128)(2,1)S(1)}, u32[]{:S(2)}, u32[]{:S(2)}) collective-permute-start(bf16[4,48,768]{2,1,0:T(8,128)(2,1)S(1)} %bitcast.54), channel_id=1, source_target_pairs={{0,4},{1,5},{2,6},{3,7},{4,0},{5,1},{6,2},{7,3},{8,12},{9,13},{10,... | collective-permute-start | bytes 884744 | tf_op jit(solution)/shard_map/ppermute | solution.py:296
  54.4 60.1 %all-to-all-start = ((bf16[8,2,96,768]{3,2,1,0:T(8,128)(2,1)}), bf16[8,2,96,768]{3,2,1,0:T(8,128)(2,1)S(1)}, u32[]{:S(2)}, u32[]{:S(2)}) async-start(bf16[8,2,96,768]{3,2,1,0:T(8,128)(2,1)} %bitcast.39), calls=%async_computation | async-start | bytes 4718592 | tf_op jit(solution)/shard_map/all_to_all | solution.py:266
  61.5 45.9 %collective-permute-start.8 = (bf16[48,3840]{1,0:T(8,128)(2,1)S(1)}, bf16[48,3840]{1,0:T(8,128)(2,1)}, u32[]{:S(2)}, u32[]{:S(2)}) collective-permute-start(bf16[48,3840]{1,0:T(8,128)(2,1)S(1)} %get-tuple-element.96), channel_id=1, source_target_pairs={{0,3},{1,0},{2,1},{3,2},{4,7},{5,4},{6,5},{7,6},{8,11},{9,8},{10,9... | collective-permute-start | bytes 1105928 | tf_op jit(solution)/shard_map/ppermute | solution.py:255
  64.4 42.9 %collective-permute-start.6 = (bf16[48,3840]{1,0:T(8,128)(2,1)S(1)}, bf16[48,3840]{1,0:T(8,128)(2,1)}, u32[]{:S(2)}, u32[]{:S(2)}) collective-permute-start(bf16[48,3840]{1,0:T(8,128)(2,1)S(1)} %get-tuple-element.98), channel_id=1, source_target_pairs={{0,1},{1,2},{2,3},{3,0},{4,5},{5,6},{6,7},{7,4},{8,9},{9,10},{10,1... | collective-permute-start | bytes 1105928 | tf_op jit(solution)/shard_map/ppermute | solution.py:255
  64.4 50.1 %collective-permute-start.7 = (bf16[48,3840]{1,0:T(8,128)(2,1)S(1)}, bf16[48,3840]{1,0:T(8,128)(2,1)}, u32[]{:S(2)}, u32[]{:S(2)}) collective-permute-start(bf16[48,3840]{1,0:T(8,128)(2,1)S(1)} %get-tuple-element.99), channel_id=1, source_target_pairs={{0,2},{1,3},{2,0},{3,1},{4,6},{5,7},{6,4},{7,5},{8,10},{9,11},{10,... | collective-permute-start | bytes 1105928 | tf_op jit(solution)/shard_map/ppermute | solution.py:255
  115.9 57.5 %all-to-all-start.1 = ((bf16[8,2,96,768]{3,2,1,0:T(8,128)(2,1)}), bf16[8,2,96,768]{3,2,1,0:T(8,128)(2,1)}, u32[]{:S(2)}, u32[]{:S(2)}) async-start(bf16[8,2,96,768]{3,2,1,0:T(8,128)(2,1)} %bitcast.38), calls=%async_computation.1 | async-start | bytes 4718592 | tf_op jit(solution)/shard_map/all_to_all | solution.py:266
  122.9 5.8 %copy-start = (bf16[8,1,96,768]{3,2,1,0:T(8,128)(2,1)}, bf16[8,1,96,768]{3,2,1,0:T(8,128)(2,1)S(1)}, u32[]{:S(2)}) copy-start(bf16[8,1,96,768]{3,2,1,0:T(8,128)(2,1)S(1)} %get-tuple-element.91) | copy-start | bytes 3538948
  122.9 25.8 %collective-permute-start.10 = (bf16[768,768]{1,0:T(8,128)(2,1)S(1)}, bf16[768,768]{1,0:T(8,128)(2,1)S(1)}, u32[]{:S(2)}, u32[]{:S(2)}) collective-permute-start(bf16[768,768]{1,0:T(8,128)(2,1)S(1)} %bitcast.45), channel_id=1, source_target_pairs={{0,16},{8,24},{16,0},{24,8},{1,17},{9,25},{17,1},{25,9},{2,18},{10... | collective-permute-start | bytes 3538952 | tf_op jit(solution)/shard_map/ppermute | solution.py:258
  124.4 27.1 %copy-start.13 = (bf16[48,3840]{1,0:T(8,128)(2,1)S(1)}, bf16[48,3840]{1,0:T(8,128)(2,1)}, u32[]{:S(2)}) copy-start(bf16[48,3840]{1,0:T(8,128)(2,1)} %get-tuple-element.92.refs_4_) | copy-start | bytes 1105924
  128.6 27.0 %collective-permute-start.9 = (bf16[768,768]{1,0:T(8,128)(2,1)S(1)}, bf16[768,768]{1,0:T(8,128)(2,1)S(1)}, u32[]{:S(2)}, u32[]{:S(2)}) collective-permute-start(bf16[768,768]{1,0:T(8,128)(2,1)S(1)} %bitcast.46), channel_id=1, source_target_pairs={{0,8},{8,0},{16,24},{24,16},{1,9},{9,1},{17,25},{25,17},{2,10},{10... | collective-permute-start | bytes 3538952 | tf_op jit(solution)/shard_map/ppermute | solution.py:258
  148.7 7.0 %collective-permute-start.11 = (bf16[768,768]{1,0:T(8,128)(2,1)S(1)}, bf16[768,768]{1,0:T(8,128)(2,1)S(1)}, u32[]{:S(2)}, u32[]{:S(2)}) collective-permute-start(bf16[768,768]{1,0:T(8,128)(2,1)S(1)} %collective-permute-done.10.refs_11_.refs_2_), channel_id=1, source_target_pairs={{0,8},{8,0},{16,24},{24,16},{1,9},{9,1},{17,25},{25,17},{2,10},{10... | collective-permute-start | bytes 3538952 | tf_op jit(solution)/shard_map/ppermute | solution.py:258
  153.3 28.5 %collective-permute-start.13 = (bf16[768,768]{1,0:T(8,128)(2,1)S(1)}, bf16[768,768]{1,0:T(8,128)(2,1)}, u32[]{:S(2)}, u32[]{:S(2)}) collective-permute-start(bf16[768,768]{1,0:T(8,128)(2,1)S(1)} %bitcast.40), channel_id=1, source_target_pairs={{0,16},{8,24},{16,0},{24,8},{1,17},{9,25},{17,1},{25,9},{2,18},{10... | collective-permute-start | bytes 3538952 | tf_op jit(solution)/shard_map/ppermute | solution.py:258
  155.7 8.0 %copy-start.7 = (bf16[768,768]{1,0:T(8,128)(2,1)}, bf16[768,768]{1,0:T(8,128)(2,1)S(1)}, u32[]{:S(2)}) copy-start(bf16[768,768]{1,0:T(8,128)(2,1)S(1)} %collective-permute-done.9.refs_10_.refs_1_) | copy-start | bytes 3538948
  155.7 8.0 %copy-start.9 = (bf16[768,768]{1,0:T(8,128)(2,1)}, bf16[768,768]{1,0:T(8,128)(2,1)S(1)}, u32[]{:S(2)}) copy-start(bf16[768,768]{1,0:T(8,128)(2,1)S(1)} %collective-permute-done.11.refs_12_.refs_3_) | copy-start | bytes 3538948
  173.4 59.6 %all-to-all-start.2 = ((bf16[8,2,96,768]{3,2,1,0:T(8,128)(2,1)}), bf16[8,2,96,768]{3,2,1,0:T(8,128)(2,1)}, u32[]{:S(2)}, u32[]{:S(2)}) async-start(bf16[8,2,96,768]{3,2,1,0:T(8,128)(2,1)} %bitcast.50), calls=%async_computation.2 | async-start | bytes 4718592 | tf_op jit(solution)/shard_map/all_to_all | solution.py:266
  178.5 3.8 %collective-permute-start.12 = (bf16[768,768]{1,0:T(8,128)(2,1)S(1)}, bf16[768,768]{1,0:T(8,128)(2,1)S(1)}, u32[]{:S(2)}, u32[]{:S(2)}) collective-permute-start(bf16[768,768]{1,0:T(8,128)(2,1)S(1)} %bitcast.41), channel_id=1, source_target_pairs={{0,8},{8,0},{16,24},{24,16},{1,9},{9,1},{17,25},{25,17},{2,10},{10... | collective-permute-start | bytes 3538952 | tf_op jit(solution)/shard_map/ppermute | solution.py:258
  181.8 3.1 %collective-permute-start.14 = (bf16[768,768]{1,0:T(8,128)(2,1)}, bf16[768,768]{1,0:T(8,128)(2,1)S(1)}, u32[]{:S(2)}, u32[]{:S(2)}) collective-permute-start(bf16[768,768]{1,0:T(8,128)(2,1)} %collective-permute-done.13.refs_2_.refs_6_), channel_id=1, source_target_pairs={{0,8},{8,0},{16,24},{24,16},{1,9},{9,1},{17,25},{25,17},{2,10},{10... | collective-permute-start | bytes 3538952 | tf_op jit(solution)/shard_map/ppermute | solution.py:258
  181.8 17.7 %collective-permute-start.22 = (bf16[768,768]{1,0:T(8,128)(2,1)}, bf16[768,768]{1,0:T(8,128)(2,1)S(1)}, u32[]{:S(2)}, u32[]{:S(2)}) collective-permute-start(bf16[768,768]{1,0:T(8,128)(2,1)} %copy-done.28), channel_id=1, source_target_pairs={{0,8},{8,0},{16,24},{24,16},{1,9},{9,1},{17,25},{25,17},{2,10},{10... | collective-permute-start | bytes 3538952 | tf_op jit(solution)/shard_map/ppermute | solution.py:258
  182.3 22.8 %collective-permute-start.21 = (bf16[768,768]{1,0:T(8,128)(2,1)}, bf16[768,768]{1,0:T(8,128)(2,1)S(1)}, u32[]{:S(2)}, u32[]{:S(2)}) collective-permute-start(bf16[768,768]{1,0:T(8,128)(2,1)} %copy-done.27), channel_id=1, source_target_pairs={{0,8},{8,0},{16,24},{24,16},{1,9},{9,1},{17,25},{25,17},{2,10},{10... | collective-permute-start | bytes 3538952 | tf_op jit(solution)/shard_map/ppermute | solution.py:258
  182.3 7.6 %copy-start.2 = (bf16[8,1,96,768]{3,2,1,0:T(8,128)(2,1)S(1)}, bf16[8,1,96,768]{3,2,1,0:T(8,128)(2,1)}, u32[]{:S(2)}) copy-start(bf16[8,1,96,768]{3,2,1,0:T(8,128)(2,1)} %copy-done) | copy-start | bytes 3538948
  182.3 7.6 %copy-start.6 = (bf16[768,768]{1,0:T(8,128)(2,1)S(1)}, bf16[768,768]{1,0:T(8,128)(2,1)}, u32[]{:S(2)}) copy-start(bf16[768,768]{1,0:T(8,128)(2,1)} %copy-done.4) | copy-start | bytes 3538948
  182.3 7.6 %copy-start.8 = (bf16[768,768]{1,0:T(8,128)(2,1)S(1)}, bf16[768,768]{1,0:T(8,128)(2,1)}, u32[]{:S(2)}) copy-start(bf16[768,768]{1,0:T(8,128)(2,1)} %copy-done.7) | copy-start | bytes 3538948
  182.3 7.6 %copy-start.10 = (bf16[768,768]{1,0:T(8,128)(2,1)S(1)}, bf16[768,768]{1,0:T(8,128)(2,1)}, u32[]{:S(2)}) copy-start(bf16[768,768]{1,0:T(8,128)(2,1)} %copy-done.9) | copy-start | bytes 3538948
  182.3 7.6 %copy-start.12 = (bf16[384,768]{1,0:T(8,128)(2,1)S(1)}, bf16[384,768]{1,0:T(8,128)(2,1)}, u32[]{:S(2)}) copy-start(bf16[384,768]{1,0:T(8,128)(2,1)} %copy-done.11) | copy-start | bytes 1769476
  199.3 6.4 %collective-permute-start.20 = (bf16[768,768]{1,0:T(8,128)(2,1)S(1)}, bf16[768,768]{1,0:T(8,128)(2,1)S(1)}, u32[]{:S(2)}, u32[]{:S(2)}) collective-permute-start(bf16[768,768]{1,0:T(8,128)(2,1)S(1)} %get-tuple-element.69), channel_id=1, source_target_pairs={{0,8},{8,0},{16,24},{24,16},{1,9},{9,1},{17,25},{25,17},{2,10},{10... | collective-permute-start | bytes 3538952 | tf_op jit(solution)/shard_map/ppermute | solution.py:258
  200.4 28.0 %collective-permute-start.23 = (bf16[768,768]{1,0:T(8,128)(2,1)S(1)}, bf16[768,768]{1,0:T(8,128)(2,1)S(1)}, u32[]{:S(2)}, u32[]{:S(2)}) collective-permute-start(bf16[768,768]{1,0:T(8,128)(2,1)S(1)} %add_convert_fusion), channel_id=1, source_target_pairs={{0,16},{8,24},{16,0},{24,8},{1,17},{9,25},{17,1},{25,9},{2,18},{10... | collective-permute-start | bytes 3538952 | tf_op jit(solution)/shard_map/ppermute | solution.py:258
  201.9 29.1 %collective-permute-start.15 = (bf16[48,3072]{1,0:T(8,128)(2,1)S(1)}, bf16[48,3072]{1,0:T(8,128)(2,1)S(1)}, u32[]{:S(2)}, u32[]{:S(2)}) collective-permute-start(bf16[48,3072]{1,0:T(8,128)(2,1)S(1)} %get-tuple-element.56), channel_id=1, source_target_pairs={{0,3},{1,0},{2,1},{3,2},{4,7},{5,4},{6,5},{7,6},{8,11},{9,8},{10,9... | collective-permute-start | bytes 884744 | tf_op jit(solution)/shard_map/ppermute | solution.py:255
  204.5 26.5 %collective-permute-start.16 = (bf16[48,3072]{1,0:T(8,128)(2,1)S(1)}, bf16[48,3072]{1,0:T(8,128)(2,1)S(1)}, u32[]{:S(2)}, u32[]{:S(2)}) collective-permute-start(bf16[48,3072]{1,0:T(8,128)(2,1)S(1)} %get-tuple-element.57), channel_id=1, source_target_pairs={{0,2},{1,3},{2,0},{3,1},{4,6},{5,7},{6,4},{7,5},{8,10},{9,11},{10,... | collective-permute-start | bytes 884744 | tf_op jit(solution)/shard_map/ppermute | solution.py:255
  205.1 25.9 %collective-permute-start.17 = (bf16[48,3072]{1,0:T(8,128)(2,1)S(1)}, bf16[48,3072]{1,0:T(8,128)(2,1)S(1)}, u32[]{:S(2)}, u32[]{:S(2)}) collective-permute-start(bf16[48,3072]{1,0:T(8,128)(2,1)S(1)} %get-tuple-element.58), channel_id=1, source_target_pairs={{0,1},{1,2},{2,3},{3,0},{4,5},{5,6},{6,7},{7,4},{8,9},{9,10},{10,1... | collective-permute-start | bytes 884744 | tf_op jit(solution)/shard_map/ppermute | solution.py:255
  205.6 32.2 %collective-permute-start.19 = (bf16[768,768]{1,0:T(8,128)(2,1)}, bf16[768,768]{1,0:T(8,128)(2,1)}, u32[]{:S(2)}, u32[]{:S(2)}) collective-permute-start(bf16[768,768]{1,0:T(8,128)(2,1)} %get-tuple-element.67), channel_id=1, source_target_pairs={{0,8},{8,0},{16,24},{24,16},{1,9},{9,1},{17,25},{25,17},{2,10},{10... | collective-permute-start | bytes 3538952 | tf_op jit(solution)/shard_map/ppermute | solution.py:258
  205.6 25.3 %copy-start.41 = (pred[192,128]{1,0:T(8,128)(4,1)S(1)}, pred[192,128]{1,0:T(8,128)(4,1)}, u32[]{:S(2)}) copy-start(pred[192,128]{1,0:T(8,128)(4,1)} %copy-done.40) | copy-start | bytes 73732
  207.0 32.6 %copy-start.16 = (bf16[768,768]{1,0:T(8,128)(2,1)S(1)}, bf16[768,768]{1,0:T(8,128)(2,1)}, u32[]{:S(2)}) copy-start(bf16[768,768]{1,0:T(8,128)(2,1)} %copy-done.15) | copy-start | bytes 3538948
  229.4 27.6 %collective-permute-start.24 = (bf16[768,768]{1,0:T(8,128)(2,1)}, bf16[768,768]{1,0:T(8,128)(2,1)}, u32[]{:S(2)}, u32[]{:S(2)}) collective-permute-start(bf16[768,768]{1,0:T(8,128)(2,1)} %add_convert_fusion.1), channel_id=1, source_target_pairs={{0,16},{8,24},{16,0},{24,8},{1,17},{9,25},{17,1},{25,9},{2,18},{10... | collective-permute-start | bytes 3538952 | tf_op jit(solution)/shard_map/ppermute | solution.py:258
  232.3 24.8 %copy-start.3 = (bf16[8,1,96,768]{3,2,1,0:T(8,128)(2,1)S(1)}, bf16[8,1,96,768]{3,2,1,0:T(8,128)(2,1)}, u32[]{:S(2)}) copy-start(bf16[8,1,96,768]{3,2,1,0:T(8,128)(2,1)} %copy-done) | copy-start | bytes 3538948
  232.9 37.5 %collective-permute-start.27 = (bf16[128,3072]{1,0:T(8,128)(2,1)}, bf16[128,3072]{1,0:T(8,128)(2,1)S(1)}, u32[]{:S(2)}, u32[]{:S(2)}) collective-permute-start(bf16[128,3072]{1,0:T(8,128)(2,1)} %convolution_convert_fusion.2), channel_id=1, source_target_pairs={{0,4},{1,5},{2,6},{3,7},{4,0},{5,1},{6,2},{7,3},{8,12},{9,13},{10,... | collective-permute-start | bytes 2359304 | tf_op jit(solution)/shard_map/ppermute | solution.py:348
  236.6 28.0 %collective-permute-start.26 = (bf16[48,3072]{1,0:T(8,128)(2,1)}, bf16[48,3072]{1,0:T(8,128)(2,1)S(1)}, u32[]{:S(2)}, u32[]{:S(2)}) collective-permute-start(bf16[48,3072]{1,0:T(8,128)(2,1)} %copy-done.33), channel_id=1, source_target_pairs={{0,1},{1,2},{2,3},{3,0},{4,5},{5,6},{6,7},{7,4},{8,9},{9,10},{10,1... | collective-permute-start | bytes 884744 | tf_op jit(solution)/shard_map/ppermute | solution.py:255
  236.6 28.0 %collective-permute-start.25 = (bf16[48,3072]{1,0:T(8,128)(2,1)}, bf16[48,3072]{1,0:T(8,128)(2,1)S(1)}, u32[]{:S(2)}, u32[]{:S(2)}) collective-permute-start(bf16[48,3072]{1,0:T(8,128)(2,1)} %copy-done.32), channel_id=1, source_target_pairs={{0,2},{1,3},{2,0},{3,1},{4,6},{5,7},{6,4},{7,5},{8,10},{9,11},{10,... | collective-permute-start | bytes 884744 | tf_op jit(solution)/shard_map/ppermute | solution.py:255
  237.8 27.9 %collective-permute-start.18 = (bf16[48,3072]{1,0:T(8,128)(2,1)}, bf16[48,3072]{1,0:T(8,128)(2,1)S(1)}, u32[]{:S(2)}, u32[]{:S(2)}) collective-permute-start(bf16[48,3072]{1,0:T(8,128)(2,1)} %copy-done.31), channel_id=1, source_target_pairs={{0,3},{1,0},{2,1},{3,2},{4,7},{5,4},{6,5},{7,6},{8,11},{9,8},{10,9... | collective-permute-start | bytes 884744 | tf_op jit(solution)/shard_map/ppermute | solution.py:255
  242.1 15.0 %copy-start.20 = (bf16[768,768]{1,0:T(8,128)(2,1)S(1)}, bf16[768,768]{1,0:T(8,128)(2,1)}, u32[]{:S(2)}) copy-start(bf16[768,768]{1,0:T(8,128)(2,1)} %copy-done.19) | copy-start | bytes 3538948
  257.1 13.4 %copy-start.30 = (bf16[48,3072]{1,0:T(8,128)(2,1)S(1)}, bf16[48,3072]{1,0:T(8,128)(2,1)}, u32[]{:S(2)}) copy-start(bf16[48,3072]{1,0:T(8,128)(2,1)} %copy-done.29) | copy-start | bytes 884740
  257.1 13.4 %copy-start.39 = (pred[192,128]{1,0:T(8,128)(4,1)S(1)}, pred[192,128]{1,0:T(8,128)(4,1)}, u32[]{:S(2)}) copy-start(pred[192,128]{1,0:T(8,128)(4,1)} %copy-done.38) | copy-start | bytes 73732
  (25 other events, 52.2 us)
